TPU v7x, 256 devices: a whole 4x4x8 slice. The times are simulated.
256 devices in a mesh: wide: 128 (over z, y, x), narrow: 2 (over core).
Axes of the slice: x: 4, y: 4, z: 8, core: 2. Of those that a mesh axis runs over, the one named last changes fastest.
Arguments:
- rhs: float32 [3072, 64, 128], P(('wide', 'narrow')), may hold values from -8 to 8
- pivot_inv: float32 [3072, 128, 128], P(('wide', 'narrow')), may hold values from -0.5 to 0.5
- lower_gain: float32 [3072, 128, 128], P(('wide', 'narrow')), may hold values from -1 to 1
- upper_gain: float32 [3072, 128, 128], P(('wide', 'narrow')), may hold values from -1 to 1
Outputs:
- solution: float32 [3072, 64, 128], P(('wide', 'narrow'))
All inputs are finite; a program needn't handle non-finite values.
Results may differ from a plain program's by a relative error of at most 0.0003.
Values sent between devices are 32-bit elements; how exact they have to be, the bound alone decides.
No kernel may reach another device: no remote copies, remote signals or barrier semaphores. Data moves between devices by JAX's collectives and lax.ppermute only.
A program may use at most 128 MiB of HBM per device.

v0:
```python
import jax
import jax.numpy as jnp
from jax import lax
from jax.experimental import pallas as pl
from jax.experimental.pallas import tpu as pltpu
from jax.sharding import PartitionSpec as P

AXES = ("wide", "narrow")
B = 128
R = 64
PACK = 3 * B + 2 * R


def halves(value):
    high = value.astype(jnp.bfloat16)
    low = (value - high.astype(jnp.float32)).astype(jnp.bfloat16)
    return high, low


def left_side(value):
    return jnp.concatenate(halves(value), axis=1)


def right_side(value):
    both = jnp.concatenate(halves(value), axis=1)
    return jnp.concatenate([both, both], axis=0)


def times(left, right):
    wide = jnp.dot(left, right, preferred_element_type=jnp.float32)
    return wide[:, :B] + wide[:, B:]


def mm(left, right):
    return times(left_side(left), right_side(right))


def local_kernel(rhs, pivot_inv, lower, upper, pack, rows, forward):
    count = rhs.shape[0]
    scaled = [mm(rhs[i], pivot_inv[i]) for i in range(count)]
    state = jnp.concatenate([-lower[0], scaled[0]], axis=0)
    forward[0] = state
    for i in range(1, count):
        moved = mm(state, lower[i])
        state = jnp.concatenate([-moved[:B], scaled[i] - moved[B:]], axis=0)
        forward[i] = state
    pack[: B + R] = state
    state = jnp.concatenate([-upper[count - 1], state], axis=0)
    rows[count - 1] = state
    for i in range(count - 2, -1, -1):
        moved = mm(state, upper[i])
        state = jnp.concatenate([-moved[:B], forward[i] - moved[B:]], axis=0)
        rows[i] = state
    pack[B + R :] = state


def local(rhs, pivot_inv, lower, upper):
    count = rhs.shape[0]
    return pl.pallas_call(
        local_kernel,
        out_shape=(
            jax.ShapeDtypeStruct((PACK, B), jnp.float32),
            jax.ShapeDtypeStruct((count, 2 * B + R, B), jnp.float32),
        ),
        in_specs=[pl.BlockSpec(memory_space=pltpu.VMEM)] * 4,
        out_specs=[pl.BlockSpec(memory_space=pltpu.VMEM)] * 2,
        scratch_shapes=[pltpu.VMEM((count, B + R, B), jnp.float32)],
        compiler_params=pltpu.CompilerParams(vmem_limit_bytes=40 * 2**20),
        name="local",
    )(rhs, pivot_inv, lower, upper)


def position():
    return lax.axis_index(AXES[0]) * lax.axis_size(AXES[1]) + lax.axis_index(AXES[1])


def join_kernel(level, own, other, pack):
    left = (position() >> level) & 1 == 0

    def join(first, second):
        early = left_side(first[: B + R])
        down = times(early, right_side(second[:B]))
        pack[:B] = down[:B]
        pack[B : B + R] = down[B:] + second[B : B + R]
        turn = times(early, right_side(second[2 * B + R : 3 * B + R]))
        back = jnp.concatenate(
            [second[B + R : 2 * B + R], turn[:B], turn[B:] + second[3 * B + R :]], axis=0
        )
        up = mm(back, first[B + R : 2 * B + R])
        pack[B + R : 2 * B + R] = up[:B]
        pack[2 * B + R :] = up[B:] + first[2 * B + R :]

    @pl.when(left)
    def _():
        join(own, other)

    @pl.when(jnp.logical_not(left))
    def _():
        join(other, own)


def join(level, own, other):
    return pl.pallas_call(
        lambda *refs: join_kernel(level, *refs),
        out_shape=jax.ShapeDtypeStruct((PACK, B), jnp.float32),
        in_specs=[pl.BlockSpec(memory_space=pltpu.VMEM)] * 2,
        out_specs=pl.BlockSpec(memory_space=pltpu.VMEM),
        name=f"join{level}",
    )(own, other)


def finish_kernel(levels, *refs):
    rows, out = refs[2 * levels], refs[2 * levels + 1]
    ahead = jnp.zeros((R, B), jnp.float32)
    behind = jnp.zeros((R, B), jnp.float32)
    for level in range(levels - 1, -1, -1):
        own, other = refs[level], refs[levels + level]
        left = (position() >> level) & 1 == 0
        pick = lambda low, high: jnp.where(left, own[low:high], other[low:high])
        skip = lambda low, high: jnp.where(left, other[low:high], own[low:high])
        middle = mm(behind, pick(0, B)) + pick(B, B + R)
        moved = (
            mm(ahead, skip(B + R, 2 * B + R))
            + mm(middle, skip(2 * B + R, 3 * B + R))
            + skip(3 * B + R, PACK)
        )
        ahead = jnp.where(left, moved, ahead)
        behind = jnp.where(left, behind, middle)
    ahead, behind = left_side(ahead), left_side(behind)
    for i in range(out.shape[0]):
        out[i] = (
            rows[i, 2 * B :]
            + times(ahead, right_side(rows[i, :B]))
            + times(behind, right_side(rows[i, B : 2 * B]))
        )


def finish(owns, others, rows):
    levels = len(owns)
    return pl.pallas_call(
        lambda *refs: finish_kernel(levels, *refs),
        out_shape=jax.ShapeDtypeStruct((rows.shape[0], R, B), jnp.float32),
        in_specs=[pl.BlockSpec(memory_space=pltpu.VMEM)] * (2 * levels + 1),
        out_specs=pl.BlockSpec(memory_space=pltpu.VMEM),
        compiler_params=pltpu.CompilerParams(vmem_limit_bytes=40 * 2**20),
        name="finish",
    )(*owns, *others, rows)


def on_device(rhs, pivot_inv, lower_gain, upper_gain):
    devices = lax.axis_size(AXES)
    levels = devices.bit_length() - 1
    pack, rows = local(rhs, pivot_inv, lower_gain, upper_gain)
    owns, others = [], []
    for level in range(levels):
        other = lax.ppermute(pack, AXES, [(i, i ^ (1 << level)) for i in range(devices)])
        owns.append(pack)
        others.append(other)
        if level < levels - 1:
            pack = join(level, pack, other)
    return finish(owns, others, rows)


def solution(mesh):
    placed = P(AXES, None, None)
    return jax.shard_map(
        on_device,
        mesh=mesh,
        in_specs=(placed,) * 4,
        out_specs=placed,
        check_vma=False,
    )
```

profile of v0, /device:TPU:98, one launch (start us, length us, event | category | flops | bytes accessed | tf_op | source)
XLA Modules:
  0.0 103.3 jit_solution(1539045510214876330)
XLA Ops:
  0.0 1.1 %copy-done.17 = f32[12,128,128]{2,1,0:T(8,128)S(1)} copy-done((f32[12,128,128]{2,1,0:T(8,128)S(1)}, f32[12,128,128]{2,1,0:T(8,128)}, u32[]{:S(2)}) %copy-start.17) | copy-done | bytes 786456
  1.1 1.1 %copy-done.18 = f32[12,128,128]{2,1,0:T(8,128)S(1)} copy-done((f32[12,128,128]{2,1,0:T(8,128)S(1)}, f32[12,128,128]{2,1,0:T(8,128)}, u32[]{:S(2)}) %copy-start.18) | copy-done | bytes 786456
  2.3 1.1 %copy-done.19 = f32[12,128,128]{2,1,0:T(8,128)S(1)} copy-done((f32[12,128,128]{2,1,0:T(8,128)S(1)}, f32[12,128,128]{2,1,0:T(8,128)}, u32[]{:S(2)}) %copy-start.19) | copy-done | bytes 786456
  3.4 1.0 copy-done.20
  4.4 3.0 %local.1 = (f32[512,128]{1,0:T(8,128)S(1)}, f32[12,320,128]{2,1,0:T(8,128)S(1)}) custom-call(f32[12,64,128]{2,1,0:T(8,128)S(1)} %copy-done.20, f32[12,128,128]{2,1,0:T(8,128)S(1)} %copy-done.17, f32[12,128,128]{2,1,0:T(8,128)S(1)} %copy-done.18, f32[12,128,128]{2,1,0:T(8,128)S(1)} %copy-done.19), custom_call_target="tpu_custom_call" | custom-call | tf_op jit(solution)/shard_map/local/pallas_call | solution.py:59
  7.6 1.5 %collective-permute-done.refs_1_.refs_8_ = f32[512,128]{1,0:T(8,128)S(1)} collective-permute-done((f32[512,128]{1,0:T(8,128)S(1)}, f32[512,128]{1,0:T(8,128)S(1)}, u32[]{:S(2)}, u32[]{:S(2)}) %collective-permute-start) | collective-permute-done | bytes 262176 | tf_op jit(solution)/shard_map/ppermute | solution.py:156
  9.8 2.1 %join0.1.refs_0_.refs_1_ = f32[512,128]{1,0:T(8,128)} custom-call(f32[512,128]{1,0:T(8,128)} %copy-done.6, f32[512,128]{1,0:T(8,128)} %copy-done.8), custom_call_target="tpu_custom_call" | custom-call | tf_op jit(solution)/shard_map/join0/pallas_call | solution.py:103
  12.4 8.0 %collective-permute-done.1.refs_1_.refs_9_ = f32[512,128]{1,0:T(8,128)S(1)} collective-permute-done((f32[512,128]{1,0:T(8,128)}, f32[512,128]{1,0:T(8,128)S(1)}, u32[]{:S(2)}, u32[]{:S(2)}) %collective-permute-start.1) | collective-permute-done | bytes 262176 | tf_op jit(solution)/shard_map/ppermute | solution.py:156
  21.1 2.1 %join1.1.refs_0_.refs_2_ = f32[512,128]{1,0:T(8,128)} custom-call(f32[512,128]{1,0:T(8,128)} %join0.1.refs_0_.refs_1_, f32[512,128]{1,0:T(8,128)} %copy-done.10), custom_call_target="tpu_custom_call" | custom-call | tf_op jit(solution)/shard_map/join1/pallas_call | solution.py:103
  23.2 2.2 %collective-permute-start.2 = (f32[512,128]{1,0:T(8,128)}, f32[512,128]{1,0:T(8,128)S(1)}, u32[]{:S(2)}, u32[]{:S(2)}) collective-permute-start(f32[512,128]{1,0:T(8,128)} %join1.1.refs_0_.refs_2_), channel_id=1, source_target_pairs={{0,4},{1,5},{2,6},{3,7},{4,0},{5,1},{6,2},{7,3},{8,12},{9,13},{10,... | collective-permute-start | bytes 786440 | tf_op jit(solution)/shard_map/ppermute | solution.py:156
  25.4 7.1 %collective-permute-done.2.refs_1_.refs_10_ = f32[512,128]{1,0:T(8,128)S(1)} collective-permute-done((f32[512,128]{1,0:T(8,128)}, f32[512,128]{1,0:T(8,128)S(1)}, u32[]{:S(2)}, u32[]{:S(2)}) %collective-permute-start.2) | collective-permute-done | bytes 262176 | tf_op jit(solution)/shard_map/ppermute | solution.py:156
  33.2 2.1 %join2.1.refs_0_.refs_3_ = f32[512,128]{1,0:T(8,128)} custom-call(f32[512,128]{1,0:T(8,128)} %join1.1.refs_0_.refs_2_, f32[512,128]{1,0:T(8,128)} %copy-done.12), custom_call_target="tpu_custom_call" | custom-call | tf_op jit(solution)/shard_map/join2/pallas_call | solution.py:103
  35.3 1.6 %collective-permute-start.3 = (f32[512,128]{1,0:T(8,128)}, f32[512,128]{1,0:T(8,128)S(1)}, u32[]{:S(2)}, u32[]{:S(2)}) collective-permute-start(f32[512,128]{1,0:T(8,128)} %join2.1.refs_0_.refs_3_), channel_id=1, source_target_pairs={{0,8},{1,9},{2,10},{3,11},{4,12},{5,13},{6,14},{7,15},{8,0},{9,1},... | collective-permute-start | bytes 786440 | tf_op jit(solution)/shard_map/ppermute | solution.py:156
  36.9 5.2 %collective-permute-done.3.refs_1_.refs_11_ = f32[512,128]{1,0:T(8,128)S(1)} collective-permute-done((f32[512,128]{1,0:T(8,128)}, f32[512,128]{1,0:T(8,128)S(1)}, u32[]{:S(2)}, u32[]{:S(2)}) %collective-permute-start.3) | collective-permute-done | bytes 262176 | tf_op jit(solution)/shard_map/ppermute | solution.py:156
  42.1 0.7 copy-done.14
  42.8 2.1 %join3.1.refs_0_.refs_4_ = f32[512,128]{1,0:T(8,128)} custom-call(f32[512,128]{1,0:T(8,128)} %join2.1.refs_0_.refs_3_, f32[512,128]{1,0:T(8,128)} %copy-done.14), custom_call_target="tpu_custom_call" | custom-call | tf_op jit(solution)/shard_map/join3/pallas_call | solution.py:103
  44.9 3.2 %collective-permute-start.4 = (f32[512,128]{1,0:T(8,128)}, f32[512,128]{1,0:T(8,128)}, u32[]{:S(2)}, u32[]{:S(2)}) collective-permute-start(f32[512,128]{1,0:T(8,128)} %join3.1.refs_0_.refs_4_), channel_id=1, source_target_pairs={{0,16},{1,17},{2,18},{3,19},{4,20},{5,21},{6,22},{7,23},{8,24},{9,... | collective-permute-start | bytes 786440 | tf_op jit(solution)/shard_map/ppermute | solution.py:156
  48.1 5.0 %collective-permute-done.4.refs_1_.refs_12_ = f32[512,128]{1,0:T(8,128)} collective-permute-done((f32[512,128]{1,0:T(8,128)}, f32[512,128]{1,0:T(8,128)}, u32[]{:S(2)}, u32[]{:S(2)}) %collective-permute-start.4) | collective-permute-done | bytes 262176 | tf_op jit(solution)/shard_map/ppermute | solution.py:156
  53.1 2.1 %join4.1.refs_0_.refs_5_ = f32[512,128]{1,0:T(8,128)} custom-call(f32[512,128]{1,0:T(8,128)} %join3.1.refs_0_.refs_4_, f32[512,128]{1,0:T(8,128)} %collective-permute-done.4.refs_1_.refs_12_), custom_call_target="tpu_custom_call" | custom-call | tf_op jit(solution)/shard_map/join4/pallas_call | solution.py:103
  55.3 6.6 %collective-permute-done.5.refs_1_.refs_13_ = f32[512,128]{1,0:T(8,128)} collective-permute-done((f32[512,128]{1,0:T(8,128)}, f32[512,128]{1,0:T(8,128)}, u32[]{:S(2)}, u32[]{:S(2)}) %collective-permute-start.5) | collective-permute-done | bytes 262176 | tf_op jit(solution)/shard_map/ppermute | solution.py:156
  61.9 2.1 %join5.1.refs_0_.refs_6_ = f32[512,128]{1,0:T(8,128)} custom-call(f32[512,128]{1,0:T(8,128)} %join4.1.refs_0_.refs_5_, f32[512,128]{1,0:T(8,128)} %collective-permute-done.5.refs_1_.refs_13_), custom_call_target="tpu_custom_call" | custom-call | tf_op jit(solution)/shard_map/join5/pallas_call | solution.py:103
  64.0 9.9 %collective-permute-done.6.refs_1_.refs_14_ = f32[512,128]{1,0:T(8,128)} collective-permute-done((f32[512,128]{1,0:T(8,128)}, f32[512,128]{1,0:T(8,128)}, u32[]{:S(2)}, u32[]{:S(2)}) %collective-permute-start.6) | collective-permute-done | bytes 262176 | tf_op jit(solution)/shard_map/ppermute | solution.py:156
  73.9 2.1 %join6.1.refs_7_ = f32[512,128]{1,0:T(8,128)} custom-call(f32[512,128]{1,0:T(8,128)} %join5.1.refs_0_.refs_6_, f32[512,128]{1,0:T(8,128)} %collective-permute-done.6.refs_1_.refs_14_), custom_call_target="tpu_custom_call" | custom-call | tf_op jit(solution)/shard_map/join6/pallas_call | solution.py:103
  76.0 10.5 %collective-permute-start.7 = (f32[512,128]{1,0:T(8,128)}, f32[512,128]{1,0:T(8,128)S(1)}, u32[]{:S(2)}, u32[]{:S(2)}) collective-permute-start(f32[512,128]{1,0:T(8,128)} %join6.1.refs_7_), channel_id=1, source_target_pairs={{0,128},{1,129},{2,130},{3,131},{4,132},{5,133},{6,134},{7,135},{8... | collective-permute-start | bytes 786440 | tf_op jit(solution)/shard_map/ppermute | solution.py:156
  86.5 7.4 %collective-permute-done.7.refs_15_ = f32[512,128]{1,0:T(8,128)S(1)} collective-permute-done((f32[512,128]{1,0:T(8,128)}, f32[512,128]{1,0:T(8,128)S(1)}, u32[]{:S(2)}, u32[]{:S(2)}) %collective-permute-start.7) | collective-permute-done | bytes 262176 | tf_op jit(solution)/shard_map/ppermute | solution.py:156
  93.9 0.9 copy-done.4
  94.9 0.9 copy-done.5
  95.8 0.9 copy-done.11
  96.8 0.9 copy-done.13
  97.7 0.9 copy-done.15
  98.7 0.9 copy-done.16
  99.6 3.7 %finish.1 = f32[12,64,128]{2,1,0:T(8,128)} custom-call(f32[512,128]{1,0:T(8,128)S(1)} %copy-done.7, f32[512,128]{1,0:T(8,128)S(1)} %copy-done, f32[512,128]{1,0:T(8,128)S(1)} %copy-done.1, f32[512,128]{1,0:T(8,128)S(1)} %copy-done.2, f32[512,128]{1,0:T(8,128)S(1)} %copy-done.3, f32[512,128]{1,0:T(8,128)S(1)} %copy-done.4, f32[512,128]{1,0:T(8,128)S(1)} %copy-done.5, ...), custom_call_target="tpu_custom_call" | custom-call | tf_op jit(solution)/shard_map/finish/pallas_call | solution.py:140
  (35 shorter events, 2.9 us)
Async XLA Ops:
  0.0 1.1 %copy-start.17 = (f32[12,128,128]{2,1,0:T(8,128)S(1)}, f32[12,128,128]{2,1,0:T(8,128)}, u32[]{:S(2)}) copy-start(f32[12,128,128]{2,1,0:T(8,128)} %pivot_inv.1) | copy-start | bytes 2359300
  1.1 1.1 %copy-start.18 = (f32[12,128,128]{2,1,0:T(8,128)S(1)}, f32[12,128,128]{2,1,0:T(8,128)}, u32[]{:S(2)}) copy-start(f32[12,128,128]{2,1,0:T(8,128)} %lower.1) | copy-start | bytes 2359300
  2.3 1.1 %copy-start.19 = (f32[12,128,128]{2,1,0:T(8,128)S(1)}, f32[12,128,128]{2,1,0:T(8,128)}, u32[]{:S(2)}) copy-start(f32[12,128,128]{2,1,0:T(8,128)} %upper.1) | copy-start | bytes 2359300
  3.4 1.0 copy-start.20
  7.4 1.6 %copy-start.6 = (f32[512,128]{1,0:T(8,128)}, f32[512,128]{1,0:T(8,128)S(1)}, u32[]{:S(2)}) copy-start(f32[512,128]{1,0:T(8,128)S(1)} %get-tuple-element.7.refs_0_) | copy-start | bytes 786436
  7.5 1.6 %collective-permute-start = (f32[512,128]{1,0:T(8,128)S(1)}, f32[512,128]{1,0:T(8,128)S(1)}, u32[]{:S(2)}, u32[]{:S(2)}) collective-permute-start(f32[512,128]{1,0:T(8,128)S(1)} %get-tuple-element.7.refs_0_), channel_id=1, source_target_pairs={{0,1},{1,0},{2,3},{3,2},{4,5},{5,4},{6,7},{7,6},{8,9},{9,8},{10,11... | collective-permute-start | bytes 786440 | tf_op jit(solution)/shard_map/ppermute | solution.py:156
  9.1 0.7 copy-start.8
  11.8 8.6 %collective-permute-start.1 = (f32[512,128]{1,0:T(8,128)}, f32[512,128]{1,0:T(8,128)S(1)}, u32[]{:S(2)}, u32[]{:S(2)}) collective-permute-start(f32[512,128]{1,0:T(8,128)} %join0.1.refs_0_.refs_1_), channel_id=1, source_target_pairs={{0,2},{1,3},{2,0},{3,1},{4,6},{5,7},{6,4},{7,5},{8,10},{9,11},{10,... | collective-permute-start | bytes 786440 | tf_op jit(solution)/shard_map/ppermute | solution.py:156
  20.4 0.7 copy-start.10
  23.2 70.7 %copy-start = (f32[512,128]{1,0:T(8,128)S(1)}, f32[512,128]{1,0:T(8,128)}, u32[]{:S(2)}) copy-start(f32[512,128]{1,0:T(8,128)} %join0.1.refs_0_.refs_1_) | copy-start | bytes 786436
  23.2 70.7 %copy-start.1 = (f32[512,128]{1,0:T(8,128)S(1)}, f32[512,128]{1,0:T(8,128)}, u32[]{:S(2)}) copy-start(f32[512,128]{1,0:T(8,128)} %join1.1.refs_0_.refs_2_) | copy-start | bytes 786436
  23.2 70.7 %copy-start.7 = (f32[512,128]{1,0:T(8,128)S(1)}, f32[512,128]{1,0:T(8,128)}, u32[]{:S(2)}) copy-start(f32[512,128]{1,0:T(8,128)} %copy-done.6) | copy-start | bytes 786436
  23.2 70.7 %copy-start.9 = (f32[512,128]{1,0:T(8,128)S(1)}, f32[512,128]{1,0:T(8,128)}, u32[]{:S(2)}) copy-start(f32[512,128]{1,0:T(8,128)} %copy-done.8) | copy-start | bytes 786436
  23.2 9.3 %collective-permute-start.2 = (f32[512,128]{1,0:T(8,128)}, f32[512,128]{1,0:T(8,128)S(1)}, u32[]{:S(2)}, u32[]{:S(2)}) collective-permute-start(f32[512,128]{1,0:T(8,128)} %join1.1.refs_0_.refs_2_), channel_id=1, source_target_pairs={{0,4},{1,5},{2,6},{3,7},{4,0},{5,1},{6,2},{7,3},{8,12},{9,13},{10,... | collective-permute-start | bytes 786440 | tf_op jit(solution)/shard_map/ppermute | solution.py:156
  32.5 0.7 copy-start.12
  35.3 58.6 %copy-start.2 = (f32[512,128]{1,0:T(8,128)S(1)}, f32[512,128]{1,0:T(8,128)}, u32[]{:S(2)}) copy-start(f32[512,128]{1,0:T(8,128)} %join2.1.refs_0_.refs_3_) | copy-start | bytes 786436
  35.3 6.8 %collective-permute-start.3 = (f32[512,128]{1,0:T(8,128)}, f32[512,128]{1,0:T(8,128)S(1)}, u32[]{:S(2)}, u32[]{:S(2)}) collective-permute-start(f32[512,128]{1,0:T(8,128)} %join2.1.refs_0_.refs_3_), channel_id=1, source_target_pairs={{0,8},{1,9},{2,10},{3,11},{4,12},{5,13},{6,14},{7,15},{8,0},{9,1},... | collective-permute-start | bytes 786440 | tf_op jit(solution)/shard_map/ppermute | solution.py:156
  42.1 0.7 copy-start.14
  44.9 49.0 %copy-start.3 = (f32[512,128]{1,0:T(8,128)S(1)}, f32[512,128]{1,0:T(8,128)}, u32[]{:S(2)}) copy-start(f32[512,128]{1,0:T(8,128)} %join3.1.refs_0_.refs_4_) | copy-start | bytes 786436
  44.9 8.2 %collective-permute-start.4 = (f32[512,128]{1,0:T(8,128)}, f32[512,128]{1,0:T(8,128)}, u32[]{:S(2)}, u32[]{:S(2)}) collective-permute-start(f32[512,128]{1,0:T(8,128)} %join3.1.refs_0_.refs_4_), channel_id=1, source_target_pairs={{0,16},{1,17},{2,18},{3,19},{4,20},{5,21},{6,22},{7,23},{8,24},{9,... | collective-permute-start | bytes 786440 | tf_op jit(solution)/shard_map/ppermute | solution.py:156
  55.2 6.7 %collective-permute-start.5 = (f32[512,128]{1,0:T(8,128)}, f32[512,128]{1,0:T(8,128)}, u32[]{:S(2)}, u32[]{:S(2)}) collective-permute-start(f32[512,128]{1,0:T(8,128)} %join4.1.refs_0_.refs_5_), channel_id=1, source_target_pairs={{0,32},{1,33},{2,34},{3,35},{4,36},{5,37},{6,38},{7,39},{8,40},{9,... | collective-permute-start | bytes 786440 | tf_op jit(solution)/shard_map/ppermute | solution.py:156
  64.0 9.9 %collective-permute-start.6 = (f32[512,128]{1,0:T(8,128)}, f32[512,128]{1,0:T(8,128)}, u32[]{:S(2)}, u32[]{:S(2)}) collective-permute-start(f32[512,128]{1,0:T(8,128)} %join5.1.refs_0_.refs_6_), channel_id=1, source_target_pairs={{0,64},{1,65},{2,66},{3,67},{4,68},{5,69},{6,70},{7,71},{8,72},{9,... | collective-permute-start | bytes 786440 | tf_op jit(solution)/shard_map/ppermute | solution.py:156
  76.0 17.9 %collective-permute-start.7 = (f32[512,128]{1,0:T(8,128)}, f32[512,128]{1,0:T(8,128)S(1)}, u32[]{:S(2)}, u32[]{:S(2)}) collective-permute-start(f32[512,128]{1,0:T(8,128)} %join6.1.refs_7_), channel_id=1, source_target_pairs={{0,128},{1,129},{2,130},{3,131},{4,132},{5,133},{6,134},{7,135},{8... | collective-permute-start | bytes 786440 | tf_op jit(solution)/shard_map/ppermute | solution.py:156
  93.9 1.0 copy-start.4
  94.9 0.9 copy-start.5
  95.8 0.9 copy-start.11
  96.8 0.9 copy-start.13
  97.7 0.9 copy-start.15
  98.7 0.9 copy-start.16
where the time goes:
time: 104 us; the launch traced here: 103 us
  waiting for transfers between devices  50.8 us (49%)
  Pallas kernels  21.3 us (20%)
  starting transfers between devices  18.2 us (18%)
  local copies, waits for them, and re-layouts  12.9 us (12%)
    ppermute x8, waiting for transfers between devices, on_device(): lax.ppermute(pack, AXES, [(i, i ^ 1 << level) for i in range(devices)])  50.8 us
    ppermute x8, starting transfers between devices, on_device(): lax.ppermute(pack, AXES, [(i, i ^ 1 << level) for i in range(devices)])  18.2 us
    pallas_call x7, Pallas kernels, join(): pl.pallas_call(lambda *refs: join_kernel(level, *refs), out_shape=jax.Sha...  14.5 us
    unnamed x42, local copies, waits for them, and re-layouts  12.9 us
    pallas_call x1, Pallas kernels, finish(): pl.pallas_call(lambda *refs: finish_kernel(levels, *refs), out_shape=jax....  3.69 us
    pallas_call x1, Pallas kernels, local(): pl.pallas_call(local_kernel, out_shape=(jax.ShapeDtypeStruct((PACK, B), j...  3.03 us
  transfers between devices with their start and end apart: 8, of which 8 were waited for; matrix products, arithmetic and copies ran while one was open for 0% of the time, Pallas kernels for 0%

commit v1 on v0

v1 whole, which is shorter than its diff:
```python
import jax
import jax.numpy as jnp
from jax import lax
from jax.experimental import pallas as pl
from jax.experimental.pallas import tpu as pltpu
from jax.sharding import PartitionSpec as P

AXES = ("wide", "narrow")
B = 128
R = 64
PACK = 3 * B + 2 * R
CHUNKS = 3
LIMIT = 12 * 2**20


def halves(value):
    high = value.astype(jnp.bfloat16)
    low = (value - high.astype(jnp.float32)).astype(jnp.bfloat16)
    return high, low


def left_side(value):
    return jnp.concatenate(halves(value), axis=1)


def right_side(value):
    both = jnp.concatenate(halves(value), axis=1)
    return jnp.concatenate([both, both], axis=0)


def times(left, right):
    wide = jnp.dot(left, right, preferred_element_type=jnp.float32)
    return wide[:, :B] + wide[:, B:]


def mm(left, right):
    return times(left_side(left), right_side(right))


def local_kernel(
    rhs_hbm, pivot_hbm, lower_hbm, upper_hbm, pack, rows, rhs, pivot_inv, lower, upper, forward, sems
):
    count = rhs.shape[0]
    pairs = ((pivot_hbm, pivot_inv), (rhs_hbm, rhs), (lower_hbm, lower), (upper_hbm, upper))
    chunk = count // CHUNKS
    copies = {}
    for part in range(CHUNKS):
        for which, (source, target) in enumerate(pairs):
            at = CHUNKS - 1 - part if which == 3 else part
            span = pl.ds(at * chunk, chunk)
            copy = pltpu.make_async_copy(source.at[span], target.at[span], sems.at[which, at])
            copy.start()
            copies[which, at] = copy
    scaled = []
    state = None
    for i in range(count):
        if i % chunk == 0:
            for which in range(3):
                copies[which, i // chunk].wait()
            scaled += [mm(rhs[j], pivot_inv[j]) for j in range(i, i + chunk)]
        if i == 0:
            state = jnp.concatenate([-lower[0], scaled[0]], axis=0)
        else:
            moved = mm(state, lower[i])
            state = jnp.concatenate([-moved[:B], scaled[i] - moved[B:]], axis=0)
        forward[i] = state
    pack[: B + R] = state
    for i in range(count - 1, -1, -1):
        if (i + 1) % chunk == 0:
            copies[3, i // chunk].wait()
        if i == count - 1:
            state = jnp.concatenate([-upper[i], state], axis=0)
        else:
            moved = mm(state, upper[i])
            state = jnp.concatenate([-moved[:B], forward[i] - moved[B:]], axis=0)
        rows[i] = state
    pack[B + R :] = state


def local(rhs, pivot_inv, lower, upper):
    count = rhs.shape[0]
    return pl.pallas_call(
        local_kernel,
        out_shape=(
            jax.ShapeDtypeStruct((PACK, B), jnp.float32),
            jax.ShapeDtypeStruct((count, 2 * B + R, B), jnp.float32),
        ),
        in_specs=[pl.BlockSpec(memory_space=pltpu.HBM)] * 4,
        out_specs=[pl.BlockSpec(memory_space=pltpu.VMEM)] * 2,
        scratch_shapes=[
            pltpu.VMEM(rhs.shape, jnp.float32),
            pltpu.VMEM(pivot_inv.shape, jnp.float32),
            pltpu.VMEM(lower.shape, jnp.float32),
            pltpu.VMEM(upper.shape, jnp.float32),
            pltpu.VMEM((count, B + R, B), jnp.float32),
            pltpu.SemaphoreType.DMA((4, CHUNKS)),
        ],
        compiler_params=pltpu.CompilerParams(vmem_limit_bytes=LIMIT),
        name="local",
    )(rhs, pivot_inv, lower, upper)


def position():
    return lax.axis_index(AXES[0]) * lax.axis_size(AXES[1]) + lax.axis_index(AXES[1])


def is_left(level):
    return (position() >> level) & 1 == 0


def ordered(level, own, other):
    left = is_left(level)
    return jnp.where(left, own, other), jnp.where(left, other, own)


def partner_pack(refs):
    if len(refs) == 1:
        return refs[0][...]
    here, there = refs[0][...], refs[1][...]
    low = position() & 1 == 0
    return jnp.concatenate([jnp.where(low, here, there), jnp.where(low, there, here)], axis=0)


def turned(first, second):
    early = left_side(first[: B + R])
    turn = times(early, right_side(second[2 * B + R : 3 * B + R]))
    back = jnp.concatenate(
        [second[B + R : 2 * B + R], turn[:B], turn[B:] + second[3 * B + R :]], axis=0
    )
    return early, back


def join_kernel(level, top, *refs):
    own, parts, (pack, send) = refs[0][...], refs[1:-2], refs[-2:]
    first, second = ordered(level, own, partner_pack(parts))
    early, back = turned(first, second)
    down = times(early, right_side(second[:B]))
    up = mm(back, first[B + R : 2 * B + R])
    ahead = jnp.concatenate([down[:B], down[B:] + second[B : B + R]], axis=0)
    behind = jnp.concatenate([up[:B], up[B:] + first[2 * B + R :]], axis=0)
    pack[: B + R] = ahead
    pack[B + R :] = behind
    if top:
        send[...] = jnp.where(is_left(level + 1), ahead, behind[B:])
    else:
        low = position() & 1 == 0
        half = PACK // 2
        send[: B + R] = jnp.where(low, ahead, behind[half - B - R : half])
        send[B + R :] = jnp.where(low, behind[: half - B - R], behind[half:])


def join(level, top, own, parts):
    return pl.pallas_call(
        lambda *refs: join_kernel(level, top, *refs),
        out_shape=(
            jax.ShapeDtypeStruct((PACK, B), jnp.float32),
            jax.ShapeDtypeStruct((B + R if top else PACK // 2, B), jnp.float32),
        ),
        in_specs=[pl.BlockSpec(memory_space=pltpu.VMEM)] * (1 + len(parts)),
        out_specs=[pl.BlockSpec(memory_space=pltpu.VMEM)] * 2,
        compiler_params=pltpu.CompilerParams(vmem_limit_bytes=LIMIT),
        name=f"join{level}",
    )(own, *parts)


def track_kernel(counts, *refs):
    *refs, track = refs
    eye = (
        lax.broadcasted_iota(jnp.int32, (B, B), 0) == lax.broadcasted_iota(jnp.int32, (B, B), 1)
    ).astype(jnp.float32)
    none = jnp.zeros((B + R, B), jnp.float32)
    ahead = jnp.concatenate([eye, none[:R]], axis=0)
    behind = jnp.concatenate([eye, none], axis=0)
    for level, count in enumerate(counts):
        own, parts, refs = refs[0][...], refs[1 : 1 + count], refs[1 + count :]
        first, second = ordered(level, own, partner_pack(parts))
        early, back = turned(first, second)
        left = is_left(level)
        through = mm(back, behind[:B])
        through = jnp.concatenate([through[:B], through[B:] + behind[B:]], axis=0)
        onward = times(early, right_side(ahead[:B]))
        onward = jnp.concatenate([onward[:B], onward[B:] + ahead[B:]], axis=0)
        cross = times(early, right_side(behind[B : 2 * B]))
        cross = jnp.concatenate([behind[:B], cross[:B], cross[B:] + behind[2 * B :]], axis=0)
        ahead = jnp.where(left, ahead, onward)
        behind = jnp.where(left, through, cross)
    track[: B + R] = ahead
    track[B + R :] = behind


def track(steps):
    counts = [len(parts) for _, parts in steps]
    operands = [array for own, parts in steps for array in (own, *parts)]
    return pl.pallas_call(
        lambda *refs: track_kernel(counts, *refs),
        out_shape=jax.ShapeDtypeStruct((PACK, B), jnp.float32),
        in_specs=[pl.BlockSpec(memory_space=pltpu.VMEM)] * len(operands),
        out_specs=pl.BlockSpec(memory_space=pltpu.VMEM),
        compiler_params=pltpu.CompilerParams(vmem_limit_bytes=LIMIT),
        cost_estimate=pl.CostEstimate(
            flops=len(steps) * 2**28, bytes_accessed=len(steps) * 2**19, transcendentals=0
        ),
        name="track",
    )(*operands)


def finish_kernel(level, own, got, track, rows, out):
    left = is_left(level)
    zero = jnp.zeros((R, B), jnp.float32)
    behind = jnp.where(left, zero, got[B:])
    ahead = jnp.where(left, mm(own[B : B + R], got[:B]) + got[B:], zero)
    ahead, behind = left_side(ahead), left_side(behind)
    ahead, behind = (
        times(ahead, right_side(track[B + R : 2 * B + R]))
        + times(behind, right_side(track[2 * B + R : 3 * B + R]))
        + track[3 * B + R :],
        times(behind, right_side(track[:B])) + track[B : B + R],
    )
    ahead, behind = left_side(ahead), left_side(behind)
    for i in range(out.shape[0]):
        out[i] = (
            rows[i, 2 * B :]
            + times(ahead, right_side(rows[i, :B]))
            + times(behind, right_side(rows[i, B : 2 * B]))
        )


def finish(level, own, got, tracked, rows):
    return pl.pallas_call(
        lambda *refs: finish_kernel(level, *refs),
        out_shape=jax.ShapeDtypeStruct((rows.shape[0], R, B), jnp.float32),
        in_specs=[pl.BlockSpec(memory_space=pltpu.VMEM)] * 4,
        out_specs=pl.BlockSpec(memory_space=pltpu.VMEM),
        compiler_params=pltpu.CompilerParams(vmem_limit_bytes=LIMIT),
        name="finish",
    )(own, got, tracked, rows)


def on_device(rhs, pivot_inv, lower_gain, upper_gain):
    devices = lax.axis_size(AXES)
    top = devices.bit_length() - 2
    swap = lambda array, level: lax.ppermute(
        array, AXES, [(i, i ^ (1 << level)) for i in range(devices)]
    )
    inputs = (rhs, pivot_inv, lower_gain, upper_gain)
    pack, rows = local(*(pltpu.with_memory_space_constraint(x, pltpu.HBM) for x in inputs))
    send = pack
    steps = []
    for level in range(top):
        got = swap(send, level)
        parts = (got,) if level == 0 else (got, swap(got, 0))
        steps.append((pack, parts))
        pack, send = join(level, level == top - 1, pack, parts)
    got = swap(send, top)
    return finish(top, pack, got, track(steps), rows)


def solution(mesh):
    placed = P(AXES, None, None)
    return jax.shard_map(
        on_device,
        mesh=mesh,
        in_specs=(placed,) * 4,
        out_specs=placed,
        check_vma=False,
    )
```

time: 104 us -> 70.1 us (0.67)
  the two profiles are of different devices: /device:TPU:98 before, /device:TPU:1 now
where the time goes in v1:
time: 70.1 us; the launch traced here: 70 us
  waiting for transfers between devices  40.2 us (57%)
  starting transfers between devices  19.4 us (28%)
  Pallas kernels  10.2 us (15%)
    ppermute x14, waiting for transfers between devices, on_device(): lax.ppermute(array, AXES, [(i, i ^ 1 << level) for i in range(devices)])  40.2 us
    ppermute x14, starting transfers between devices, on_device(): lax.ppermute(array, AXES, [(i, i ^ 1 << level) for i in range(devices)])  19.4 us
    pallas_call x1, Pallas kernels, local(): pl.pallas_call(local_kernel, out_shape=(jax.ShapeDtypeStruct((PACK, B), j...  4.73 us
    pallas_call x7, Pallas kernels, join(): pl.pallas_call(lambda *refs: join_kernel(level, top, *refs), out_shape=(j...  2.36 us
    pallas_call x1, Pallas kernels, finish(): pl.pallas_call(lambda *refs: finish_kernel(level, *refs), out_shape=jax.S...  1.7 us
    pallas_call x1, Pallas kernels, track(): pl.pallas_call(lambda *refs: track_kernel(counts, *refs), out_shape=jax.S...  1.45 us
  transfers between devices with their start and end apart: 14, of which 14 were waited for; matrix products, arithmetic and copies ran while one was open for 0% of the time, Pallas kernels for 2%

profile of v1, /device:TPU:1, one launch (start us, length us, event | category | flops | bytes accessed | tf_op | source)
XLA Modules:
  0.0 70.0 jit_solution(12724564493122925097)
XLA Ops:
  0.0 4.7 %local.1 = (f32[512,128]{1,0:T(8,128)S(1)}, f32[12,320,128]{2,1,0:T(8,128)S(1)}) custom-call(f32[12,64,128]{2,1,0:T(8,128)} %rhs_hbm.1, f32[12,128,128]{2,1,0:T(8,128)} %pivot_hbm.1, f32[12,128,128]{2,1,0:T(8,128)} %lower_hbm.1, f32[12,128,128]{2,1,0:T(8,128)} %upper_hbm.1), custom_call_target="tpu_custom_call" | custom-call | tf_op jit(solution)/shard_map/local/pallas_call | solution.py:82
  4.7 3.3 %collective-permute-start = (f32[512,128]{1,0:T(8,128)S(1)}, f32[512,128]{1,0:T(8,128)S(1)}, u32[]{:S(2)}, u32[]{:S(2)}) collective-permute-start(f32[512,128]{1,0:T(8,128)S(1)} %get-tuple-element.21.refs_0_), channel_id=1, source_target_pairs={{0,1},{1,0},{2,3},{3,2},{4,5},{5,4},{6,7},{7,6},{8,9},{9,8},{10,11... | collective-permute-start | bytes 786440 | tf_op jit(solution)/shard_map/ppermute | solution.py:242
  8.1 1.2 %collective-permute-done.refs_1_ = f32[512,128]{1,0:T(8,128)S(1)} collective-permute-done((f32[512,128]{1,0:T(8,128)S(1)}, f32[512,128]{1,0:T(8,128)S(1)}, u32[]{:S(2)}, u32[]{:S(2)}) %collective-permute-start) | collective-permute-done | bytes 262176 | tf_op jit(solution)/shard_map/ppermute | solution.py:242
  9.7 4.7 %collective-permute-done.1.refs_1_.refs_3_ = f32[256,128]{1,0:T(8,128)S(1)} collective-permute-done((f32[256,128]{1,0:T(8,128)S(1)}, f32[256,128]{1,0:T(8,128)S(1)}, u32[]{:S(2)}, u32[]{:S(2)}) %collective-permute-start.1) | collective-permute-done | bytes 131104 | tf_op jit(solution)/shard_map/ppermute | solution.py:242
  14.4 1.2 %collective-permute-start.2 = (f32[256,128]{1,0:T(8,128)S(1)}, f32[256,128]{1,0:T(8,128)S(1)}, u32[]{:S(2)}, u32[]{:S(2)}) collective-permute-start(f32[256,128]{1,0:T(8,128)S(1)} %collective-permute-done.1.refs_1_.refs_3_), channel_id=1, source_target_pairs={{0,1},{1,0},{2,3},{3,2},{4,5},{5,4},{6,7},{7,6},{8,9},{9,8},{10,11... | collective-permute-start | bytes 393224 | tf_op jit(solution)/shard_map/ppermute | solution.py:242
  15.6 1.0 %collective-permute-done.2.refs_2_.refs_4_ = f32[256,128]{1,0:T(8,128)S(1)} collective-permute-done((f32[256,128]{1,0:T(8,128)S(1)}, f32[256,128]{1,0:T(8,128)S(1)}, u32[]{:S(2)}, u32[]{:S(2)}) %collective-permute-start.2) | collective-permute-done | bytes 131104 | tf_op jit(solution)/shard_map/ppermute | solution.py:242
  16.6 0.3 join1.1
  16.9 1.1 %collective-permute-start.3 = (f32[256,128]{1,0:T(8,128)S(1)}, f32[256,128]{1,0:T(8,128)S(1)}, u32[]{:S(2)}, u32[]{:S(2)}) collective-permute-start(f32[256,128]{1,0:T(8,128)S(1)} %get-tuple-element.25), channel_id=1, source_target_pairs={{0,4},{1,5},{2,6},{3,7},{4,0},{5,1},{6,2},{7,3},{8,12},{9,13},{10,... | collective-permute-start | bytes 393224 | tf_op jit(solution)/shard_map/ppermute | solution.py:242
  18.0 5.2 %collective-permute-done.3.refs_1_.refs_6_ = f32[256,128]{1,0:T(8,128)S(1)} collective-permute-done((f32[256,128]{1,0:T(8,128)S(1)}, f32[256,128]{1,0:T(8,128)S(1)}, u32[]{:S(2)}, u32[]{:S(2)}) %collective-permute-start.3) | collective-permute-done | bytes 131104 | tf_op jit(solution)/shard_map/ppermute | solution.py:242
  23.2 1.2 %collective-permute-start.4 = (f32[256,128]{1,0:T(8,128)S(1)}, f32[256,128]{1,0:T(8,128)S(1)}, u32[]{:S(2)}, u32[]{:S(2)}) collective-permute-start(f32[256,128]{1,0:T(8,128)S(1)} %collective-permute-done.3.refs_1_.refs_6_), channel_id=1, source_target_pairs={{0,1},{1,0},{2,3},{3,2},{4,5},{5,4},{6,7},{7,6},{8,9},{9,8},{10,11... | collective-permute-start | bytes 393224 | tf_op jit(solution)/shard_map/ppermute | solution.py:242
  24.4 1.0 %collective-permute-done.4.refs_2_.refs_7_ = f32[256,128]{1,0:T(8,128)S(1)} collective-permute-done((f32[256,128]{1,0:T(8,128)S(1)}, f32[256,128]{1,0:T(8,128)S(1)}, u32[]{:S(2)}, u32[]{:S(2)}) %collective-permute-start.4) | collective-permute-done | bytes 131104 | tf_op jit(solution)/shard_map/ppermute | solution.py:242
  25.4 0.3 join2.1
  25.8 4.7 %collective-permute-done.5.refs_1_.refs_9_ = f32[256,128]{1,0:T(8,128)S(1)} collective-permute-done((f32[256,128]{1,0:T(8,128)S(1)}, f32[256,128]{1,0:T(8,128)S(1)}, u32[]{:S(2)}, u32[]{:S(2)}) %collective-permute-start.5) | collective-permute-done | bytes 131104 | tf_op jit(solution)/shard_map/ppermute | solution.py:242
  30.5 1.2 %collective-permute-start.6 = (f32[256,128]{1,0:T(8,128)S(1)}, f32[256,128]{1,0:T(8,128)S(1)}, u32[]{:S(2)}, u32[]{:S(2)}) collective-permute-start(f32[256,128]{1,0:T(8,128)S(1)} %collective-permute-done.5.refs_1_.refs_9_), channel_id=1, source_target_pairs={{0,1},{1,0},{2,3},{3,2},{4,5},{5,4},{6,7},{7,6},{8,9},{9,8},{10,11... | collective-permute-start | bytes 393224 | tf_op jit(solution)/shard_map/ppermute | solution.py:242
  31.7 1.0 %collective-permute-done.6.refs_2_.refs_10_ = f32[256,128]{1,0:T(8,128)S(1)} collective-permute-done((f32[256,128]{1,0:T(8,128)S(1)}, f32[256,128]{1,0:T(8,128)S(1)}, u32[]{:S(2)}, u32[]{:S(2)}) %collective-permute-start.6) | collective-permute-done | bytes 131104 | tf_op jit(solution)/shard_map/ppermute | solution.py:242
  32.7 0.3 join3.1
  33.1 1.3 %collective-permute-start.7 = (f32[256,128]{1,0:T(8,128)S(1)}, f32[256,128]{1,0:T(8,128)S(1)}, u32[]{:S(2)}, u32[]{:S(2)}) collective-permute-start(f32[256,128]{1,0:T(8,128)S(1)} %get-tuple-element.29), channel_id=1, source_target_pairs={{0,16},{1,17},{2,18},{3,19},{4,20},{5,21},{6,22},{7,23},{8,24},{9,... | collective-permute-start | bytes 393224 | tf_op jit(solution)/shard_map/ppermute | solution.py:242
  34.3 5.0 %collective-permute-done.7.refs_1_.refs_12_ = f32[256,128]{1,0:T(8,128)S(1)} collective-permute-done((f32[256,128]{1,0:T(8,128)S(1)}, f32[256,128]{1,0:T(8,128)S(1)}, u32[]{:S(2)}, u32[]{:S(2)}) %collective-permute-start.7) | collective-permute-done | bytes 131104 | tf_op jit(solution)/shard_map/ppermute | solution.py:242
  39.4 1.2 %collective-permute-start.8 = (f32[256,128]{1,0:T(8,128)S(1)}, f32[256,128]{1,0:T(8,128)S(1)}, u32[]{:S(2)}, u32[]{:S(2)}) collective-permute-start(f32[256,128]{1,0:T(8,128)S(1)} %collective-permute-done.7.refs_1_.refs_12_), channel_id=1, source_target_pairs={{0,1},{1,0},{2,3},{3,2},{4,5},{5,4},{6,7},{7,6},{8,9},{9,8},{10,11... | collective-permute-start | bytes 393224 | tf_op jit(solution)/shard_map/ppermute | solution.py:242
  40.6 1.0 %collective-permute-done.8.refs_2_.refs_13_ = f32[256,128]{1,0:T(8,128)S(1)} collective-permute-done((f32[256,128]{1,0:T(8,128)S(1)}, f32[256,128]{1,0:T(8,128)S(1)}, u32[]{:S(2)}, u32[]{:S(2)}) %collective-permute-start.8) | collective-permute-done | bytes 131104 | tf_op jit(solution)/shard_map/ppermute | solution.py:242
  42.0 4.7 %collective-permute-done.9.refs_1_.refs_15_ = f32[256,128]{1,0:T(8,128)S(1)} collective-permute-done((f32[256,128]{1,0:T(8,128)S(1)}, f32[256,128]{1,0:T(8,128)S(1)}, u32[]{:S(2)}, u32[]{:S(2)}) %collective-permute-start.9) | collective-permute-done | bytes 131104 | tf_op jit(solution)/shard_map/ppermute | solution.py:242
  46.7 1.2 %collective-permute-start.10 = (f32[256,128]{1,0:T(8,128)S(1)}, f32[256,128]{1,0:T(8,128)S(1)}, u32[]{:S(2)}, u32[]{:S(2)}) collective-permute-start(f32[256,128]{1,0:T(8,128)S(1)} %collective-permute-done.9.refs_1_.refs_15_), channel_id=1, source_target_pairs={{0,1},{1,0},{2,3},{3,2},{4,5},{5,4},{6,7},{7,6},{8,9},{9,8},{10,11... | collective-permute-start | bytes 393224 | tf_op jit(solution)/shard_map/ppermute | solution.py:242
  47.9 1.0 %collective-permute-done.10.refs_2_.refs_16_ = f32[256,128]{1,0:T(8,128)S(1)} collective-permute-done((f32[256,128]{1,0:T(8,128)S(1)}, f32[256,128]{1,0:T(8,128)S(1)}, u32[]{:S(2)}, u32[]{:S(2)}) %collective-permute-start.10) | collective-permute-done | bytes 131104 | tf_op jit(solution)/shard_map/ppermute | solution.py:242
  48.9 0.3 join5.1
  49.2 1.5 %collective-permute-start.11 = (f32[256,128]{1,0:T(8,128)S(1)}, f32[256,128]{1,0:T(8,128)S(1)}, u32[]{:S(2)}, u32[]{:S(2)}) collective-permute-start(f32[256,128]{1,0:T(8,128)S(1)} %get-tuple-element.33), channel_id=1, source_target_pairs={{0,64},{1,65},{2,66},{3,67},{4,68},{5,69},{6,70},{7,71},{8,72},{9,... | collective-permute-start | bytes 393224 | tf_op jit(solution)/shard_map/ppermute | solution.py:242
  50.7 7.5 %collective-permute-done.11.refs_1_.refs_18_ = f32[256,128]{1,0:T(8,128)S(1)} collective-permute-done((f32[256,128]{1,0:T(8,128)S(1)}, f32[256,128]{1,0:T(8,128)S(1)}, u32[]{:S(2)}, u32[]{:S(2)}) %collective-permute-start.11) | collective-permute-done | bytes 131104 | tf_op jit(solution)/shard_map/ppermute | solution.py:242
  58.2 0.7 %collective-permute-start.12 = (f32[256,128]{1,0:T(8,128)S(1)}, f32[256,128]{1,0:T(8,128)S(1)}, u32[]{:S(2)}, u32[]{:S(2)}) collective-permute-start(f32[256,128]{1,0:T(8,128)S(1)} %collective-permute-done.11.refs_1_.refs_18_), channel_id=1, source_target_pairs={{0,1},{1,0},{2,3},{3,2},{4,5},{5,4},{6,7},{7,6},{8,9},{9,8},{10,11... | collective-permute-start | bytes 393224 | tf_op jit(solution)/shard_map/ppermute | solution.py:242
  58.9 1.0 %collective-permute-done.12.refs_2_.refs_19_ = f32[256,128]{1,0:T(8,128)S(1)} collective-permute-done((f32[256,128]{1,0:T(8,128)S(1)}, f32[256,128]{1,0:T(8,128)S(1)}, u32[]{:S(2)}, u32[]{:S(2)}) %collective-permute-start.12) | collective-permute-done | bytes 131104 | tf_op jit(solution)/shard_map/ppermute | solution.py:242
  60.3 5.3 %collective-permute-start.13 = (f32[192,128]{1,0:T(8,128)S(1)}, f32[192,128]{1,0:T(8,128)S(1)}, u32[]{:S(2)}, u32[]{:S(2)}) collective-permute-start(f32[192,128]{1,0:T(8,128)S(1)} %get-tuple-element.35), channel_id=1, source_target_pairs={{0,128},{1,129},{2,130},{3,131},{4,132},{5,133},{6,134},{7,135},{8... | collective-permute-start | bytes 294920 | tf_op jit(solution)/shard_map/ppermute | solution.py:242
  65.5 1.5 %track.1.refs_2_ = f32[512,128]{1,0:T(8,128)S(1)} custom-call(f32[512,128]{1,0:T(8,128)S(1)} %get-tuple-element.21.refs_0_, f32[512,128]{1,0:T(8,128)S(1)} %collective-permute-done.refs_1_, f32[512,128]{1,0:T(8,128)S(1)} %get-tuple-element.22.refs_0_.refs_2_, f32[256,128]{1,0:T(8,128)S(1)} %collective-permute-done.1.refs_1_.refs_3_, ...), custom_call_target="tpu_custom_call" | custom-call | flops 1879048192 | bytes 3670016 | tf_op jit(solution)/shard_map/track/pallas_call | solution.py:194
  67.0 1.3 %collective-permute-done.13.refs_1_ = f32[192,128]{1,0:T(8,128)S(1)} collective-permute-done((f32[192,128]{1,0:T(8,128)S(1)}, f32[192,128]{1,0:T(8,128)S(1)}, u32[]{:S(2)}, u32[]{:S(2)}) %collective-permute-start.13) | collective-permute-done | bytes 98336 | tf_op jit(solution)/shard_map/ppermute | solution.py:242
  68.3 1.7 %finish.1 = f32[12,64,128]{2,1,0:T(8,128)} custom-call(f32[512,128]{1,0:T(8,128)S(1)} %get-tuple-element.34.refs_0_, f32[192,128]{1,0:T(8,128)S(1)} %collective-permute-done.13.refs_1_, f32[512,128]{1,0:T(8,128)S(1)} %track.1.refs_2_, f32[12,320,128]{2,1,0:T(8,128)S(1)} %get-tuple-element.36.refs_3_), custom_call_target="tpu_custom_call" | custom-call | tf_op jit(solution)/shard_map/finish/pallas_call | solution.py:229
  (6 shorter events, 1.3 us)
Async XLA Ops:
  4.7 4.5 %collective-permute-start = (f32[512,128]{1,0:T(8,128)S(1)}, f32[512,128]{1,0:T(8,128)S(1)}, u32[]{:S(2)}, u32[]{:S(2)}) collective-permute-start(f32[512,128]{1,0:T(8,128)S(1)} %get-tuple-element.21.refs_0_), channel_id=1, source_target_pairs={{0,1},{1,0},{2,3},{3,2},{4,5},{5,4},{6,7},{7,6},{8,9},{9,8},{10,11... | collective-permute-start | bytes 786440 | tf_op jit(solution)/shard_map/ppermute | solution.py:242
  9.6 4.8 %collective-permute-start.1 = (f32[256,128]{1,0:T(8,128)S(1)}, f32[256,128]{1,0:T(8,128)S(1)}, u32[]{:S(2)}, u32[]{:S(2)}) collective-permute-start(f32[256,128]{1,0:T(8,128)S(1)} %get-tuple-element.23), channel_id=1, source_target_pairs={{0,2},{1,3},{2,0},{3,1},{4,6},{5,7},{6,4},{7,5},{8,10},{9,11},{10,... | collective-permute-start | bytes 393224 | tf_op jit(solution)/shard_map/ppermute | solution.py:242
  14.4 2.2 %collective-permute-start.2 = (f32[256,128]{1,0:T(8,128)S(1)}, f32[256,128]{1,0:T(8,128)S(1)}, u32[]{:S(2)}, u32[]{:S(2)}) collective-permute-start(f32[256,128]{1,0:T(8,128)S(1)} %collective-permute-done.1.refs_1_.refs_3_), channel_id=1, source_target_pairs={{0,1},{1,0},{2,3},{3,2},{4,5},{5,4},{6,7},{7,6},{8,9},{9,8},{10,11... | collective-permute-start | bytes 393224 | tf_op jit(solution)/shard_map/ppermute | solution.py:242
  16.9 6.3 %collective-permute-start.3 = (f32[256,128]{1,0:T(8,128)S(1)}, f32[256,128]{1,0:T(8,128)S(1)}, u32[]{:S(2)}, u32[]{:S(2)}) collective-permute-start(f32[256,128]{1,0:T(8,128)S(1)} %get-tuple-element.25), channel_id=1, source_target_pairs={{0,4},{1,5},{2,6},{3,7},{4,0},{5,1},{6,2},{7,3},{8,12},{9,13},{10,... | collective-permute-start | bytes 393224 | tf_op jit(solution)/shard_map/ppermute | solution.py:242
  23.2 2.2 %collective-permute-start.4 = (f32[256,128]{1,0:T(8,128)S(1)}, f32[256,128]{1,0:T(8,128)S(1)}, u32[]{:S(2)}, u32[]{:S(2)}) collective-permute-start(f32[256,128]{1,0:T(8,128)S(1)} %collective-permute-done.3.refs_1_.refs_6_), channel_id=1, source_target_pairs={{0,1},{1,0},{2,3},{3,2},{4,5},{5,4},{6,7},{7,6},{8,9},{9,8},{10,11... | collective-permute-start | bytes 393224 | tf_op jit(solution)/shard_map/ppermute | solution.py:242
  25.7 4.8 %collective-permute-start.5 = (f32[256,128]{1,0:T(8,128)S(1)}, f32[256,128]{1,0:T(8,128)S(1)}, u32[]{:S(2)}, u32[]{:S(2)}) collective-permute-start(f32[256,128]{1,0:T(8,128)S(1)} %get-tuple-element.27), channel_id=1, source_target_pairs={{0,8},{1,9},{2,10},{3,11},{4,12},{5,13},{6,14},{7,15},{8,0},{9,1},... | collective-permute-start | bytes 393224 | tf_op jit(solution)/shard_map/ppermute | solution.py:242
  30.5 2.2 %collective-permute-start.6 = (f32[256,128]{1,0:T(8,128)S(1)}, f32[256,128]{1,0:T(8,128)S(1)}, u32[]{:S(2)}, u32[]{:S(2)}) collective-permute-start(f32[256,128]{1,0:T(8,128)S(1)} %collective-permute-done.5.refs_1_.refs_9_), channel_id=1, source_target_pairs={{0,1},{1,0},{2,3},{3,2},{4,5},{5,4},{6,7},{7,6},{8,9},{9,8},{10,11... | collective-permute-start | bytes 393224 | tf_op jit(solution)/shard_map/ppermute | solution.py:242
  33.1 6.3 %collective-permute-start.7 = (f32[256,128]{1,0:T(8,128)S(1)}, f32[256,128]{1,0:T(8,128)S(1)}, u32[]{:S(2)}, u32[]{:S(2)}) collective-permute-start(f32[256,128]{1,0:T(8,128)S(1)} %get-tuple-element.29), channel_id=1, source_target_pairs={{0,16},{1,17},{2,18},{3,19},{4,20},{5,21},{6,22},{7,23},{8,24},{9,... | collective-permute-start | bytes 393224 | tf_op jit(solution)/shard_map/ppermute | solution.py:242
  39.4 2.2 %collective-permute-start.8 = (f32[256,128]{1,0:T(8,128)S(1)}, f32[256,128]{1,0:T(8,128)S(1)}, u32[]{:S(2)}, u32[]{:S(2)}) collective-permute-start(f32[256,128]{1,0:T(8,128)S(1)} %collective-permute-done.7.refs_1_.refs_12_), channel_id=1, source_target_pairs={{0,1},{1,0},{2,3},{3,2},{4,5},{5,4},{6,7},{7,6},{8,9},{9,8},{10,11... | collective-permute-start | bytes 393224 | tf_op jit(solution)/shard_map/ppermute | solution.py:242
  41.9 4.8 %collective-permute-start.9 = (f32[256,128]{1,0:T(8,128)S(1)}, f32[256,128]{1,0:T(8,128)S(1)}, u32[]{:S(2)}, u32[]{:S(2)}) collective-permute-start(f32[256,128]{1,0:T(8,128)S(1)} %get-tuple-element.31), channel_id=1, source_target_pairs={{0,32},{1,33},{2,34},{3,35},{4,36},{5,37},{6,38},{7,39},{8,40},{9,... | collective-permute-start | bytes 393224 | tf_op jit(solution)/shard_map/ppermute | solution.py:242
  46.7 2.2 %collective-permute-start.10 = (f32[256,128]{1,0:T(8,128)S(1)}, f32[256,128]{1,0:T(8,128)S(1)}, u32[]{:S(2)}, u32[]{:S(2)}) collective-permute-start(f32[256,128]{1,0:T(8,128)S(1)} %collective-permute-done.9.refs_1_.refs_15_), channel_id=1, source_target_pairs={{0,1},{1,0},{2,3},{3,2},{4,5},{5,4},{6,7},{7,6},{8,9},{9,8},{10,11... | collective-permute-start | bytes 393224 | tf_op jit(solution)/shard_map/ppermute | solution.py:242
  49.2 9.0 %collective-permute-start.11 = (f32[256,128]{1,0:T(8,128)S(1)}, f32[256,128]{1,0:T(8,128)S(1)}, u32[]{:S(2)}, u32[]{:S(2)}) collective-permute-start(f32[256,128]{1,0:T(8,128)S(1)} %get-tuple-element.33), channel_id=1, source_target_pairs={{0,64},{1,65},{2,66},{3,67},{4,68},{5,69},{6,70},{7,71},{8,72},{9,... | collective-permute-start | bytes 393224 | tf_op jit(solution)/shard_map/ppermute | solution.py:242
  58.2 1.7 %collective-permute-start.12 = (f32[256,128]{1,0:T(8,128)S(1)}, f32[256,128]{1,0:T(8,128)S(1)}, u32[]{:S(2)}, u32[]{:S(2)}) collective-permute-start(f32[256,128]{1,0:T(8,128)S(1)} %collective-permute-done.11.refs_1_.refs_18_), channel_id=1, source_target_pairs={{0,1},{1,0},{2,3},{3,2},{4,5},{5,4},{6,7},{7,6},{8,9},{9,8},{10,11... | collective-permute-start | bytes 393224 | tf_op jit(solution)/shard_map/ppermute | solution.py:242
  60.3 8.0 %collective-permute-start.13 = (f32[192,128]{1,0:T(8,128)S(1)}, f32[192,128]{1,0:T(8,128)S(1)}, u32[]{:S(2)}, u32[]{:S(2)}) collective-permute-start(f32[192,128]{1,0:T(8,128)S(1)} %get-tuple-element.35), channel_id=1, source_target_pairs={{0,128},{1,129},{2,130},{3,131},{4,132},{5,133},{6,134},{7,135},{8... | collective-permute-start | bytes 294920 | tf_op jit(solution)/shard_map/ppermute | solution.py:242

commit v2 on v1

--- a/solution.py
+++ b/solution.py
@@ -10,6 +10,7 @@
 R = 64
 PACK = 3 * B + 2 * R
 CHUNKS = 3
+ORDER = (2, 1, 3)
 LIMIT = 12 * 2**20
 
 
@@ -130,36 +131,50 @@
     return early, back
 
 
-def join_kernel(level, top, *refs):
-    own, parts, (pack, send) = refs[0][...], refs[1:-2], refs[-2:]
-    first, second = ordered(level, own, partner_pack(parts))
+def joined(first, second):
     early, back = turned(first, second)
     down = times(early, right_side(second[:B]))
     up = mm(back, first[B + R : 2 * B + R])
-    ahead = jnp.concatenate([down[:B], down[B:] + second[B : B + R]], axis=0)
-    behind = jnp.concatenate([up[:B], up[B:] + first[2 * B + R :]], axis=0)
-    pack[: B + R] = ahead
-    pack[B + R :] = behind
+    return jnp.concatenate(
+        [down[:B], down[B:] + second[B : B + R], up[:B], up[B:] + first[2 * B + R :]], axis=0
+    )
+
+
+def store_half(send, pack):
+    half = PACK // 2
+    send[...] = jnp.where(position() & 1 == 0, pack[:half], pack[half:])
+
+
+def pair_kernel(own, other, pack, send):
+    value = joined(*ordered(0, own[...], other[...]))
+    pack[...] = value
+    store_half(send, value)
+
+
+def quad_kernel(level, top, *refs):
+    own, parts, (near, far, pack, send) = refs[0][...], refs[1:7], refs[7:]
+    one, two, three = (partner_pack(parts[2 * i : 2 * i + 2]) for i in range(3))
+    mine = joined(*ordered(level, own, one))
+    theirs = joined(*ordered(level, two, three))
+    near[...] = mine
+    far[...] = theirs
+    value = joined(*ordered(level + 1, mine, theirs))
+    pack[...] = value
     if top:
-        send[...] = jnp.where(is_left(level + 1), ahead, behind[B:])
+        send[...] = jnp.where(is_left(level + 2), value[: B + R], value[2 * B + R :])
     else:
-        low = position() & 1 == 0
-        half = PACK // 2
-        send[: B + R] = jnp.where(low, ahead, behind[half - B - R : half])
-        send[B + R :] = jnp.where(low, behind[: half - B - R], behind[half:])
-
-
-def join(level, top, own, parts):
-    return pl.pallas_call(
-        lambda *refs: join_kernel(level, top, *refs),
-        out_shape=(
-            jax.ShapeDtypeStruct((PACK, B), jnp.float32),
-            jax.ShapeDtypeStruct((B + R if top else PACK // 2, B), jnp.float32),
-        ),
+        store_half(send, value)
+
+
+def combine(kernel, name, own, parts, extra, send_rows):
+    whole = jax.ShapeDtypeStruct((PACK, B), jnp.float32)
+    return pl.pallas_call(
+        kernel,
+        out_shape=(whole,) * (1 + extra) + (jax.ShapeDtypeStruct((send_rows, B), jnp.float32),),
         in_specs=[pl.BlockSpec(memory_space=pltpu.VMEM)] * (1 + len(parts)),
-        out_specs=[pl.BlockSpec(memory_space=pltpu.VMEM)] * 2,
-        compiler_params=pltpu.CompilerParams(vmem_limit_bytes=LIMIT),
-        name=f"join{level}",
+        out_specs=[pl.BlockSpec(memory_space=pltpu.VMEM)] * (2 + extra),
+        compiler_params=pltpu.CompilerParams(vmem_limit_bytes=LIMIT),
+        name=name,
     )(own, *parts)
 
 
@@ -239,19 +254,30 @@
 def on_device(rhs, pivot_inv, lower_gain, upper_gain):
     devices = lax.axis_size(AXES)
     top = devices.bit_length() - 2
-    swap = lambda array, level: lax.ppermute(
-        array, AXES, [(i, i ^ (1 << level)) for i in range(devices)]
-    )
+    plane = devices >> 3
+    swap = lambda array, bits: lax.ppermute(array, AXES, [(i, i ^ bits) for i in range(devices)])
     inputs = (rhs, pivot_inv, lower_gain, upper_gain)
     pack, rows = local(*(pltpu.with_memory_space_constraint(x, pltpu.HBM) for x in inputs))
-    send = pack
-    steps = []
-    for level in range(top):
-        got = swap(send, level)
-        parts = (got,) if level == 0 else (got, swap(got, 0))
-        steps.append((pack, parts))
-        pack, send = join(level, level == top - 1, pack, parts)
-    got = swap(send, top)
+    other = swap(pack, 1)
+    steps = [(pack, (other,))]
+    pack, send = combine(pair_kernel, "pair", pack, (other,), 0, PACK // 2)
+    for level in range(1, top, 2):
+        last = level == top - 2
+        got = {bits: swap(send, bits << level) for bits in ORDER}
+        twin = {bits: swap(got[bits], 1) for bits in ORDER}
+        parts = [part for bits in (1, 2, 3) for part in (got[bits], twin[bits])]
+        steps.append((pack, tuple(parts[:2])))
+        near, far, pack, send = combine(
+            lambda *refs, level=level, last=last: quad_kernel(level, last, *refs),
+            f"quad{level}",
+            pack,
+            parts,
+            2,
+            B + R if last else PACK // 2,
+        )
+        steps.append((near, (far,)))
+    mirror = [(i, devices - plane - i + 2 * (i % plane)) for i in range(devices)]
+    got = lax.ppermute(send, AXES, mirror)
     return finish(top, pack, got, track(steps), rows)
 
 

time: 70.1 us -> 62.8 us (0.90)
  waiting for transfers between devices: 40.2 us -> 25.2 us
  starting transfers between devices: 19.4 us -> 27 us
    ppermute x14 -> x20, waiting for transfers between devices: 40.2 us -> 25.2 us  [the longest x19 22.5 us: on_device(): lax.ppermute(array, AXES, [(i, i ^ bits) for i in range(devices)])]
    ppermute x14 -> x20, starting transfers between devices: 19.4 us -> 27 us  [the longest x19 22.5 us: on_device(): lax.ppermute(array, AXES, [(i, i ^ bits) for i in range(devices)])]
    pallas_call x7 -> x4, Pallas kernels: 2.36 us -> 2.59 us  [combine(): pl.pallas_call(kernel, out_shape=(whole,) * (1 + extra) + (jax.ShapeDtype...]
  transfers between devices with their start and end apart: 14 -> 20, of which waited for: 14 -> 14; matrix products, arithmetic and copies ran while one was open for 0% -> 0% of each run, Pallas kernels for 2% -> 2%
where the time goes in v2:
time: 62.8 us; the launch traced here: 62.7 us
  starting transfers between devices  27 us (43%)
  waiting for transfers between devices  25.2 us (40%)
  Pallas kernels  10.5 us (17%)
    ppermute x19, waiting for transfers between devices, on_device(): lax.ppermute(array, AXES, [(i, i ^ bits) for i in range(devices)])  22.5 us
    ppermute x19, starting transfers between devices, on_device(): lax.ppermute(array, AXES, [(i, i ^ bits) for i in range(devices)])  22.5 us
    pallas_call x1, Pallas kernels, local(): pl.pallas_call(local_kernel, out_shape=(jax.ShapeDtypeStruct((PACK, B), j...  4.73 us
    ppermute x1, starting transfers between devices, on_device(): got = lax.ppermute(send, AXES, mirror)  4.59 us
    ppermute x1, waiting for transfers between devices, on_device(): got = lax.ppermute(send, AXES, mirror)  2.62 us
    pallas_call x4, Pallas kernels, combine(): pl.pallas_call(kernel, out_shape=(whole,) * (1 + extra) + (jax.ShapeDtype...  2.59 us
    pallas_call x1, Pallas kernels, finish(): pl.pallas_call(lambda *refs: finish_kernel(level, *refs), out_shape=jax.S...  1.7 us
    pallas_call x1, Pallas kernels, track(): pl.pallas_call(lambda *refs: track_kernel(counts, *refs), out_shape=jax.S...  1.45 us
  transfers between devices with their start and end apart: 20, of which 14 were waited for; matrix products, arithmetic and copies ran while one was open for 0% of the time, Pallas kernels for 2%

profile of v2, /device:TPU:1, one launch (start us, length us, event | category | flops | bytes accessed | tf_op | source)
XLA Modules:
  0.0 62.7 jit_solution(6527600315809120734)
XLA Ops:
  0.0 4.7 %local.1 = (f32[512,128]{1,0:T(8,128)S(1)}, f32[12,320,128]{2,1,0:T(8,128)S(1)}) custom-call(f32[12,64,128]{2,1,0:T(8,128)} %rhs_hbm.1, f32[12,128,128]{2,1,0:T(8,128)} %pivot_hbm.1, f32[12,128,128]{2,1,0:T(8,128)} %lower_hbm.1, f32[12,128,128]{2,1,0:T(8,128)} %upper_hbm.1), custom_call_target="tpu_custom_call" | custom-call | tf_op jit(solution)/shard_map/local/pallas_call | solution.py:83
  4.7 3.3 %collective-permute-start = (f32[512,128]{1,0:T(8,128)S(1)}, f32[512,128]{1,0:T(8,128)S(1)}, u32[]{:S(2)}, u32[]{:S(2)}) collective-permute-start(f32[512,128]{1,0:T(8,128)S(1)} %get-tuple-element.21.own.refs_0_), channel_id=1, source_target_pairs={{0,1},{1,0},{2,3},{3,2},{4,5},{5,4},{6,7},{7,6},{8,9},{9,8},{10,11... | collective-permute-start | bytes 786440 | tf_op jit(solution)/shard_map/ppermute | solution.py:258
  8.1 1.2 %collective-permute-done.other.refs_1_ = f32[512,128]{1,0:T(8,128)S(1)} collective-permute-done((f32[512,128]{1,0:T(8,128)S(1)}, f32[512,128]{1,0:T(8,128)S(1)}, u32[]{:S(2)}, u32[]{:S(2)}) %collective-permute-start) | collective-permute-done | bytes 262176 | tf_op jit(solution)/shard_map/ppermute | solution.py:258
  9.6 0.8 %collective-permute-start.5 = (f32[256,128]{1,0:T(8,128)S(1)}, f32[256,128]{1,0:T(8,128)S(1)}, u32[]{:S(2)}, u32[]{:S(2)}) collective-permute-start(f32[256,128]{1,0:T(8,128)S(1)} %get-tuple-element.23), channel_id=1, source_target_pairs={{0,6},{1,7},{2,4},{3,5},{4,2},{5,3},{6,0},{7,1},{8,14},{9,15},{10,... | collective-permute-start | bytes 393224 | tf_op jit(solution)/shard_map/ppermute | solution.py:258
  10.4 0.5 collective-permute-start.3
  10.9 2.0 %collective-permute-start.1 = (f32[256,128]{1,0:T(8,128)S(1)}, f32[256,128]{1,0:T(8,128)S(1)}, u32[]{:S(2)}, u32[]{:S(2)}) collective-permute-start(f32[256,128]{1,0:T(8,128)S(1)} %get-tuple-element.23), channel_id=1, source_target_pairs={{0,2},{1,3},{2,0},{3,1},{4,6},{5,7},{6,4},{7,5},{8,10},{9,11},{10,... | collective-permute-start | bytes 393224 | tf_op jit(solution)/shard_map/ppermute | solution.py:258
  12.9 5.3 %collective-permute-done.5.refs_5_ = f32[256,128]{1,0:T(8,128)S(1)} collective-permute-done((f32[256,128]{1,0:T(8,128)S(1)}, f32[256,128]{1,0:T(8,128)S(1)}, u32[]{:S(2)}, u32[]{:S(2)}) %collective-permute-start.5) | collective-permute-done | bytes 131104 | tf_op jit(solution)/shard_map/ppermute | solution.py:258
  18.2 1.4 %collective-permute-start.6 = (f32[256,128]{1,0:T(8,128)S(1)}, f32[256,128]{1,0:T(8,128)S(1)}, u32[]{:S(2)}, u32[]{:S(2)}) collective-permute-start(f32[256,128]{1,0:T(8,128)S(1)} %collective-permute-done.5.refs_5_), channel_id=1, source_target_pairs={{0,1},{1,0},{2,3},{3,2},{4,5},{5,4},{6,7},{7,6},{8,9},{9,8},{10,11... | collective-permute-start | bytes 393224 | tf_op jit(solution)/shard_map/ppermute | solution.py:258
  19.6 0.6 collective-permute-start.2
  20.6 0.4 collective-permute-done.4.refs_4_
  21.2 0.8 %quad1.1 = (f32[512,128]{1,0:T(8,128)S(1)}, f32[512,128]{1,0:T(8,128)S(1)}, f32[512,128]{1,0:T(8,128)S(1)}, f32[256,128]{1,0:T(8,128)S(1)}) custom-call(f32[512,128]{1,0:T(8,128)S(1)} %get-tuple-element.22.refs_0_.refs_2_, f32[256,128]{1,0:T(8,128)S(1)} %collective-permute-done.1.refs_1_.refs_3_, f32[256,128]{1,0:T(8,128)S(1)} %collective-permute-done.2.refs_2_.refs_4_, ...), custom_call_target="tpu_custom_call" | custom-call | tf_op jit(solution)/shard_map/quad1/pallas_call | solution.py:171
  22.0 1.9 %collective-permute-start.11 = (f32[256,128]{1,0:T(8,128)S(1)}, f32[256,128]{1,0:T(8,128)S(1)}, u32[]{:S(2)}, u32[]{:S(2)}) collective-permute-start(f32[256,128]{1,0:T(8,128)S(1)} %get-tuple-element.25), channel_id=1, source_target_pairs={{0,24},{1,25},{2,26},{3,27},{4,28},{5,29},{6,30},{7,31},{8,16},{9,... | collective-permute-start | bytes 393224 | tf_op jit(solution)/shard_map/ppermute | solution.py:258
  24.2 1.1 %collective-permute-start.7 = (f32[256,128]{1,0:T(8,128)S(1)}, f32[256,128]{1,0:T(8,128)S(1)}, u32[]{:S(2)}, u32[]{:S(2)}) collective-permute-start(f32[256,128]{1,0:T(8,128)S(1)} %get-tuple-element.25), channel_id=1, source_target_pairs={{0,8},{1,9},{2,10},{3,11},{4,12},{5,13},{6,14},{7,15},{8,0},{9,1},... | collective-permute-start | bytes 393224 | tf_op jit(solution)/shard_map/ppermute | solution.py:258
  25.3 3.6 %collective-permute-done.11.refs_5_ = f32[256,128]{1,0:T(8,128)S(1)} collective-permute-done((f32[256,128]{1,0:T(8,128)S(1)}, f32[256,128]{1,0:T(8,128)S(1)}, u32[]{:S(2)}, u32[]{:S(2)}) %collective-permute-start.11) | collective-permute-done | bytes 131104 | tf_op jit(solution)/shard_map/ppermute | solution.py:258
  28.9 2.8 %collective-permute-start.12 = (f32[256,128]{1,0:T(8,128)S(1)}, f32[256,128]{1,0:T(8,128)S(1)}, u32[]{:S(2)}, u32[]{:S(2)}) collective-permute-start(f32[256,128]{1,0:T(8,128)S(1)} %collective-permute-done.11.refs_5_), channel_id=1, source_target_pairs={{0,1},{1,0},{2,3},{3,2},{4,5},{5,4},{6,7},{7,6},{8,9},{9,8},{10,11... | collective-permute-start | bytes 393224 | tf_op jit(solution)/shard_map/ppermute | solution.py:258
  31.7 0.5 collective-permute-start.10
  32.7 0.6 collective-permute-done.10.refs_4_
  33.2 0.4 collective-permute-done.8.refs_2_.refs_9_
  33.6 0.8 %quad3.1 = (f32[512,128]{1,0:T(8,128)S(1)}, f32[512,128]{1,0:T(8,128)S(1)}, f32[512,128]{1,0:T(8,128)S(1)}, f32[256,128]{1,0:T(8,128)S(1)}) custom-call(f32[512,128]{1,0:T(8,128)S(1)} %get-tuple-element.24.refs_0_.refs_7_, f32[256,128]{1,0:T(8,128)S(1)} %collective-permute-done.7.refs_1_.refs_8_, f32[256,128]{1,0:T(8,128)S(1)} %collective-permute-done.8.refs_2_.refs_9_, ...), custom_call_target="tpu_custom_call" | custom-call | tf_op jit(solution)/shard_map/quad3/pallas_call | solution.py:171
  34.4 4.4 %collective-permute-start.17 = (f32[256,128]{1,0:T(8,128)S(1)}, f32[256,128]{1,0:T(8,128)S(1)}, u32[]{:S(2)}, u32[]{:S(2)}) collective-permute-start(f32[256,128]{1,0:T(8,128)S(1)} %get-tuple-element.27), channel_id=1, source_target_pairs={{0,96},{1,97},{2,98},{3,99},{4,100},{5,101},{6,102},{7,103},{8,104... | collective-permute-start | bytes 393224 | tf_op jit(solution)/shard_map/ppermute | solution.py:258
  38.8 0.6 collective-permute-start.13
  39.3 3.3 %collective-permute-done.17.refs_5_ = f32[256,128]{1,0:T(8,128)S(1)} collective-permute-done((f32[256,128]{1,0:T(8,128)S(1)}, f32[256,128]{1,0:T(8,128)S(1)}, u32[]{:S(2)}, u32[]{:S(2)}) %collective-permute-start.17) | collective-permute-done | bytes 131104 | tf_op jit(solution)/shard_map/ppermute | solution.py:258
  42.6 1.0 %collective-permute-start.18 = (f32[256,128]{1,0:T(8,128)S(1)}, f32[256,128]{1,0:T(8,128)S(1)}, u32[]{:S(2)}, u32[]{:S(2)}) collective-permute-start(f32[256,128]{1,0:T(8,128)S(1)} %collective-permute-done.17.refs_5_), channel_id=1, source_target_pairs={{0,1},{1,0},{2,3},{3,2},{4,5},{5,4},{6,7},{7,6},{8,9},{9,8},{10,11... | collective-permute-start | bytes 393224 | tf_op jit(solution)/shard_map/ppermute | solution.py:258
  43.6 5.9 %collective-permute-done.15.refs_3_ = f32[256,128]{1,0:T(8,128)S(1)} collective-permute-done((f32[256,128]{1,0:T(8,128)S(1)}, f32[256,128]{1,0:T(8,128)S(1)}, u32[]{:S(2)}, u32[]{:S(2)}) %collective-permute-start.15) | collective-permute-done | bytes 131104 | tf_op jit(solution)/shard_map/ppermute | solution.py:258
  49.5 0.8 %collective-permute-start.16 = (f32[256,128]{1,0:T(8,128)S(1)}, f32[256,128]{1,0:T(8,128)S(1)}, u32[]{:S(2)}, u32[]{:S(2)}) collective-permute-start(f32[256,128]{1,0:T(8,128)S(1)} %collective-permute-done.15.refs_3_), channel_id=1, source_target_pairs={{0,1},{1,0},{2,3},{3,2},{4,5},{5,4},{6,7},{7,6},{8,9},{9,8},{10,11... | collective-permute-start | bytes 393224 | tf_op jit(solution)/shard_map/ppermute | solution.py:258
  50.3 1.0 %collective-permute-done.16.refs_4_ = f32[256,128]{1,0:T(8,128)S(1)} collective-permute-done((f32[256,128]{1,0:T(8,128)S(1)}, f32[256,128]{1,0:T(8,128)S(1)}, u32[]{:S(2)}, u32[]{:S(2)}) %collective-permute-start.16) | collective-permute-done | bytes 131104 | tf_op jit(solution)/shard_map/ppermute | solution.py:258
  51.3 0.4 collective-permute-done.14.refs_2_.refs_14_
  51.6 0.8 %quad5.1 = (f32[512,128]{1,0:T(8,128)S(1)}, f32[512,128]{1,0:T(8,128)S(1)}, f32[512,128]{1,0:T(8,128)S(1)}, f32[192,128]{1,0:T(8,128)S(1)}) custom-call(f32[512,128]{1,0:T(8,128)S(1)} %get-tuple-element.26.refs_0_.refs_12_, f32[256,128]{1,0:T(8,128)S(1)} %collective-permute-done.13.refs_1_.refs_13_, f32[256,128]{1,0:T(8,128)S(1)} %collective-permute-done.14.refs_2_.refs_14_, ...), custom_call_target="tpu_custom_call" | custom-call | tf_op jit(solution)/shard_map/quad5/pallas_call | solution.py:171
  52.4 4.6 %collective-permute-start.19 = (f32[192,128]{1,0:T(8,128)S(1)}, f32[192,128]{1,0:T(8,128)S(1)}, u32[]{:S(2)}, u32[]{:S(2)}) collective-permute-start(f32[192,128]{1,0:T(8,128)S(1)} %get-tuple-element.29), channel_id=1, source_target_pairs={{0,224},{1,225},{2,226},{3,227},{4,228},{5,229},{6,230},{7,231},{8... | collective-permute-start | bytes 294920 | tf_op jit(solution)/shard_map/ppermute | solution.py:280
  57.0 1.5 %track.1.refs_2_ = f32[512,128]{1,0:T(8,128)S(1)} custom-call(f32[512,128]{1,0:T(8,128)S(1)} %get-tuple-element.21.own.refs_0_, f32[512,128]{1,0:T(8,128)S(1)} %collective-permute-done.other.refs_1_, f32[512,128]{1,0:T(8,128)S(1)} %get-tuple-element.22.refs_0_.refs_2_, f32[256,128]{1,0:T(8,128)S(1)} %collective-permute-done.1.refs_1_.refs_3_, ...), custom_call_target="tpu_custom_call" | custom-call | flops 1879048192 | bytes 3670016 | tf_op jit(solution)/shard_map/track/pallas_call | solution.py:209
  58.4 2.6 %collective-permute-done.19.refs_1_ = f32[192,128]{1,0:T(8,128)S(1)} collective-permute-done((f32[192,128]{1,0:T(8,128)S(1)}, f32[192,128]{1,0:T(8,128)S(1)}, u32[]{:S(2)}, u32[]{:S(2)}) %collective-permute-start.19) | collective-permute-done | bytes 98336 | tf_op jit(solution)/shard_map/ppermute | solution.py:280
  61.0 1.7 %finish.1 = f32[12,64,128]{2,1,0:T(8,128)} custom-call(f32[512,128]{1,0:T(8,128)S(1)} %get-tuple-element.28.refs_0_, f32[192,128]{1,0:T(8,128)S(1)} %collective-permute-done.19.refs_1_, f32[512,128]{1,0:T(8,128)S(1)} %track.1.refs_2_, f32[12,320,128]{2,1,0:T(8,128)S(1)} %get-tuple-element.36.refs_3_), custom_call_target="tpu_custom_call" | custom-call | tf_op jit(solution)/shard_map/finish/pallas_call | solution.py:244
  (15 shorter events, 1.8 us)
Async XLA Ops:
  4.7 4.5 %collective-permute-start = (f32[512,128]{1,0:T(8,128)S(1)}, f32[512,128]{1,0:T(8,128)S(1)}, u32[]{:S(2)}, u32[]{:S(2)}) collective-permute-start(f32[512,128]{1,0:T(8,128)S(1)} %get-tuple-element.21.own.refs_0_), channel_id=1, source_target_pairs={{0,1},{1,0},{2,3},{3,2},{4,5},{5,4},{6,7},{7,6},{8,9},{9,8},{10,11... | collective-permute-start | bytes 786440 | tf_op jit(solution)/shard_map/ppermute | solution.py:258
  9.6 8.6 %collective-permute-start.5 = (f32[256,128]{1,0:T(8,128)S(1)}, f32[256,128]{1,0:T(8,128)S(1)}, u32[]{:S(2)}, u32[]{:S(2)}) collective-permute-start(f32[256,128]{1,0:T(8,128)S(1)} %get-tuple-element.23), channel_id=1, source_target_pairs={{0,6},{1,7},{2,4},{3,5},{4,2},{5,3},{6,0},{7,1},{8,14},{9,15},{10,... | collective-permute-start | bytes 393224 | tf_op jit(solution)/shard_map/ppermute | solution.py:258
  10.4 9.2 %collective-permute-start.3 = (f32[256,128]{1,0:T(8,128)S(1)}, f32[256,128]{1,0:T(8,128)S(1)}, u32[]{:S(2)}, u32[]{:S(2)}) collective-permute-start(f32[256,128]{1,0:T(8,128)S(1)} %get-tuple-element.23), channel_id=1, source_target_pairs={{0,4},{1,5},{2,6},{3,7},{4,0},{5,1},{6,2},{7,3},{8,12},{9,13},{10,... | collective-permute-start | bytes 393224 | tf_op jit(solution)/shard_map/ppermute | solution.py:258
  10.9 8.7 %collective-permute-start.1 = (f32[256,128]{1,0:T(8,128)S(1)}, f32[256,128]{1,0:T(8,128)S(1)}, u32[]{:S(2)}, u32[]{:S(2)}) collective-permute-start(f32[256,128]{1,0:T(8,128)S(1)} %get-tuple-element.23), channel_id=1, source_target_pairs={{0,2},{1,3},{2,0},{3,1},{4,6},{5,7},{6,4},{7,5},{8,10},{9,11},{10,... | collective-permute-start | bytes 393224 | tf_op jit(solution)/shard_map/ppermute | solution.py:258
  18.2 2.4 %collective-permute-start.6 = (f32[256,128]{1,0:T(8,128)S(1)}, f32[256,128]{1,0:T(8,128)S(1)}, u32[]{:S(2)}, u32[]{:S(2)}) collective-permute-start(f32[256,128]{1,0:T(8,128)S(1)} %collective-permute-done.5.refs_5_), channel_id=1, source_target_pairs={{0,1},{1,0},{2,3},{3,2},{4,5},{5,4},{6,7},{7,6},{8,9},{9,8},{10,11... | collective-permute-start | bytes 393224 | tf_op jit(solution)/shard_map/ppermute | solution.py:258
  19.6 1.3 %collective-permute-start.4 = (f32[256,128]{1,0:T(8,128)S(1)}, f32[256,128]{1,0:T(8,128)S(1)}, u32[]{:S(2)}, u32[]{:S(2)}) collective-permute-start(f32[256,128]{1,0:T(8,128)S(1)} %collective-permute-done.3.refs_3_), channel_id=1, source_target_pairs={{0,1},{1,0},{2,3},{3,2},{4,5},{5,4},{6,7},{7,6},{8,9},{9,8},{10,11... | collective-permute-start | bytes 393224 | tf_op jit(solution)/shard_map/ppermute | solution.py:258
  19.6 1.6 %collective-permute-start.2 = (f32[256,128]{1,0:T(8,128)S(1)}, f32[256,128]{1,0:T(8,128)S(1)}, u32[]{:S(2)}, u32[]{:S(2)}) collective-permute-start(f32[256,128]{1,0:T(8,128)S(1)} %collective-permute-done.1.refs_1_.refs_3_), channel_id=1, source_target_pairs={{0,1},{1,0},{2,3},{3,2},{4,5},{5,4},{6,7},{7,6},{8,9},{9,8},{10,11... | collective-permute-start | bytes 393224 | tf_op jit(solution)/shard_map/ppermute | solution.py:258
  22.0 6.9 %collective-permute-start.11 = (f32[256,128]{1,0:T(8,128)S(1)}, f32[256,128]{1,0:T(8,128)S(1)}, u32[]{:S(2)}, u32[]{:S(2)}) collective-permute-start(f32[256,128]{1,0:T(8,128)S(1)} %get-tuple-element.25), channel_id=1, source_target_pairs={{0,24},{1,25},{2,26},{3,27},{4,28},{5,29},{6,30},{7,31},{8,16},{9,... | collective-permute-start | bytes 393224 | tf_op jit(solution)/shard_map/ppermute | solution.py:258
  23.9 7.8 %collective-permute-start.9 = (f32[256,128]{1,0:T(8,128)S(1)}, f32[256,128]{1,0:T(8,128)S(1)}, u32[]{:S(2)}, u32[]{:S(2)}) collective-permute-start(f32[256,128]{1,0:T(8,128)S(1)} %get-tuple-element.25), channel_id=1, source_target_pairs={{0,16},{1,17},{2,18},{3,19},{4,20},{5,21},{6,22},{7,23},{8,24},{9,... | collective-permute-start | bytes 393224 | tf_op jit(solution)/shard_map/ppermute | solution.py:258
  24.2 8.0 %collective-permute-start.7 = (f32[256,128]{1,0:T(8,128)S(1)}, f32[256,128]{1,0:T(8,128)S(1)}, u32[]{:S(2)}, u32[]{:S(2)}) collective-permute-start(f32[256,128]{1,0:T(8,128)S(1)} %get-tuple-element.25), channel_id=1, source_target_pairs={{0,8},{1,9},{2,10},{3,11},{4,12},{5,13},{6,14},{7,15},{8,0},{9,1},... | collective-permute-start | bytes 393224 | tf_op jit(solution)/shard_map/ppermute | solution.py:258
  28.9 3.8 %collective-permute-start.12 = (f32[256,128]{1,0:T(8,128)S(1)}, f32[256,128]{1,0:T(8,128)S(1)}, u32[]{:S(2)}, u32[]{:S(2)}) collective-permute-start(f32[256,128]{1,0:T(8,128)S(1)} %collective-permute-done.11.refs_5_), channel_id=1, source_target_pairs={{0,1},{1,0},{2,3},{3,2},{4,5},{5,4},{6,7},{7,6},{8,9},{9,8},{10,11... | collective-permute-start | bytes 393224 | tf_op jit(solution)/shard_map/ppermute | solution.py:258
  31.7 1.5 %collective-permute-start.10 = (f32[256,128]{1,0:T(8,128)S(1)}, f32[256,128]{1,0:T(8,128)S(1)}, u32[]{:S(2)}, u32[]{:S(2)}) collective-permute-start(f32[256,128]{1,0:T(8,128)S(1)} %collective-permute-done.9.refs_3_), channel_id=1, source_target_pairs={{0,1},{1,0},{2,3},{3,2},{4,5},{5,4},{6,7},{7,6},{8,9},{9,8},{10,11... | collective-permute-start | bytes 393224 | tf_op jit(solution)/shard_map/ppermute | solution.py:258
  32.3 1.3 %collective-permute-start.8 = (f32[256,128]{1,0:T(8,128)S(1)}, f32[256,128]{1,0:T(8,128)S(1)}, u32[]{:S(2)}, u32[]{:S(2)}) collective-permute-start(f32[256,128]{1,0:T(8,128)S(1)} %collective-permute-done.7.refs_1_.refs_8_), channel_id=1, source_target_pairs={{0,1},{1,0},{2,3},{3,2},{4,5},{5,4},{6,7},{7,6},{8,9},{9,8},{10,11... | collective-permute-start | bytes 393224 | tf_op jit(solution)/shard_map/ppermute | solution.py:258
  34.4 8.2 %collective-permute-start.17 = (f32[256,128]{1,0:T(8,128)S(1)}, f32[256,128]{1,0:T(8,128)S(1)}, u32[]{:S(2)}, u32[]{:S(2)}) collective-permute-start(f32[256,128]{1,0:T(8,128)S(1)} %get-tuple-element.27), channel_id=1, source_target_pairs={{0,96},{1,97},{2,98},{3,99},{4,100},{5,101},{6,102},{7,103},{8,104... | collective-permute-start | bytes 393224 | tf_op jit(solution)/shard_map/ppermute | solution.py:258
  38.7 10.7 %collective-permute-start.15 = (f32[256,128]{1,0:T(8,128)S(1)}, f32[256,128]{1,0:T(8,128)S(1)}, u32[]{:S(2)}, u32[]{:S(2)}) collective-permute-start(f32[256,128]{1,0:T(8,128)S(1)} %get-tuple-element.27), channel_id=1, source_target_pairs={{0,64},{1,65},{2,66},{3,67},{4,68},{5,69},{6,70},{7,71},{8,72},{9,... | collective-permute-start | bytes 393224 | tf_op jit(solution)/shard_map/ppermute | solution.py:258
  38.8 11.5 %collective-permute-start.13 = (f32[256,128]{1,0:T(8,128)S(1)}, f32[256,128]{1,0:T(8,128)S(1)}, u32[]{:S(2)}, u32[]{:S(2)}) collective-permute-start(f32[256,128]{1,0:T(8,128)S(1)} %get-tuple-element.27), channel_id=1, source_target_pairs={{0,32},{1,33},{2,34},{3,35},{4,36},{5,37},{6,38},{7,39},{8,40},{9,... | collective-permute-start | bytes 393224 | tf_op jit(solution)/shard_map/ppermute | solution.py:258
  42.6 7.7 %collective-permute-start.18 = (f32[256,128]{1,0:T(8,128)S(1)}, f32[256,128]{1,0:T(8,128)S(1)}, u32[]{:S(2)}, u32[]{:S(2)}) collective-permute-start(f32[256,128]{1,0:T(8,128)S(1)} %collective-permute-done.17.refs_5_), channel_id=1, source_target_pairs={{0,1},{1,0},{2,3},{3,2},{4,5},{5,4},{6,7},{7,6},{8,9},{9,8},{10,11... | collective-permute-start | bytes 393224 | tf_op jit(solution)/shard_map/ppermute | solution.py:258
  49.5 1.8 %collective-permute-start.16 = (f32[256,128]{1,0:T(8,128)S(1)}, f32[256,128]{1,0:T(8,128)S(1)}, u32[]{:S(2)}, u32[]{:S(2)}) collective-permute-start(f32[256,128]{1,0:T(8,128)S(1)} %collective-permute-done.15.refs_3_), channel_id=1, source_target_pairs={{0,1},{1,0},{2,3},{3,2},{4,5},{5,4},{6,7},{7,6},{8,9},{9,8},{10,11... | collective-permute-start | bytes 393224 | tf_op jit(solution)/shard_map/ppermute | solution.py:258
  50.3 1.3 %collective-permute-start.14 = (f32[256,128]{1,0:T(8,128)S(1)}, f32[256,128]{1,0:T(8,128)S(1)}, u32[]{:S(2)}, u32[]{:S(2)}) collective-permute-start(f32[256,128]{1,0:T(8,128)S(1)} %collective-permute-done.13.refs_1_.refs_13_), channel_id=1, source_target_pairs={{0,1},{1,0},{2,3},{3,2},{4,5},{5,4},{6,7},{7,6},{8,9},{9,8},{10,11... | collective-permute-start | bytes 393224 | tf_op jit(solution)/shard_map/ppermute | solution.py:258
  52.4 8.7 %collective-permute-start.19 = (f32[192,128]{1,0:T(8,128)S(1)}, f32[192,128]{1,0:T(8,128)S(1)}, u32[]{:S(2)}, u32[]{:S(2)}) collective-permute-start(f32[192,128]{1,0:T(8,128)S(1)} %get-tuple-element.29), channel_id=1, source_target_pairs={{0,224},{1,225},{2,226},{3,227},{4,228},{5,229},{6,230},{7,231},{8... | collective-permute-start | bytes 294920 | tf_op jit(solution)/shard_map/ppermute | solution.py:280

commit v3 on v2

v3 whole, which is shorter than its diff:
```python
import jax
import jax.numpy as jnp
from jax import lax
from jax.experimental import pallas as pl
from jax.experimental.pallas import tpu as pltpu
from jax.sharding import PartitionSpec as P

AXES = ("wide", "narrow")
B = 128
R = 64
PACK = 3 * B + 2 * R
PARTS = 2
OUT_ROWS = 3
PLANS = ((1, (1, 2)), (3, (1, 2)), (5, (1, 3)))
LIMIT = 12 * 2**20


def halves(value):
    high = value.astype(jnp.bfloat16)
    low = (value - high.astype(jnp.float32)).astype(jnp.bfloat16)
    return high, low


def left_side(value):
    return jnp.concatenate(halves(value), axis=1)


def right_side(value):
    both = jnp.concatenate(halves(value), axis=1)
    return jnp.concatenate([both, both], axis=0)


def times(left, right):
    wide = jnp.dot(left, right, preferred_element_type=jnp.float32)
    return wide[:, :B] + wide[:, B:]


def mm(left, right):
    return times(left_side(left), right_side(right))


def local_kernel(
    rhs_hbm,
    pivot_hbm,
    lower_hbm,
    upper_hbm,
    pack,
    parts,
    rows,
    rhs,
    pivot_inv,
    lower,
    upper,
    forward,
    sems,
):
    count = rhs.shape[1]
    pairs = ((pivot_hbm, pivot_inv), (rhs_hbm, rhs), (lower_hbm, lower), (upper_hbm, upper))
    edges = (0, 1, count // 2, count)
    spans = list(zip(edges[:-1], edges[1:]))
    waits = {}

    def fetch(which, slot, start, stop, row):
        source, target = pairs[which]
        span = (slice(None), pl.ds(start, stop - start))
        copy = pltpu.make_async_copy(source.at[span], target.at[span], sems.at[which, slot])
        copy.start()
        waits.setdefault((which // 3, row), []).append(copy)

    for slot, (start, stop) in enumerate(spans):
        for which in range(3):
            fetch(which, slot, start, stop, start)
    fetch(3, 1, count // 2, count, count - 1)
    fetch(3, 0, 0, count // 2, count // 2 - 1)
    states = [None] * PARTS
    scaled = {}
    for i in range(count):
        if (0, i) in waits:
            for copy in waits[0, i]:
                copy.wait()
            stop = next(stop for start, stop in spans if start == i)
            for j in range(i, stop):
                for part in range(PARTS):
                    scaled[part, j] = mm(rhs[part, j], pivot_inv[part, j])
        for part in range(PARTS):
            if i == 0:
                state = jnp.concatenate([-lower[part, 0], scaled[part, 0]], axis=0)
            else:
                moved = mm(states[part], lower[part, i])
                state = jnp.concatenate([-moved[:B], scaled[part, i] - moved[B:]], axis=0)
            forward[part, i] = state
            states[part] = state
    for part in range(PARTS):
        parts[part, : B + R] = states[part]
    for i in range(count - 1, -1, -1):
        for copy in waits.get((1, i), []):
            copy.wait()
        for part in range(PARTS):
            if i == count - 1:
                state = jnp.concatenate([-upper[part, i], states[part]], axis=0)
            else:
                moved = mm(states[part], upper[part, i])
                state = jnp.concatenate([-moved[:B], forward[part, i] - moved[B:]], axis=0)
            rows[part, i] = state
            states[part] = state
    for part in range(PARTS):
        parts[part, B + R :] = states[part]
    pack[...] = joined(parts[0], parts[1])


def local(rhs, pivot_inv, lower, upper):
    inputs = [
        pltpu.with_memory_space_constraint(
            x.reshape((PARTS, x.shape[0] // PARTS) + x.shape[1:]), pltpu.HBM
        )
        for x in (rhs, pivot_inv, lower, upper)
    ]
    count = inputs[0].shape[1]
    return pl.pallas_call(
        local_kernel,
        out_shape=(
            jax.ShapeDtypeStruct((PACK, B), jnp.float32),
            jax.ShapeDtypeStruct((PARTS, PACK, B), jnp.float32),
            jax.ShapeDtypeStruct((PARTS, count, 2 * B + R, B), jnp.float32),
        ),
        in_specs=[pl.BlockSpec(memory_space=pltpu.HBM)] * 4,
        out_specs=[pl.BlockSpec(memory_space=pltpu.VMEM)] * 3,
        scratch_shapes=[pltpu.VMEM(x.shape, jnp.float32) for x in inputs]
        + [
            pltpu.VMEM((PARTS, count, B + R, B), jnp.float32),
            pltpu.SemaphoreType.DMA((4, 3)),
        ],
        compiler_params=pltpu.CompilerParams(vmem_limit_bytes=LIMIT),
        name="local",
    )(*inputs)


def position():
    return lax.axis_index(AXES[0]) * lax.axis_size(AXES[1]) + lax.axis_index(AXES[1])


def is_left(level):
    return (position() >> level) & 1 == 0


def ordered(level, own, other):
    left = is_left(level)
    return jnp.where(left, own, other), jnp.where(left, other, own)


def by_core(here, there):
    low = position() & 1 == 0
    return jnp.where(low, here, there), jnp.where(low, there, here)


def turned(first, second):
    early = left_side(first[: B + R])
    turn = times(early, right_side(second[2 * B + R : 3 * B + R]))
    back = jnp.concatenate(
        [second[B + R : 2 * B + R], turn[:B], turn[B:] + second[3 * B + R :]], axis=0
    )
    return early, back


def joined(first, second):
    early, back = turned(first, second)
    down = times(early, right_side(second[:B]))
    up = mm(back, first[B + R : 2 * B + R])
    return jnp.concatenate(
        [down[:B], down[B:] + second[B : B + R], up[:B], up[B:] + first[2 * B + R :]], axis=0
    )


def store_half(send, pack):
    half = PACK // 2
    send[...] = jnp.where(position() & 1 == 0, pack[:half], pack[half:])


def pair_kernel(own, other, pack, send):
    value = joined(*ordered(0, own[...], other[...]))
    pack[...] = value
    store_half(send, value)


def quad_kernel(level, plan, top, *refs):
    own, whole, whole_twin, half, half_twin, one, near, far, pack, send = refs
    partner = dict(zip(plan, by_core(whole[...], whole_twin[...])))
    partner[6 - sum(plan)] = jnp.concatenate(by_core(half[...], half_twin[...]), axis=0)
    one[...] = partner[1]
    mine = joined(*ordered(level, own[...], partner[1]))
    theirs = joined(*ordered(level, partner[2], partner[3]))
    near[...] = mine
    far[...] = theirs
    value = joined(*ordered(level + 1, mine, theirs))
    pack[...] = value
    if top:
        send[...] = jnp.where(is_left(level + 2), value[: B + R], value[2 * B + R :])
    else:
        store_half(send, value)


def combine(kernel, name, own, parts, extra, send_rows):
    whole = jax.ShapeDtypeStruct((PACK, B), jnp.float32)
    return pl.pallas_call(
        kernel,
        out_shape=(whole,) * (1 + extra) + (jax.ShapeDtypeStruct((send_rows, B), jnp.float32),),
        in_specs=[pl.BlockSpec(memory_space=pltpu.VMEM)] * (1 + len(parts)),
        out_specs=[pl.BlockSpec(memory_space=pltpu.VMEM)] * (2 + extra),
        compiler_params=pltpu.CompilerParams(vmem_limit_bytes=LIMIT),
        name=name,
    )(own, *parts)


def track_kernel(levels, *refs):
    parts, track = refs[0], refs[-1]
    eye = (
        lax.broadcasted_iota(jnp.int32, (B, B), 0) == lax.broadcasted_iota(jnp.int32, (B, B), 1)
    ).astype(jnp.float32)
    none = jnp.zeros((B + R, B), jnp.float32)
    _, back = turned(parts[0], parts[1])
    aheads = [jnp.concatenate([eye, none[:R]], axis=0), parts[0, : B + R]]
    behinds = [back, jnp.concatenate([eye, none], axis=0)]
    for level in range(levels):
        first, second = ordered(level, refs[1 + 2 * level][...], refs[2 + 2 * level][...])
        early, back = turned(first, second)
        late = left_side(back)
        left = is_left(level)
        for part in range(PARTS):
            ahead, behind = aheads[part], behinds[part]
            through = times(late, right_side(behind[:B]))
            through = jnp.concatenate([through[:B], through[B:] + behind[B:]], axis=0)
            onward = times(early, right_side(ahead[:B]))
            onward = jnp.concatenate([onward[:B], onward[B:] + ahead[B:]], axis=0)
            cross = times(early, right_side(behind[B : 2 * B]))
            cross = jnp.concatenate([behind[:B], cross[:B], cross[B:] + behind[2 * B :]], axis=0)
            aheads[part] = jnp.where(left, ahead, onward)
            behinds[part] = jnp.where(left, through, cross)
    for part in range(PARTS):
        track[part, : B + R] = aheads[part]
        track[part, B + R :] = behinds[part]


def track(parts, steps):
    return pl.pallas_call(
        lambda *refs: track_kernel(len(steps), *refs),
        out_shape=jax.ShapeDtypeStruct((PARTS, PACK, B), jnp.float32),
        in_specs=[pl.BlockSpec(memory_space=pltpu.VMEM)] * (1 + 2 * len(steps)),
        out_specs=pl.BlockSpec(memory_space=pltpu.VMEM),
        compiler_params=pltpu.CompilerParams(vmem_limit_bytes=LIMIT),
        cost_estimate=pl.CostEstimate(
            flops=len(steps) * 2**28, bytes_accessed=len(steps) * 2**19, transcendentals=0
        ),
        name="track",
    )(parts, *(array for step in steps for array in step))


def finish_kernel(level, own, got, track, rows, out_hbm, out, sems):
    left = is_left(level)
    zero = jnp.zeros((R, B), jnp.float32)
    behind = jnp.where(left, zero, got[B:])
    ahead = jnp.where(left, mm(own[B : B + R], got[:B]) + got[B:], zero)
    ahead, behind = left_side(ahead), left_side(behind)
    count = rows.shape[1]
    copies = []
    for part in range(PARTS):
        x_in = (
            times(ahead, right_side(track[part, B + R : 2 * B + R]))
            + times(behind, right_side(track[part, 2 * B + R : 3 * B + R]))
            + track[part, 3 * B + R :]
        )
        f_in = times(behind, right_side(track[part, :B])) + track[part, B : B + R]
        x_in, f_in = left_side(x_in), left_side(f_in)
        for i in range(count):
            out[part * count + i] = (
                rows[part, i, 2 * B :]
                + times(x_in, right_side(rows[part, i, :B]))
                + times(f_in, right_side(rows[part, i, B : 2 * B]))
            )
            done = part * count + i + 1
            if done % OUT_ROWS == 0:
                span = pl.ds(done - OUT_ROWS, OUT_ROWS)
                copies.append(
                    pltpu.make_async_copy(out.at[span], out_hbm.at[span], sems.at[len(copies)])
                )
                copies[-1].start()
    for copy in copies:
        copy.wait()


def finish(level, own, got, tracked, rows):
    shape = (rows.shape[0] * rows.shape[1], R, B)
    return pl.pallas_call(
        lambda *refs: finish_kernel(level, *refs),
        out_shape=jax.ShapeDtypeStruct(shape, jnp.float32),
        in_specs=[pl.BlockSpec(memory_space=pltpu.VMEM)] * 4,
        out_specs=pl.BlockSpec(memory_space=pltpu.HBM),
        scratch_shapes=[
            pltpu.VMEM(shape, jnp.float32),
            pltpu.SemaphoreType.DMA((shape[0] // OUT_ROWS,)),
        ],
        compiler_params=pltpu.CompilerParams(vmem_limit_bytes=LIMIT),
        name="finish",
    )(own, got, tracked, rows)


def on_device(rhs, pivot_inv, lower_gain, upper_gain):
    devices = lax.axis_size(AXES)
    top = devices.bit_length() - 2
    plane = devices >> 3
    swap = lambda array, even, odd: lax.ppermute(
        array, AXES, [(i, i ^ (odd if i & 1 else even)) for i in range(devices)]
    )
    pack, parts, rows = local(rhs, pivot_inv, lower_gain, upper_gain)
    other = swap(pack, 1, 1)
    steps = [(pack, other)]
    pack, half = combine(pair_kernel, "pair", pack, (other,), 0, PACK // 2)
    for level, plan in PLANS:
        last = level == top - 2
        third = 6 - sum(plan)
        halves = swap(half, third << level, third << level)
        whole = swap(pack, plan[0] << level, plan[1] << level)
        received = (whole, swap(whole, 1, 1), halves, swap(halves, 1, 1))
        own = pack
        one, near, far, pack, half = combine(
            lambda *refs, level=level, plan=plan, last=last: quad_kernel(level, plan, last, *refs),
            f"quad{level}",
            own,
            received,
            3,
            B + R if last else PACK // 2,
        )
        steps += [(own, one), (near, far)]
    mirror = [(i, devices - plane - i + 2 * (i % plane)) for i in range(devices)]
    got = lax.ppermute(half, AXES, mirror)
    return finish(top, pack, got, track(parts, steps), rows)


def solution(mesh):
    placed = P(AXES, None, None)
    return jax.shard_map(
        on_device,
        mesh=mesh,
        in_specs=(placed,) * 4,
        out_specs=placed,
        check_vma=False,
    )
```

time: 62.8 us -> 59.4 us (0.946)
  starting transfers between devices: 27 us -> 16.7 us
  waiting for transfers between devices: 25.2 us -> 32.2 us
    ppermute x20 -> x14, starting transfers between devices: 27 us -> 16.7 us  [the longest x13 11.9 us: on_device(): lax.ppermute(array, AXES, [(i, i ^ (odd if i & 1 else even)) for i in ran...]
    ppermute x20 -> x14, waiting for transfers between devices: 25.2 us -> 32.2 us  [the longest x13 29.9 us: on_device(): lax.ppermute(array, AXES, [(i, i ^ (odd if i & 1 else even)) for i in ran...]
    pallas_call x1, Pallas kernels: 4.73 us -> 3.66 us  [local(): pl.pallas_call(local_kernel, out_shape=(jax.ShapeDtypeStruct((PACK, B), j...]
  transfers between devices with their start and end apart: 20 -> 14, of which waited for: 14 -> 11; matrix products, arithmetic and copies ran while one was open for 0% -> 0% of each run, Pallas kernels for 2% -> 3%
where the time goes in v3:
time: 59.4 us; the launch traced here: 59.2 us
  waiting for transfers between devices  32.2 us (54%)
  starting transfers between devices  16.7 us (28%)
  Pallas kernels  10.1 us (17%)
    ppermute x13, waiting for transfers between devices, on_device(): lax.ppermute(array, AXES, [(i, i ^ (odd if i & 1 else even)) for i in ran...  29.9 us
    ppermute x13, starting transfers between devices, on_device(): lax.ppermute(array, AXES, [(i, i ^ (odd if i & 1 else even)) for i in ran...  11.9 us
    ppermute x1, starting transfers between devices, on_device(): got = lax.ppermute(half, AXES, mirror)  4.76 us
    pallas_call x1, Pallas kernels, local(): pl.pallas_call(local_kernel, out_shape=(jax.ShapeDtypeStruct((PACK, B), j...  3.66 us
    pallas_call x4, Pallas kernels, combine(): pl.pallas_call(kernel, out_shape=(whole,) * (1 + extra) + (jax.ShapeDtype...  2.61 us
    ppermute x1, waiting for transfers between devices, on_device(): got = lax.ppermute(half, AXES, mirror)  2.31 us
    pallas_call x1, Pallas kernels, track(): pl.pallas_call(lambda *refs: track_kernel(len(steps), *refs), out_shape=j...  2.05 us
    pallas_call x1, Pallas kernels, finish(): pl.pallas_call(lambda *refs: finish_kernel(level, *refs), out_shape=jax.S...  1.78 us
  transfers between devices with their start and end apart: 14, of which 11 were waited for; matrix products, arithmetic and copies ran while one was open for 0% of the time, Pallas kernels for 3%

profile of v3, /device:TPU:1, one launch (start us, length us, event | category | flops | bytes accessed | tf_op | source)
XLA Modules:
  0.0 59.2 jit_solution(302042846985611903)
XLA Ops:
  0.0 3.7 %local.1 = (f32[512,128]{1,0:T(8,128)S(1)}, f32[2,512,128]{2,1,0:T(8,128)S(1)}, f32[2,6,320,128]{3,2,1,0:T(8,128)S(1)}) custom-call(f32[2,6,64,128]{3,2,1,0:T(8,128)} %bitcast.7, f32[2,6,128,128]{3,2,1,0:T(8,128)} %bitcast.4, f32[2,6,128,128]{3,2,1,0:T(8,128)} %bitcast.5, f32[2,6,128,128]{3,2,1,0:T(8,128)} %bitcast.6), custom_call_target="tpu_custom_call" | custom-call | tf_op jit(solution)/shard_map/local/pallas_call | solution.py:119
  3.7 3.3 %collective-permute-start = (f32[512,128]{1,0:T(8,128)S(1)}, f32[512,128]{1,0:T(8,128)S(1)}, u32[]{:S(2)}, u32[]{:S(2)}) collective-permute-start(f32[512,128]{1,0:T(8,128)S(1)} %get-tuple-element.25.own.refs_1_), channel_id=1, source_target_pairs={{0,1},{1,0},{2,3},{3,2},{4,5},{5,4},{6,7},{7,6},{8,9},{9,8},{10,11... | collective-permute-start | bytes 786440 | tf_op jit(solution)/shard_map/ppermute | solution.py:310
  7.0 1.2 %collective-permute-done.other.refs_2_ = f32[512,128]{1,0:T(8,128)S(1)} collective-permute-done((f32[512,128]{1,0:T(8,128)S(1)}, f32[512,128]{1,0:T(8,128)S(1)}, u32[]{:S(2)}, u32[]{:S(2)}) %collective-permute-start) | collective-permute-done | bytes 262176 | tf_op jit(solution)/shard_map/ppermute | solution.py:310
  8.2 0.3 pair.1
  8.5 1.1 %collective-permute-start.1 = (f32[512,128]{1,0:T(8,128)S(1)}, f32[512,128]{1,0:T(8,128)S(1)}, u32[]{:S(2)}, u32[]{:S(2)}) collective-permute-start(f32[512,128]{1,0:T(8,128)S(1)} %get-tuple-element.26.refs_0_.refs_3_), channel_id=1, source_target_pairs={{0,2},{1,5},{2,0},{3,7},{4,6},{5,1},{6,4},{7,3},{8,10},{9,13},{10,... | collective-permute-start | bytes 786440 | tf_op jit(solution)/shard_map/ppermute | solution.py:310
  9.6 0.9 %collective-permute-start.3 = (f32[256,128]{1,0:T(8,128)S(1)}, f32[256,128]{1,0:T(8,128)S(1)}, u32[]{:S(2)}, u32[]{:S(2)}) collective-permute-start(f32[256,128]{1,0:T(8,128)S(1)} %get-tuple-element.27), channel_id=1, source_target_pairs={{0,6},{1,7},{2,4},{3,5},{4,2},{5,3},{6,0},{7,1},{8,14},{9,15},{10,... | collective-permute-start | bytes 393224 | tf_op jit(solution)/shard_map/ppermute | solution.py:310
  10.5 7.5 %collective-permute-done.1.refs_1_ = f32[512,128]{1,0:T(8,128)S(1)} collective-permute-done((f32[512,128]{1,0:T(8,128)S(1)}, f32[512,128]{1,0:T(8,128)S(1)}, u32[]{:S(2)}, u32[]{:S(2)}) %collective-permute-start.1) | collective-permute-done | bytes 262176 | tf_op jit(solution)/shard_map/ppermute | solution.py:310
  18.0 0.0 collective-permute-start.2
  18.0 0.7 %collective-permute-done.3.refs_3_ = f32[256,128]{1,0:T(8,128)S(1)} collective-permute-done((f32[256,128]{1,0:T(8,128)S(1)}, f32[256,128]{1,0:T(8,128)S(1)}, u32[]{:S(2)}, u32[]{:S(2)}) %collective-permute-start.3) | collective-permute-done | bytes 131104 | tf_op jit(solution)/shard_map/ppermute | solution.py:310
  18.7 0.4 collective-permute-start.4
  19.1 1.0 %collective-permute-done.4.refs_4_ = f32[256,128]{1,0:T(8,128)S(1)} collective-permute-done((f32[256,128]{1,0:T(8,128)S(1)}, f32[256,128]{1,0:T(8,128)S(1)}, u32[]{:S(2)}, u32[]{:S(2)}) %collective-permute-start.4) | collective-permute-done | bytes 131104 | tf_op jit(solution)/shard_map/ppermute | solution.py:310
  20.1 0.0 collective-permute-done.2.refs_2_
  20.1 0.8 %quad1.1 = (f32[512,128]{1,0:T(8,128)S(1)}, f32[512,128]{1,0:T(8,128)S(1)}, f32[512,128]{1,0:T(8,128)S(1)}, f32[512,128]{1,0:T(8,128)S(1)}, f32[256,128]{1,0:T(8,128)S(1)}) custom-call(f32[512,128]{1,0:T(8,128)S(1)} %get-tuple-element.26.refs_0_.refs_3_, f32[512,128]{1,0:T(8,128)S(1)} %collective-permute-done.1.refs_1_, ...), custom_call_target="tpu_custom_call" | custom-call | tf_op jit(solution)/shard_map/quad1/pallas_call | solution.py:204
  20.9 1.0 %collective-permute-start.5 = (f32[512,128]{1,0:T(8,128)S(1)}, f32[512,128]{1,0:T(8,128)S(1)}, u32[]{:S(2)}, u32[]{:S(2)}) collective-permute-start(f32[512,128]{1,0:T(8,128)S(1)} %get-tuple-element.28.refs_0_.refs_7_), channel_id=1, source_target_pairs={{0,8},{1,17},{2,10},{3,19},{4,12},{5,21},{6,14},{7,23},{8,0},{9,25... | collective-permute-start | bytes 786440 | tf_op jit(solution)/shard_map/ppermute | solution.py:310
  21.8 0.8 %collective-permute-start.7 = (f32[256,128]{1,0:T(8,128)S(1)}, f32[256,128]{1,0:T(8,128)S(1)}, u32[]{:S(2)}, u32[]{:S(2)}) collective-permute-start(f32[256,128]{1,0:T(8,128)S(1)} %get-tuple-element.29), channel_id=1, source_target_pairs={{0,24},{1,25},{2,26},{3,27},{4,28},{5,29},{6,30},{7,31},{8,16},{9,... | collective-permute-start | bytes 393224 | tf_op jit(solution)/shard_map/ppermute | solution.py:310
  22.6 7.7 %collective-permute-done.5.refs_1_ = f32[512,128]{1,0:T(8,128)S(1)} collective-permute-done((f32[512,128]{1,0:T(8,128)S(1)}, f32[512,128]{1,0:T(8,128)S(1)}, u32[]{:S(2)}, u32[]{:S(2)}) %collective-permute-start.5) | collective-permute-done | bytes 262176 | tf_op jit(solution)/shard_map/ppermute | solution.py:310
  30.3 0.7 %collective-permute-done.7.refs_3_ = f32[256,128]{1,0:T(8,128)S(1)} collective-permute-done((f32[256,128]{1,0:T(8,128)S(1)}, f32[256,128]{1,0:T(8,128)S(1)}, u32[]{:S(2)}, u32[]{:S(2)}) %collective-permute-start.7) | collective-permute-done | bytes 131104 | tf_op jit(solution)/shard_map/ppermute | solution.py:310
  31.1 0.4 collective-permute-start.8
  31.5 1.0 %collective-permute-done.8.refs_4_ = f32[256,128]{1,0:T(8,128)S(1)} collective-permute-done((f32[256,128]{1,0:T(8,128)S(1)}, f32[256,128]{1,0:T(8,128)S(1)}, u32[]{:S(2)}, u32[]{:S(2)}) %collective-permute-start.8) | collective-permute-done | bytes 131104 | tf_op jit(solution)/shard_map/ppermute | solution.py:310
  32.5 0.0 collective-permute-done.6.refs_2_
  32.5 0.8 %quad3.1 = (f32[512,128]{1,0:T(8,128)S(1)}, f32[512,128]{1,0:T(8,128)S(1)}, f32[512,128]{1,0:T(8,128)S(1)}, f32[512,128]{1,0:T(8,128)S(1)}, f32[256,128]{1,0:T(8,128)S(1)}) custom-call(f32[512,128]{1,0:T(8,128)S(1)} %get-tuple-element.28.refs_0_.refs_7_, f32[512,128]{1,0:T(8,128)S(1)} %collective-permute-done.5.refs_1_, ...), custom_call_target="tpu_custom_call" | custom-call | tf_op jit(solution)/shard_map/quad3/pallas_call | solution.py:204
  33.2 2.0 %collective-permute-start.9 = (f32[512,128]{1,0:T(8,128)S(1)}, f32[512,128]{1,0:T(8,128)S(1)}, u32[]{:S(2)}, u32[]{:S(2)}) collective-permute-start(f32[512,128]{1,0:T(8,128)S(1)} %get-tuple-element.30.refs_0_.refs_11_), channel_id=1, source_target_pairs={{0,32},{1,97},{2,34},{3,99},{4,36},{5,101},{6,38},{7,103},{8,40},{... | collective-permute-start | bytes 786440 | tf_op jit(solution)/shard_map/ppermute | solution.py:310
  35.2 7.9 %collective-permute-done.9.refs_1_ = f32[512,128]{1,0:T(8,128)S(1)} collective-permute-done((f32[512,128]{1,0:T(8,128)S(1)}, f32[512,128]{1,0:T(8,128)S(1)}, u32[]{:S(2)}, u32[]{:S(2)}) %collective-permute-start.9) | collective-permute-done | bytes 262176 | tf_op jit(solution)/shard_map/ppermute | solution.py:310
  43.1 1.8 %collective-permute-start.10 = (f32[512,128]{1,0:T(8,128)S(1)}, f32[512,128]{1,0:T(8,128)S(1)}, u32[]{:S(2)}, u32[]{:S(2)}) collective-permute-start(f32[512,128]{1,0:T(8,128)S(1)} %collective-permute-done.9.refs_1_), channel_id=1, source_target_pairs={{0,1},{1,0},{2,3},{3,2},{4,5},{5,4},{6,7},{7,6},{8,9},{9,8},{10,11... | collective-permute-start | bytes 786440 | tf_op jit(solution)/shard_map/ppermute | solution.py:310
  44.9 1.2 %collective-permute-done.11.refs_3_ = f32[256,128]{1,0:T(8,128)S(1)} collective-permute-done((f32[256,128]{1,0:T(8,128)S(1)}, f32[256,128]{1,0:T(8,128)S(1)}, u32[]{:S(2)}, u32[]{:S(2)}) %collective-permute-start.11) | collective-permute-done | bytes 131104 | tf_op jit(solution)/shard_map/ppermute | solution.py:310
  46.0 0.3 collective-permute-start.12
  46.4 1.0 %collective-permute-done.12.refs_4_ = f32[256,128]{1,0:T(8,128)S(1)} collective-permute-done((f32[256,128]{1,0:T(8,128)S(1)}, f32[256,128]{1,0:T(8,128)S(1)}, u32[]{:S(2)}, u32[]{:S(2)}) %collective-permute-start.12) | collective-permute-done | bytes 131104 | tf_op jit(solution)/shard_map/ppermute | solution.py:310
  47.4 0.8 %quad5.1 = (f32[512,128]{1,0:T(8,128)S(1)}, f32[512,128]{1,0:T(8,128)S(1)}, f32[512,128]{1,0:T(8,128)S(1)}, f32[512,128]{1,0:T(8,128)S(1)}, f32[192,128]{1,0:T(8,128)S(1)}) custom-call(f32[512,128]{1,0:T(8,128)S(1)} %get-tuple-element.30.refs_0_.refs_11_, f32[512,128]{1,0:T(8,128)S(1)} %collective-permute-done.9.refs_1_, ...), custom_call_target="tpu_custom_call" | custom-call | tf_op jit(solution)/shard_map/quad5/pallas_call | solution.py:204
  48.2 4.8 %collective-permute-start.13 = (f32[192,128]{1,0:T(8,128)S(1)}, f32[192,128]{1,0:T(8,128)S(1)}, u32[]{:S(2)}, u32[]{:S(2)}) collective-permute-start(f32[192,128]{1,0:T(8,128)S(1)} %get-tuple-element.33), channel_id=1, source_target_pairs={{0,224},{1,225},{2,226},{3,227},{4,228},{5,229},{6,230},{7,231},{8... | collective-permute-start | bytes 294920 | tf_op jit(solution)/shard_map/ppermute | solution.py:334
  52.9 2.1 %track.1.refs_2_ = f32[2,512,128]{2,1,0:T(8,128)S(1)} custom-call(f32[2,512,128]{2,1,0:T(8,128)S(1)} %get-tuple-element.34.refs_0_, f32[512,128]{1,0:T(8,128)S(1)} %get-tuple-element.25.own.refs_1_, f32[512,128]{1,0:T(8,128)S(1)} %collective-permute-done.other.refs_2_, f32[512,128]{1,0:T(8,128)S(1)} %get-tuple-element.26.refs_0_.refs_3_, ...), custom_call_target="tpu_custom_call" | custom-call | flops 1879048192 | bytes 3670016 | tf_op jit(solution)/shard_map/track/pallas_call | solution.py:244
  55.0 2.3 %collective-permute-done.13.refs_1_ = f32[192,128]{1,0:T(8,128)S(1)} collective-permute-done((f32[192,128]{1,0:T(8,128)S(1)}, f32[192,128]{1,0:T(8,128)S(1)}, u32[]{:S(2)}, u32[]{:S(2)}) %collective-permute-start.13) | collective-permute-done | bytes 98336 | tf_op jit(solution)/shard_map/ppermute | solution.py:334
  57.3 1.8 %finish.1 = f32[12,64,128]{2,1,0:T(8,128)} custom-call(f32[512,128]{1,0:T(8,128)S(1)} %get-tuple-element.32.refs_0_, f32[192,128]{1,0:T(8,128)S(1)} %collective-permute-done.13.refs_1_, f32[2,512,128]{2,1,0:T(8,128)S(1)} %track.1.refs_2_, f32[2,6,320,128]{3,2,1,0:T(8,128)S(1)} %get-tuple-element.44.refs_3_), custom_call_target="tpu_custom_call" | custom-call | tf_op jit(solution)/shard_map/finish/pallas_call | solution.py:292
  (3 shorter events, 0.0 us)
Async XLA Ops:
  3.7 4.5 %collective-permute-start = (f32[512,128]{1,0:T(8,128)S(1)}, f32[512,128]{1,0:T(8,128)S(1)}, u32[]{:S(2)}, u32[]{:S(2)}) collective-permute-start(f32[512,128]{1,0:T(8,128)S(1)} %get-tuple-element.25.own.refs_1_), channel_id=1, source_target_pairs={{0,1},{1,0},{2,3},{3,2},{4,5},{5,4},{6,7},{7,6},{8,9},{9,8},{10,11... | collective-permute-start | bytes 786440 | tf_op jit(solution)/shard_map/ppermute | solution.py:310
  8.5 9.5 %collective-permute-start.1 = (f32[512,128]{1,0:T(8,128)S(1)}, f32[512,128]{1,0:T(8,128)S(1)}, u32[]{:S(2)}, u32[]{:S(2)}) collective-permute-start(f32[512,128]{1,0:T(8,128)S(1)} %get-tuple-element.26.refs_0_.refs_3_), channel_id=1, source_target_pairs={{0,2},{1,5},{2,0},{3,7},{4,6},{5,1},{6,4},{7,3},{8,10},{9,13},{10,... | collective-permute-start | bytes 786440 | tf_op jit(solution)/shard_map/ppermute | solution.py:310
  9.6 9.1 %collective-permute-start.3 = (f32[256,128]{1,0:T(8,128)S(1)}, f32[256,128]{1,0:T(8,128)S(1)}, u32[]{:S(2)}, u32[]{:S(2)}) collective-permute-start(f32[256,128]{1,0:T(8,128)S(1)} %get-tuple-element.27), channel_id=1, source_target_pairs={{0,6},{1,7},{2,4},{3,5},{4,2},{5,3},{6,0},{7,1},{8,14},{9,15},{10,... | collective-permute-start | bytes 393224 | tf_op jit(solution)/shard_map/ppermute | solution.py:310
  18.0 2.1 %collective-permute-start.2 = (f32[512,128]{1,0:T(8,128)S(1)}, f32[512,128]{1,0:T(8,128)S(1)}, u32[]{:S(2)}, u32[]{:S(2)}) collective-permute-start(f32[512,128]{1,0:T(8,128)S(1)} %collective-permute-done.1.refs_1_), channel_id=1, source_target_pairs={{0,1},{1,0},{2,3},{3,2},{4,5},{5,4},{6,7},{7,6},{8,9},{9,8},{10,11... | collective-permute-start | bytes 786440 | tf_op jit(solution)/shard_map/ppermute | solution.py:310
  18.7 1.4 %collective-permute-start.4 = (f32[256,128]{1,0:T(8,128)S(1)}, f32[256,128]{1,0:T(8,128)S(1)}, u32[]{:S(2)}, u32[]{:S(2)}) collective-permute-start(f32[256,128]{1,0:T(8,128)S(1)} %collective-permute-done.3.refs_3_), channel_id=1, source_target_pairs={{0,1},{1,0},{2,3},{3,2},{4,5},{5,4},{6,7},{7,6},{8,9},{9,8},{10,11... | collective-permute-start | bytes 393224 | tf_op jit(solution)/shard_map/ppermute | solution.py:310
  20.9 9.5 %collective-permute-start.5 = (f32[512,128]{1,0:T(8,128)S(1)}, f32[512,128]{1,0:T(8,128)S(1)}, u32[]{:S(2)}, u32[]{:S(2)}) collective-permute-start(f32[512,128]{1,0:T(8,128)S(1)} %get-tuple-element.28.refs_0_.refs_7_), channel_id=1, source_target_pairs={{0,8},{1,17},{2,10},{3,19},{4,12},{5,21},{6,14},{7,23},{8,0},{9,25... | collective-permute-start | bytes 786440 | tf_op jit(solution)/shard_map/ppermute | solution.py:310
  21.8 9.2 %collective-permute-start.7 = (f32[256,128]{1,0:T(8,128)S(1)}, f32[256,128]{1,0:T(8,128)S(1)}, u32[]{:S(2)}, u32[]{:S(2)}) collective-permute-start(f32[256,128]{1,0:T(8,128)S(1)} %get-tuple-element.29), channel_id=1, source_target_pairs={{0,24},{1,25},{2,26},{3,27},{4,28},{5,29},{6,30},{7,31},{8,16},{9,... | collective-permute-start | bytes 393224 | tf_op jit(solution)/shard_map/ppermute | solution.py:310
  30.3 2.1 %collective-permute-start.6 = (f32[512,128]{1,0:T(8,128)S(1)}, f32[512,128]{1,0:T(8,128)S(1)}, u32[]{:S(2)}, u32[]{:S(2)}) collective-permute-start(f32[512,128]{1,0:T(8,128)S(1)} %collective-permute-done.5.refs_1_), channel_id=1, source_target_pairs={{0,1},{1,0},{2,3},{3,2},{4,5},{5,4},{6,7},{7,6},{8,9},{9,8},{10,11... | collective-permute-start | bytes 786440 | tf_op jit(solution)/shard_map/ppermute | solution.py:310
  31.1 1.4 %collective-permute-start.8 = (f32[256,128]{1,0:T(8,128)S(1)}, f32[256,128]{1,0:T(8,128)S(1)}, u32[]{:S(2)}, u32[]{:S(2)}) collective-permute-start(f32[256,128]{1,0:T(8,128)S(1)} %collective-permute-done.7.refs_3_), channel_id=1, source_target_pairs={{0,1},{1,0},{2,3},{3,2},{4,5},{5,4},{6,7},{7,6},{8,9},{9,8},{10,11... | collective-permute-start | bytes 393224 | tf_op jit(solution)/shard_map/ppermute | solution.py:310
  33.2 9.9 %collective-permute-start.9 = (f32[512,128]{1,0:T(8,128)S(1)}, f32[512,128]{1,0:T(8,128)S(1)}, u32[]{:S(2)}, u32[]{:S(2)}) collective-permute-start(f32[512,128]{1,0:T(8,128)S(1)} %get-tuple-element.30.refs_0_.refs_11_), channel_id=1, source_target_pairs={{0,32},{1,97},{2,34},{3,99},{4,36},{5,101},{6,38},{7,103},{8,40},{... | collective-permute-start | bytes 786440 | tf_op jit(solution)/shard_map/ppermute | solution.py:310
  35.2 10.8 %collective-permute-start.11 = (f32[256,128]{1,0:T(8,128)S(1)}, f32[256,128]{1,0:T(8,128)S(1)}, u32[]{:S(2)}, u32[]{:S(2)}) collective-permute-start(f32[256,128]{1,0:T(8,128)S(1)} %get-tuple-element.31), channel_id=1, source_target_pairs={{0,64},{1,65},{2,66},{3,67},{4,68},{5,69},{6,70},{7,71},{8,72},{9,... | collective-permute-start | bytes 393224 | tf_op jit(solution)/shard_map/ppermute | solution.py:310
  43.1 4.3 %collective-permute-start.10 = (f32[512,128]{1,0:T(8,128)S(1)}, f32[512,128]{1,0:T(8,128)S(1)}, u32[]{:S(2)}, u32[]{:S(2)}) collective-permute-start(f32[512,128]{1,0:T(8,128)S(1)} %collective-permute-done.9.refs_1_), channel_id=1, source_target_pairs={{0,1},{1,0},{2,3},{3,2},{4,5},{5,4},{6,7},{7,6},{8,9},{9,8},{10,11... | collective-permute-start | bytes 786440 | tf_op jit(solution)/shard_map/ppermute | solution.py:310
  46.0 1.3 %collective-permute-start.12 = (f32[256,128]{1,0:T(8,128)S(1)}, f32[256,128]{1,0:T(8,128)S(1)}, u32[]{:S(2)}, u32[]{:S(2)}) collective-permute-start(f32[256,128]{1,0:T(8,128)S(1)} %collective-permute-done.11.refs_3_), channel_id=1, source_target_pairs={{0,1},{1,0},{2,3},{3,2},{4,5},{5,4},{6,7},{7,6},{8,9},{9,8},{10,11... | collective-permute-start | bytes 393224 | tf_op jit(solution)/shard_map/ppermute | solution.py:310
  48.2 9.1 %collective-permute-start.13 = (f32[192,128]{1,0:T(8,128)S(1)}, f32[192,128]{1,0:T(8,128)S(1)}, u32[]{:S(2)}, u32[]{:S(2)}) collective-permute-start(f32[192,128]{1,0:T(8,128)S(1)} %get-tuple-element.33), channel_id=1, source_target_pairs={{0,224},{1,225},{2,226},{3,227},{4,228},{5,229},{6,230},{7,231},{8... | collective-permute-start | bytes 294920 | tf_op jit(solution)/shard_map/ppermute | solution.py:334

commit v4 on v3

--- a/solution.py
+++ b/solution.py
@@ -11,6 +11,7 @@
 PACK = 3 * B + 2 * R
 PARTS = 2
 OUT_ROWS = 3
+FACING = (6, 7, 4, 5, 2, 3, 0, 1)
 PLANS = ((1, (1, 2)), (3, (1, 2)), (5, (1, 3)))
 LIMIT = 12 * 2**20
 
@@ -211,8 +212,24 @@
     )(own, *parts)
 
 
-def track_kernel(levels, *refs):
-    parts, track = refs[0], refs[-1]
+def advanced(level, first, second, aheads, behinds):
+    early, back = turned(first, second)
+    late = left_side(back)
+    left = is_left(level)
+    for part in range(PARTS):
+        ahead, behind = aheads[part], behinds[part]
+        through = times(late, right_side(behind[:B]))
+        through = jnp.concatenate([through[:B], through[B:] + behind[B:]], axis=0)
+        onward = times(early, right_side(ahead[:B]))
+        onward = jnp.concatenate([onward[:B], onward[B:] + ahead[B:]], axis=0)
+        cross = times(early, right_side(behind[B : 2 * B]))
+        cross = jnp.concatenate([behind[:B], cross[:B], cross[B:] + behind[2 * B :]], axis=0)
+        aheads[part] = jnp.where(left, ahead, onward)
+        behinds[part] = jnp.where(left, through, cross)
+
+
+def prepare_kernel(levels, *refs):
+    parts, rows, pairs, (track, spread) = refs[0], refs[1], refs[2:-2], refs[-2:]
     eye = (
         lax.broadcasted_iota(jnp.int32, (B, B), 0) == lax.broadcasted_iota(jnp.int32, (B, B), 1)
     ).astype(jnp.float32)
@@ -221,61 +238,75 @@
     aheads = [jnp.concatenate([eye, none[:R]], axis=0), parts[0, : B + R]]
     behinds = [back, jnp.concatenate([eye, none], axis=0)]
     for level in range(levels):
-        first, second = ordered(level, refs[1 + 2 * level][...], refs[2 + 2 * level][...])
-        early, back = turned(first, second)
-        late = left_side(back)
-        left = is_left(level)
-        for part in range(PARTS):
-            ahead, behind = aheads[part], behinds[part]
-            through = times(late, right_side(behind[:B]))
-            through = jnp.concatenate([through[:B], through[B:] + behind[B:]], axis=0)
-            onward = times(early, right_side(ahead[:B]))
-            onward = jnp.concatenate([onward[:B], onward[B:] + ahead[B:]], axis=0)
-            cross = times(early, right_side(behind[B : 2 * B]))
-            cross = jnp.concatenate([behind[:B], cross[:B], cross[B:] + behind[2 * B :]], axis=0)
-            aheads[part] = jnp.where(left, ahead, onward)
-            behinds[part] = jnp.where(left, through, cross)
+        first, second = ordered(level, pairs[2 * level][...], pairs[2 * level + 1][...])
+        advanced(level, first, second, aheads, behinds)
     for part in range(PARTS):
         track[part, : B + R] = aheads[part]
         track[part, B + R :] = behinds[part]
-
-
-def track(parts, steps):
-    return pl.pallas_call(
-        lambda *refs: track_kernel(len(steps), *refs),
-        out_shape=jax.ShapeDtypeStruct((PARTS, PACK, B), jnp.float32),
+        for i in range(rows.shape[1]):
+            spread[part, i] = left_side(rows[part, i, : 2 * B])
+
+
+def prepare(parts, rows, steps):
+    return pl.pallas_call(
+        lambda *refs: prepare_kernel(len(steps), *refs),
+        out_shape=(
+            jax.ShapeDtypeStruct((PARTS, PACK, B), jnp.float32),
+            jax.ShapeDtypeStruct(rows.shape[:2] + (2 * B, 2 * B), jnp.bfloat16),
+        ),
+        in_specs=[pl.BlockSpec(memory_space=pltpu.VMEM)] * (2 + 2 * len(steps)),
+        out_specs=[pl.BlockSpec(memory_space=pltpu.VMEM)] * 2,
+        compiler_params=pltpu.CompilerParams(vmem_limit_bytes=LIMIT),
+        cost_estimate=pl.CostEstimate(flops=2**31, bytes_accessed=2**23, transcendentals=0),
+        name="prepare",
+    )(parts, rows, *(array for step in steps for array in step))
+
+
+def refine_kernel(start, top, *refs):
+    track, pairs, (weights, offsets) = refs[0], refs[1:-2], refs[-2:]
+    aheads = [track[part, : B + R] for part in range(PARTS)]
+    behinds = [track[part, B + R :] for part in range(PARTS)]
+    for i in range(len(pairs) // 2):
+        first, second = ordered(start + i, pairs[2 * i][...], pairs[2 * i + 1][...])
+        advanced(start + i, first, second, aheads, behinds)
+    left = is_left(top)
+    for part in range(PARTS):
+        ahead, behind = aheads[part], behinds[part]
+        weights[part, 0] = right_side(jnp.where(left, behind[:B], behind[B : 2 * B]))
+        weights[part, 1] = right_side(jnp.where(left, 0.0, ahead[:B]))
+        offsets[part, 0] = behind[2 * B :]
+        offsets[part, 1] = ahead[B:]
+
+
+def refine(start, top, tracked, steps):
+    return pl.pallas_call(
+        lambda *refs: refine_kernel(start, top, *refs),
+        out_shape=(
+            jax.ShapeDtypeStruct((PARTS, 2, 2 * B, 2 * B), jnp.bfloat16),
+            jax.ShapeDtypeStruct((PARTS, 2, R, B), jnp.float32),
+        ),
         in_specs=[pl.BlockSpec(memory_space=pltpu.VMEM)] * (1 + 2 * len(steps)),
-        out_specs=pl.BlockSpec(memory_space=pltpu.VMEM),
-        compiler_params=pltpu.CompilerParams(vmem_limit_bytes=LIMIT),
-        cost_estimate=pl.CostEstimate(
-            flops=len(steps) * 2**28, bytes_accessed=len(steps) * 2**19, transcendentals=0
-        ),
-        name="track",
-    )(parts, *(array for step in steps for array in step))
-
-
-def finish_kernel(level, own, got, track, rows, out_hbm, out, sems):
-    left = is_left(level)
-    zero = jnp.zeros((R, B), jnp.float32)
-    behind = jnp.where(left, zero, got[B:])
-    ahead = jnp.where(left, mm(own[B : B + R], got[:B]) + got[B:], zero)
-    ahead, behind = left_side(ahead), left_side(behind)
+        out_specs=[pl.BlockSpec(memory_space=pltpu.VMEM)] * 2,
+        compiler_params=pltpu.CompilerParams(vmem_limit_bytes=LIMIT),
+        cost_estimate=pl.CostEstimate(flops=2**30, bytes_accessed=2**22, transcendentals=0),
+        name="refine",
+    )(tracked, *(array for step in steps for array in step))
+
+
+def finish_kernel(level, own, got, weights, offsets, spread, rows, out_hbm, out, sems):
+    carry = jnp.where(is_left(level), mm(own[B : B + R], got[:B]), 0.0) + got[B:]
+    carry = left_side(carry)
     count = rows.shape[1]
     copies = []
     for part in range(PARTS):
-        x_in = (
-            times(ahead, right_side(track[part, B + R : 2 * B + R]))
-            + times(behind, right_side(track[part, 2 * B + R : 3 * B + R]))
-            + track[part, 3 * B + R :]
+        both = jnp.concatenate(
+            [times(carry, weights[part, i]) + offsets[part, i] for i in range(2)], axis=1
         )
-        f_in = times(behind, right_side(track[part, :B])) + track[part, B : B + R]
-        x_in, f_in = left_side(x_in), left_side(f_in)
+        both = jnp.concatenate(halves(both), axis=0)
         for i in range(count):
-            out[part * count + i] = (
-                rows[part, i, 2 * B :]
-                + times(x_in, right_side(rows[part, i, :B]))
-                + times(f_in, right_side(rows[part, i, B : 2 * B]))
-            )
+            wide = jnp.dot(both, spread[part, i], preferred_element_type=jnp.float32)
+            wide = wide[:R] + wide[R:]
+            out[part * count + i] = rows[part, i, 2 * B :] + wide[:, :B] + wide[:, B:]
             done = part * count + i + 1
             if done % OUT_ROWS == 0:
                 span = pl.ds(done - OUT_ROWS, OUT_ROWS)
@@ -287,12 +318,12 @@
         copy.wait()
 
 
-def finish(level, own, got, tracked, rows):
+def finish(level, own, got, weights, offsets, spread, rows):
     shape = (rows.shape[0] * rows.shape[1], R, B)
     return pl.pallas_call(
         lambda *refs: finish_kernel(level, *refs),
         out_shape=jax.ShapeDtypeStruct(shape, jnp.float32),
-        in_specs=[pl.BlockSpec(memory_space=pltpu.VMEM)] * 4,
+        in_specs=[pl.BlockSpec(memory_space=pltpu.VMEM)] * 6,
         out_specs=pl.BlockSpec(memory_space=pltpu.HBM),
         scratch_shapes=[
             pltpu.VMEM(shape, jnp.float32),
@@ -300,7 +331,7 @@
         ],
         compiler_params=pltpu.CompilerParams(vmem_limit_bytes=LIMIT),
         name="finish",
-    )(own, got, tracked, rows)
+    )(own, got, weights, offsets, spread, rows)
 
 
 def on_device(rhs, pivot_inv, lower_gain, upper_gain):
@@ -319,6 +350,9 @@
         third = 6 - sum(plan)
         halves = swap(half, third << level, third << level)
         whole = swap(pack, plan[0] << level, plan[1] << level)
+        if last:
+            aside = prepare(parts, rows, steps)
+            whole, aside = lax.optimization_barrier((whole, aside))
         received = (whole, swap(whole, 1, 1), halves, swap(halves, 1, 1))
         own = pack
         one, near, far, pack, half = combine(
@@ -330,9 +364,11 @@
             B + R if last else PACK // 2,
         )
         steps += [(own, one), (near, far)]
-    mirror = [(i, devices - plane - i + 2 * (i % plane)) for i in range(devices)]
-    got = lax.ppermute(half, AXES, mirror)
-    return finish(top, pack, got, track(parts, steps), rows)
+    facing = [(i, FACING[i // plane] * plane + i % plane) for i in range(devices)]
+    got = lax.ppermute(half, AXES, facing)
+    tracked, spread = aside
+    weights, offsets = refine(top - 2, top, tracked, steps[top - 2 :])
+    return finish(top, pack, got, weights, offsets, spread, rows)
 
 
 def solution(mesh):

time: 59.4 us -> 58.6 us (0.987)
  the two profiles are of different devices: /device:TPU:1 before, /device:TPU:63 now
where the time goes in v4:
time: 58.6 us; the launch traced here: 58.5 us
  waiting for transfers between devices  30.8 us (53%)
  starting transfers between devices  17.2 us (29%)
  Pallas kernels  10.2 us (17%)
    ppermute x13, waiting for transfers between devices, on_device(): lax.ppermute(array, AXES, [(i, i ^ (odd if i & 1 else even)) for i in ran...  27.1 us
    ppermute x13, starting transfers between devices, on_device(): lax.ppermute(array, AXES, [(i, i ^ (odd if i & 1 else even)) for i in ran...  11.3 us
    ppermute x1, starting transfers between devices, on_device(): got = lax.ppermute(half, AXES, facing)  5.92 us
    ppermute x1, waiting for transfers between devices, on_device(): got = lax.ppermute(half, AXES, facing)  3.77 us
    pallas_call x1, Pallas kernels, local(): pl.pallas_call(local_kernel, out_shape=(jax.ShapeDtypeStruct((PACK, B), j...  3.66 us
    pallas_call x4, Pallas kernels, combine(): pl.pallas_call(kernel, out_shape=(whole,) * (1 + extra) + (jax.ShapeDtype...  2.61 us
    pallas_call x1, Pallas kernels, prepare(): pl.pallas_call(lambda *refs: prepare_kernel(len(steps), *refs), out_shape...  1.72 us
    pallas_call x1, Pallas kernels, finish(): pl.pallas_call(lambda *refs: finish_kernel(level, *refs), out_shape=jax.S...  1.47 us
  transfers between devices with their start and end apart: 14, of which 11 were waited for; matrix products, arithmetic and copies ran while one was open for 0% of the time, Pallas kernels for 4%

profile of v4, /device:TPU:63, one launch (start us, length us, event | category | flops | bytes accessed | tf_op | source)
XLA Modules:
  0.0 58.5 jit_solution(8093198931725011669)
XLA Ops:
  0.0 3.7 %local.1 = (f32[512,128]{1,0:T(8,128)S(1)}, f32[2,512,128]{2,1,0:T(8,128)S(1)}, f32[2,6,320,128]{3,2,1,0:T(8,128)S(1)}) custom-call(f32[2,6,64,128]{3,2,1,0:T(8,128)} %bitcast.7, f32[2,6,128,128]{3,2,1,0:T(8,128)} %bitcast.4, f32[2,6,128,128]{3,2,1,0:T(8,128)} %bitcast.5, f32[2,6,128,128]{3,2,1,0:T(8,128)} %bitcast.6), custom_call_target="tpu_custom_call" | custom-call | tf_op jit(solution)/shard_map/local/pallas_call | solution.py:120
  3.7 0.8 %collective-permute-start = (f32[512,128]{1,0:T(8,128)S(1)}, f32[512,128]{1,0:T(8,128)S(1)}, u32[]{:S(2)}, u32[]{:S(2)}) collective-permute-start(f32[512,128]{1,0:T(8,128)S(1)} %get-tuple-element.32.own.refs_2_), channel_id=1, source_target_pairs={{0,1},{1,0},{2,3},{3,2},{4,5},{5,4},{6,7},{7,6},{8,9},{9,8},{10,11... | collective-permute-start | bytes 786440 | tf_op jit(solution)/shard_map/ppermute | solution.py:341
  4.4 1.2 %collective-permute-done.other.refs_3_ = f32[512,128]{1,0:T(8,128)S(1)} collective-permute-done((f32[512,128]{1,0:T(8,128)S(1)}, f32[512,128]{1,0:T(8,128)S(1)}, u32[]{:S(2)}, u32[]{:S(2)}) %collective-permute-start) | collective-permute-done | bytes 262176 | tf_op jit(solution)/shard_map/ppermute | solution.py:341
  5.6 0.3 pair.1
  5.9 1.2 %collective-permute-start.1 = (f32[512,128]{1,0:T(8,128)S(1)}, f32[512,128]{1,0:T(8,128)S(1)}, u32[]{:S(2)}, u32[]{:S(2)}) collective-permute-start(f32[512,128]{1,0:T(8,128)S(1)} %get-tuple-element.33.refs_0_.refs_4_), channel_id=1, source_target_pairs={{0,2},{1,5},{2,0},{3,7},{4,6},{5,1},{6,4},{7,3},{8,10},{9,13},{10,... | collective-permute-start | bytes 786440 | tf_op jit(solution)/shard_map/ppermute | solution.py:341
  7.2 1.8 %collective-permute-start.3 = (f32[256,128]{1,0:T(8,128)S(1)}, f32[256,128]{1,0:T(8,128)S(1)}, u32[]{:S(2)}, u32[]{:S(2)}) collective-permute-start(f32[256,128]{1,0:T(8,128)S(1)} %get-tuple-element.34), channel_id=1, source_target_pairs={{0,6},{1,7},{2,4},{3,5},{4,2},{5,3},{6,0},{7,1},{8,14},{9,15},{10,... | collective-permute-start | bytes 393224 | tf_op jit(solution)/shard_map/ppermute | solution.py:341
  9.0 5.9 %collective-permute-done.1.refs_1_ = f32[512,128]{1,0:T(8,128)S(1)} collective-permute-done((f32[512,128]{1,0:T(8,128)S(1)}, f32[512,128]{1,0:T(8,128)S(1)}, u32[]{:S(2)}, u32[]{:S(2)}) %collective-permute-start.1) | collective-permute-done | bytes 262176 | tf_op jit(solution)/shard_map/ppermute | solution.py:341
  14.9 0.0 collective-permute-start.2
  14.9 1.1 %collective-permute-done.3.refs_3_ = f32[256,128]{1,0:T(8,128)S(1)} collective-permute-done((f32[256,128]{1,0:T(8,128)S(1)}, f32[256,128]{1,0:T(8,128)S(1)}, u32[]{:S(2)}, u32[]{:S(2)}) %collective-permute-start.3) | collective-permute-done | bytes 131104 | tf_op jit(solution)/shard_map/ppermute | solution.py:341
  16.0 0.7 %collective-permute-start.4 = (f32[256,128]{1,0:T(8,128)S(1)}, f32[256,128]{1,0:T(8,128)S(1)}, u32[]{:S(2)}, u32[]{:S(2)}) collective-permute-start(f32[256,128]{1,0:T(8,128)S(1)} %collective-permute-done.3.refs_3_), channel_id=1, source_target_pairs={{0,1},{1,0},{2,3},{3,2},{4,5},{5,4},{6,7},{7,6},{8,9},{9,8},{10,11... | collective-permute-start | bytes 393224 | tf_op jit(solution)/shard_map/ppermute | solution.py:341
  16.6 1.0 %collective-permute-done.4.refs_4_ = f32[256,128]{1,0:T(8,128)S(1)} collective-permute-done((f32[256,128]{1,0:T(8,128)S(1)}, f32[256,128]{1,0:T(8,128)S(1)}, u32[]{:S(2)}, u32[]{:S(2)}) %collective-permute-start.4) | collective-permute-done | bytes 131104 | tf_op jit(solution)/shard_map/ppermute | solution.py:341
  17.6 0.0 collective-permute-done.2.refs_2_
  17.6 0.8 %quad1.1 = (f32[512,128]{1,0:T(8,128)S(1)}, f32[512,128]{1,0:T(8,128)S(1)}, f32[512,128]{1,0:T(8,128)S(1)}, f32[512,128]{1,0:T(8,128)S(1)}, f32[256,128]{1,0:T(8,128)S(1)}) custom-call(f32[512,128]{1,0:T(8,128)S(1)} %get-tuple-element.33.refs_0_.refs_4_, f32[512,128]{1,0:T(8,128)S(1)} %collective-permute-done.1.refs_1_, ...), custom_call_target="tpu_custom_call" | custom-call | tf_op jit(solution)/shard_map/quad1/pallas_call | solution.py:205
  18.4 1.0 %collective-permute-start.5 = (f32[512,128]{1,0:T(8,128)S(1)}, f32[512,128]{1,0:T(8,128)S(1)}, u32[]{:S(2)}, u32[]{:S(2)}) collective-permute-start(f32[512,128]{1,0:T(8,128)S(1)} %get-tuple-element.35.refs_0_.refs_8_), channel_id=1, source_target_pairs={{0,8},{1,17},{2,10},{3,19},{4,12},{5,21},{6,14},{7,23},{8,0},{9,25... | collective-permute-start | bytes 786440 | tf_op jit(solution)/shard_map/ppermute | solution.py:341
  19.4 1.9 %collective-permute-start.7 = (f32[256,128]{1,0:T(8,128)S(1)}, f32[256,128]{1,0:T(8,128)S(1)}, u32[]{:S(2)}, u32[]{:S(2)}) collective-permute-start(f32[256,128]{1,0:T(8,128)S(1)} %get-tuple-element.36), channel_id=1, source_target_pairs={{0,24},{1,25},{2,26},{3,27},{4,28},{5,29},{6,30},{7,31},{8,16},{9,... | collective-permute-start | bytes 393224 | tf_op jit(solution)/shard_map/ppermute | solution.py:341
  21.3 5.8 %collective-permute-done.5.refs_1_ = f32[512,128]{1,0:T(8,128)S(1)} collective-permute-done((f32[512,128]{1,0:T(8,128)S(1)}, f32[512,128]{1,0:T(8,128)S(1)}, u32[]{:S(2)}, u32[]{:S(2)}) %collective-permute-start.5) | collective-permute-done | bytes 262176 | tf_op jit(solution)/shard_map/ppermute | solution.py:341
  27.1 1.2 %collective-permute-done.7.refs_3_ = f32[256,128]{1,0:T(8,128)S(1)} collective-permute-done((f32[256,128]{1,0:T(8,128)S(1)}, f32[256,128]{1,0:T(8,128)S(1)}, u32[]{:S(2)}, u32[]{:S(2)}) %collective-permute-start.7) | collective-permute-done | bytes 131104 | tf_op jit(solution)/shard_map/ppermute | solution.py:341
  28.3 0.7 %collective-permute-start.8 = (f32[256,128]{1,0:T(8,128)S(1)}, f32[256,128]{1,0:T(8,128)S(1)}, u32[]{:S(2)}, u32[]{:S(2)}) collective-permute-start(f32[256,128]{1,0:T(8,128)S(1)} %collective-permute-done.7.refs_3_), channel_id=1, source_target_pairs={{0,1},{1,0},{2,3},{3,2},{4,5},{5,4},{6,7},{7,6},{8,9},{9,8},{10,11... | collective-permute-start | bytes 393224 | tf_op jit(solution)/shard_map/ppermute | solution.py:341
  29.0 1.0 %collective-permute-done.8.refs_4_ = f32[256,128]{1,0:T(8,128)S(1)} collective-permute-done((f32[256,128]{1,0:T(8,128)S(1)}, f32[256,128]{1,0:T(8,128)S(1)}, u32[]{:S(2)}, u32[]{:S(2)}) %collective-permute-start.8) | collective-permute-done | bytes 131104 | tf_op jit(solution)/shard_map/ppermute | solution.py:341
  30.0 0.8 %quad3.1 = (f32[512,128]{1,0:T(8,128)S(1)}, f32[512,128]{1,0:T(8,128)S(1)}, f32[512,128]{1,0:T(8,128)S(1)}, f32[512,128]{1,0:T(8,128)S(1)}, f32[256,128]{1,0:T(8,128)S(1)}) custom-call(f32[512,128]{1,0:T(8,128)S(1)} %get-tuple-element.35.refs_0_.refs_8_, f32[512,128]{1,0:T(8,128)S(1)} %collective-permute-done.5.refs_1_, ...), custom_call_target="tpu_custom_call" | custom-call | tf_op jit(solution)/shard_map/quad3/pallas_call | solution.py:205
  30.8 1.7 %collective-permute-start.9 = (f32[512,128]{1,0:T(8,128)S(1)}, f32[512,128]{1,0:T(8,128)S(1)}, u32[]{:S(2)}, u32[]{:S(2)}) collective-permute-start(f32[512,128]{1,0:T(8,128)S(1)} %get-tuple-element.37.refs_0_.refs_1_), channel_id=1, source_target_pairs={{0,32},{1,97},{2,34},{3,99},{4,36},{5,101},{6,38},{7,103},{8,40},{... | collective-permute-start | bytes 786440 | tf_op jit(solution)/shard_map/ppermute | solution.py:341
  32.5 1.4 %collective-permute-start.11 = (f32[256,128]{1,0:T(8,128)S(1)}, f32[256,128]{1,0:T(8,128)S(1)}, u32[]{:S(2)}, u32[]{:S(2)}) collective-permute-start(f32[256,128]{1,0:T(8,128)S(1)} %get-tuple-element.49), channel_id=1, source_target_pairs={{0,64},{1,65},{2,66},{3,67},{4,68},{5,69},{6,70},{7,71},{8,72},{9,... | collective-permute-start | bytes 393224 | tf_op jit(solution)/shard_map/ppermute | solution.py:341
  34.0 1.7 %prepare.1 = (f32[2,512,128]{2,1,0:T(8,128)S(1)}, bf16[2,6,256,256]{3,2,1,0:T(8,128)(2,1)S(1)}) custom-call(f32[2,512,128]{2,1,0:T(8,128)S(1)} %get-tuple-element.38.refs_0_, f32[2,6,320,128]{3,2,1,0:T(8,128)S(1)} %get-tuple-element.39.refs_1_.refs_5_, f32[512,128]{1,0:T(8,128)S(1)} %get-tuple-element.32.own.refs_2_, ...), custom_call_target="tpu_custom_call" | custom-call | flops 2147483648 | bytes 8388608 | tf_op jit(solution)/shard_map/prepare/pallas_call | solution.py:251
  35.7 4.9 %collective-permute-done.9.refs_1_ = f32[512,128]{1,0:T(8,128)S(1)} collective-permute-done((f32[512,128]{1,0:T(8,128)S(1)}, f32[512,128]{1,0:T(8,128)S(1)}, u32[]{:S(2)}, u32[]{:S(2)}) %collective-permute-start.9) | collective-permute-done | bytes 262176 | tf_op jit(solution)/shard_map/ppermute | solution.py:341
  40.6 3.7 %collective-permute-done.11.refs_3_ = f32[256,128]{1,0:T(8,128)S(1)} collective-permute-done((f32[256,128]{1,0:T(8,128)S(1)}, f32[256,128]{1,0:T(8,128)S(1)}, u32[]{:S(2)}, u32[]{:S(2)}) %collective-permute-start.11) | collective-permute-done | bytes 131104 | tf_op jit(solution)/shard_map/ppermute | solution.py:341
  44.3 0.0 collective-permute-start.12
  44.3 1.3 %collective-permute-done.12.refs_4_ = f32[256,128]{1,0:T(8,128)S(1)} collective-permute-done((f32[256,128]{1,0:T(8,128)S(1)}, f32[256,128]{1,0:T(8,128)S(1)}, u32[]{:S(2)}, u32[]{:S(2)}) %collective-permute-start.12) | collective-permute-done | bytes 131104 | tf_op jit(solution)/shard_map/ppermute | solution.py:341
  45.6 0.8 %quad5.1 = (f32[512,128]{1,0:T(8,128)S(1)}, f32[512,128]{1,0:T(8,128)S(1)}, f32[512,128]{1,0:T(8,128)S(1)}, f32[512,128]{1,0:T(8,128)S(1)}, f32[192,128]{1,0:T(8,128)S(1)}) custom-call(f32[512,128]{1,0:T(8,128)S(1)} %get-tuple-element.37.refs_0_.refs_1_, f32[512,128]{1,0:T(8,128)S(1)} %collective-permute-done.9.refs_1_, ...), custom_call_target="tpu_custom_call" | custom-call | tf_op jit(solution)/shard_map/quad5/pallas_call | solution.py:205
  46.4 5.9 %collective-permute-start.13 = (f32[192,128]{1,0:T(8,128)S(1)}, f32[192,128]{1,0:T(8,128)S(1)}, u32[]{:S(2)}, u32[]{:S(2)}) collective-permute-start(f32[192,128]{1,0:T(8,128)S(1)} %get-tuple-element.51), channel_id=1, source_target_pairs={{0,192},{1,193},{2,194},{3,195},{4,196},{5,197},{6,198},{7,199},{8... | collective-permute-start | bytes 294920 | tf_op jit(solution)/shard_map/ppermute | solution.py:368
  52.3 0.7 %refine.1 = (bf16[2,2,256,256]{3,2,1,0:T(8,128)(2,1)S(1)}, f32[2,2,64,128]{3,2,1,0:T(8,128)S(1)}) custom-call(f32[2,512,128]{2,1,0:T(8,128)S(1)} %get-tuple-element.52.refs_0_, f32[512,128]{1,0:T(8,128)S(1)} %get-tuple-element.37.refs_0_.refs_1_, f32[512,128]{1,0:T(8,128)S(1)} %get-tuple-element.53.refs_2_, f32[512,128]{1,0:T(8,128)S(1)} %get-tuple-element.54.refs_3_, ...), custom_call_target="tpu_custom_call" | custom-call | flops 1073741824 | bytes 4194304 | tf_op jit(solution)/shard_map/refine/pallas_call | solution.py:282
  53.1 3.8 %collective-permute-done.13.refs_1_ = f32[192,128]{1,0:T(8,128)S(1)} collective-permute-done((f32[192,128]{1,0:T(8,128)S(1)}, f32[192,128]{1,0:T(8,128)S(1)}, u32[]{:S(2)}, u32[]{:S(2)}) %collective-permute-start.13) | collective-permute-done | bytes 98336 | tf_op jit(solution)/shard_map/ppermute | solution.py:368
  56.8 1.5 %finish.1 = f32[12,64,128]{2,1,0:T(8,128)} custom-call(f32[512,128]{1,0:T(8,128)S(1)} %get-tuple-element.50.refs_0_, f32[192,128]{1,0:T(8,128)S(1)} %collective-permute-done.13.refs_1_, bf16[2,2,256,256]{3,2,1,0:T(8,128)(2,1)S(1)} %get-tuple-element.56.refs_2_, f32[2,2,64,128]{3,2,1,0:T(8,128)S(1)} %get-tuple-element.57.refs_3_, ...), custom_call_target="tpu_custom_call" | custom-call | tf_op jit(solution)/shard_map/finish/pallas_call | solution.py:323
  (4 shorter events, 0.0 us)
Async XLA Ops:
  3.7 1.9 %collective-permute-start = (f32[512,128]{1,0:T(8,128)S(1)}, f32[512,128]{1,0:T(8,128)S(1)}, u32[]{:S(2)}, u32[]{:S(2)}) collective-permute-start(f32[512,128]{1,0:T(8,128)S(1)} %get-tuple-element.32.own.refs_2_), channel_id=1, source_target_pairs={{0,1},{1,0},{2,3},{3,2},{4,5},{5,4},{6,7},{7,6},{8,9},{9,8},{10,11... | collective-permute-start | bytes 786440 | tf_op jit(solution)/shard_map/ppermute | solution.py:341
  5.9 9.0 %collective-permute-start.1 = (f32[512,128]{1,0:T(8,128)S(1)}, f32[512,128]{1,0:T(8,128)S(1)}, u32[]{:S(2)}, u32[]{:S(2)}) collective-permute-start(f32[512,128]{1,0:T(8,128)S(1)} %get-tuple-element.33.refs_0_.refs_4_), channel_id=1, source_target_pairs={{0,2},{1,5},{2,0},{3,7},{4,6},{5,1},{6,4},{7,3},{8,10},{9,13},{10,... | collective-permute-start | bytes 786440 | tf_op jit(solution)/shard_map/ppermute | solution.py:341
  7.2 8.8 %collective-permute-start.3 = (f32[256,128]{1,0:T(8,128)S(1)}, f32[256,128]{1,0:T(8,128)S(1)}, u32[]{:S(2)}, u32[]{:S(2)}) collective-permute-start(f32[256,128]{1,0:T(8,128)S(1)} %get-tuple-element.34), channel_id=1, source_target_pairs={{0,6},{1,7},{2,4},{3,5},{4,2},{5,3},{6,0},{7,1},{8,14},{9,15},{10,... | collective-permute-start | bytes 393224 | tf_op jit(solution)/shard_map/ppermute | solution.py:341
  14.9 2.7 %collective-permute-start.2 = (f32[512,128]{1,0:T(8,128)S(1)}, f32[512,128]{1,0:T(8,128)S(1)}, u32[]{:S(2)}, u32[]{:S(2)}) collective-permute-start(f32[512,128]{1,0:T(8,128)S(1)} %collective-permute-done.1.refs_1_), channel_id=1, source_target_pairs={{0,1},{1,0},{2,3},{3,2},{4,5},{5,4},{6,7},{7,6},{8,9},{9,8},{10,11... | collective-permute-start | bytes 786440 | tf_op jit(solution)/shard_map/ppermute | solution.py:341
  16.0 1.6 %collective-permute-start.4 = (f32[256,128]{1,0:T(8,128)S(1)}, f32[256,128]{1,0:T(8,128)S(1)}, u32[]{:S(2)}, u32[]{:S(2)}) collective-permute-start(f32[256,128]{1,0:T(8,128)S(1)} %collective-permute-done.3.refs_3_), channel_id=1, source_target_pairs={{0,1},{1,0},{2,3},{3,2},{4,5},{5,4},{6,7},{7,6},{8,9},{9,8},{10,11... | collective-permute-start | bytes 393224 | tf_op jit(solution)/shard_map/ppermute | solution.py:341
  18.4 8.7 %collective-permute-start.5 = (f32[512,128]{1,0:T(8,128)S(1)}, f32[512,128]{1,0:T(8,128)S(1)}, u32[]{:S(2)}, u32[]{:S(2)}) collective-permute-start(f32[512,128]{1,0:T(8,128)S(1)} %get-tuple-element.35.refs_0_.refs_8_), channel_id=1, source_target_pairs={{0,8},{1,17},{2,10},{3,19},{4,12},{5,21},{6,14},{7,23},{8,0},{9,25... | collective-permute-start | bytes 786440 | tf_op jit(solution)/shard_map/ppermute | solution.py:341
  19.4 8.9 %collective-permute-start.7 = (f32[256,128]{1,0:T(8,128)S(1)}, f32[256,128]{1,0:T(8,128)S(1)}, u32[]{:S(2)}, u32[]{:S(2)}) collective-permute-start(f32[256,128]{1,0:T(8,128)S(1)} %get-tuple-element.36), channel_id=1, source_target_pairs={{0,24},{1,25},{2,26},{3,27},{4,28},{5,29},{6,30},{7,31},{8,16},{9,... | collective-permute-start | bytes 393224 | tf_op jit(solution)/shard_map/ppermute | solution.py:341
  27.1 2.9 %collective-permute-start.6 = (f32[512,128]{1,0:T(8,128)S(1)}, f32[512,128]{1,0:T(8,128)S(1)}, u32[]{:S(2)}, u32[]{:S(2)}) collective-permute-start(f32[512,128]{1,0:T(8,128)S(1)} %collective-permute-done.5.refs_1_), channel_id=1, source_target_pairs={{0,1},{1,0},{2,3},{3,2},{4,5},{5,4},{6,7},{7,6},{8,9},{9,8},{10,11... | collective-permute-start | bytes 786440 | tf_op jit(solution)/shard_map/ppermute | solution.py:341
  28.3 1.7 %collective-permute-start.8 = (f32[256,128]{1,0:T(8,128)S(1)}, f32[256,128]{1,0:T(8,128)S(1)}, u32[]{:S(2)}, u32[]{:S(2)}) collective-permute-start(f32[256,128]{1,0:T(8,128)S(1)} %collective-permute-done.7.refs_3_), channel_id=1, source_target_pairs={{0,1},{1,0},{2,3},{3,2},{4,5},{5,4},{6,7},{7,6},{8,9},{9,8},{10,11... | collective-permute-start | bytes 393224 | tf_op jit(solution)/shard_map/ppermute | solution.py:341
  30.8 9.8 %collective-permute-start.9 = (f32[512,128]{1,0:T(8,128)S(1)}, f32[512,128]{1,0:T(8,128)S(1)}, u32[]{:S(2)}, u32[]{:S(2)}) collective-permute-start(f32[512,128]{1,0:T(8,128)S(1)} %get-tuple-element.37.refs_0_.refs_1_), channel_id=1, source_target_pairs={{0,32},{1,97},{2,34},{3,99},{4,36},{5,101},{6,38},{7,103},{8,40},{... | collective-permute-start | bytes 786440 | tf_op jit(solution)/shard_map/ppermute | solution.py:341
  32.5 11.7 %collective-permute-start.11 = (f32[256,128]{1,0:T(8,128)S(1)}, f32[256,128]{1,0:T(8,128)S(1)}, u32[]{:S(2)}, u32[]{:S(2)}) collective-permute-start(f32[256,128]{1,0:T(8,128)S(1)} %get-tuple-element.49), channel_id=1, source_target_pairs={{0,64},{1,65},{2,66},{3,67},{4,68},{5,69},{6,70},{7,71},{8,72},{9,... | collective-permute-start | bytes 393224 | tf_op jit(solution)/shard_map/ppermute | solution.py:341
  40.6 5.0 %collective-permute-start.10 = (f32[512,128]{1,0:T(8,128)S(1)}, f32[512,128]{1,0:T(8,128)S(1)}, u32[]{:S(2)}, u32[]{:S(2)}) collective-permute-start(f32[512,128]{1,0:T(8,128)S(1)} %collective-permute-done.9.refs_1_), channel_id=1, source_target_pairs={{0,1},{1,0},{2,3},{3,2},{4,5},{5,4},{6,7},{7,6},{8,9},{9,8},{10,11... | collective-permute-start | bytes 786440 | tf_op jit(solution)/shard_map/ppermute | solution.py:341
  44.3 1.3 %collective-permute-start.12 = (f32[256,128]{1,0:T(8,128)S(1)}, f32[256,128]{1,0:T(8,128)S(1)}, u32[]{:S(2)}, u32[]{:S(2)}) collective-permute-start(f32[256,128]{1,0:T(8,128)S(1)} %collective-permute-done.11.refs_3_), channel_id=1, source_target_pairs={{0,1},{1,0},{2,3},{3,2},{4,5},{5,4},{6,7},{7,6},{8,9},{9,8},{10,11... | collective-permute-start | bytes 393224 | tf_op jit(solution)/shard_map/ppermute | solution.py:341
  46.4 10.4 %collective-permute-start.13 = (f32[192,128]{1,0:T(8,128)S(1)}, f32[192,128]{1,0:T(8,128)S(1)}, u32[]{:S(2)}, u32[]{:S(2)}) collective-permute-start(f32[192,128]{1,0:T(8,128)S(1)} %get-tuple-element.51), channel_id=1, source_target_pairs={{0,192},{1,193},{2,194},{3,195},{4,196},{5,197},{6,198},{7,199},{8... | collective-permute-start | bytes 294920 | tf_op jit(solution)/shard_map/ppermute | solution.py:368

commit v5 on v4

--- a/solution.py
+++ b/solution.py
@@ -12,7 +12,7 @@
 PARTS = 2
 OUT_ROWS = 3
 FACING = (6, 7, 4, 5, 2, 3, 0, 1)
-PLANS = ((1, (1, 2)), (3, (1, 2)), (5, (1, 3)))
+ROUNDS = (1, 3, 5)
 LIMIT = 12 * 2**20
 
 
@@ -183,13 +183,16 @@
     store_half(send, value)
 
 
-def quad_kernel(level, plan, top, *refs):
-    own, whole, whole_twin, half, half_twin, one, near, far, pack, send = refs
-    partner = dict(zip(plan, by_core(whole[...], whole_twin[...])))
-    partner[6 - sum(plan)] = jnp.concatenate(by_core(half[...], half_twin[...]), axis=0)
-    one[...] = partner[1]
-    mine = joined(*ordered(level, own[...], partner[1]))
-    theirs = joined(*ordered(level, partner[2], partner[3]))
+def quad_kernel(level, top, own, *refs):
+    gots, (twin, one, near, far, pack, send) = refs[:3], refs[3:]
+    half = PACK // 2
+    partners = [
+        jnp.concatenate(by_core(got[...], twin[i * half : (i + 1) * half]), axis=0)
+        for i, got in enumerate(gots)
+    ]
+    one[...] = partners[0]
+    mine = joined(*ordered(level, own[...], partners[0]))
+    theirs = joined(*ordered(level, partners[1], partners[2]))
     near[...] = mine
     far[...] = theirs
     value = joined(*ordered(level + 1, mine, theirs))
@@ -338,25 +341,21 @@
     devices = lax.axis_size(AXES)
     top = devices.bit_length() - 2
     plane = devices >> 3
-    swap = lambda array, even, odd: lax.ppermute(
-        array, AXES, [(i, i ^ (odd if i & 1 else even)) for i in range(devices)]
-    )
+    swap = lambda array, bits: lax.ppermute(array, AXES, [(i, i ^ bits) for i in range(devices)])
     pack, parts, rows = local(rhs, pivot_inv, lower_gain, upper_gain)
-    other = swap(pack, 1, 1)
+    other = swap(pack, 1)
     steps = [(pack, other)]
     pack, half = combine(pair_kernel, "pair", pack, (other,), 0, PACK // 2)
-    for level, plan in PLANS:
+    for level in ROUNDS:
         last = level == top - 2
-        third = 6 - sum(plan)
-        halves = swap(half, third << level, third << level)
-        whole = swap(pack, plan[0] << level, plan[1] << level)
+        gots = tuple(swap(half, bits << level) for bits in (1, 2, 3))
         if last:
             aside = prepare(parts, rows, steps)
-            whole, aside = lax.optimization_barrier((whole, aside))
-        received = (whole, swap(whole, 1, 1), halves, swap(halves, 1, 1))
+            gots, aside = lax.optimization_barrier((gots, aside))
+        received = gots + (swap(jnp.concatenate(gots, axis=0), 1),)
         own = pack
         one, near, far, pack, half = combine(
-            lambda *refs, level=level, plan=plan, last=last: quad_kernel(level, plan, last, *refs),
+            lambda *refs, level=level, last=last: quad_kernel(level, last, *refs),
             f"quad{level}",
             own,
             received,

time: 58.6 us -> 61.6 us (1.051)
  the two profiles are of different devices: /device:TPU:63 before, /device:TPU:33 now
where the time goes in v5:
time: 61.6 us; the launch traced here: 61.5 us
  waiting for transfers between devices  27.9 us (45%)
  starting transfers between devices  23 us (37%)
  Pallas kernels  10.2 us (17%)
    ppermute x13, waiting for transfers between devices, on_device(): lax.ppermute(array, AXES, [(i, i ^ bits) for i in range(devices)])  24.2 us
    ppermute x13, starting transfers between devices, on_device(): lax.ppermute(array, AXES, [(i, i ^ bits) for i in range(devices)])  17.3 us
    ppermute x1, starting transfers between devices, on_device(): got = lax.ppermute(half, AXES, facing)  5.68 us
    ppermute x1, waiting for transfers between devices, on_device(): got = lax.ppermute(half, AXES, facing)  3.74 us
    pallas_call x1, Pallas kernels, local(): pl.pallas_call(local_kernel, out_shape=(jax.ShapeDtypeStruct((PACK, B), j...  3.66 us
    pallas_call x4, Pallas kernels, combine(): pl.pallas_call(kernel, out_shape=(whole,) * (1 + extra) + (jax.ShapeDtype...  2.59 us
    pallas_call x1, Pallas kernels, prepare(): pl.pallas_call(lambda *refs: prepare_kernel(len(steps), *refs), out_shape...  1.72 us
    pallas_call x1, Pallas kernels, finish(): pl.pallas_call(lambda *refs: finish_kernel(level, *refs), out_shape=jax.S...  1.47 us
  transfers between devices with their start and end apart: 14, of which 14 were waited for; matrix products, arithmetic and copies ran while one was open for 0% of the time, Pallas kernels for 4%

profile of v5, /device:TPU:33, one launch (start us, length us, event | category | flops | bytes accessed | tf_op | source)
XLA Modules:
  0.0 61.5 jit_solution(14905655937807997721)
XLA Ops:
  0.0 3.7 %local.1 = (f32[512,128]{1,0:T(8,128)S(1)}, f32[2,512,128]{2,1,0:T(8,128)S(1)}, f32[2,6,320,128]{3,2,1,0:T(8,128)S(1)}) custom-call(f32[2,6,64,128]{3,2,1,0:T(8,128)} %bitcast.7, f32[2,6,128,128]{3,2,1,0:T(8,128)} %bitcast.4, f32[2,6,128,128]{3,2,1,0:T(8,128)} %bitcast.5, f32[2,6,128,128]{3,2,1,0:T(8,128)} %bitcast.6), custom_call_target="tpu_custom_call" | custom-call | tf_op jit(solution)/shard_map/local/pallas_call | solution.py:120
  3.7 0.8 %collective-permute-start = (f32[512,128]{1,0:T(8,128)S(1)}, f32[512,128]{1,0:T(8,128)S(1)}, u32[]{:S(2)}, u32[]{:S(2)}) collective-permute-start(f32[512,128]{1,0:T(8,128)S(1)} %get-tuple-element.34.own.refs_2_), channel_id=1, source_target_pairs={{0,1},{1,0},{2,3},{3,2},{4,5},{5,4},{6,7},{7,6},{8,9},{9,8},{10,11... | collective-permute-start | bytes 786440 | tf_op jit(solution)/shard_map/ppermute | solution.py:344
  4.4 1.2 %collective-permute-done.other.refs_3_ = f32[512,128]{1,0:T(8,128)S(1)} collective-permute-done((f32[512,128]{1,0:T(8,128)S(1)}, f32[512,128]{1,0:T(8,128)S(1)}, u32[]{:S(2)}, u32[]{:S(2)}) %collective-permute-start) | collective-permute-done | bytes 262176 | tf_op jit(solution)/shard_map/ppermute | solution.py:344
  5.9 2.6 %collective-permute-start.3 = (f32[256,128]{1,0:T(8,128)S(1)}, f32[256,128]{1,0:T(8,128)S(1)}, u32[]{:S(2)}, u32[]{:S(2)}) collective-permute-start(f32[256,128]{1,0:T(8,128)S(1)} %get-tuple-element.36), channel_id=1, source_target_pairs={{0,6},{1,7},{2,4},{3,5},{4,2},{5,3},{6,0},{7,1},{8,14},{9,15},{10,... | collective-permute-start | bytes 393224 | tf_op jit(solution)/shard_map/ppermute | solution.py:344
  8.5 0.5 collective-permute-start.2
  9.3 4.6 %collective-permute-done.3.refs_3_ = f32[256,128]{1,0:T(8,128)S(1)} collective-permute-done((f32[256,128]{1,0:T(8,128)S(1)}, f32[256,128]{1,0:T(8,128)S(1)}, u32[]{:S(2)}, u32[]{:S(2)}) %collective-permute-start.3) | collective-permute-done | bytes 131104 | tf_op jit(solution)/shard_map/ppermute | solution.py:344
  13.9 0.5 collective-permute-done.2.refs_2_
  14.4 0.7 %collective-permute-done.1.refs_1_ = f32[256,128]{1,0:T(8,128)S(1)} collective-permute-done((f32[256,128]{1,0:T(8,128)S(1)}, f32[256,128]{1,0:T(8,128)S(1)}, u32[]{:S(2)}, u32[]{:S(2)}) %collective-permute-start.1) | collective-permute-done | bytes 131104 | tf_op jit(solution)/shard_map/ppermute | solution.py:344
  15.1 2.0 %collective-permute-start.4 = (f32[768,128]{1,0:T(8,128)S(1)}, f32[768,128]{1,0:T(8,128)S(1)}, u32[]{:S(2)}, u32[]{:S(2)}) collective-permute-start(f32[768,128]{1,0:T(8,128)S(1)} %pad_maximum_fusion), channel_id=1, source_target_pairs={{0,1},{1,0},{2,3},{3,2},{4,5},{5,4},{6,7},{7,6},{8,9},{9,8},{10,11... | collective-permute-start | bytes 1179656 | tf_op jit(solution)/shard_map/ppermute | solution.py:344
  17.2 1.3 %collective-permute-done.4.refs_4_ = f32[768,128]{1,0:T(8,128)S(1)} collective-permute-done((f32[768,128]{1,0:T(8,128)S(1)}, f32[768,128]{1,0:T(8,128)S(1)}, u32[]{:S(2)}, u32[]{:S(2)}) %collective-permute-start.4) | collective-permute-done | bytes 393248 | tf_op jit(solution)/shard_map/ppermute | solution.py:344
  18.5 0.8 %quad1.1 = (f32[512,128]{1,0:T(8,128)S(1)}, f32[512,128]{1,0:T(8,128)S(1)}, f32[512,128]{1,0:T(8,128)S(1)}, f32[512,128]{1,0:T(8,128)S(1)}, f32[256,128]{1,0:T(8,128)S(1)}) custom-call(f32[512,128]{1,0:T(8,128)S(1)} %get-tuple-element.35.refs_0_.refs_4_, f32[256,128]{1,0:T(8,128)S(1)} %collective-permute-done.1.refs_1_, ...), custom_call_target="tpu_custom_call" | custom-call | tf_op jit(solution)/shard_map/quad1/pallas_call | solution.py:208
  19.3 2.8 %collective-permute-start.7 = (f32[256,128]{1,0:T(8,128)S(1)}, f32[256,128]{1,0:T(8,128)S(1)}, u32[]{:S(2)}, u32[]{:S(2)}) collective-permute-start(f32[256,128]{1,0:T(8,128)S(1)} %get-tuple-element.38), channel_id=1, source_target_pairs={{0,24},{1,25},{2,26},{3,27},{4,28},{5,29},{6,30},{7,31},{8,16},{9,... | collective-permute-start | bytes 393224 | tf_op jit(solution)/shard_map/ppermute | solution.py:344
  22.8 4.8 %collective-permute-done.7.refs_3_ = f32[256,128]{1,0:T(8,128)S(1)} collective-permute-done((f32[256,128]{1,0:T(8,128)S(1)}, f32[256,128]{1,0:T(8,128)S(1)}, u32[]{:S(2)}, u32[]{:S(2)}) %collective-permute-start.7) | collective-permute-done | bytes 131104 | tf_op jit(solution)/shard_map/ppermute | solution.py:344
  27.6 0.4 collective-permute-done.6.refs_2_
  28.0 0.8 %collective-permute-done.5.refs_1_ = f32[256,128]{1,0:T(8,128)S(1)} collective-permute-done((f32[256,128]{1,0:T(8,128)S(1)}, f32[256,128]{1,0:T(8,128)S(1)}, u32[]{:S(2)}, u32[]{:S(2)}) %collective-permute-start.5) | collective-permute-done | bytes 131104 | tf_op jit(solution)/shard_map/ppermute | solution.py:344
  28.8 2.0 %collective-permute-start.8 = (f32[768,128]{1,0:T(8,128)S(1)}, f32[768,128]{1,0:T(8,128)S(1)}, u32[]{:S(2)}, u32[]{:S(2)}) collective-permute-start(f32[768,128]{1,0:T(8,128)S(1)} %pad_maximum_fusion.1), channel_id=1, source_target_pairs={{0,1},{1,0},{2,3},{3,2},{4,5},{5,4},{6,7},{7,6},{8,9},{9,8},{10,11... | collective-permute-start | bytes 1179656 | tf_op jit(solution)/shard_map/ppermute | solution.py:344
  30.8 1.3 %collective-permute-done.8.refs_4_ = f32[768,128]{1,0:T(8,128)S(1)} collective-permute-done((f32[768,128]{1,0:T(8,128)S(1)}, f32[768,128]{1,0:T(8,128)S(1)}, u32[]{:S(2)}, u32[]{:S(2)}) %collective-permute-start.8) | collective-permute-done | bytes 393248 | tf_op jit(solution)/shard_map/ppermute | solution.py:344
  32.1 0.8 %quad3.1 = (f32[512,128]{1,0:T(8,128)S(1)}, f32[512,128]{1,0:T(8,128)S(1)}, f32[512,128]{1,0:T(8,128)S(1)}, f32[512,128]{1,0:T(8,128)S(1)}, f32[256,128]{1,0:T(8,128)S(1)}) custom-call(f32[512,128]{1,0:T(8,128)S(1)} %get-tuple-element.37.refs_0_.refs_8_, f32[256,128]{1,0:T(8,128)S(1)} %collective-permute-done.5.refs_1_, ...), custom_call_target="tpu_custom_call" | custom-call | tf_op jit(solution)/shard_map/quad3/pallas_call | solution.py:208
  32.9 1.7 %collective-permute-start.11 = (f32[256,128]{1,0:T(8,128)S(1)}, f32[256,128]{1,0:T(8,128)S(1)}, u32[]{:S(2)}, u32[]{:S(2)}) collective-permute-start(f32[256,128]{1,0:T(8,128)S(1)} %get-tuple-element.40), channel_id=1, source_target_pairs={{0,96},{1,97},{2,98},{3,99},{4,100},{5,101},{6,102},{7,103},{8,104... | collective-permute-start | bytes 393224 | tf_op jit(solution)/shard_map/ppermute | solution.py:344
  34.6 1.4 %collective-permute-start.10 = (f32[256,128]{1,0:T(8,128)S(1)}, f32[256,128]{1,0:T(8,128)S(1)}, u32[]{:S(2)}, u32[]{:S(2)}) collective-permute-start(f32[256,128]{1,0:T(8,128)S(1)} %get-tuple-element.40), channel_id=1, source_target_pairs={{0,64},{1,65},{2,66},{3,67},{4,68},{5,69},{6,70},{7,71},{8,72},{9,... | collective-permute-start | bytes 393224 | tf_op jit(solution)/shard_map/ppermute | solution.py:344
  36.0 1.1 %collective-permute-start.9 = (f32[256,128]{1,0:T(8,128)S(1)}, f32[256,128]{1,0:T(8,128)S(1)}, u32[]{:S(2)}, u32[]{:S(2)}) collective-permute-start(f32[256,128]{1,0:T(8,128)S(1)} %get-tuple-element.40), channel_id=1, source_target_pairs={{0,32},{1,33},{2,34},{3,35},{4,36},{5,37},{6,38},{7,39},{8,40},{9,... | collective-permute-start | bytes 393224 | tf_op jit(solution)/shard_map/ppermute | solution.py:344
  37.1 1.7 %prepare.1 = (f32[2,512,128]{2,1,0:T(8,128)S(1)}, bf16[2,6,256,256]{3,2,1,0:T(8,128)(2,1)S(1)}) custom-call(f32[2,512,128]{2,1,0:T(8,128)S(1)} %get-tuple-element.41.refs_0_, f32[2,6,320,128]{3,2,1,0:T(8,128)S(1)} %get-tuple-element.42.refs_1_.refs_5_, f32[512,128]{1,0:T(8,128)S(1)} %get-tuple-element.34.own.refs_2_, ...), custom_call_target="tpu_custom_call" | custom-call | flops 2147483648 | bytes 8388608 | tf_op jit(solution)/shard_map/prepare/pallas_call | solution.py:254
  38.9 4.8 %collective-permute-done.11.refs_3_ = f32[256,128]{1,0:T(8,128)S(1)} collective-permute-done((f32[256,128]{1,0:T(8,128)S(1)}, f32[256,128]{1,0:T(8,128)S(1)}, u32[]{:S(2)}, u32[]{:S(2)}) %collective-permute-start.11) | collective-permute-done | bytes 131104 | tf_op jit(solution)/shard_map/ppermute | solution.py:344
  43.6 1.9 %collective-permute-done.10.refs_2_ = f32[256,128]{1,0:T(8,128)S(1)} collective-permute-done((f32[256,128]{1,0:T(8,128)S(1)}, f32[256,128]{1,0:T(8,128)S(1)}, u32[]{:S(2)}, u32[]{:S(2)}) %collective-permute-start.10) | collective-permute-done | bytes 131104 | tf_op jit(solution)/shard_map/ppermute | solution.py:344
  45.6 0.5 collective-permute-done.9.refs_1_
  46.1 1.5 %collective-permute-start.12 = (f32[768,128]{1,0:T(8,128)S(1)}, f32[768,128]{1,0:T(8,128)S(1)}, u32[]{:S(2)}, u32[]{:S(2)}) collective-permute-start(f32[768,128]{1,0:T(8,128)S(1)} %pad_maximum_fusion.2), channel_id=1, source_target_pairs={{0,1},{1,0},{2,3},{3,2},{4,5},{5,4},{6,7},{7,6},{8,9},{9,8},{10,11... | collective-permute-start | bytes 1179656 | tf_op jit(solution)/shard_map/ppermute | solution.py:344
  47.6 1.3 %collective-permute-done.12.refs_4_ = f32[768,128]{1,0:T(8,128)S(1)} collective-permute-done((f32[768,128]{1,0:T(8,128)S(1)}, f32[768,128]{1,0:T(8,128)S(1)}, u32[]{:S(2)}, u32[]{:S(2)}) %collective-permute-start.12) | collective-permute-done | bytes 393248 | tf_op jit(solution)/shard_map/ppermute | solution.py:344
  48.9 0.8 %quad5.1 = (f32[512,128]{1,0:T(8,128)S(1)}, f32[512,128]{1,0:T(8,128)S(1)}, f32[512,128]{1,0:T(8,128)S(1)}, f32[512,128]{1,0:T(8,128)S(1)}, f32[192,128]{1,0:T(8,128)S(1)}) custom-call(f32[512,128]{1,0:T(8,128)S(1)} %get-tuple-element.39.refs_0_.refs_1_, f32[256,128]{1,0:T(8,128)S(1)} %collective-permute-done.9.refs_1_, ...), custom_call_target="tpu_custom_call" | custom-call | tf_op jit(solution)/shard_map/quad5/pallas_call | solution.py:208
  49.7 5.7 %collective-permute-start.13 = (f32[192,128]{1,0:T(8,128)S(1)}, f32[192,128]{1,0:T(8,128)S(1)}, u32[]{:S(2)}, u32[]{:S(2)}) collective-permute-start(f32[192,128]{1,0:T(8,128)S(1)} %get-tuple-element.55), channel_id=1, source_target_pairs={{0,192},{1,193},{2,194},{3,195},{4,196},{5,197},{6,198},{7,199},{8... | collective-permute-start | bytes 294920 | tf_op jit(solution)/shard_map/ppermute | solution.py:367
  55.4 0.7 %refine.1 = (bf16[2,2,256,256]{3,2,1,0:T(8,128)(2,1)S(1)}, f32[2,2,64,128]{3,2,1,0:T(8,128)S(1)}) custom-call(f32[2,512,128]{2,1,0:T(8,128)S(1)} %get-tuple-element.56.refs_0_, f32[512,128]{1,0:T(8,128)S(1)} %get-tuple-element.39.refs_0_.refs_1_, f32[512,128]{1,0:T(8,128)S(1)} %get-tuple-element.57.refs_2_, f32[512,128]{1,0:T(8,128)S(1)} %get-tuple-element.58.refs_3_, ...), custom_call_target="tpu_custom_call" | custom-call | flops 1073741824 | bytes 4194304 | tf_op jit(solution)/shard_map/refine/pallas_call | solution.py:285
  56.1 3.7 %collective-permute-done.13.refs_1_ = f32[192,128]{1,0:T(8,128)S(1)} collective-permute-done((f32[192,128]{1,0:T(8,128)S(1)}, f32[192,128]{1,0:T(8,128)S(1)}, u32[]{:S(2)}, u32[]{:S(2)}) %collective-permute-start.13) | collective-permute-done | bytes 98336 | tf_op jit(solution)/shard_map/ppermute | solution.py:367
  59.8 1.5 %finish.1 = f32[12,64,128]{2,1,0:T(8,128)} custom-call(f32[512,128]{1,0:T(8,128)S(1)} %get-tuple-element.54.refs_0_, f32[192,128]{1,0:T(8,128)S(1)} %collective-permute-done.13.refs_1_, bf16[2,2,256,256]{3,2,1,0:T(8,128)(2,1)S(1)} %get-tuple-element.60.refs_2_, f32[2,2,64,128]{3,2,1,0:T(8,128)S(1)} %get-tuple-element.61.refs_3_, ...), custom_call_target="tpu_custom_call" | custom-call | tf_op jit(solution)/shard_map/finish/pallas_call | solution.py:326
  (7 shorter events, 1.4 us)
Async XLA Ops:
  3.7 1.9 %collective-permute-start = (f32[512,128]{1,0:T(8,128)S(1)}, f32[512,128]{1,0:T(8,128)S(1)}, u32[]{:S(2)}, u32[]{:S(2)}) collective-permute-start(f32[512,128]{1,0:T(8,128)S(1)} %get-tuple-element.34.own.refs_2_), channel_id=1, source_target_pairs={{0,1},{1,0},{2,3},{3,2},{4,5},{5,4},{6,7},{7,6},{8,9},{9,8},{10,11... | collective-permute-start | bytes 786440 | tf_op jit(solution)/shard_map/ppermute | solution.py:344
  5.9 8.0 %collective-permute-start.3 = (f32[256,128]{1,0:T(8,128)S(1)}, f32[256,128]{1,0:T(8,128)S(1)}, u32[]{:S(2)}, u32[]{:S(2)}) collective-permute-start(f32[256,128]{1,0:T(8,128)S(1)} %get-tuple-element.36), channel_id=1, source_target_pairs={{0,6},{1,7},{2,4},{3,5},{4,2},{5,3},{6,0},{7,1},{8,14},{9,15},{10,... | collective-permute-start | bytes 393224 | tf_op jit(solution)/shard_map/ppermute | solution.py:344
  8.5 5.9 %collective-permute-start.2 = (f32[256,128]{1,0:T(8,128)S(1)}, f32[256,128]{1,0:T(8,128)S(1)}, u32[]{:S(2)}, u32[]{:S(2)}) collective-permute-start(f32[256,128]{1,0:T(8,128)S(1)} %get-tuple-element.36), channel_id=1, source_target_pairs={{0,4},{1,5},{2,6},{3,7},{4,0},{5,1},{6,2},{7,3},{8,12},{9,13},{10,... | collective-permute-start | bytes 393224 | tf_op jit(solution)/shard_map/ppermute | solution.py:344
  9.0 6.1 %collective-permute-start.1 = (f32[256,128]{1,0:T(8,128)S(1)}, f32[256,128]{1,0:T(8,128)S(1)}, u32[]{:S(2)}, u32[]{:S(2)}) collective-permute-start(f32[256,128]{1,0:T(8,128)S(1)} %get-tuple-element.36), channel_id=1, source_target_pairs={{0,2},{1,3},{2,0},{3,1},{4,6},{5,7},{6,4},{7,5},{8,10},{9,11},{10,... | collective-permute-start | bytes 393224 | tf_op jit(solution)/shard_map/ppermute | solution.py:344
  15.1 3.4 %collective-permute-start.4 = (f32[768,128]{1,0:T(8,128)S(1)}, f32[768,128]{1,0:T(8,128)S(1)}, u32[]{:S(2)}, u32[]{:S(2)}) collective-permute-start(f32[768,128]{1,0:T(8,128)S(1)} %pad_maximum_fusion), channel_id=1, source_target_pairs={{0,1},{1,0},{2,3},{3,2},{4,5},{5,4},{6,7},{7,6},{8,9},{9,8},{10,11... | collective-permute-start | bytes 1179656 | tf_op jit(solution)/shard_map/ppermute | solution.py:344
  19.3 8.3 %collective-permute-start.7 = (f32[256,128]{1,0:T(8,128)S(1)}, f32[256,128]{1,0:T(8,128)S(1)}, u32[]{:S(2)}, u32[]{:S(2)}) collective-permute-start(f32[256,128]{1,0:T(8,128)S(1)} %get-tuple-element.38), channel_id=1, source_target_pairs={{0,24},{1,25},{2,26},{3,27},{4,28},{5,29},{6,30},{7,31},{8,16},{9,... | collective-permute-start | bytes 393224 | tf_op jit(solution)/shard_map/ppermute | solution.py:344
  22.1 5.9 %collective-permute-start.6 = (f32[256,128]{1,0:T(8,128)S(1)}, f32[256,128]{1,0:T(8,128)S(1)}, u32[]{:S(2)}, u32[]{:S(2)}) collective-permute-start(f32[256,128]{1,0:T(8,128)S(1)} %get-tuple-element.38), channel_id=1, source_target_pairs={{0,16},{1,17},{2,18},{3,19},{4,20},{5,21},{6,22},{7,23},{8,24},{9,... | collective-permute-start | bytes 393224 | tf_op jit(solution)/shard_map/ppermute | solution.py:344
  22.4 6.3 %collective-permute-start.5 = (f32[256,128]{1,0:T(8,128)S(1)}, f32[256,128]{1,0:T(8,128)S(1)}, u32[]{:S(2)}, u32[]{:S(2)}) collective-permute-start(f32[256,128]{1,0:T(8,128)S(1)} %get-tuple-element.38), channel_id=1, source_target_pairs={{0,8},{1,9},{2,10},{3,11},{4,12},{5,13},{6,14},{7,15},{8,0},{9,1},... | collective-permute-start | bytes 393224 | tf_op jit(solution)/shard_map/ppermute | solution.py:344
  28.8 3.3 %collective-permute-start.8 = (f32[768,128]{1,0:T(8,128)S(1)}, f32[768,128]{1,0:T(8,128)S(1)}, u32[]{:S(2)}, u32[]{:S(2)}) collective-permute-start(f32[768,128]{1,0:T(8,128)S(1)} %pad_maximum_fusion.1), channel_id=1, source_target_pairs={{0,1},{1,0},{2,3},{3,2},{4,5},{5,4},{6,7},{7,6},{8,9},{9,8},{10,11... | collective-permute-start | bytes 1179656 | tf_op jit(solution)/shard_map/ppermute | solution.py:344
  32.9 10.8 %collective-permute-start.11 = (f32[256,128]{1,0:T(8,128)S(1)}, f32[256,128]{1,0:T(8,128)S(1)}, u32[]{:S(2)}, u32[]{:S(2)}) collective-permute-start(f32[256,128]{1,0:T(8,128)S(1)} %get-tuple-element.40), channel_id=1, source_target_pairs={{0,96},{1,97},{2,98},{3,99},{4,100},{5,101},{6,102},{7,103},{8,104... | collective-permute-start | bytes 393224 | tf_op jit(solution)/shard_map/ppermute | solution.py:344
  34.6 11.0 %collective-permute-start.10 = (f32[256,128]{1,0:T(8,128)S(1)}, f32[256,128]{1,0:T(8,128)S(1)}, u32[]{:S(2)}, u32[]{:S(2)}) collective-permute-start(f32[256,128]{1,0:T(8,128)S(1)} %get-tuple-element.40), channel_id=1, source_target_pairs={{0,64},{1,65},{2,66},{3,67},{4,68},{5,69},{6,70},{7,71},{8,72},{9,... | collective-permute-start | bytes 393224 | tf_op jit(solution)/shard_map/ppermute | solution.py:344
  36.0 10.0 %collective-permute-start.9 = (f32[256,128]{1,0:T(8,128)S(1)}, f32[256,128]{1,0:T(8,128)S(1)}, u32[]{:S(2)}, u32[]{:S(2)}) collective-permute-start(f32[256,128]{1,0:T(8,128)S(1)} %get-tuple-element.40), channel_id=1, source_target_pairs={{0,32},{1,33},{2,34},{3,35},{4,36},{5,37},{6,38},{7,39},{8,40},{9,... | collective-permute-start | bytes 393224 | tf_op jit(solution)/shard_map/ppermute | solution.py:344
  46.1 2.8 %collective-permute-start.12 = (f32[768,128]{1,0:T(8,128)S(1)}, f32[768,128]{1,0:T(8,128)S(1)}, u32[]{:S(2)}, u32[]{:S(2)}) collective-permute-start(f32[768,128]{1,0:T(8,128)S(1)} %pad_maximum_fusion.2), channel_id=1, source_target_pairs={{0,1},{1,0},{2,3},{3,2},{4,5},{5,4},{6,7},{7,6},{8,9},{9,8},{10,11... | collective-permute-start | bytes 1179656 | tf_op jit(solution)/shard_map/ppermute | solution.py:344
  49.7 10.2 %collective-permute-start.13 = (f32[192,128]{1,0:T(8,128)S(1)}, f32[192,128]{1,0:T(8,128)S(1)}, u32[]{:S(2)}, u32[]{:S(2)}) collective-permute-start(f32[192,128]{1,0:T(8,128)S(1)} %get-tuple-element.55), channel_id=1, source_target_pairs={{0,192},{1,193},{2,194},{3,195},{4,196},{5,197},{6,198},{7,199},{8... | collective-permute-start | bytes 294920 | tf_op jit(solution)/shard_map/ppermute | solution.py:367

commit v6 on v4

--- a/solution.py
+++ b/solution.py
@@ -11,8 +11,9 @@
 PACK = 3 * B + 2 * R
 PARTS = 2
 OUT_ROWS = 3
-FACING = (6, 7, 4, 5, 2, 3, 0, 1)
-PLANS = ((1, (1, 2)), (3, (1, 2)), (5, (1, 3)))
+PLANS = ((1, (1, 2)), (3, (1, 2)))
+TOP = {(z, c): ((6, 7, 4, 5)[z], c) for z in range(4) for c in range(2)}
+TOP |= {(4, 0): (1, 0), (4, 1): (2, 1), (5, 0): (0, 0), (5, 1): (3, 1)}
 LIMIT = 12 * 2**20
 
 
@@ -57,7 +58,7 @@
 ):
     count = rhs.shape[1]
     pairs = ((pivot_hbm, pivot_inv), (rhs_hbm, rhs), (lower_hbm, lower), (upper_hbm, upper))
-    edges = (0, 1, count // 2, count)
+    edges = (0, count // 3, count)
     spans = list(zip(edges[:-1], edges[1:]))
     waits = {}
 
@@ -71,8 +72,7 @@
     for slot, (start, stop) in enumerate(spans):
         for which in range(3):
             fetch(which, slot, start, stop, start)
-    fetch(3, 1, count // 2, count, count - 1)
-    fetch(3, 0, 0, count // 2, count // 2 - 1)
+    fetch(3, 0, 0, count, count - 1)
     states = [None] * PARTS
     scaled = {}
     for i in range(count):
@@ -129,7 +129,7 @@
         scratch_shapes=[pltpu.VMEM(x.shape, jnp.float32) for x in inputs]
         + [
             pltpu.VMEM((PARTS, count, B + R, B), jnp.float32),
-            pltpu.SemaphoreType.DMA((4, 3)),
+            pltpu.SemaphoreType.DMA((4, 2)),
         ],
         compiler_params=pltpu.CompilerParams(vmem_limit_bytes=LIMIT),
         name="local",
@@ -183,8 +183,7 @@
     store_half(send, value)
 
 
-def quad_kernel(level, plan, top, *refs):
-    own, whole, whole_twin, half, half_twin, one, near, far, pack, send = refs
+def quad_kernel(level, plan, own, whole, whole_twin, half, half_twin, one, near, far, pack, send):
     partner = dict(zip(plan, by_core(whole[...], whole_twin[...])))
     partner[6 - sum(plan)] = jnp.concatenate(by_core(half[...], half_twin[...]), axis=0)
     one[...] = partner[1]
@@ -194,19 +193,35 @@
     far[...] = theirs
     value = joined(*ordered(level + 1, mine, theirs))
     pack[...] = value
-    if top:
-        send[...] = jnp.where(is_left(level + 2), value[: B + R], value[2 * B + R :])
-    else:
-        store_half(send, value)
-
-
-def combine(kernel, name, own, parts, extra, send_rows):
-    whole = jax.ShapeDtypeStruct((PACK, B), jnp.float32)
+    store_half(send, value)
+
+
+def planes_kernel(level, own, half, half_twin, other, pack, rest, send):
+    other[...] = jnp.concatenate(by_core(half[...], half_twin[...]), axis=0)
+    value = joined(*ordered(level, own[...], other[...]))
+    pack[...] = value
+    rest[...] = value[B + R :]
+    send[...] = jnp.where(position() >> (level + 1) == 3, value[2 * B + R :], value[: B + R])
+
+
+def meet_kernel(level, own, got, send):
+    pair = position() >> level
+    gain, shift = own[:B], own[B : B + R]
+    second = pair == 1
+    moved = mm(
+        jnp.where(second, got[...], own[: B + R]), jnp.where(second, gain, got[:B])
+    )
+    moved = jnp.concatenate([moved[:B], moved[B:] + jnp.where(second, shift, got[B:])], axis=0)
+    back = mm(moved, own[B + R : 2 * B + R]) + own[2 * B + R :]
+    send[...] = jnp.where(pair < 2, moved, back)
+
+
+def combine(kernel, name, own, parts, *out_rows):
     return pl.pallas_call(
         kernel,
-        out_shape=(whole,) * (1 + extra) + (jax.ShapeDtypeStruct((send_rows, B), jnp.float32),),
+        out_shape=tuple(jax.ShapeDtypeStruct((rows, B), jnp.float32) for rows in out_rows),
         in_specs=[pl.BlockSpec(memory_space=pltpu.VMEM)] * (1 + len(parts)),
-        out_specs=[pl.BlockSpec(memory_space=pltpu.VMEM)] * (2 + extra),
+        out_specs=[pl.BlockSpec(memory_space=pltpu.VMEM)] * len(out_rows),
         compiler_params=pltpu.CompilerParams(vmem_limit_bytes=LIMIT),
         name=name,
     )(own, *parts)
@@ -262,39 +277,57 @@
     )(parts, rows, *(array for step in steps for array in step))
 
 
-def refine_kernel(start, top, *refs):
-    track, pairs, (weights, offsets) = refs[0], refs[1:-2], refs[-2:]
-    aheads = [track[part, : B + R] for part in range(PARTS)]
-    behinds = [track[part, B + R :] for part in range(PARTS)]
-    for i in range(len(pairs) // 2):
-        first, second = ordered(start + i, pairs[2 * i][...], pairs[2 * i + 1][...])
-        advanced(start + i, first, second, aheads, behinds)
-    left = is_left(top)
-    for part in range(PARTS):
-        ahead, behind = aheads[part], behinds[part]
-        weights[part, 0] = right_side(jnp.where(left, behind[:B], behind[B : 2 * B]))
-        weights[part, 1] = right_side(jnp.where(left, 0.0, ahead[:B]))
-        offsets[part, 0] = behind[2 * B :]
-        offsets[part, 1] = ahead[B:]
-
-
-def refine(start, top, tracked, steps):
+def refine_kernel(level, track, own, got, rest, weights, offsets):
+    pair = position() >> level
+    eye = (
+        lax.broadcasted_iota(jnp.int32, (B, B), 0) == lax.broadcasted_iota(jnp.int32, (B, B), 1)
+    ).astype(jnp.float32)
+    unit = jnp.concatenate([eye, jnp.zeros((R, B), jnp.float32)], axis=0)
+    first = pair == 0
+    turn = mm(own[: B + R], jnp.where(first, rest[B : 2 * B], got[:B]))
+    turn = jnp.concatenate(
+        [
+            jnp.where(first, rest[:B], turn[:B]),
+            turn[B:] + jnp.where(first, rest[2 * B :], got[B:]),
+        ],
+        axis=0,
+    )
+    x_map = jnp.where(pair == 1, unit, jnp.where(pair == 3, 0.0, turn))
+    earlier = jnp.concatenate([jnp.where(pair == 1, 0.0, got[:B]), got[B:]], axis=0)
+    f_map = jnp.where(first, 0.0, jnp.where(pair == 2, unit, earlier))
+    x_left, f_left = left_side(x_map), left_side(f_map)
+    for part in range(PARTS):
+        ahead, behind = track[part, : B + R], track[part, B + R :]
+        x_out = times(x_left, right_side(behind[:B])) + times(
+            f_left, right_side(behind[B : 2 * B])
+        )
+        f_out = times(f_left, right_side(ahead[:B]))
+        weights[part, 0] = right_side(x_out[:B])
+        weights[part, 1] = right_side(f_out[:B])
+        offsets[part, 0] = x_out[B:] + behind[2 * B :]
+        offsets[part, 1] = f_out[B:] + ahead[B:]
+
+
+def refine(level, tracked, own, got, rest):
     return pl.pallas_call(
-        lambda *refs: refine_kernel(start, top, *refs),
+        lambda *refs: refine_kernel(level, *refs),
         out_shape=(
             jax.ShapeDtypeStruct((PARTS, 2, 2 * B, 2 * B), jnp.bfloat16),
             jax.ShapeDtypeStruct((PARTS, 2, R, B), jnp.float32),
         ),
-        in_specs=[pl.BlockSpec(memory_space=pltpu.VMEM)] * (1 + 2 * len(steps)),
+        in_specs=[pl.BlockSpec(memory_space=pltpu.VMEM)] * 4,
         out_specs=[pl.BlockSpec(memory_space=pltpu.VMEM)] * 2,
         compiler_params=pltpu.CompilerParams(vmem_limit_bytes=LIMIT),
         cost_estimate=pl.CostEstimate(flops=2**30, bytes_accessed=2**22, transcendentals=0),
         name="refine",
-    )(tracked, *(array for step in steps for array in step))
-
-
-def finish_kernel(level, own, got, weights, offsets, spread, rows, out_hbm, out, sems):
-    carry = jnp.where(is_left(level), mm(own[B : B + R], got[:B]), 0.0) + got[B:]
+    )(tracked, own, got, rest)
+
+
+def finish_kernel(level, own, here, twin, weights, offsets, spread, rows, out_hbm, out, sems):
+    left = is_left(level)
+    other_core = (position() & 1) != ((position() >> (level - 1)) & 1)
+    got = jnp.where(jnp.logical_and(left, other_core), twin[...], here[...])
+    carry = jnp.where(left, mm(own[B:], got[:B]), 0.0) + got[B:]
     carry = left_side(carry)
     count = rows.shape[1]
     copies = []
@@ -318,12 +351,12 @@
         copy.wait()
 
 
-def finish(level, own, got, weights, offsets, spread, rows):
+def finish(level, own, here, twin, weights, offsets, spread, rows):
     shape = (rows.shape[0] * rows.shape[1], R, B)
     return pl.pallas_call(
         lambda *refs: finish_kernel(level, *refs),
         out_shape=jax.ShapeDtypeStruct(shape, jnp.float32),
-        in_specs=[pl.BlockSpec(memory_space=pltpu.VMEM)] * 6,
+        in_specs=[pl.BlockSpec(memory_space=pltpu.VMEM)] * 7,
         out_specs=pl.BlockSpec(memory_space=pltpu.HBM),
         scratch_shapes=[
             pltpu.VMEM(shape, jnp.float32),
@@ -331,44 +364,71 @@
         ],
         compiler_params=pltpu.CompilerParams(vmem_limit_bytes=LIMIT),
         name="finish",
-    )(own, got, weights, offsets, spread, rows)
+    )(own, here, twin, weights, offsets, spread, rows)
 
 
 def on_device(rhs, pivot_inv, lower_gain, upper_gain):
     devices = lax.axis_size(AXES)
-    top = devices.bit_length() - 2
-    plane = devices >> 3
-    swap = lambda array, even, odd: lax.ppermute(
-        array, AXES, [(i, i ^ (odd if i & 1 else even)) for i in range(devices)]
-    )
+    plane = devices // 8
+
+    def send(array, pairs):
+        return lax.ppermute(array, AXES, pairs)
+
+    def swap(array, even, odd):
+        return send(array, [(i, i ^ (odd if i & 1 else even)) for i in range(devices)])
+
+    def at(i, z, core):
+        return z * plane + i % plane // 2 * 2 + core
+
     pack, parts, rows = local(rhs, pivot_inv, lower_gain, upper_gain)
     other = swap(pack, 1, 1)
     steps = [(pack, other)]
-    pack, half = combine(pair_kernel, "pair", pack, (other,), 0, PACK // 2)
+    pack, half = combine(pair_kernel, "pair", pack, (other,), PACK, PACK // 2)
     for level, plan in PLANS:
-        last = level == top - 2
         third = 6 - sum(plan)
-        halves = swap(half, third << level, third << level)
         whole = swap(pack, plan[0] << level, plan[1] << level)
-        if last:
-            aside = prepare(parts, rows, steps)
-            whole, aside = lax.optimization_barrier((whole, aside))
-        received = (whole, swap(whole, 1, 1), halves, swap(halves, 1, 1))
+        halves_got = swap(half, third << level, third << level)
+        received = (whole, swap(whole, 1, 1), halves_got, swap(halves_got, 1, 1))
         own = pack
         one, near, far, pack, half = combine(
-            lambda *refs, level=level, plan=plan, last=last: quad_kernel(level, plan, last, *refs),
+            lambda *refs, level=level, plan=plan: quad_kernel(level, plan, *refs),
             f"quad{level}",
             own,
             received,
-            3,
-            B + R if last else PACK // 2,
+            *(PACK,) * 4,
+            PACK // 2,
         )
         steps += [(own, one), (near, far)]
-    facing = [(i, FACING[i // plane] * plane + i % plane) for i in range(devices)]
-    got = lax.ppermute(half, AXES, facing)
+    level = 5
+    half = swap(half, 1 << level, 1 << level)
+    own = pack
+    other, pack, rest, edge = combine(
+        lambda *refs: planes_kernel(level, *refs),
+        "planes",
+        own,
+        (half, swap(half, 1, 1)),
+        PACK,
+        PACK,
+        PACK - B - R,
+        B + R,
+    )
+    steps.append((own, other))
+    bit = 2 * plane
+    got = swap(edge, bit, bit)
+    rest = send(rest, [(i, i ^ bit) for i in range(devices) if i // bit == 1])
+    aside = prepare(parts, rows, steps)
+    got, aside = lax.optimization_barrier((got, aside))
+    (edge,) = combine(
+        lambda *refs: meet_kernel(level + 1, *refs), "meet", pack, (got,), B + R
+    )
+    target = {i: TOP.get((i // plane, i & 1)) for i in range(devices)}
+    here = send(edge, [(i, at(i, *goal)) for i, goal in target.items() if goal])
     tracked, spread = aside
-    weights, offsets = refine(top - 2, top, tracked, steps[top - 2 :])
-    return finish(top, pack, got, weights, offsets, spread, rows)
+    maps = refine(level + 1, tracked, pack, got, rest)
+    here, maps = lax.optimization_barrier((here, maps))
+    chips = range(0, plane, 2)
+    twin = send(here, [(at(i, z, z // 2), at(i, z, 1 - z // 2)) for z in range(4) for i in chips])
+    return finish(level + 2, edge, here, twin, *maps, spread, rows)
 
 
 def solution(mesh):

time: 58.6 us -> 65.7 us (1.12)
  the two profiles are of different devices: /device:TPU:63 before, /device:TPU:1 now
where the time goes in v6:
time: 65.7 us; the launch traced here: 65.5 us
  waiting for transfers between devices  39.2 us (60%)
  starting transfers between devices  16.1 us (25%)
  Pallas kernels  9.94 us (15%)
    ppermute x15, waiting for transfers between devices, send(): return lax.ppermute(array, AXES, pairs)  39.2 us
    ppermute x15, starting transfers between devices, send(): return lax.ppermute(array, AXES, pairs)  16.1 us
    pallas_call x1, Pallas kernels, local(): pl.pallas_call(local_kernel, out_shape=(jax.ShapeDtypeStruct((PACK, B), j...  3.47 us
    pallas_call x5, Pallas kernels, combine(): pl.pallas_call(kernel, out_shape=tuple((jax.ShapeDtypeStruct((rows, B), j...  2.52 us
    pallas_call x1, Pallas kernels, prepare(): pl.pallas_call(lambda *refs: prepare_kernel(len(steps), *refs), out_shape...  1.99 us
    pallas_call x1, Pallas kernels, finish(): pl.pallas_call(lambda *refs: finish_kernel(level, *refs), out_shape=jax.S...  1.49 us
  transfers between devices with their start and end apart: 15, of which 12 were waited for; matrix products, arithmetic and copies ran while one was open for 0% of the time, Pallas kernels for 4%

profile of v6, /device:TPU:1, one launch (start us, length us, event | category | flops | bytes accessed | tf_op | source)
XLA Modules:
  0.0 65.5 jit_solution(15576027403075795321)
XLA Ops:
  0.0 3.5 %local.1 = (f32[512,128]{1,0:T(8,128)S(1)}, f32[2,512,128]{2,1,0:T(8,128)S(1)}, f32[2,6,320,128]{3,2,1,0:T(8,128)S(1)}) custom-call(f32[2,6,64,128]{3,2,1,0:T(8,128)} %bitcast.7, f32[2,6,128,128]{3,2,1,0:T(8,128)} %bitcast.4, f32[2,6,128,128]{3,2,1,0:T(8,128)} %bitcast.5, f32[2,6,128,128]{3,2,1,0:T(8,128)} %bitcast.6), custom_call_target="tpu_custom_call" | custom-call | tf_op jit(solution)/shard_map/local/pallas_call | solution.py:120
  3.5 3.3 %collective-permute-start = (f32[512,128]{1,0:T(8,128)S(1)}, f32[512,128]{1,0:T(8,128)S(1)}, u32[]{:S(2)}, u32[]{:S(2)}) collective-permute-start(f32[512,128]{1,0:T(8,128)S(1)} %get-tuple-element.34.own.refs_2_), channel_id=1, source_target_pairs={{0,1},{1,0},{2,3},{3,2},{4,5},{5,4},{6,7},{7,6},{8,9},{9,8},{10,11... | collective-permute-start | bytes 786440 | tf_op jit(solution)/shard_map/ppermute | solution.py:375
  6.8 1.2 %collective-permute-done.other.refs_3_ = f32[512,128]{1,0:T(8,128)S(1)} collective-permute-done((f32[512,128]{1,0:T(8,128)S(1)}, f32[512,128]{1,0:T(8,128)S(1)}, u32[]{:S(2)}, u32[]{:S(2)}) %collective-permute-start) | collective-permute-done | bytes 262176 | tf_op jit(solution)/shard_map/ppermute | solution.py:375
  8.0 0.3 pair.1
  8.3 1.1 %collective-permute-start.1 = (f32[512,128]{1,0:T(8,128)S(1)}, f32[512,128]{1,0:T(8,128)S(1)}, u32[]{:S(2)}, u32[]{:S(2)}) collective-permute-start(f32[512,128]{1,0:T(8,128)S(1)} %get-tuple-element.35.refs_0_.refs_4_), channel_id=1, source_target_pairs={{0,2},{1,5},{2,0},{3,7},{4,6},{5,1},{6,4},{7,3},{8,10},{9,13},{10,... | collective-permute-start | bytes 786440 | tf_op jit(solution)/shard_map/ppermute | solution.py:375
  9.4 0.9 %collective-permute-start.3 = (f32[256,128]{1,0:T(8,128)S(1)}, f32[256,128]{1,0:T(8,128)S(1)}, u32[]{:S(2)}, u32[]{:S(2)}) collective-permute-start(f32[256,128]{1,0:T(8,128)S(1)} %get-tuple-element.36), channel_id=1, source_target_pairs={{0,6},{1,7},{2,4},{3,5},{4,2},{5,3},{6,0},{7,1},{8,14},{9,15},{10,... | collective-permute-start | bytes 393224 | tf_op jit(solution)/shard_map/ppermute | solution.py:375
  10.3 7.6 %collective-permute-done.1.refs_1_ = f32[512,128]{1,0:T(8,128)S(1)} collective-permute-done((f32[512,128]{1,0:T(8,128)S(1)}, f32[512,128]{1,0:T(8,128)S(1)}, u32[]{:S(2)}, u32[]{:S(2)}) %collective-permute-start.1) | collective-permute-done | bytes 262176 | tf_op jit(solution)/shard_map/ppermute | solution.py:375
  17.8 0.7 %collective-permute-done.3.refs_3_ = f32[256,128]{1,0:T(8,128)S(1)} collective-permute-done((f32[256,128]{1,0:T(8,128)S(1)}, f32[256,128]{1,0:T(8,128)S(1)}, u32[]{:S(2)}, u32[]{:S(2)}) %collective-permute-start.3) | collective-permute-done | bytes 131104 | tf_op jit(solution)/shard_map/ppermute | solution.py:375
  18.5 0.4 collective-permute-start.4
  18.9 1.0 %collective-permute-done.4.refs_4_ = f32[256,128]{1,0:T(8,128)S(1)} collective-permute-done((f32[256,128]{1,0:T(8,128)S(1)}, f32[256,128]{1,0:T(8,128)S(1)}, u32[]{:S(2)}, u32[]{:S(2)}) %collective-permute-start.4) | collective-permute-done | bytes 131104 | tf_op jit(solution)/shard_map/ppermute | solution.py:375
  19.9 0.8 %quad1.1 = (f32[512,128]{1,0:T(8,128)S(1)}, f32[512,128]{1,0:T(8,128)S(1)}, f32[512,128]{1,0:T(8,128)S(1)}, f32[512,128]{1,0:T(8,128)S(1)}, f32[256,128]{1,0:T(8,128)S(1)}) custom-call(f32[512,128]{1,0:T(8,128)S(1)} %get-tuple-element.35.refs_0_.refs_4_, f32[512,128]{1,0:T(8,128)S(1)} %collective-permute-done.1.refs_1_, ...), custom_call_target="tpu_custom_call" | custom-call | tf_op jit(solution)/shard_map/quad1/pallas_call | solution.py:220
  20.7 1.0 %collective-permute-start.5 = (f32[512,128]{1,0:T(8,128)S(1)}, f32[512,128]{1,0:T(8,128)S(1)}, u32[]{:S(2)}, u32[]{:S(2)}) collective-permute-start(f32[512,128]{1,0:T(8,128)S(1)} %get-tuple-element.37.refs_0_.refs_8_), channel_id=1, source_target_pairs={{0,8},{1,17},{2,10},{3,19},{4,12},{5,21},{6,14},{7,23},{8,0},{9,25... | collective-permute-start | bytes 786440 | tf_op jit(solution)/shard_map/ppermute | solution.py:375
  21.6 0.8 %collective-permute-start.7 = (f32[256,128]{1,0:T(8,128)S(1)}, f32[256,128]{1,0:T(8,128)S(1)}, u32[]{:S(2)}, u32[]{:S(2)}) collective-permute-start(f32[256,128]{1,0:T(8,128)S(1)} %get-tuple-element.38), channel_id=1, source_target_pairs={{0,24},{1,25},{2,26},{3,27},{4,28},{5,29},{6,30},{7,31},{8,16},{9,... | collective-permute-start | bytes 393224 | tf_op jit(solution)/shard_map/ppermute | solution.py:375
  22.4 7.7 %collective-permute-done.5.refs_1_ = f32[512,128]{1,0:T(8,128)S(1)} collective-permute-done((f32[512,128]{1,0:T(8,128)S(1)}, f32[512,128]{1,0:T(8,128)S(1)}, u32[]{:S(2)}, u32[]{:S(2)}) %collective-permute-start.5) | collective-permute-done | bytes 262176 | tf_op jit(solution)/shard_map/ppermute | solution.py:375
  30.1 0.7 %collective-permute-done.7.refs_3_ = f32[256,128]{1,0:T(8,128)S(1)} collective-permute-done((f32[256,128]{1,0:T(8,128)S(1)}, f32[256,128]{1,0:T(8,128)S(1)}, u32[]{:S(2)}, u32[]{:S(2)}) %collective-permute-start.7) | collective-permute-done | bytes 131104 | tf_op jit(solution)/shard_map/ppermute | solution.py:375
  30.9 0.4 collective-permute-start.8
  31.3 1.0 %collective-permute-done.8.refs_4_ = f32[256,128]{1,0:T(8,128)S(1)} collective-permute-done((f32[256,128]{1,0:T(8,128)S(1)}, f32[256,128]{1,0:T(8,128)S(1)}, u32[]{:S(2)}, u32[]{:S(2)}) %collective-permute-start.8) | collective-permute-done | bytes 131104 | tf_op jit(solution)/shard_map/ppermute | solution.py:375
  32.3 0.8 %quad3.1 = (f32[512,128]{1,0:T(8,128)S(1)}, f32[512,128]{1,0:T(8,128)S(1)}, f32[512,128]{1,0:T(8,128)S(1)}, f32[512,128]{1,0:T(8,128)S(1)}, f32[256,128]{1,0:T(8,128)S(1)}) custom-call(f32[512,128]{1,0:T(8,128)S(1)} %get-tuple-element.37.refs_0_.refs_8_, f32[512,128]{1,0:T(8,128)S(1)} %collective-permute-done.5.refs_1_, ...), custom_call_target="tpu_custom_call" | custom-call | tf_op jit(solution)/shard_map/quad3/pallas_call | solution.py:220
  33.1 4.7 %collective-permute-done.9.refs_1_ = f32[256,128]{1,0:T(8,128)S(1)} collective-permute-done((f32[256,128]{1,0:T(8,128)S(1)}, f32[256,128]{1,0:T(8,128)S(1)}, u32[]{:S(2)}, u32[]{:S(2)}) %collective-permute-start.9) | collective-permute-done | bytes 131104 | tf_op jit(solution)/shard_map/ppermute | solution.py:375
  37.8 1.2 %collective-permute-start.10 = (f32[256,128]{1,0:T(8,128)S(1)}, f32[256,128]{1,0:T(8,128)S(1)}, u32[]{:S(2)}, u32[]{:S(2)}) collective-permute-start(f32[256,128]{1,0:T(8,128)S(1)} %collective-permute-done.9.refs_1_), channel_id=1, source_target_pairs={{0,1},{1,0},{2,3},{3,2},{4,5},{5,4},{6,7},{7,6},{8,9},{9,8},{10,11... | collective-permute-start | bytes 393224 | tf_op jit(solution)/shard_map/ppermute | solution.py:375
  39.0 1.0 %collective-permute-done.10.refs_2_ = f32[256,128]{1,0:T(8,128)S(1)} collective-permute-done((f32[256,128]{1,0:T(8,128)S(1)}, f32[256,128]{1,0:T(8,128)S(1)}, u32[]{:S(2)}, u32[]{:S(2)}) %collective-permute-start.10) | collective-permute-done | bytes 131104 | tf_op jit(solution)/shard_map/ppermute | solution.py:375
  40.0 0.3 planes.1
  40.4 0.8 %collective-permute-start.11 = (f32[192,128]{1,0:T(8,128)S(1)}, f32[192,128]{1,0:T(8,128)S(1)}, u32[]{:S(2)}, u32[]{:S(2)}) collective-permute-start(f32[192,128]{1,0:T(8,128)S(1)} %get-tuple-element.42), channel_id=1, source_target_pairs={{0,64},{1,65},{2,66},{3,67},{4,68},{5,69},{6,70},{7,71},{8,72},{9,... | collective-permute-start | bytes 294920 | tf_op jit(solution)/shard_map/ppermute | solution.py:375
  41.2 1.5 %collective-permute-start.13 = (f32[320,128]{1,0:T(8,128)S(1)}, f32[320,128]{1,0:T(8,128)S(1)}, u32[]{:S(2)}, u32[]{:S(2)}) collective-permute-start(f32[320,128]{1,0:T(8,128)S(1)} %get-tuple-element.56), channel_id=1, source_target_pairs={{64,0},{65,1},{66,2},{67,3},{68,4},{69,5},{70,6},{71,7},{72,8},{73... | collective-permute-start | bytes 491528 | tf_op jit(solution)/shard_map/ppermute | solution.py:375
  42.6 2.0 %prepare.1 = (f32[2,512,128]{2,1,0:T(8,128)S(1)}, bf16[2,6,256,256]{3,2,1,0:T(8,128)(2,1)S(1)}) custom-call(f32[2,512,128]{2,1,0:T(8,128)S(1)} %get-tuple-element.43.refs_0_, f32[2,6,320,128]{3,2,1,0:T(8,128)S(1)} %get-tuple-element.44.refs_1_.refs_6_, f32[512,128]{1,0:T(8,128)S(1)} %get-tuple-element.34.own.refs_2_, ...), custom_call_target="tpu_custom_call" | custom-call | flops 2147483648 | bytes 8388608 | tf_op jit(solution)/shard_map/prepare/pallas_call | solution.py:266
  44.6 3.3 %collective-permute-done.11.refs_1_.refs_2_ = f32[192,128]{1,0:T(8,128)S(1)} collective-permute-done((f32[192,128]{1,0:T(8,128)S(1)}, f32[192,128]{1,0:T(8,128)S(1)}, u32[]{:S(2)}, u32[]{:S(2)}) %collective-permute-start.11) | collective-permute-done | bytes 98336 | tf_op jit(solution)/shard_map/ppermute | solution.py:375
  48.3 3.4 %collective-permute-start.12 = (f32[192,128]{1,0:T(8,128)S(1)}, f32[192,128]{1,0:T(8,128)S(1)}, u32[]{:S(2)}, u32[]{:S(2)}) collective-permute-start(f32[192,128]{1,0:T(8,128)S(1)} %meet.1.refs_0_), channel_id=1, source_target_pairs={{0,192},{1,193},{2,194},{3,195},{4,196},{5,197},{6,198},{7,199},{8... | collective-permute-start | bytes 294920 | tf_op jit(solution)/shard_map/ppermute | solution.py:375
  51.7 3.3 %collective-permute-done.13.refs_3_ = f32[320,128]{1,0:T(8,128)S(1)} collective-permute-done((f32[320,128]{1,0:T(8,128)S(1)}, f32[320,128]{1,0:T(8,128)S(1)}, u32[]{:S(2)}, u32[]{:S(2)}) %collective-permute-start.13) | collective-permute-done | bytes 163872 | tf_op jit(solution)/shard_map/ppermute | solution.py:375
  54.9 0.5 refine.1
  55.4 1.3 %collective-permute-start.14 = (f32[192,128]{1,0:T(8,128)S(1)}, f32[192,128]{1,0:T(8,128)S(1)}, u32[]{:S(2)}, u32[]{:S(2)}) collective-permute-start(f32[192,128]{1,0:T(8,128)S(1)} %collective-permute-done.12.refs_1_), channel_id=1, source_target_pairs={{0,1},{2,3},{4,5},{6,7},{8,9},{10,11},{12,13},{14,15},{16,17},{18,... | collective-permute-start | bytes 294920 | tf_op jit(solution)/shard_map/ppermute | solution.py:375
  56.7 7.2 %collective-permute-done.14.refs_2_ = f32[192,128]{1,0:T(8,128)S(1)} collective-permute-done((f32[192,128]{1,0:T(8,128)S(1)}, f32[192,128]{1,0:T(8,128)S(1)}, u32[]{:S(2)}, u32[]{:S(2)}) %collective-permute-start.14) | collective-permute-done | bytes 98336 | tf_op jit(solution)/shard_map/ppermute | solution.py:375
  63.9 1.5 %finish.1 = f32[12,64,128]{2,1,0:T(8,128)} custom-call(f32[192,128]{1,0:T(8,128)S(1)} %meet.1.refs_0_, f32[192,128]{1,0:T(8,128)S(1)} %collective-permute-done.12.refs_1_, f32[192,128]{1,0:T(8,128)S(1)} %collective-permute-done.14.refs_2_, bf16[2,2,256,256]{3,2,1,0:T(8,128)(2,1)S(1)} %get-tuple-element.60.refs_3_, ...), custom_call_target="tpu_custom_call" | custom-call | tf_op jit(solution)/shard_map/finish/pallas_call | solution.py:356
  (7 shorter events, 0.4 us)
Async XLA Ops:
  3.5 4.5 %collective-permute-start = (f32[512,128]{1,0:T(8,128)S(1)}, f32[512,128]{1,0:T(8,128)S(1)}, u32[]{:S(2)}, u32[]{:S(2)}) collective-permute-start(f32[512,128]{1,0:T(8,128)S(1)} %get-tuple-element.34.own.refs_2_), channel_id=1, source_target_pairs={{0,1},{1,0},{2,3},{3,2},{4,5},{5,4},{6,7},{7,6},{8,9},{9,8},{10,11... | collective-permute-start | bytes 786440 | tf_op jit(solution)/shard_map/ppermute | solution.py:375
  8.3 9.5 %collective-permute-start.1 = (f32[512,128]{1,0:T(8,128)S(1)}, f32[512,128]{1,0:T(8,128)S(1)}, u32[]{:S(2)}, u32[]{:S(2)}) collective-permute-start(f32[512,128]{1,0:T(8,128)S(1)} %get-tuple-element.35.refs_0_.refs_4_), channel_id=1, source_target_pairs={{0,2},{1,5},{2,0},{3,7},{4,6},{5,1},{6,4},{7,3},{8,10},{9,13},{10,... | collective-permute-start | bytes 786440 | tf_op jit(solution)/shard_map/ppermute | solution.py:375
  9.4 9.1 %collective-permute-start.3 = (f32[256,128]{1,0:T(8,128)S(1)}, f32[256,128]{1,0:T(8,128)S(1)}, u32[]{:S(2)}, u32[]{:S(2)}) collective-permute-start(f32[256,128]{1,0:T(8,128)S(1)} %get-tuple-element.36), channel_id=1, source_target_pairs={{0,6},{1,7},{2,4},{3,5},{4,2},{5,3},{6,0},{7,1},{8,14},{9,15},{10,... | collective-permute-start | bytes 393224 | tf_op jit(solution)/shard_map/ppermute | solution.py:375
  17.8 2.1 %collective-permute-start.2 = (f32[512,128]{1,0:T(8,128)S(1)}, f32[512,128]{1,0:T(8,128)S(1)}, u32[]{:S(2)}, u32[]{:S(2)}) collective-permute-start(f32[512,128]{1,0:T(8,128)S(1)} %collective-permute-done.1.refs_1_), channel_id=1, source_target_pairs={{0,1},{1,0},{2,3},{3,2},{4,5},{5,4},{6,7},{7,6},{8,9},{9,8},{10,11... | collective-permute-start | bytes 786440 | tf_op jit(solution)/shard_map/ppermute | solution.py:375
  18.5 1.4 %collective-permute-start.4 = (f32[256,128]{1,0:T(8,128)S(1)}, f32[256,128]{1,0:T(8,128)S(1)}, u32[]{:S(2)}, u32[]{:S(2)}) collective-permute-start(f32[256,128]{1,0:T(8,128)S(1)} %collective-permute-done.3.refs_3_), channel_id=1, source_target_pairs={{0,1},{1,0},{2,3},{3,2},{4,5},{5,4},{6,7},{7,6},{8,9},{9,8},{10,11... | collective-permute-start | bytes 393224 | tf_op jit(solution)/shard_map/ppermute | solution.py:375
  20.7 9.5 %collective-permute-start.5 = (f32[512,128]{1,0:T(8,128)S(1)}, f32[512,128]{1,0:T(8,128)S(1)}, u32[]{:S(2)}, u32[]{:S(2)}) collective-permute-start(f32[512,128]{1,0:T(8,128)S(1)} %get-tuple-element.37.refs_0_.refs_8_), channel_id=1, source_target_pairs={{0,8},{1,17},{2,10},{3,19},{4,12},{5,21},{6,14},{7,23},{8,0},{9,25... | collective-permute-start | bytes 786440 | tf_op jit(solution)/shard_map/ppermute | solution.py:375
  21.6 9.2 %collective-permute-start.7 = (f32[256,128]{1,0:T(8,128)S(1)}, f32[256,128]{1,0:T(8,128)S(1)}, u32[]{:S(2)}, u32[]{:S(2)}) collective-permute-start(f32[256,128]{1,0:T(8,128)S(1)} %get-tuple-element.38), channel_id=1, source_target_pairs={{0,24},{1,25},{2,26},{3,27},{4,28},{5,29},{6,30},{7,31},{8,16},{9,... | collective-permute-start | bytes 393224 | tf_op jit(solution)/shard_map/ppermute | solution.py:375
  30.1 2.1 %collective-permute-start.6 = (f32[512,128]{1,0:T(8,128)S(1)}, f32[512,128]{1,0:T(8,128)S(1)}, u32[]{:S(2)}, u32[]{:S(2)}) collective-permute-start(f32[512,128]{1,0:T(8,128)S(1)} %collective-permute-done.5.refs_1_), channel_id=1, source_target_pairs={{0,1},{1,0},{2,3},{3,2},{4,5},{5,4},{6,7},{7,6},{8,9},{9,8},{10,11... | collective-permute-start | bytes 786440 | tf_op jit(solution)/shard_map/ppermute | solution.py:375
  30.9 1.4 %collective-permute-start.8 = (f32[256,128]{1,0:T(8,128)S(1)}, f32[256,128]{1,0:T(8,128)S(1)}, u32[]{:S(2)}, u32[]{:S(2)}) collective-permute-start(f32[256,128]{1,0:T(8,128)S(1)} %collective-permute-done.7.refs_3_), channel_id=1, source_target_pairs={{0,1},{1,0},{2,3},{3,2},{4,5},{5,4},{6,7},{7,6},{8,9},{9,8},{10,11... | collective-permute-start | bytes 393224 | tf_op jit(solution)/shard_map/ppermute | solution.py:375
  33.0 4.8 %collective-permute-start.9 = (f32[256,128]{1,0:T(8,128)S(1)}, f32[256,128]{1,0:T(8,128)S(1)}, u32[]{:S(2)}, u32[]{:S(2)}) collective-permute-start(f32[256,128]{1,0:T(8,128)S(1)} %get-tuple-element.40), channel_id=1, source_target_pairs={{0,32},{1,33},{2,34},{3,35},{4,36},{5,37},{6,38},{7,39},{8,40},{9,... | collective-permute-start | bytes 393224 | tf_op jit(solution)/shard_map/ppermute | solution.py:375
  37.8 2.2 %collective-permute-start.10 = (f32[256,128]{1,0:T(8,128)S(1)}, f32[256,128]{1,0:T(8,128)S(1)}, u32[]{:S(2)}, u32[]{:S(2)}) collective-permute-start(f32[256,128]{1,0:T(8,128)S(1)} %collective-permute-done.9.refs_1_), channel_id=1, source_target_pairs={{0,1},{1,0},{2,3},{3,2},{4,5},{5,4},{6,7},{7,6},{8,9},{9,8},{10,11... | collective-permute-start | bytes 393224 | tf_op jit(solution)/shard_map/ppermute | solution.py:375
  40.4 7.6 %collective-permute-start.11 = (f32[192,128]{1,0:T(8,128)S(1)}, f32[192,128]{1,0:T(8,128)S(1)}, u32[]{:S(2)}, u32[]{:S(2)}) collective-permute-start(f32[192,128]{1,0:T(8,128)S(1)} %get-tuple-element.42), channel_id=1, source_target_pairs={{0,64},{1,65},{2,66},{3,67},{4,68},{5,69},{6,70},{7,71},{8,72},{9,... | collective-permute-start | bytes 294920 | tf_op jit(solution)/shard_map/ppermute | solution.py:375
  41.2 13.8 %collective-permute-start.13 = (f32[320,128]{1,0:T(8,128)S(1)}, f32[320,128]{1,0:T(8,128)S(1)}, u32[]{:S(2)}, u32[]{:S(2)}) collective-permute-start(f32[320,128]{1,0:T(8,128)S(1)} %get-tuple-element.56), channel_id=1, source_target_pairs={{64,0},{65,1},{66,2},{67,3},{68,4},{69,5},{70,6},{71,7},{72,8},{73... | collective-permute-start | bytes 491528 | tf_op jit(solution)/shard_map/ppermute | solution.py:375
  48.3 7.2 %collective-permute-start.12 = (f32[192,128]{1,0:T(8,128)S(1)}, f32[192,128]{1,0:T(8,128)S(1)}, u32[]{:S(2)}, u32[]{:S(2)}) collective-permute-start(f32[192,128]{1,0:T(8,128)S(1)} %meet.1.refs_0_), channel_id=1, source_target_pairs={{0,192},{1,193},{2,194},{3,195},{4,196},{5,197},{6,198},{7,199},{8... | collective-permute-start | bytes 294920 | tf_op jit(solution)/shard_map/ppermute | solution.py:375
  55.4 8.5 %collective-permute-start.14 = (f32[192,128]{1,0:T(8,128)S(1)}, f32[192,128]{1,0:T(8,128)S(1)}, u32[]{:S(2)}, u32[]{:S(2)}) collective-permute-start(f32[192,128]{1,0:T(8,128)S(1)} %collective-permute-done.12.refs_1_), channel_id=1, source_target_pairs={{0,1},{2,3},{4,5},{6,7},{8,9},{10,11},{12,13},{14,15},{16,17},{18,... | collective-permute-start | bytes 294920 | tf_op jit(solution)/shard_map/ppermute | solution.py:375

commit v7 on v4

--- a/solution.py
+++ b/solution.py
@@ -57,7 +57,7 @@
 ):
     count = rhs.shape[1]
     pairs = ((pivot_hbm, pivot_inv), (rhs_hbm, rhs), (lower_hbm, lower), (upper_hbm, upper))
-    edges = (0, 1, count // 2, count)
+    edges = (0, count // 3, count)
     spans = list(zip(edges[:-1], edges[1:]))
     waits = {}
 
@@ -71,8 +71,7 @@
     for slot, (start, stop) in enumerate(spans):
         for which in range(3):
             fetch(which, slot, start, stop, start)
-    fetch(3, 1, count // 2, count, count - 1)
-    fetch(3, 0, 0, count // 2, count // 2 - 1)
+    fetch(3, 0, 0, count, count - 1)
     states = [None] * PARTS
     scaled = {}
     for i in range(count):
@@ -129,7 +128,7 @@
         scratch_shapes=[pltpu.VMEM(x.shape, jnp.float32) for x in inputs]
         + [
             pltpu.VMEM((PARTS, count, B + R, B), jnp.float32),
-            pltpu.SemaphoreType.DMA((4, 3)),
+            pltpu.SemaphoreType.DMA((4, 2)),
         ],
         compiler_params=pltpu.CompilerParams(vmem_limit_bytes=LIMIT),
         name="local",
@@ -173,7 +172,7 @@
 
 
 def store_half(send, pack):
-    half = PACK // 2
+    half = pack.shape[0] // 2
     send[...] = jnp.where(position() & 1 == 0, pack[:half], pack[half:])
 
 
@@ -195,7 +194,7 @@
     value = joined(*ordered(level + 1, mine, theirs))
     pack[...] = value
     if top:
-        send[...] = jnp.where(is_left(level + 2), value[: B + R], value[2 * B + R :])
+        store_half(send, jnp.where(is_left(level + 2), value[: B + R], value[2 * B + R :]))
     else:
         store_half(send, value)
 
@@ -293,7 +292,8 @@
     )(tracked, *(array for step in steps for array in step))
 
 
-def finish_kernel(level, own, got, weights, offsets, spread, rows, out_hbm, out, sems):
+def finish_kernel(level, own, here, twin, weights, offsets, spread, rows, out_hbm, out, sems):
+    got = jnp.concatenate(by_core(here[...], twin[...]), axis=0)
     carry = jnp.where(is_left(level), mm(own[B : B + R], got[:B]), 0.0) + got[B:]
     carry = left_side(carry)
     count = rows.shape[1]
@@ -318,12 +318,12 @@
         copy.wait()
 
 
-def finish(level, own, got, weights, offsets, spread, rows):
+def finish(level, own, here, twin, weights, offsets, spread, rows):
     shape = (rows.shape[0] * rows.shape[1], R, B)
     return pl.pallas_call(
         lambda *refs: finish_kernel(level, *refs),
         out_shape=jax.ShapeDtypeStruct(shape, jnp.float32),
-        in_specs=[pl.BlockSpec(memory_space=pltpu.VMEM)] * 6,
+        in_specs=[pl.BlockSpec(memory_space=pltpu.VMEM)] * 7,
         out_specs=pl.BlockSpec(memory_space=pltpu.HBM),
         scratch_shapes=[
             pltpu.VMEM(shape, jnp.float32),
@@ -331,7 +331,7 @@
         ],
         compiler_params=pltpu.CompilerParams(vmem_limit_bytes=LIMIT),
         name="finish",
-    )(own, got, weights, offsets, spread, rows)
+    )(own, here, twin, weights, offsets, spread, rows)
 
 
 def on_device(rhs, pivot_inv, lower_gain, upper_gain):
@@ -361,14 +361,15 @@
             own,
             received,
             3,
-            B + R if last else PACK // 2,
+            (B + R) // 2 if last else PACK // 2,
         )
         steps += [(own, one), (near, far)]
     facing = [(i, FACING[i // plane] * plane + i % plane) for i in range(devices)]
     got = lax.ppermute(half, AXES, facing)
     tracked, spread = aside
-    weights, offsets = refine(top - 2, top, tracked, steps[top - 2 :])
-    return finish(top, pack, got, weights, offsets, spread, rows)
+    maps = refine(top - 2, top, tracked, steps[top - 2 :])
+    got, maps = lax.optimization_barrier((got, maps))
+    return finish(top, pack, got, swap(got, 1, 1), *maps, spread, rows)
 
 
 def solution(mesh):

time: 58.6 us -> 57.7 us (0.985)
  the two profiles are of different devices: /device:TPU:63 before, /device:TPU:1 now
where the time goes in v7:
time: 57.7 us; the launch traced here: 57.1 us
  waiting for transfers between devices  30.1 us (52%)
  starting transfers between devices  16.8 us (29%)
  Pallas kernels  10 us (17%)
    ppermute x14, waiting for transfers between devices, on_device(): lax.ppermute(array, AXES, [(i, i ^ (odd if i & 1 else even)) for i in ran...  29.1 us
    ppermute x14, starting transfers between devices, on_device(): lax.ppermute(array, AXES, [(i, i ^ (odd if i & 1 else even)) for i in ran...  13.4 us
    pallas_call x1, Pallas kernels, local(): pl.pallas_call(local_kernel, out_shape=(jax.ShapeDtypeStruct((PACK, B), j...  3.47 us
    ppermute x1, starting transfers between devices, on_device(): got = lax.ppermute(half, AXES, facing)  3.41 us
    pallas_call x4, Pallas kernels, combine(): pl.pallas_call(kernel, out_shape=(whole,) * (1 + extra) + (jax.ShapeDtype...  2.61 us
    pallas_call x1, Pallas kernels, prepare(): pl.pallas_call(lambda *refs: prepare_kernel(len(steps), *refs), out_shape...  1.72 us
    pallas_call x1, Pallas kernels, finish(): pl.pallas_call(lambda *refs: finish_kernel(level, *refs), out_shape=jax.S...  1.49 us
  transfers between devices with their start and end apart: 15, of which 12 were waited for; matrix products, arithmetic and copies ran while one was open for 0% of the time, Pallas kernels for 4%

profile of v7, /device:TPU:1, one launch (start us, length us, event | category | flops | bytes accessed | tf_op | source)
XLA Modules:
  0.0 57.1 jit_solution(15372846635941146759)
XLA Ops:
  0.0 3.5 %local.1 = (f32[512,128]{1,0:T(8,128)S(1)}, f32[2,512,128]{2,1,0:T(8,128)S(1)}, f32[2,6,320,128]{3,2,1,0:T(8,128)S(1)}) custom-call(f32[2,6,64,128]{3,2,1,0:T(8,128)} %bitcast.7, f32[2,6,128,128]{3,2,1,0:T(8,128)} %bitcast.4, f32[2,6,128,128]{3,2,1,0:T(8,128)} %bitcast.5, f32[2,6,128,128]{3,2,1,0:T(8,128)} %bitcast.6), custom_call_target="tpu_custom_call" | custom-call | tf_op jit(solution)/shard_map/local/pallas_call | solution.py:119
  3.5 3.3 %collective-permute-start = (f32[512,128]{1,0:T(8,128)S(1)}, f32[512,128]{1,0:T(8,128)S(1)}, u32[]{:S(2)}, u32[]{:S(2)}) collective-permute-start(f32[512,128]{1,0:T(8,128)S(1)} %get-tuple-element.35.own.refs_2_), channel_id=1, source_target_pairs={{0,1},{1,0},{2,3},{3,2},{4,5},{5,4},{6,7},{7,6},{8,9},{9,8},{10,11... | collective-permute-start | bytes 786440 | tf_op jit(solution)/shard_map/ppermute | solution.py:341
  6.8 1.2 %collective-permute-done.other.refs_3_ = f32[512,128]{1,0:T(8,128)S(1)} collective-permute-done((f32[512,128]{1,0:T(8,128)S(1)}, f32[512,128]{1,0:T(8,128)S(1)}, u32[]{:S(2)}, u32[]{:S(2)}) %collective-permute-start) | collective-permute-done | bytes 262176 | tf_op jit(solution)/shard_map/ppermute | solution.py:341
  8.0 0.3 pair.1
  8.3 1.1 %collective-permute-start.1 = (f32[512,128]{1,0:T(8,128)S(1)}, f32[512,128]{1,0:T(8,128)S(1)}, u32[]{:S(2)}, u32[]{:S(2)}) collective-permute-start(f32[512,128]{1,0:T(8,128)S(1)} %get-tuple-element.36.refs_0_.refs_4_), channel_id=1, source_target_pairs={{0,2},{1,5},{2,0},{3,7},{4,6},{5,1},{6,4},{7,3},{8,10},{9,13},{10,... | collective-permute-start | bytes 786440 | tf_op jit(solution)/shard_map/ppermute | solution.py:341
  9.4 0.9 %collective-permute-start.3 = (f32[256,128]{1,0:T(8,128)S(1)}, f32[256,128]{1,0:T(8,128)S(1)}, u32[]{:S(2)}, u32[]{:S(2)}) collective-permute-start(f32[256,128]{1,0:T(8,128)S(1)} %get-tuple-element.37), channel_id=1, source_target_pairs={{0,6},{1,7},{2,4},{3,5},{4,2},{5,3},{6,0},{7,1},{8,14},{9,15},{10,... | collective-permute-start | bytes 393224 | tf_op jit(solution)/shard_map/ppermute | solution.py:341
  10.3 7.6 %collective-permute-done.1.refs_1_ = f32[512,128]{1,0:T(8,128)S(1)} collective-permute-done((f32[512,128]{1,0:T(8,128)S(1)}, f32[512,128]{1,0:T(8,128)S(1)}, u32[]{:S(2)}, u32[]{:S(2)}) %collective-permute-start.1) | collective-permute-done | bytes 262176 | tf_op jit(solution)/shard_map/ppermute | solution.py:341
  17.8 0.7 %collective-permute-done.3.refs_3_ = f32[256,128]{1,0:T(8,128)S(1)} collective-permute-done((f32[256,128]{1,0:T(8,128)S(1)}, f32[256,128]{1,0:T(8,128)S(1)}, u32[]{:S(2)}, u32[]{:S(2)}) %collective-permute-start.3) | collective-permute-done | bytes 131104 | tf_op jit(solution)/shard_map/ppermute | solution.py:341
  18.5 0.4 collective-permute-start.4
  18.9 1.0 %collective-permute-done.4.refs_4_ = f32[256,128]{1,0:T(8,128)S(1)} collective-permute-done((f32[256,128]{1,0:T(8,128)S(1)}, f32[256,128]{1,0:T(8,128)S(1)}, u32[]{:S(2)}, u32[]{:S(2)}) %collective-permute-start.4) | collective-permute-done | bytes 131104 | tf_op jit(solution)/shard_map/ppermute | solution.py:341
  19.9 0.8 %quad1.1 = (f32[512,128]{1,0:T(8,128)S(1)}, f32[512,128]{1,0:T(8,128)S(1)}, f32[512,128]{1,0:T(8,128)S(1)}, f32[512,128]{1,0:T(8,128)S(1)}, f32[256,128]{1,0:T(8,128)S(1)}) custom-call(f32[512,128]{1,0:T(8,128)S(1)} %get-tuple-element.36.refs_0_.refs_4_, f32[512,128]{1,0:T(8,128)S(1)} %collective-permute-done.1.refs_1_, ...), custom_call_target="tpu_custom_call" | custom-call | tf_op jit(solution)/shard_map/quad1/pallas_call | solution.py:204
  20.7 1.0 %collective-permute-start.5 = (f32[512,128]{1,0:T(8,128)S(1)}, f32[512,128]{1,0:T(8,128)S(1)}, u32[]{:S(2)}, u32[]{:S(2)}) collective-permute-start(f32[512,128]{1,0:T(8,128)S(1)} %get-tuple-element.38.refs_0_.refs_8_), channel_id=1, source_target_pairs={{0,8},{1,17},{2,10},{3,19},{4,12},{5,21},{6,14},{7,23},{8,0},{9,25... | collective-permute-start | bytes 786440 | tf_op jit(solution)/shard_map/ppermute | solution.py:341
  21.6 0.8 %collective-permute-start.7 = (f32[256,128]{1,0:T(8,128)S(1)}, f32[256,128]{1,0:T(8,128)S(1)}, u32[]{:S(2)}, u32[]{:S(2)}) collective-permute-start(f32[256,128]{1,0:T(8,128)S(1)} %get-tuple-element.39), channel_id=1, source_target_pairs={{0,24},{1,25},{2,26},{3,27},{4,28},{5,29},{6,30},{7,31},{8,16},{9,... | collective-permute-start | bytes 393224 | tf_op jit(solution)/shard_map/ppermute | solution.py:341
  22.4 7.7 %collective-permute-done.5.refs_1_ = f32[512,128]{1,0:T(8,128)S(1)} collective-permute-done((f32[512,128]{1,0:T(8,128)S(1)}, f32[512,128]{1,0:T(8,128)S(1)}, u32[]{:S(2)}, u32[]{:S(2)}) %collective-permute-start.5) | collective-permute-done | bytes 262176 | tf_op jit(solution)/shard_map/ppermute | solution.py:341
  30.1 0.7 %collective-permute-done.7.refs_3_ = f32[256,128]{1,0:T(8,128)S(1)} collective-permute-done((f32[256,128]{1,0:T(8,128)S(1)}, f32[256,128]{1,0:T(8,128)S(1)}, u32[]{:S(2)}, u32[]{:S(2)}) %collective-permute-start.7) | collective-permute-done | bytes 131104 | tf_op jit(solution)/shard_map/ppermute | solution.py:341
  30.9 0.4 collective-permute-start.8
  31.3 1.0 %collective-permute-done.8.refs_4_ = f32[256,128]{1,0:T(8,128)S(1)} collective-permute-done((f32[256,128]{1,0:T(8,128)S(1)}, f32[256,128]{1,0:T(8,128)S(1)}, u32[]{:S(2)}, u32[]{:S(2)}) %collective-permute-start.8) | collective-permute-done | bytes 131104 | tf_op jit(solution)/shard_map/ppermute | solution.py:341
  32.3 0.8 %quad3.1 = (f32[512,128]{1,0:T(8,128)S(1)}, f32[512,128]{1,0:T(8,128)S(1)}, f32[512,128]{1,0:T(8,128)S(1)}, f32[512,128]{1,0:T(8,128)S(1)}, f32[256,128]{1,0:T(8,128)S(1)}) custom-call(f32[512,128]{1,0:T(8,128)S(1)} %get-tuple-element.38.refs_0_.refs_8_, f32[512,128]{1,0:T(8,128)S(1)} %collective-permute-done.5.refs_1_, ...), custom_call_target="tpu_custom_call" | custom-call | tf_op jit(solution)/shard_map/quad3/pallas_call | solution.py:204
  33.0 2.0 %collective-permute-start.9 = (f32[512,128]{1,0:T(8,128)S(1)}, f32[512,128]{1,0:T(8,128)S(1)}, u32[]{:S(2)}, u32[]{:S(2)}) collective-permute-start(f32[512,128]{1,0:T(8,128)S(1)} %get-tuple-element.40.refs_0_.refs_1_), channel_id=1, source_target_pairs={{0,32},{1,97},{2,34},{3,99},{4,36},{5,101},{6,38},{7,103},{8,40},{... | collective-permute-start | bytes 786440 | tf_op jit(solution)/shard_map/ppermute | solution.py:341
  35.0 1.7 %prepare.1 = (f32[2,512,128]{2,1,0:T(8,128)S(1)}, bf16[2,6,256,256]{3,2,1,0:T(8,128)(2,1)S(1)}) custom-call(f32[2,512,128]{2,1,0:T(8,128)S(1)} %get-tuple-element.41.refs_0_, f32[2,6,320,128]{3,2,1,0:T(8,128)S(1)} %get-tuple-element.42.refs_1_.refs_6_, f32[512,128]{1,0:T(8,128)S(1)} %get-tuple-element.35.own.refs_2_, ...), custom_call_target="tpu_custom_call" | custom-call | flops 2147483648 | bytes 8388608 | tf_op jit(solution)/shard_map/prepare/pallas_call | solution.py:250
  36.7 6.2 %collective-permute-done.9.refs_1_ = f32[512,128]{1,0:T(8,128)S(1)} collective-permute-done((f32[512,128]{1,0:T(8,128)S(1)}, f32[512,128]{1,0:T(8,128)S(1)}, u32[]{:S(2)}, u32[]{:S(2)}) %collective-permute-start.9) | collective-permute-done | bytes 262176 | tf_op jit(solution)/shard_map/ppermute | solution.py:341
  42.9 1.8 %collective-permute-start.10 = (f32[512,128]{1,0:T(8,128)S(1)}, f32[512,128]{1,0:T(8,128)S(1)}, u32[]{:S(2)}, u32[]{:S(2)}) collective-permute-start(f32[512,128]{1,0:T(8,128)S(1)} %collective-permute-done.9.refs_1_), channel_id=1, source_target_pairs={{0,1},{1,0},{2,3},{3,2},{4,5},{5,4},{6,7},{7,6},{8,9},{9,8},{10,11... | collective-permute-start | bytes 786440 | tf_op jit(solution)/shard_map/ppermute | solution.py:341
  44.7 1.2 %collective-permute-done.11.refs_3_ = f32[256,128]{1,0:T(8,128)S(1)} collective-permute-done((f32[256,128]{1,0:T(8,128)S(1)}, f32[256,128]{1,0:T(8,128)S(1)}, u32[]{:S(2)}, u32[]{:S(2)}) %collective-permute-start.11) | collective-permute-done | bytes 131104 | tf_op jit(solution)/shard_map/ppermute | solution.py:341
  45.8 0.3 collective-permute-start.12
  46.1 1.0 %collective-permute-done.12.refs_4_ = f32[256,128]{1,0:T(8,128)S(1)} collective-permute-done((f32[256,128]{1,0:T(8,128)S(1)}, f32[256,128]{1,0:T(8,128)S(1)}, u32[]{:S(2)}, u32[]{:S(2)}) %collective-permute-start.12) | collective-permute-done | bytes 131104 | tf_op jit(solution)/shard_map/ppermute | solution.py:341
  47.2 0.8 %quad5.1 = (f32[512,128]{1,0:T(8,128)S(1)}, f32[512,128]{1,0:T(8,128)S(1)}, f32[512,128]{1,0:T(8,128)S(1)}, f32[512,128]{1,0:T(8,128)S(1)}, f32[96,128]{1,0:T(8,128)S(1)}) custom-call(f32[512,128]{1,0:T(8,128)S(1)} %get-tuple-element.40.refs_0_.refs_1_, f32[512,128]{1,0:T(8,128)S(1)} %collective-permute-done.9.refs_1_, ...), custom_call_target="tpu_custom_call" | custom-call | tf_op jit(solution)/shard_map/quad5/pallas_call | solution.py:204
  48.0 3.4 %collective-permute-start.13 = (f32[96,128]{1,0:T(8,128)S(1)}, f32[96,128]{1,0:T(8,128)S(1)}, u32[]{:S(2)}, u32[]{:S(2)}) collective-permute-start(f32[96,128]{1,0:T(8,128)S(1)} %get-tuple-element.54), channel_id=1, source_target_pairs={{0,192},{1,193},{2,194},{3,195},{4,196},{5,197},{6,198},{7,199},{8... | collective-permute-start | bytes 147464 | tf_op jit(solution)/shard_map/ppermute | solution.py:368
  51.4 0.7 %refine.1 = (bf16[2,2,256,256]{3,2,1,0:T(8,128)(2,1)S(1)}, f32[2,2,64,128]{3,2,1,0:T(8,128)S(1)}) custom-call(f32[2,512,128]{2,1,0:T(8,128)S(1)} %get-tuple-element.55.refs_0_, f32[512,128]{1,0:T(8,128)S(1)} %get-tuple-element.40.refs_0_.refs_1_, f32[512,128]{1,0:T(8,128)S(1)} %get-tuple-element.56.refs_2_, f32[512,128]{1,0:T(8,128)S(1)} %get-tuple-element.57.refs_3_, ...), custom_call_target="tpu_custom_call" | custom-call | flops 1073741824 | bytes 4194304 | tf_op jit(solution)/shard_map/refine/pallas_call | solution.py:281
  52.1 1.0 %collective-permute-done.13.refs_1_ = f32[96,128]{1,0:T(8,128)S(1)} collective-permute-done((f32[96,128]{1,0:T(8,128)S(1)}, f32[96,128]{1,0:T(8,128)S(1)}, u32[]{:S(2)}, u32[]{:S(2)}) %collective-permute-start.13) | collective-permute-done | bytes 49184 | tf_op jit(solution)/shard_map/ppermute | solution.py:368
  53.1 1.5 %collective-permute-start.14 = (f32[96,128]{1,0:T(8,128)S(1)}, f32[96,128]{1,0:T(8,128)S(1)}, u32[]{:S(2)}, u32[]{:S(2)}) collective-permute-start(f32[96,128]{1,0:T(8,128)S(1)} %collective-permute-done.13.refs_1_), channel_id=1, source_target_pairs={{0,1},{1,0},{2,3},{3,2},{4,5},{5,4},{6,7},{7,6},{8,9},{9,8},{10,11... | collective-permute-start | bytes 147464 | tf_op jit(solution)/shard_map/ppermute | solution.py:341
  54.6 0.9 %collective-permute-done.14.refs_2_ = f32[96,128]{1,0:T(8,128)S(1)} collective-permute-done((f32[96,128]{1,0:T(8,128)S(1)}, f32[96,128]{1,0:T(8,128)S(1)}, u32[]{:S(2)}, u32[]{:S(2)}) %collective-permute-start.14) | collective-permute-done | bytes 49184 | tf_op jit(solution)/shard_map/ppermute | solution.py:341
  55.5 1.5 %finish.1 = f32[12,64,128]{2,1,0:T(8,128)} custom-call(f32[512,128]{1,0:T(8,128)S(1)} %get-tuple-element.53.refs_0_, f32[96,128]{1,0:T(8,128)S(1)} %collective-permute-done.13.refs_1_, f32[96,128]{1,0:T(8,128)S(1)} %collective-permute-done.14.refs_2_, bf16[2,2,256,256]{3,2,1,0:T(8,128)(2,1)S(1)} %get-tuple-element.62.refs_3_, ...), custom_call_target="tpu_custom_call" | custom-call | tf_op jit(solution)/shard_map/finish/pallas_call | solution.py:323
  (6 shorter events, 0.0 us)
Async XLA Ops:
  3.5 4.5 %collective-permute-start = (f32[512,128]{1,0:T(8,128)S(1)}, f32[512,128]{1,0:T(8,128)S(1)}, u32[]{:S(2)}, u32[]{:S(2)}) collective-permute-start(f32[512,128]{1,0:T(8,128)S(1)} %get-tuple-element.35.own.refs_2_), channel_id=1, source_target_pairs={{0,1},{1,0},{2,3},{3,2},{4,5},{5,4},{6,7},{7,6},{8,9},{9,8},{10,11... | collective-permute-start | bytes 786440 | tf_op jit(solution)/shard_map/ppermute | solution.py:341
  8.3 9.5 %collective-permute-start.1 = (f32[512,128]{1,0:T(8,128)S(1)}, f32[512,128]{1,0:T(8,128)S(1)}, u32[]{:S(2)}, u32[]{:S(2)}) collective-permute-start(f32[512,128]{1,0:T(8,128)S(1)} %get-tuple-element.36.refs_0_.refs_4_), channel_id=1, source_target_pairs={{0,2},{1,5},{2,0},{3,7},{4,6},{5,1},{6,4},{7,3},{8,10},{9,13},{10,... | collective-permute-start | bytes 786440 | tf_op jit(solution)/shard_map/ppermute | solution.py:341
  9.4 9.1 %collective-permute-start.3 = (f32[256,128]{1,0:T(8,128)S(1)}, f32[256,128]{1,0:T(8,128)S(1)}, u32[]{:S(2)}, u32[]{:S(2)}) collective-permute-start(f32[256,128]{1,0:T(8,128)S(1)} %get-tuple-element.37), channel_id=1, source_target_pairs={{0,6},{1,7},{2,4},{3,5},{4,2},{5,3},{6,0},{7,1},{8,14},{9,15},{10,... | collective-permute-start | bytes 393224 | tf_op jit(solution)/shard_map/ppermute | solution.py:341
  17.8 2.1 %collective-permute-start.2 = (f32[512,128]{1,0:T(8,128)S(1)}, f32[512,128]{1,0:T(8,128)S(1)}, u32[]{:S(2)}, u32[]{:S(2)}) collective-permute-start(f32[512,128]{1,0:T(8,128)S(1)} %collective-permute-done.1.refs_1_), channel_id=1, source_target_pairs={{0,1},{1,0},{2,3},{3,2},{4,5},{5,4},{6,7},{7,6},{8,9},{9,8},{10,11... | collective-permute-start | bytes 786440 | tf_op jit(solution)/shard_map/ppermute | solution.py:341
  18.5 1.4 %collective-permute-start.4 = (f32[256,128]{1,0:T(8,128)S(1)}, f32[256,128]{1,0:T(8,128)S(1)}, u32[]{:S(2)}, u32[]{:S(2)}) collective-permute-start(f32[256,128]{1,0:T(8,128)S(1)} %collective-permute-done.3.refs_3_), channel_id=1, source_target_pairs={{0,1},{1,0},{2,3},{3,2},{4,5},{5,4},{6,7},{7,6},{8,9},{9,8},{10,11... | collective-permute-start | bytes 393224 | tf_op jit(solution)/shard_map/ppermute | solution.py:341
  20.7 9.5 %collective-permute-start.5 = (f32[512,128]{1,0:T(8,128)S(1)}, f32[512,128]{1,0:T(8,128)S(1)}, u32[]{:S(2)}, u32[]{:S(2)}) collective-permute-start(f32[512,128]{1,0:T(8,128)S(1)} %get-tuple-element.38.refs_0_.refs_8_), channel_id=1, source_target_pairs={{0,8},{1,17},{2,10},{3,19},{4,12},{5,21},{6,14},{7,23},{8,0},{9,25... | collective-permute-start | bytes 786440 | tf_op jit(solution)/shard_map/ppermute | solution.py:341
  21.6 9.2 %collective-permute-start.7 = (f32[256,128]{1,0:T(8,128)S(1)}, f32[256,128]{1,0:T(8,128)S(1)}, u32[]{:S(2)}, u32[]{:S(2)}) collective-permute-start(f32[256,128]{1,0:T(8,128)S(1)} %get-tuple-element.39), channel_id=1, source_target_pairs={{0,24},{1,25},{2,26},{3,27},{4,28},{5,29},{6,30},{7,31},{8,16},{9,... | collective-permute-start | bytes 393224 | tf_op jit(solution)/shard_map/ppermute | solution.py:341
  30.1 2.1 %collective-permute-start.6 = (f32[512,128]{1,0:T(8,128)S(1)}, f32[512,128]{1,0:T(8,128)S(1)}, u32[]{:S(2)}, u32[]{:S(2)}) collective-permute-start(f32[512,128]{1,0:T(8,128)S(1)} %collective-permute-done.5.refs_1_), channel_id=1, source_target_pairs={{0,1},{1,0},{2,3},{3,2},{4,5},{5,4},{6,7},{7,6},{8,9},{9,8},{10,11... | collective-permute-start | bytes 786440 | tf_op jit(solution)/shard_map/ppermute | solution.py:341
  30.9 1.4 %collective-permute-start.8 = (f32[256,128]{1,0:T(8,128)S(1)}, f32[256,128]{1,0:T(8,128)S(1)}, u32[]{:S(2)}, u32[]{:S(2)}) collective-permute-start(f32[256,128]{1,0:T(8,128)S(1)} %collective-permute-done.7.refs_3_), channel_id=1, source_target_pairs={{0,1},{1,0},{2,3},{3,2},{4,5},{5,4},{6,7},{7,6},{8,9},{9,8},{10,11... | collective-permute-start | bytes 393224 | tf_op jit(solution)/shard_map/ppermute | solution.py:341
  33.0 9.9 %collective-permute-start.9 = (f32[512,128]{1,0:T(8,128)S(1)}, f32[512,128]{1,0:T(8,128)S(1)}, u32[]{:S(2)}, u32[]{:S(2)}) collective-permute-start(f32[512,128]{1,0:T(8,128)S(1)} %get-tuple-element.40.refs_0_.refs_1_), channel_id=1, source_target_pairs={{0,32},{1,97},{2,34},{3,99},{4,36},{5,101},{6,38},{7,103},{8,40},{... | collective-permute-start | bytes 786440 | tf_op jit(solution)/shard_map/ppermute | solution.py:341
  35.0 10.8 %collective-permute-start.11 = (f32[256,128]{1,0:T(8,128)S(1)}, f32[256,128]{1,0:T(8,128)S(1)}, u32[]{:S(2)}, u32[]{:S(2)}) collective-permute-start(f32[256,128]{1,0:T(8,128)S(1)} %get-tuple-element.52), channel_id=1, source_target_pairs={{0,64},{1,65},{2,66},{3,67},{4,68},{5,69},{6,70},{7,71},{8,72},{9,... | collective-permute-start | bytes 393224 | tf_op jit(solution)/shard_map/ppermute | solution.py:341
  42.9 4.3 %collective-permute-start.10 = (f32[512,128]{1,0:T(8,128)S(1)}, f32[512,128]{1,0:T(8,128)S(1)}, u32[]{:S(2)}, u32[]{:S(2)}) collective-permute-start(f32[512,128]{1,0:T(8,128)S(1)} %collective-permute-done.9.refs_1_), channel_id=1, source_target_pairs={{0,1},{1,0},{2,3},{3,2},{4,5},{5,4},{6,7},{7,6},{8,9},{9,8},{10,11... | collective-permute-start | bytes 786440 | tf_op jit(solution)/shard_map/ppermute | solution.py:341
  45.8 1.3 %collective-permute-start.12 = (f32[256,128]{1,0:T(8,128)S(1)}, f32[256,128]{1,0:T(8,128)S(1)}, u32[]{:S(2)}, u32[]{:S(2)}) collective-permute-start(f32[256,128]{1,0:T(8,128)S(1)} %collective-permute-done.11.refs_3_), channel_id=1, source_target_pairs={{0,1},{1,0},{2,3},{3,2},{4,5},{5,4},{6,7},{7,6},{8,9},{9,8},{10,11... | collective-permute-start | bytes 393224 | tf_op jit(solution)/shard_map/ppermute | solution.py:341
  48.0 5.1 %collective-permute-start.13 = (f32[96,128]{1,0:T(8,128)S(1)}, f32[96,128]{1,0:T(8,128)S(1)}, u32[]{:S(2)}, u32[]{:S(2)}) collective-permute-start(f32[96,128]{1,0:T(8,128)S(1)} %get-tuple-element.54), channel_id=1, source_target_pairs={{0,192},{1,193},{2,194},{3,195},{4,196},{5,197},{6,198},{7,199},{8... | collective-permute-start | bytes 147464 | tf_op jit(solution)/shard_map/ppermute | solution.py:368
  53.1 2.4 %collective-permute-start.14 = (f32[96,128]{1,0:T(8,128)S(1)}, f32[96,128]{1,0:T(8,128)S(1)}, u32[]{:S(2)}, u32[]{:S(2)}) collective-permute-start(f32[96,128]{1,0:T(8,128)S(1)} %collective-permute-done.13.refs_1_), channel_id=1, source_target_pairs={{0,1},{1,0},{2,3},{3,2},{4,5},{5,4},{6,7},{7,6},{8,9},{9,8},{10,11... | collective-permute-start | bytes 147464 | tf_op jit(solution)/shard_map/ppermute | solution.py:341

commit v8 on v7

v8 whole, which is shorter than its diff:
```python
import jax
import jax.numpy as jnp
from jax import lax
from jax.experimental import pallas as pl
from jax.experimental.pallas import tpu as pltpu
from jax.sharding import PartitionSpec as P

AXES = ("wide", "narrow")
B = 128
R = 64
PACK = 3 * B + 2 * R
PARTS = 2
OUT_ROWS = 3
FACING = (6, 7, 4, 5, 2, 3, 0, 1)
ROUNDS = ((1, (8, 24, 32)), (3, (2, 6, 32)), (5, (2, 6, 8)))
ASIDE_TOP = 8
LIMIT = 12 * 2**20


def halves(value):
    high = value.astype(jnp.bfloat16)
    low = (value - high.astype(jnp.float32)).astype(jnp.bfloat16)
    return high, low


def left_side(value):
    return jnp.concatenate(halves(value), axis=1)


def right_side(value):
    both = jnp.concatenate(halves(value), axis=1)
    return jnp.concatenate([both, both], axis=0)


def times(left, right):
    wide = jnp.dot(left, right, preferred_element_type=jnp.float32)
    return wide[:, :B] + wide[:, B:]


def mm(left, right):
    return times(left_side(left), right_side(right))


def local_kernel(
    rhs_hbm,
    pivot_hbm,
    lower_hbm,
    upper_hbm,
    pack,
    parts,
    rows,
    rhs,
    pivot_inv,
    lower,
    upper,
    forward,
    sems,
):
    count = rhs.shape[1]
    pairs = ((pivot_hbm, pivot_inv), (rhs_hbm, rhs), (lower_hbm, lower), (upper_hbm, upper))
    edges = (0, count // 3, count)
    spans = list(zip(edges[:-1], edges[1:]))
    waits = {}

    def fetch(which, slot, start, stop, row):
        source, target = pairs[which]
        span = (slice(None), pl.ds(start, stop - start))
        copy = pltpu.make_async_copy(source.at[span], target.at[span], sems.at[which, slot])
        copy.start()
        waits.setdefault((which // 3, row), []).append(copy)

    for slot, (start, stop) in enumerate(spans):
        for which in range(3):
            fetch(which, slot, start, stop, start)
    fetch(3, 0, 0, count, count - 1)
    states = [None] * PARTS
    scaled = {}
    for i in range(count):
        if (0, i) in waits:
            for copy in waits[0, i]:
                copy.wait()
            stop = next(stop for start, stop in spans if start == i)
            for j in range(i, stop):
                for part in range(PARTS):
                    scaled[part, j] = mm(rhs[part, j], pivot_inv[part, j])
        for part in range(PARTS):
            if i == 0:
                state = jnp.concatenate([-lower[part, 0], scaled[part, 0]], axis=0)
            else:
                moved = mm(states[part], lower[part, i])
                state = jnp.concatenate([-moved[:B], scaled[part, i] - moved[B:]], axis=0)
            forward[part, i] = state
            states[part] = state
    for part in range(PARTS):
        parts[part, : B + R] = states[part]
    for i in range(count - 1, -1, -1):
        for copy in waits.get((1, i), []):
            copy.wait()
        for part in range(PARTS):
            if i == count - 1:
                state = jnp.concatenate([-upper[part, i], states[part]], axis=0)
            else:
                moved = mm(states[part], upper[part, i])
                state = jnp.concatenate([-moved[:B], forward[part, i] - moved[B:]], axis=0)
            rows[part, i] = state
            states[part] = state
    for part in range(PARTS):
        parts[part, B + R :] = states[part]
    pack[...] = joined(parts[0], parts[1])


def local(rhs, pivot_inv, lower, upper):
    inputs = [
        pltpu.with_memory_space_constraint(
            x.reshape((PARTS, x.shape[0] // PARTS) + x.shape[1:]), pltpu.HBM
        )
        for x in (rhs, pivot_inv, lower, upper)
    ]
    count = inputs[0].shape[1]
    return pl.pallas_call(
        local_kernel,
        out_shape=(
            jax.ShapeDtypeStruct((PACK, B), jnp.float32),
            jax.ShapeDtypeStruct((PARTS, PACK, B), jnp.float32),
            jax.ShapeDtypeStruct((PARTS, count, 2 * B + R, B), jnp.float32),
        ),
        in_specs=[pl.BlockSpec(memory_space=pltpu.HBM)] * 4,
        out_specs=[pl.BlockSpec(memory_space=pltpu.VMEM)] * 3,
        scratch_shapes=[pltpu.VMEM(x.shape, jnp.float32) for x in inputs]
        + [
            pltpu.VMEM((PARTS, count, B + R, B), jnp.float32),
            pltpu.SemaphoreType.DMA((4, 2)),
        ],
        compiler_params=pltpu.CompilerParams(vmem_limit_bytes=LIMIT),
        name="local",
    )(*inputs)


def position():
    return lax.axis_index(AXES[0]) * lax.axis_size(AXES[1]) + lax.axis_index(AXES[1])


def is_left(level):
    return (position() >> level) & 1 == 0


def ordered(level, own, other):
    left = is_left(level)
    return jnp.where(left, own, other), jnp.where(left, other, own)


def turned(first, second):
    early = left_side(first[: B + R])
    turn = times(early, right_side(second[2 * B + R : 3 * B + R]))
    back = jnp.concatenate(
        [second[B + R : 2 * B + R], turn[:B], turn[B:] + second[3 * B + R :]], axis=0
    )
    return early, back


def joined(first, second):
    early, back = turned(first, second)
    down = times(early, right_side(second[:B]))
    up = mm(back, first[B + R : 2 * B + R])
    return jnp.concatenate(
        [down[:B], down[B:] + second[B : B + R], up[:B], up[B:] + first[2 * B + R :]], axis=0
    )


def pair_kernel(own, other, pack):
    pack[...] = joined(*ordered(0, own[...], other[...]))


def quad_kernel(level, own, one, two, three, near, far, pack, *send):
    mine = joined(*ordered(level, own[...], one[...]))
    theirs = joined(*ordered(level, two[...], three[...]))
    near[...] = mine
    far[...] = theirs
    value = joined(*ordered(level + 1, mine, theirs))
    pack[...] = value
    if send:
        send[0][...] = jnp.where(is_left(level + 2), value[: B + R], value[2 * B + R :])


def combine(kernel, name, own, parts, *out_rows):
    return pl.pallas_call(
        kernel,
        out_shape=tuple(jax.ShapeDtypeStruct((rows, B), jnp.float32) for rows in out_rows),
        in_specs=[pl.BlockSpec(memory_space=pltpu.VMEM)] * (1 + len(parts)),
        out_specs=[pl.BlockSpec(memory_space=pltpu.VMEM)] * len(out_rows),
        compiler_params=pltpu.CompilerParams(vmem_limit_bytes=LIMIT),
        name=name,
    )(own, *parts)


def advanced(level, first, second, ahead, behind):
    early, back = turned(first, second)
    left = is_left(level)
    through = mm(back, behind[:B])
    through = jnp.concatenate([through[:B], through[B:] + behind[B:]], axis=0)
    onward = times(early, right_side(ahead[:B]))
    onward = jnp.concatenate([onward[:B], onward[B:] + ahead[B:]], axis=0)
    cross = times(early, right_side(behind[B : 2 * B]))
    cross = jnp.concatenate([behind[:B], cross[:B], cross[B:] + behind[2 * B :]], axis=0)
    return jnp.where(left, ahead, onward), jnp.where(left, through, cross)


def identity():
    rows = lax.broadcasted_iota(jnp.int32, (2 * B + R, B), 0)
    unit = (rows == lax.broadcasted_iota(jnp.int32, (2 * B + R, B), 1)).astype(jnp.float32)
    return unit[: B + R], unit


def prepare_kernel(parts, rows, own, other, weights, offsets, spread):
    ahead, behind = identity()
    _, back = turned(parts[0], parts[1])
    maps = ((ahead, back), (parts[0, : B + R], behind))
    first, second = ordered(0, own[...], other[...])
    for part in range(PARTS):
        ahead, behind = advanced(0, first, second, *maps[part])
        weights[part, 0] = left_side(behind[: 2 * B])
        weights[part, 1] = right_side(ahead[:B])
        offsets[part, 0] = behind[2 * B :]
        offsets[part, 1] = ahead[B:]
        for i in range(rows.shape[1]):
            spread[part, i] = left_side(rows[part, i, : 2 * B])


def prepare(parts, rows, own, other):
    return pl.pallas_call(
        prepare_kernel,
        out_shape=(
            jax.ShapeDtypeStruct((PARTS, 2, 2 * B, 2 * B), jnp.bfloat16),
            jax.ShapeDtypeStruct((PARTS, 2, R, B), jnp.float32),
            jax.ShapeDtypeStruct(rows.shape[:2] + (2 * B, 2 * B), jnp.bfloat16),
        ),
        in_specs=[pl.BlockSpec(memory_space=pltpu.VMEM)] * 4,
        out_specs=[pl.BlockSpec(memory_space=pltpu.VMEM)] * 3,
        compiler_params=pltpu.CompilerParams(vmem_limit_bytes=LIMIT),
        cost_estimate=pl.CostEstimate(flops=2**31, bytes_accessed=2**23, transcendentals=0),
        name="prepare",
    )(parts, rows, own, other)


def climb_kernel(start, top, *refs):
    pairs, (weights, offsets) = refs[:-2], refs[-2:]
    ahead, behind = identity()
    for i in range(len(pairs) // 2):
        first, second = ordered(start + i, pairs[2 * i][...], pairs[2 * i + 1][...])
        ahead, behind = advanced(start + i, first, second, ahead, behind)
    left = is_left(top)
    weights[0] = right_side(jnp.where(left, behind[:B], behind[B : 2 * B]))
    weights[1] = right_side(jnp.where(left, 0.0, ahead[:B]))
    offsets[0] = behind[2 * B :]
    offsets[1] = ahead[B:]


def climb(start, top, steps):
    return pl.pallas_call(
        lambda *refs: climb_kernel(start, top, *refs),
        out_shape=(
            jax.ShapeDtypeStruct((2, 2 * B, 2 * B), jnp.bfloat16),
            jax.ShapeDtypeStruct((2, R, B), jnp.float32),
        ),
        in_specs=[pl.BlockSpec(memory_space=pltpu.VMEM)] * (2 * len(steps)),
        out_specs=[pl.BlockSpec(memory_space=pltpu.VMEM)] * 2,
        compiler_params=pltpu.CompilerParams(vmem_limit_bytes=LIMIT),
        cost_estimate=pl.CostEstimate(flops=2**31, bytes_accessed=2**23, transcendentals=0),
        name="climb",
    )(*(array for step in steps for array in step))


def carry_kernel(level, own, got, weights, offsets, carries):
    carry = jnp.where(is_left(level), mm(own[B : B + R], got[:B]), 0.0) + got[B:]
    carry = left_side(carry)
    for i in range(2):
        carries[i * R : (i + 1) * R] = times(carry, weights[i]) + offsets[i]


def carry(level, own, got, weights, offsets):
    return pl.pallas_call(
        lambda *refs: carry_kernel(level, *refs),
        out_shape=jax.ShapeDtypeStruct((2 * R, B), jnp.float32),
        in_specs=[pl.BlockSpec(memory_space=pltpu.VMEM)] * 4,
        out_specs=pl.BlockSpec(memory_space=pltpu.VMEM),
        compiler_params=pltpu.CompilerParams(vmem_limit_bytes=LIMIT),
        name="carry",
    )(own, got, weights, offsets)


def finish_kernel(here, twin, weights, offsets, spread, rows, out_hbm, out, sems):
    carries = jnp.where(position() & 1 == 0, here[...], twin[...])
    both = jnp.concatenate([carries[:R], carries[R:]], axis=1)
    both = jnp.concatenate(halves(both), axis=0)
    f_in = left_side(carries[R:])
    count = rows.shape[1]
    copies = []

    def applied(lhs, weight):
        wide = jnp.dot(lhs, weight, preferred_element_type=jnp.float32)
        wide = wide[:R] + wide[R:]
        return wide[:, :B] + wide[:, B:]

    for part in range(PARTS):
        inner = jnp.concatenate(
            [
                applied(both, weights[part, 0]) + offsets[part, 0],
                times(f_in, weights[part, 1]) + offsets[part, 1],
            ],
            axis=1,
        )
        inner = jnp.concatenate(halves(inner), axis=0)
        for i in range(count):
            out[part * count + i] = rows[part, i, 2 * B :] + applied(inner, spread[part, i])
            done = part * count + i + 1
            if done % OUT_ROWS == 0:
                span = pl.ds(done - OUT_ROWS, OUT_ROWS)
                copies.append(
                    pltpu.make_async_copy(out.at[span], out_hbm.at[span], sems.at[len(copies)])
                )
                copies[-1].start()
    for copy in copies:
        copy.wait()


def finish(here, twin, weights, offsets, spread, rows):
    shape = (rows.shape[0] * rows.shape[1], R, B)
    return pl.pallas_call(
        finish_kernel,
        out_shape=jax.ShapeDtypeStruct(shape, jnp.float32),
        in_specs=[pl.BlockSpec(memory_space=pltpu.VMEM)] * 6,
        out_specs=pl.BlockSpec(memory_space=pltpu.HBM),
        scratch_shapes=[
            pltpu.VMEM(shape, jnp.float32),
            pltpu.SemaphoreType.DMA((shape[0] // OUT_ROWS,)),
        ],
        compiler_params=pltpu.CompilerParams(vmem_limit_bytes=LIMIT),
        name="finish",
    )(here, twin, weights, offsets, spread, rows)


def on_device(rhs, pivot_inv, lower_gain, upper_gain):
    devices = lax.axis_size(AXES)
    top = devices.bit_length() - 2
    plane = devices >> 3

    def swap(array, even, odd):
        pairs = [(i, i ^ (odd if i & 1 else even)) for i in range(devices)]
        return lax.ppermute(array, AXES, pairs)

    own, parts, rows = local(rhs, pivot_inv, lower_gain, upper_gain)
    other = swap(own, 1, 1)
    (pack,) = combine(pair_kernel, "pair", own, (other,), PACK)
    steps = []
    for level, aside in ROUNDS:
        last = level == top - 2
        gots = tuple(swap(pack, bits << level, aside[bits - 1]) for bits in (1, 2, 3))
        if level == 1:
            maps = prepare(parts, rows, own, other)
            gots, maps = lax.optimization_barrier((gots, maps))
        near, far, joint, *send = combine(
            lambda *refs, level=level: quad_kernel(level, *refs),
            f"quad{level}",
            pack,
            gots,
            *(PACK,) * 3,
            *((B + R,) if last else ()),
        )
        steps += [(pack, gots[0]), (near, far)]
        pack = joint
    facing = [
        (i, i ^ ASIDE_TOP if i & 1 else FACING[i // plane] * plane + i % plane)
        for i in range(devices)
    ]
    got = lax.ppermute(send[0], AXES, facing)
    climbed = climb(1, top, steps)
    got, climbed = lax.optimization_barrier((got, climbed))
    here = carry(top, pack, got, *climbed)
    return finish(here, swap(here, 1, 1), *maps, rows)


def solution(mesh):
    placed = P(AXES, None, None)
    return jax.shard_map(
        on_device,
        mesh=mesh,
        in_specs=(placed,) * 4,
        out_specs=placed,
        check_vma=False,
    )
```

time: 57.7 us -> 60.5 us (1.049)
  starting transfers between devices: 16.8 us -> 28.7 us
  waiting for transfers between devices: 30.1 us -> 21.5 us
    ppermute x15 -> x12, starting transfers between devices: 16.8 us -> 28.7 us  [the longest x11 28.6 us: swap(): return lax.ppermute(array, AXES, pairs)]
    ppermute x15 -> x12, waiting for transfers between devices: 30.1 us -> 21.5 us  [the longest x11 19.3 us: swap(): return lax.ppermute(array, AXES, pairs)]
    pallas_call x7 -> x8, Pallas kernels: 6.55 us -> 6.14 us  [the longest x4 2.56 us: combine(): pl.pallas_call(kernel, out_shape=tuple((jax.ShapeDtypeStruct((rows, B), j...]
  transfers between devices with their start and end apart: 15 -> 12, of which waited for: 12 -> 10; matrix products, arithmetic and copies ran while one was open for 0% -> 0% of each run, Pallas kernels for 4% -> 3%
where the time goes in v8:
time: 60.5 us; the launch traced here: 59.9 us
  starting transfers between devices  28.7 us (47%)
  waiting for transfers between devices  21.5 us (36%)
  Pallas kernels  9.6 us (16%)
    ppermute x11, starting transfers between devices, swap(): return lax.ppermute(array, AXES, pairs)  28.6 us
    ppermute x11, waiting for transfers between devices, swap(): return lax.ppermute(array, AXES, pairs)  19.3 us
    pallas_call x1, Pallas kernels, local(): pl.pallas_call(local_kernel, out_shape=(jax.ShapeDtypeStruct((PACK, B), j...  3.46 us
    pallas_call x4, Pallas kernels, combine(): pl.pallas_call(kernel, out_shape=tuple((jax.ShapeDtypeStruct((rows, B), j...  2.56 us
    ppermute x1, waiting for transfers between devices, on_device(): got = lax.ppermute(send[0], AXES, facing)  2.16 us
    pallas_call x1, Pallas kernels, finish(): pl.pallas_call(finish_kernel, out_shape=jax.ShapeDtypeStruct(shape, jnp.f...  1.37 us
    pallas_call x1, Pallas kernels, climb(): pl.pallas_call(lambda *refs: climb_kernel(start, top, *refs), out_shape=(...  1.28 us
  transfers between devices with their start and end apart: 12, of which 10 were waited for; matrix products, arithmetic and copies ran while one was open for 0% of the time, Pallas kernels for 3%

profile of v8, /device:TPU:1, one launch (start us, length us, event | category | flops | bytes accessed | tf_op | source)
XLA Modules:
  0.0 59.9 jit_solution(14449851926521937751)
XLA Ops:
  0.0 3.5 %local.1 = (f32[512,128]{1,0:T(8,128)S(1)}, f32[2,512,128]{2,1,0:T(8,128)S(1)}, f32[2,6,320,128]{3,2,1,0:T(8,128)S(1)}) custom-call(f32[2,6,64,128]{3,2,1,0:T(8,128)} %bitcast.7, f32[2,6,128,128]{3,2,1,0:T(8,128)} %bitcast.4, f32[2,6,128,128]{3,2,1,0:T(8,128)} %bitcast.5, f32[2,6,128,128]{3,2,1,0:T(8,128)} %bitcast.6), custom_call_target="tpu_custom_call" | custom-call | tf_op jit(solution)/shard_map/local/pallas_call | solution.py:120
  3.5 3.3 %collective-permute-start = (f32[512,128]{1,0:T(8,128)S(1)}, f32[512,128]{1,0:T(8,128)S(1)}, u32[]{:S(2)}, u32[]{:S(2)}) collective-permute-start(f32[512,128]{1,0:T(8,128)S(1)} %get-tuple-element.32.own), channel_id=1, source_target_pairs={{0,1},{1,0},{2,3},{3,2},{4,5},{5,4},{6,7},{7,6},{8,9},{9,8},{10,11... | collective-permute-start | bytes 786440 | tf_op jit(solution)/shard_map/ppermute | solution.py:349
  6.8 1.2 %collective-permute-done.other = f32[512,128]{1,0:T(8,128)S(1)} collective-permute-done((f32[512,128]{1,0:T(8,128)S(1)}, f32[512,128]{1,0:T(8,128)S(1)}, u32[]{:S(2)}, u32[]{:S(2)}) %collective-permute-start) | collective-permute-done | bytes 262176 | tf_op jit(solution)/shard_map/ppermute | solution.py:349
  8.0 0.3 pair.1.refs_0_
  8.3 0.1 collective-permute-start.3
  8.4 2.6 %collective-permute-start.2 = (f32[512,128]{1,0:T(8,128)S(1)}, f32[512,128]{1,0:T(8,128)S(1)}, u32[]{:S(2)}, u32[]{:S(2)}) collective-permute-start(f32[512,128]{1,0:T(8,128)S(1)} %pair.1.refs_0_), channel_id=1, source_target_pairs={{0,4},{1,25},{2,6},{3,27},{4,0},{5,29},{6,2},{7,31},{8,12},{9,17},... | collective-permute-start | bytes 786440 | tf_op jit(solution)/shard_map/ppermute | solution.py:349
  11.0 0.0 collective-permute-start.1
  11.0 0.6 %prepare.1 = (bf16[2,2,256,256]{3,2,1,0:T(8,128)(2,1)S(1)}, f32[2,2,64,128]{3,2,1,0:T(8,128)S(1)}, bf16[2,6,256,256]{3,2,1,0:T(8,128)(2,1)S(1)}) custom-call(f32[2,512,128]{2,1,0:T(8,128)S(1)} %get-tuple-element.33.parts, f32[2,6,320,128]{3,2,1,0:T(8,128)S(1)} %get-tuple-element.34.rows, f32[512,128]{1,0:T(8,128)S(1)} %get-tuple-element.32.own, ...), custom_call_target="tpu_custom_call" | custom-call | flops 2147483648 | bytes 8388608 | tf_op jit(solution)/shard_map/prepare/pallas_call | solution.py:230
  11.7 2.2 %collective-permute-done.3.refs_3_ = f32[512,128]{1,0:T(8,128)S(1)} collective-permute-done((f32[512,128]{1,0:T(8,128)S(1)}, f32[512,128]{1,0:T(8,128)S(1)}, u32[]{:S(2)}, u32[]{:S(2)}) %collective-permute-start.3) | collective-permute-done | bytes 262176 | tf_op jit(solution)/shard_map/ppermute | solution.py:349
  13.9 1.3 %collective-permute-done.2.refs_2_ = f32[512,128]{1,0:T(8,128)S(1)} collective-permute-done((f32[512,128]{1,0:T(8,128)S(1)}, f32[512,128]{1,0:T(8,128)S(1)}, u32[]{:S(2)}, u32[]{:S(2)}) %collective-permute-start.2) | collective-permute-done | bytes 262176 | tf_op jit(solution)/shard_map/ppermute | solution.py:349
  15.2 1.3 %collective-permute-done.1.refs_1_ = f32[512,128]{1,0:T(8,128)S(1)} collective-permute-done((f32[512,128]{1,0:T(8,128)S(1)}, f32[512,128]{1,0:T(8,128)S(1)}, u32[]{:S(2)}, u32[]{:S(2)}) %collective-permute-start.1) | collective-permute-done | bytes 262176 | tf_op jit(solution)/shard_map/ppermute | solution.py:349
  16.5 0.7 %quad1.1 = (f32[512,128]{1,0:T(8,128)S(1)}, f32[512,128]{1,0:T(8,128)S(1)}, f32[512,128]{1,0:T(8,128)S(1)}) custom-call(f32[512,128]{1,0:T(8,128)S(1)} %pair.1.refs_0_, f32[512,128]{1,0:T(8,128)S(1)} %collective-permute-done.1.refs_1_, f32[512,128]{1,0:T(8,128)S(1)} %collective-permute-done.2.refs_2_, f32[512,128]{1,0:T(8,128)S(1)} %collective-permute-done.3.refs_3_), custom_call_target="tpu_custom_call" | custom-call | tf_op jit(solution)/shard_map/quad1/pallas_call | solution.py:186
  17.3 0.2 collective-permute-start.6
  17.5 2.5 %collective-permute-start.5 = (f32[512,128]{1,0:T(8,128)S(1)}, f32[512,128]{1,0:T(8,128)S(1)}, u32[]{:S(2)}, u32[]{:S(2)}) collective-permute-start(f32[512,128]{1,0:T(8,128)S(1)} %get-tuple-element.41.refs_0_.refs_4_), channel_id=1, source_target_pairs={{0,16},{1,7},{2,18},{3,5},{4,20},{5,3},{6,22},{7,1},{8,24},{9,15},... | collective-permute-start | bytes 786440 | tf_op jit(solution)/shard_map/ppermute | solution.py:349
  20.0 2.6 %collective-permute-done.6.refs_3_ = f32[512,128]{1,0:T(8,128)S(1)} collective-permute-done((f32[512,128]{1,0:T(8,128)S(1)}, f32[512,128]{1,0:T(8,128)S(1)}, u32[]{:S(2)}, u32[]{:S(2)}) %collective-permute-start.6) | collective-permute-done | bytes 262176 | tf_op jit(solution)/shard_map/ppermute | solution.py:349
  22.6 1.3 %collective-permute-done.5.refs_2_ = f32[512,128]{1,0:T(8,128)S(1)} collective-permute-done((f32[512,128]{1,0:T(8,128)S(1)}, f32[512,128]{1,0:T(8,128)S(1)}, u32[]{:S(2)}, u32[]{:S(2)}) %collective-permute-start.5) | collective-permute-done | bytes 262176 | tf_op jit(solution)/shard_map/ppermute | solution.py:349
  23.9 1.6 %collective-permute-done.4.refs_1_.refs_5_ = f32[512,128]{1,0:T(8,128)S(1)} collective-permute-done((f32[512,128]{1,0:T(8,128)S(1)}, f32[512,128]{1,0:T(8,128)S(1)}, u32[]{:S(2)}, u32[]{:S(2)}) %collective-permute-start.4) | collective-permute-done | bytes 262176 | tf_op jit(solution)/shard_map/ppermute | solution.py:349
  25.5 0.7 %quad3.1 = (f32[512,128]{1,0:T(8,128)S(1)}, f32[512,128]{1,0:T(8,128)S(1)}, f32[512,128]{1,0:T(8,128)S(1)}) custom-call(f32[512,128]{1,0:T(8,128)S(1)} %get-tuple-element.41.refs_0_.refs_4_, f32[512,128]{1,0:T(8,128)S(1)} %collective-permute-done.4.refs_1_.refs_5_, f32[512,128]{1,0:T(8,128)S(1)} %collective-permute-done.5.refs_2_, ...), custom_call_target="tpu_custom_call" | custom-call | tf_op jit(solution)/shard_map/quad3/pallas_call | solution.py:186
  26.2 0.1 collective-permute-start.9
  26.3 1.3 %collective-permute-start.8 = (f32[512,128]{1,0:T(8,128)S(1)}, f32[512,128]{1,0:T(8,128)S(1)}, u32[]{:S(2)}, u32[]{:S(2)}) collective-permute-start(f32[512,128]{1,0:T(8,128)S(1)} %get-tuple-element.42.refs_0_.refs_8_), channel_id=1, source_target_pairs={{0,64},{1,7},{2,66},{3,5},{4,68},{5,3},{6,70},{7,1},{8,72},{9,15},... | collective-permute-start | bytes 786440 | tf_op jit(solution)/shard_map/ppermute | solution.py:349
  27.6 0.0 collective-permute-start.7
  27.6 6.9 %collective-permute-done.9.refs_3_ = f32[512,128]{1,0:T(8,128)S(1)} collective-permute-done((f32[512,128]{1,0:T(8,128)S(1)}, f32[512,128]{1,0:T(8,128)S(1)}, u32[]{:S(2)}, u32[]{:S(2)}) %collective-permute-start.9) | collective-permute-done | bytes 262176 | tf_op jit(solution)/shard_map/ppermute | solution.py:349
  34.5 0.0 collective-permute-done.8.refs_2_
  34.5 0.0 collective-permute-done.7.refs_1_.refs_9_
  34.5 0.7 %quad5.1 = (f32[512,128]{1,0:T(8,128)S(1)}, f32[512,128]{1,0:T(8,128)S(1)}, f32[512,128]{1,0:T(8,128)S(1)}, f32[192,128]{1,0:T(8,128)S(1)}) custom-call(f32[512,128]{1,0:T(8,128)S(1)} %get-tuple-element.42.refs_0_.refs_8_, f32[512,128]{1,0:T(8,128)S(1)} %collective-permute-done.7.refs_1_.refs_9_, f32[512,128]{1,0:T(8,128)S(1)} %collective-permute-done.8.refs_2_, ...), custom_call_target="tpu_custom_call" | custom-call | tf_op jit(solution)/shard_map/quad5/pallas_call | solution.py:186
  35.3 0.1 collective-permute-start.10
  35.4 1.3 %climb.1 = (bf16[2,256,256]{2,1,0:T(8,128)(2,1)S(1)}, f32[2,64,128]{2,1,0:T(8,128)S(1)}) custom-call(f32[512,128]{1,0:T(8,128)S(1)} %pair.1.refs_0_, f32[512,128]{1,0:T(8,128)S(1)} %collective-permute-done.1.refs_1_, f32[512,128]{1,0:T(8,128)S(1)} %get-tuple-element.45.refs_2_, f32[512,128]{1,0:T(8,128)S(1)} %get-tuple-element.46.refs_3_, ...), custom_call_target="tpu_custom_call" | custom-call | flops 2147483648 | bytes 8388608 | tf_op jit(solution)/shard_map/climb/pallas_call | solution.py:259
  36.7 2.2 %collective-permute-done.10.refs_1_ = f32[192,128]{1,0:T(8,128)S(1)} collective-permute-done((f32[192,128]{1,0:T(8,128)S(1)}, f32[192,128]{1,0:T(8,128)S(1)}, u32[]{:S(2)}, u32[]{:S(2)}) %collective-permute-start.10) | collective-permute-done | bytes 98336 | tf_op jit(solution)/shard_map/ppermute | solution.py:375
  38.8 0.3 carry.1.here
  39.1 18.5 %collective-permute-start.11 = (f32[128,128]{1,0:T(8,128)S(1)}, f32[128,128]{1,0:T(8,128)S(1)}, u32[]{:S(2)}, u32[]{:S(2)}) collective-permute-start(f32[128,128]{1,0:T(8,128)S(1)} %carry.1.here), channel_id=1, source_target_pairs={{0,1},{1,0},{2,3},{3,2},{4,5},{5,4},{6,7},{7,6},{8,9},{9,8},{10,11... | collective-permute-start | bytes 196616 | tf_op jit(solution)/shard_map/ppermute | solution.py:349
  57.6 0.9 %collective-permute-done.11.twin = f32[128,128]{1,0:T(8,128)S(1)} collective-permute-done((f32[128,128]{1,0:T(8,128)S(1)}, f32[128,128]{1,0:T(8,128)S(1)}, u32[]{:S(2)}, u32[]{:S(2)}) %collective-permute-start.11) | collective-permute-done | bytes 65568 | tf_op jit(solution)/shard_map/ppermute | solution.py:349
  58.5 1.4 %finish.1 = f32[12,64,128]{2,1,0:T(8,128)} custom-call(f32[128,128]{1,0:T(8,128)S(1)} %carry.1.here, f32[128,128]{1,0:T(8,128)S(1)} %collective-permute-done.11.twin, bf16[2,2,256,256]{3,2,1,0:T(8,128)(2,1)S(1)} %get-tuple-element.56.weights, f32[2,2,64,128]{3,2,1,0:T(8,128)S(1)} %get-tuple-element.57.offsets, ...), custom_call_target="tpu_custom_call" | custom-call | tf_op jit(solution)/shard_map/finish/pallas_call | solution.py:328
  (1 shorter events, 0.0 us)
Async XLA Ops:
  3.5 4.5 %collective-permute-start = (f32[512,128]{1,0:T(8,128)S(1)}, f32[512,128]{1,0:T(8,128)S(1)}, u32[]{:S(2)}, u32[]{:S(2)}) collective-permute-start(f32[512,128]{1,0:T(8,128)S(1)} %get-tuple-element.32.own), channel_id=1, source_target_pairs={{0,1},{1,0},{2,3},{3,2},{4,5},{5,4},{6,7},{7,6},{8,9},{9,8},{10,11... | collective-permute-start | bytes 786440 | tf_op jit(solution)/shard_map/ppermute | solution.py:349
  8.3 5.6 %collective-permute-start.3 = (f32[512,128]{1,0:T(8,128)S(1)}, f32[512,128]{1,0:T(8,128)S(1)}, u32[]{:S(2)}, u32[]{:S(2)}) collective-permute-start(f32[512,128]{1,0:T(8,128)S(1)} %pair.1.refs_0_), channel_id=1, source_target_pairs={{0,6},{1,33},{2,4},{3,35},{4,2},{5,37},{6,0},{7,39},{8,14},{9,41},... | collective-permute-start | bytes 786440 | tf_op jit(solution)/shard_map/ppermute | solution.py:349
  8.4 6.8 %collective-permute-start.2 = (f32[512,128]{1,0:T(8,128)S(1)}, f32[512,128]{1,0:T(8,128)S(1)}, u32[]{:S(2)}, u32[]{:S(2)}) collective-permute-start(f32[512,128]{1,0:T(8,128)S(1)} %pair.1.refs_0_), channel_id=1, source_target_pairs={{0,4},{1,25},{2,6},{3,27},{4,0},{5,29},{6,2},{7,31},{8,12},{9,17},... | collective-permute-start | bytes 786440 | tf_op jit(solution)/shard_map/ppermute | solution.py:349
  11.0 5.5 %collective-permute-start.1 = (f32[512,128]{1,0:T(8,128)S(1)}, f32[512,128]{1,0:T(8,128)S(1)}, u32[]{:S(2)}, u32[]{:S(2)}) collective-permute-start(f32[512,128]{1,0:T(8,128)S(1)} %pair.1.refs_0_), channel_id=1, source_target_pairs={{0,2},{1,9},{2,0},{3,11},{4,6},{5,13},{6,4},{7,15},{8,10},{9,1},{1... | collective-permute-start | bytes 786440 | tf_op jit(solution)/shard_map/ppermute | solution.py:349
  17.3 5.3 %collective-permute-start.6 = (f32[512,128]{1,0:T(8,128)S(1)}, f32[512,128]{1,0:T(8,128)S(1)}, u32[]{:S(2)}, u32[]{:S(2)}) collective-permute-start(f32[512,128]{1,0:T(8,128)S(1)} %get-tuple-element.41.refs_0_.refs_4_), channel_id=1, source_target_pairs={{0,24},{1,33},{2,26},{3,35},{4,28},{5,37},{6,30},{7,39},{8,16},{9,... | collective-permute-start | bytes 786440 | tf_op jit(solution)/shard_map/ppermute | solution.py:349
  17.5 6.4 %collective-permute-start.5 = (f32[512,128]{1,0:T(8,128)S(1)}, f32[512,128]{1,0:T(8,128)S(1)}, u32[]{:S(2)}, u32[]{:S(2)}) collective-permute-start(f32[512,128]{1,0:T(8,128)S(1)} %get-tuple-element.41.refs_0_.refs_4_), channel_id=1, source_target_pairs={{0,16},{1,7},{2,18},{3,5},{4,20},{5,3},{6,22},{7,1},{8,24},{9,15},... | collective-permute-start | bytes 786440 | tf_op jit(solution)/shard_map/ppermute | solution.py:349
  20.0 5.5 %collective-permute-start.4 = (f32[512,128]{1,0:T(8,128)S(1)}, f32[512,128]{1,0:T(8,128)S(1)}, u32[]{:S(2)}, u32[]{:S(2)}) collective-permute-start(f32[512,128]{1,0:T(8,128)S(1)} %get-tuple-element.41.refs_0_.refs_4_), channel_id=1, source_target_pairs={{0,8},{1,3},{2,10},{3,1},{4,12},{5,7},{6,14},{7,5},{8,0},{9,11},{1... | collective-permute-start | bytes 786440 | tf_op jit(solution)/shard_map/ppermute | solution.py:349
  26.2 8.3 %collective-permute-start.9 = (f32[512,128]{1,0:T(8,128)S(1)}, f32[512,128]{1,0:T(8,128)S(1)}, u32[]{:S(2)}, u32[]{:S(2)}) collective-permute-start(f32[512,128]{1,0:T(8,128)S(1)} %get-tuple-element.42.refs_0_.refs_8_), channel_id=1, source_target_pairs={{0,96},{1,9},{2,98},{3,11},{4,100},{5,13},{6,102},{7,15},{8,104},{... | collective-permute-start | bytes 786440 | tf_op jit(solution)/shard_map/ppermute | solution.py:349
  26.3 8.2 %collective-permute-start.8 = (f32[512,128]{1,0:T(8,128)S(1)}, f32[512,128]{1,0:T(8,128)S(1)}, u32[]{:S(2)}, u32[]{:S(2)}) collective-permute-start(f32[512,128]{1,0:T(8,128)S(1)} %get-tuple-element.42.refs_0_.refs_8_), channel_id=1, source_target_pairs={{0,64},{1,7},{2,66},{3,5},{4,68},{5,3},{6,70},{7,1},{8,72},{9,15},... | collective-permute-start | bytes 786440 | tf_op jit(solution)/shard_map/ppermute | solution.py:349
  27.6 6.9 %collective-permute-start.7 = (f32[512,128]{1,0:T(8,128)S(1)}, f32[512,128]{1,0:T(8,128)S(1)}, u32[]{:S(2)}, u32[]{:S(2)}) collective-permute-start(f32[512,128]{1,0:T(8,128)S(1)} %get-tuple-element.42.refs_0_.refs_8_), channel_id=1, source_target_pairs={{0,32},{1,3},{2,34},{3,1},{4,36},{5,7},{6,38},{7,5},{8,40},{9,11},... | collective-permute-start | bytes 786440 | tf_op jit(solution)/shard_map/ppermute | solution.py:349
  35.3 3.6 %collective-permute-start.10 = (f32[192,128]{1,0:T(8,128)S(1)}, f32[192,128]{1,0:T(8,128)S(1)}, u32[]{:S(2)}, u32[]{:S(2)}) collective-permute-start(f32[192,128]{1,0:T(8,128)S(1)} %get-tuple-element.44), channel_id=1, source_target_pairs={{0,192},{1,9},{2,194},{3,11},{4,196},{5,13},{6,198},{7,15},{8,200}... | collective-permute-start | bytes 294920 | tf_op jit(solution)/shard_map/ppermute | solution.py:375
  39.1 19.4 %collective-permute-start.11 = (f32[128,128]{1,0:T(8,128)S(1)}, f32[128,128]{1,0:T(8,128)S(1)}, u32[]{:S(2)}, u32[]{:S(2)}) collective-permute-start(f32[128,128]{1,0:T(8,128)S(1)} %carry.1.here), channel_id=1, source_target_pairs={{0,1},{1,0},{2,3},{3,2},{4,5},{5,4},{6,7},{7,6},{8,9},{9,8},{10,11... | collective-permute-start | bytes 196616 | tf_op jit(solution)/shard_map/ppermute | solution.py:349

commit v9 on v7

--- a/solution.py
+++ b/solution.py
@@ -11,7 +11,7 @@
 PACK = 3 * B + 2 * R
 PARTS = 2
 OUT_ROWS = 3
-FACING = (6, 7, 4, 5, 2, 3, 0, 1)
+FACING = (7, 6, 5, 4, 3, 2, 1, 0)
 PLANS = ((1, (1, 2)), (3, (1, 2)), (5, (1, 3)))
 LIMIT = 12 * 2**20
 

time: 57.7 us -> 58 us (level)
    ppermute x1, starting transfers between devices: 3.41 us -> 4.6 us  [on_device(): got = lax.ppermute(half, AXES, facing)]
    ppermute x14, starting transfers between devices: 13.4 us -> 12.7 us  [on_device(): lax.ppermute(array, AXES, [(i, i ^ (odd if i & 1 else even)) for i in ran...]
where the time goes in v9:
time: 58 us; the launch traced here: 57.8 us
  waiting for transfers between devices  30.3 us (52%)
  starting transfers between devices  17.3 us (30%)
  Pallas kernels  10 us (17%)
    ppermute x14, waiting for transfers between devices, on_device(): lax.ppermute(array, AXES, [(i, i ^ (odd if i & 1 else even)) for i in ran...  29.1 us
    ppermute x14, starting transfers between devices, on_device(): lax.ppermute(array, AXES, [(i, i ^ (odd if i & 1 else even)) for i in ran...  12.7 us
    ppermute x1, starting transfers between devices, on_device(): got = lax.ppermute(half, AXES, facing)  4.6 us
    pallas_call x1, Pallas kernels, local(): pl.pallas_call(local_kernel, out_shape=(jax.ShapeDtypeStruct((PACK, B), j...  3.47 us
    pallas_call x4, Pallas kernels, combine(): pl.pallas_call(kernel, out_shape=(whole,) * (1 + extra) + (jax.ShapeDtype...  2.61 us
    pallas_call x1, Pallas kernels, prepare(): pl.pallas_call(lambda *refs: prepare_kernel(len(steps), *refs), out_shape...  1.72 us
    pallas_call x1, Pallas kernels, finish(): pl.pallas_call(lambda *refs: finish_kernel(level, *refs), out_shape=jax.S...  1.49 us
    ppermute x1, waiting for transfers between devices, on_device(): got = lax.ppermute(half, AXES, facing)  1.23 us
  transfers between devices with their start and end apart: 15, of which 12 were waited for; matrix products, arithmetic and copies ran while one was open for 0% of the time, Pallas kernels for 4%

profile of v9, /device:TPU:1, one launch (start us, length us, event | category | flops | bytes accessed | tf_op | source)
XLA Modules:
  0.0 57.8 jit_solution(3727584447917178787)
XLA Ops:
  0.0 3.5 %local.1 = (f32[512,128]{1,0:T(8,128)S(1)}, f32[2,512,128]{2,1,0:T(8,128)S(1)}, f32[2,6,320,128]{3,2,1,0:T(8,128)S(1)}) custom-call(f32[2,6,64,128]{3,2,1,0:T(8,128)} %bitcast.7, f32[2,6,128,128]{3,2,1,0:T(8,128)} %bitcast.4, f32[2,6,128,128]{3,2,1,0:T(8,128)} %bitcast.5, f32[2,6,128,128]{3,2,1,0:T(8,128)} %bitcast.6), custom_call_target="tpu_custom_call" | custom-call | tf_op jit(solution)/shard_map/local/pallas_call | solution.py:119
  3.5 3.3 %collective-permute-start = (f32[512,128]{1,0:T(8,128)S(1)}, f32[512,128]{1,0:T(8,128)S(1)}, u32[]{:S(2)}, u32[]{:S(2)}) collective-permute-start(f32[512,128]{1,0:T(8,128)S(1)} %get-tuple-element.35.own.refs_2_), channel_id=1, source_target_pairs={{0,1},{1,0},{2,3},{3,2},{4,5},{5,4},{6,7},{7,6},{8,9},{9,8},{10,11... | collective-permute-start | bytes 786440 | tf_op jit(solution)/shard_map/ppermute | solution.py:341
  6.8 1.2 %collective-permute-done.other.refs_3_ = f32[512,128]{1,0:T(8,128)S(1)} collective-permute-done((f32[512,128]{1,0:T(8,128)S(1)}, f32[512,128]{1,0:T(8,128)S(1)}, u32[]{:S(2)}, u32[]{:S(2)}) %collective-permute-start) | collective-permute-done | bytes 262176 | tf_op jit(solution)/shard_map/ppermute | solution.py:341
  8.0 0.3 pair.1
  8.3 1.1 %collective-permute-start.1 = (f32[512,128]{1,0:T(8,128)S(1)}, f32[512,128]{1,0:T(8,128)S(1)}, u32[]{:S(2)}, u32[]{:S(2)}) collective-permute-start(f32[512,128]{1,0:T(8,128)S(1)} %get-tuple-element.36.refs_0_.refs_4_), channel_id=1, source_target_pairs={{0,2},{1,5},{2,0},{3,7},{4,6},{5,1},{6,4},{7,3},{8,10},{9,13},{10,... | collective-permute-start | bytes 786440 | tf_op jit(solution)/shard_map/ppermute | solution.py:341
  9.4 0.9 %collective-permute-start.3 = (f32[256,128]{1,0:T(8,128)S(1)}, f32[256,128]{1,0:T(8,128)S(1)}, u32[]{:S(2)}, u32[]{:S(2)}) collective-permute-start(f32[256,128]{1,0:T(8,128)S(1)} %get-tuple-element.37), channel_id=1, source_target_pairs={{0,6},{1,7},{2,4},{3,5},{4,2},{5,3},{6,0},{7,1},{8,14},{9,15},{10,... | collective-permute-start | bytes 393224 | tf_op jit(solution)/shard_map/ppermute | solution.py:341
  10.3 7.6 %collective-permute-done.1.refs_1_ = f32[512,128]{1,0:T(8,128)S(1)} collective-permute-done((f32[512,128]{1,0:T(8,128)S(1)}, f32[512,128]{1,0:T(8,128)S(1)}, u32[]{:S(2)}, u32[]{:S(2)}) %collective-permute-start.1) | collective-permute-done | bytes 262176 | tf_op jit(solution)/shard_map/ppermute | solution.py:341
  17.8 0.7 %collective-permute-done.3.refs_3_ = f32[256,128]{1,0:T(8,128)S(1)} collective-permute-done((f32[256,128]{1,0:T(8,128)S(1)}, f32[256,128]{1,0:T(8,128)S(1)}, u32[]{:S(2)}, u32[]{:S(2)}) %collective-permute-start.3) | collective-permute-done | bytes 131104 | tf_op jit(solution)/shard_map/ppermute | solution.py:341
  18.5 0.4 collective-permute-start.4
  18.9 1.0 %collective-permute-done.4.refs_4_ = f32[256,128]{1,0:T(8,128)S(1)} collective-permute-done((f32[256,128]{1,0:T(8,128)S(1)}, f32[256,128]{1,0:T(8,128)S(1)}, u32[]{:S(2)}, u32[]{:S(2)}) %collective-permute-start.4) | collective-permute-done | bytes 131104 | tf_op jit(solution)/shard_map/ppermute | solution.py:341
  19.9 0.8 %quad1.1 = (f32[512,128]{1,0:T(8,128)S(1)}, f32[512,128]{1,0:T(8,128)S(1)}, f32[512,128]{1,0:T(8,128)S(1)}, f32[512,128]{1,0:T(8,128)S(1)}, f32[256,128]{1,0:T(8,128)S(1)}) custom-call(f32[512,128]{1,0:T(8,128)S(1)} %get-tuple-element.36.refs_0_.refs_4_, f32[512,128]{1,0:T(8,128)S(1)} %collective-permute-done.1.refs_1_, ...), custom_call_target="tpu_custom_call" | custom-call | tf_op jit(solution)/shard_map/quad1/pallas_call | solution.py:204
  20.7 1.0 %collective-permute-start.5 = (f32[512,128]{1,0:T(8,128)S(1)}, f32[512,128]{1,0:T(8,128)S(1)}, u32[]{:S(2)}, u32[]{:S(2)}) collective-permute-start(f32[512,128]{1,0:T(8,128)S(1)} %get-tuple-element.38.refs_0_.refs_8_), channel_id=1, source_target_pairs={{0,8},{1,17},{2,10},{3,19},{4,12},{5,21},{6,14},{7,23},{8,0},{9,25... | collective-permute-start | bytes 786440 | tf_op jit(solution)/shard_map/ppermute | solution.py:341
  21.6 0.8 %collective-permute-start.7 = (f32[256,128]{1,0:T(8,128)S(1)}, f32[256,128]{1,0:T(8,128)S(1)}, u32[]{:S(2)}, u32[]{:S(2)}) collective-permute-start(f32[256,128]{1,0:T(8,128)S(1)} %get-tuple-element.39), channel_id=1, source_target_pairs={{0,24},{1,25},{2,26},{3,27},{4,28},{5,29},{6,30},{7,31},{8,16},{9,... | collective-permute-start | bytes 393224 | tf_op jit(solution)/shard_map/ppermute | solution.py:341
  22.4 7.7 %collective-permute-done.5.refs_1_ = f32[512,128]{1,0:T(8,128)S(1)} collective-permute-done((f32[512,128]{1,0:T(8,128)S(1)}, f32[512,128]{1,0:T(8,128)S(1)}, u32[]{:S(2)}, u32[]{:S(2)}) %collective-permute-start.5) | collective-permute-done | bytes 262176 | tf_op jit(solution)/shard_map/ppermute | solution.py:341
  30.1 0.7 %collective-permute-done.7.refs_3_ = f32[256,128]{1,0:T(8,128)S(1)} collective-permute-done((f32[256,128]{1,0:T(8,128)S(1)}, f32[256,128]{1,0:T(8,128)S(1)}, u32[]{:S(2)}, u32[]{:S(2)}) %collective-permute-start.7) | collective-permute-done | bytes 131104 | tf_op jit(solution)/shard_map/ppermute | solution.py:341
  30.9 0.4 collective-permute-start.8
  31.3 1.0 %collective-permute-done.8.refs_4_ = f32[256,128]{1,0:T(8,128)S(1)} collective-permute-done((f32[256,128]{1,0:T(8,128)S(1)}, f32[256,128]{1,0:T(8,128)S(1)}, u32[]{:S(2)}, u32[]{:S(2)}) %collective-permute-start.8) | collective-permute-done | bytes 131104 | tf_op jit(solution)/shard_map/ppermute | solution.py:341
  32.3 0.8 %quad3.1 = (f32[512,128]{1,0:T(8,128)S(1)}, f32[512,128]{1,0:T(8,128)S(1)}, f32[512,128]{1,0:T(8,128)S(1)}, f32[512,128]{1,0:T(8,128)S(1)}, f32[256,128]{1,0:T(8,128)S(1)}) custom-call(f32[512,128]{1,0:T(8,128)S(1)} %get-tuple-element.38.refs_0_.refs_8_, f32[512,128]{1,0:T(8,128)S(1)} %collective-permute-done.5.refs_1_, ...), custom_call_target="tpu_custom_call" | custom-call | tf_op jit(solution)/shard_map/quad3/pallas_call | solution.py:204
  33.0 2.0 %collective-permute-start.9 = (f32[512,128]{1,0:T(8,128)S(1)}, f32[512,128]{1,0:T(8,128)S(1)}, u32[]{:S(2)}, u32[]{:S(2)}) collective-permute-start(f32[512,128]{1,0:T(8,128)S(1)} %get-tuple-element.40.refs_0_.refs_1_), channel_id=1, source_target_pairs={{0,32},{1,97},{2,34},{3,99},{4,36},{5,101},{6,38},{7,103},{8,40},{... | collective-permute-start | bytes 786440 | tf_op jit(solution)/shard_map/ppermute | solution.py:341
  35.0 1.7 %prepare.1 = (f32[2,512,128]{2,1,0:T(8,128)S(1)}, bf16[2,6,256,256]{3,2,1,0:T(8,128)(2,1)S(1)}) custom-call(f32[2,512,128]{2,1,0:T(8,128)S(1)} %get-tuple-element.41.refs_0_, f32[2,6,320,128]{3,2,1,0:T(8,128)S(1)} %get-tuple-element.42.refs_1_.refs_6_, f32[512,128]{1,0:T(8,128)S(1)} %get-tuple-element.35.own.refs_2_, ...), custom_call_target="tpu_custom_call" | custom-call | flops 2147483648 | bytes 8388608 | tf_op jit(solution)/shard_map/prepare/pallas_call | solution.py:250
  36.7 6.2 %collective-permute-done.9.refs_1_ = f32[512,128]{1,0:T(8,128)S(1)} collective-permute-done((f32[512,128]{1,0:T(8,128)S(1)}, f32[512,128]{1,0:T(8,128)S(1)}, u32[]{:S(2)}, u32[]{:S(2)}) %collective-permute-start.9) | collective-permute-done | bytes 262176 | tf_op jit(solution)/shard_map/ppermute | solution.py:341
  42.9 1.8 %collective-permute-start.10 = (f32[512,128]{1,0:T(8,128)S(1)}, f32[512,128]{1,0:T(8,128)S(1)}, u32[]{:S(2)}, u32[]{:S(2)}) collective-permute-start(f32[512,128]{1,0:T(8,128)S(1)} %collective-permute-done.9.refs_1_), channel_id=1, source_target_pairs={{0,1},{1,0},{2,3},{3,2},{4,5},{5,4},{6,7},{7,6},{8,9},{9,8},{10,11... | collective-permute-start | bytes 786440 | tf_op jit(solution)/shard_map/ppermute | solution.py:341
  44.7 1.2 %collective-permute-done.11.refs_3_ = f32[256,128]{1,0:T(8,128)S(1)} collective-permute-done((f32[256,128]{1,0:T(8,128)S(1)}, f32[256,128]{1,0:T(8,128)S(1)}, u32[]{:S(2)}, u32[]{:S(2)}) %collective-permute-start.11) | collective-permute-done | bytes 131104 | tf_op jit(solution)/shard_map/ppermute | solution.py:341
  45.8 0.3 collective-permute-start.12
  46.1 1.0 %collective-permute-done.12.refs_4_ = f32[256,128]{1,0:T(8,128)S(1)} collective-permute-done((f32[256,128]{1,0:T(8,128)S(1)}, f32[256,128]{1,0:T(8,128)S(1)}, u32[]{:S(2)}, u32[]{:S(2)}) %collective-permute-start.12) | collective-permute-done | bytes 131104 | tf_op jit(solution)/shard_map/ppermute | solution.py:341
  47.2 0.8 %quad5.1 = (f32[512,128]{1,0:T(8,128)S(1)}, f32[512,128]{1,0:T(8,128)S(1)}, f32[512,128]{1,0:T(8,128)S(1)}, f32[512,128]{1,0:T(8,128)S(1)}, f32[96,128]{1,0:T(8,128)S(1)}) custom-call(f32[512,128]{1,0:T(8,128)S(1)} %get-tuple-element.40.refs_0_.refs_1_, f32[512,128]{1,0:T(8,128)S(1)} %collective-permute-done.9.refs_1_, ...), custom_call_target="tpu_custom_call" | custom-call | tf_op jit(solution)/shard_map/quad5/pallas_call | solution.py:204
  48.0 4.6 %collective-permute-start.13 = (f32[96,128]{1,0:T(8,128)S(1)}, f32[96,128]{1,0:T(8,128)S(1)}, u32[]{:S(2)}, u32[]{:S(2)}) collective-permute-start(f32[96,128]{1,0:T(8,128)S(1)} %get-tuple-element.54), channel_id=1, source_target_pairs={{0,224},{1,225},{2,226},{3,227},{4,228},{5,229},{6,230},{7,231},{8... | collective-permute-start | bytes 147464 | tf_op jit(solution)/shard_map/ppermute | solution.py:368
  52.6 0.7 %refine.1 = (bf16[2,2,256,256]{3,2,1,0:T(8,128)(2,1)S(1)}, f32[2,2,64,128]{3,2,1,0:T(8,128)S(1)}) custom-call(f32[2,512,128]{2,1,0:T(8,128)S(1)} %get-tuple-element.55.refs_0_, f32[512,128]{1,0:T(8,128)S(1)} %get-tuple-element.40.refs_0_.refs_1_, f32[512,128]{1,0:T(8,128)S(1)} %get-tuple-element.56.refs_2_, f32[512,128]{1,0:T(8,128)S(1)} %get-tuple-element.57.refs_3_, ...), custom_call_target="tpu_custom_call" | custom-call | flops 1073741824 | bytes 4194304 | tf_op jit(solution)/shard_map/refine/pallas_call | solution.py:281
  53.3 1.2 %collective-permute-done.13.refs_1_ = f32[96,128]{1,0:T(8,128)S(1)} collective-permute-done((f32[96,128]{1,0:T(8,128)S(1)}, f32[96,128]{1,0:T(8,128)S(1)}, u32[]{:S(2)}, u32[]{:S(2)}) %collective-permute-start.13) | collective-permute-done | bytes 49184 | tf_op jit(solution)/shard_map/ppermute | solution.py:368
  54.5 0.8 %collective-permute-start.14 = (f32[96,128]{1,0:T(8,128)S(1)}, f32[96,128]{1,0:T(8,128)S(1)}, u32[]{:S(2)}, u32[]{:S(2)}) collective-permute-start(f32[96,128]{1,0:T(8,128)S(1)} %collective-permute-done.13.refs_1_), channel_id=1, source_target_pairs={{0,1},{1,0},{2,3},{3,2},{4,5},{5,4},{6,7},{7,6},{8,9},{9,8},{10,11... | collective-permute-start | bytes 147464 | tf_op jit(solution)/shard_map/ppermute | solution.py:341
  55.3 0.9 %collective-permute-done.14.refs_2_ = f32[96,128]{1,0:T(8,128)S(1)} collective-permute-done((f32[96,128]{1,0:T(8,128)S(1)}, f32[96,128]{1,0:T(8,128)S(1)}, u32[]{:S(2)}, u32[]{:S(2)}) %collective-permute-start.14) | collective-permute-done | bytes 49184 | tf_op jit(solution)/shard_map/ppermute | solution.py:341
  56.2 1.5 %finish.1 = f32[12,64,128]{2,1,0:T(8,128)} custom-call(f32[512,128]{1,0:T(8,128)S(1)} %get-tuple-element.53.refs_0_, f32[96,128]{1,0:T(8,128)S(1)} %collective-permute-done.13.refs_1_, f32[96,128]{1,0:T(8,128)S(1)} %collective-permute-done.14.refs_2_, bf16[2,2,256,256]{3,2,1,0:T(8,128)(2,1)S(1)} %get-tuple-element.62.refs_3_, ...), custom_call_target="tpu_custom_call" | custom-call | tf_op jit(solution)/shard_map/finish/pallas_call | solution.py:323
  (6 shorter events, 0.0 us)
Async XLA Ops:
  3.5 4.5 %collective-permute-start = (f32[512,128]{1,0:T(8,128)S(1)}, f32[512,128]{1,0:T(8,128)S(1)}, u32[]{:S(2)}, u32[]{:S(2)}) collective-permute-start(f32[512,128]{1,0:T(8,128)S(1)} %get-tuple-element.35.own.refs_2_), channel_id=1, source_target_pairs={{0,1},{1,0},{2,3},{3,2},{4,5},{5,4},{6,7},{7,6},{8,9},{9,8},{10,11... | collective-permute-start | bytes 786440 | tf_op jit(solution)/shard_map/ppermute | solution.py:341
  8.3 9.5 %collective-permute-start.1 = (f32[512,128]{1,0:T(8,128)S(1)}, f32[512,128]{1,0:T(8,128)S(1)}, u32[]{:S(2)}, u32[]{:S(2)}) collective-permute-start(f32[512,128]{1,0:T(8,128)S(1)} %get-tuple-element.36.refs_0_.refs_4_), channel_id=1, source_target_pairs={{0,2},{1,5},{2,0},{3,7},{4,6},{5,1},{6,4},{7,3},{8,10},{9,13},{10,... | collective-permute-start | bytes 786440 | tf_op jit(solution)/shard_map/ppermute | solution.py:341
  9.4 9.1 %collective-permute-start.3 = (f32[256,128]{1,0:T(8,128)S(1)}, f32[256,128]{1,0:T(8,128)S(1)}, u32[]{:S(2)}, u32[]{:S(2)}) collective-permute-start(f32[256,128]{1,0:T(8,128)S(1)} %get-tuple-element.37), channel_id=1, source_target_pairs={{0,6},{1,7},{2,4},{3,5},{4,2},{5,3},{6,0},{7,1},{8,14},{9,15},{10,... | collective-permute-start | bytes 393224 | tf_op jit(solution)/shard_map/ppermute | solution.py:341
  17.8 2.1 %collective-permute-start.2 = (f32[512,128]{1,0:T(8,128)S(1)}, f32[512,128]{1,0:T(8,128)S(1)}, u32[]{:S(2)}, u32[]{:S(2)}) collective-permute-start(f32[512,128]{1,0:T(8,128)S(1)} %collective-permute-done.1.refs_1_), channel_id=1, source_target_pairs={{0,1},{1,0},{2,3},{3,2},{4,5},{5,4},{6,7},{7,6},{8,9},{9,8},{10,11... | collective-permute-start | bytes 786440 | tf_op jit(solution)/shard_map/ppermute | solution.py:341
  18.5 1.4 %collective-permute-start.4 = (f32[256,128]{1,0:T(8,128)S(1)}, f32[256,128]{1,0:T(8,128)S(1)}, u32[]{:S(2)}, u32[]{:S(2)}) collective-permute-start(f32[256,128]{1,0:T(8,128)S(1)} %collective-permute-done.3.refs_3_), channel_id=1, source_target_pairs={{0,1},{1,0},{2,3},{3,2},{4,5},{5,4},{6,7},{7,6},{8,9},{9,8},{10,11... | collective-permute-start | bytes 393224 | tf_op jit(solution)/shard_map/ppermute | solution.py:341
  20.7 9.5 %collective-permute-start.5 = (f32[512,128]{1,0:T(8,128)S(1)}, f32[512,128]{1,0:T(8,128)S(1)}, u32[]{:S(2)}, u32[]{:S(2)}) collective-permute-start(f32[512,128]{1,0:T(8,128)S(1)} %get-tuple-element.38.refs_0_.refs_8_), channel_id=1, source_target_pairs={{0,8},{1,17},{2,10},{3,19},{4,12},{5,21},{6,14},{7,23},{8,0},{9,25... | collective-permute-start | bytes 786440 | tf_op jit(solution)/shard_map/ppermute | solution.py:341
  21.6 9.2 %collective-permute-start.7 = (f32[256,128]{1,0:T(8,128)S(1)}, f32[256,128]{1,0:T(8,128)S(1)}, u32[]{:S(2)}, u32[]{:S(2)}) collective-permute-start(f32[256,128]{1,0:T(8,128)S(1)} %get-tuple-element.39), channel_id=1, source_target_pairs={{0,24},{1,25},{2,26},{3,27},{4,28},{5,29},{6,30},{7,31},{8,16},{9,... | collective-permute-start | bytes 393224 | tf_op jit(solution)/shard_map/ppermute | solution.py:341
  30.1 2.1 %collective-permute-start.6 = (f32[512,128]{1,0:T(8,128)S(1)}, f32[512,128]{1,0:T(8,128)S(1)}, u32[]{:S(2)}, u32[]{:S(2)}) collective-permute-start(f32[512,128]{1,0:T(8,128)S(1)} %collective-permute-done.5.refs_1_), channel_id=1, source_target_pairs={{0,1},{1,0},{2,3},{3,2},{4,5},{5,4},{6,7},{7,6},{8,9},{9,8},{10,11... | collective-permute-start | bytes 786440 | tf_op jit(solution)/shard_map/ppermute | solution.py:341
  30.9 1.4 %collective-permute-start.8 = (f32[256,128]{1,0:T(8,128)S(1)}, f32[256,128]{1,0:T(8,128)S(1)}, u32[]{:S(2)}, u32[]{:S(2)}) collective-permute-start(f32[256,128]{1,0:T(8,128)S(1)} %collective-permute-done.7.refs_3_), channel_id=1, source_target_pairs={{0,1},{1,0},{2,3},{3,2},{4,5},{5,4},{6,7},{7,6},{8,9},{9,8},{10,11... | collective-permute-start | bytes 393224 | tf_op jit(solution)/shard_map/ppermute | solution.py:341
  33.0 9.9 %collective-permute-start.9 = (f32[512,128]{1,0:T(8,128)S(1)}, f32[512,128]{1,0:T(8,128)S(1)}, u32[]{:S(2)}, u32[]{:S(2)}) collective-permute-start(f32[512,128]{1,0:T(8,128)S(1)} %get-tuple-element.40.refs_0_.refs_1_), channel_id=1, source_target_pairs={{0,32},{1,97},{2,34},{3,99},{4,36},{5,101},{6,38},{7,103},{8,40},{... | collective-permute-start | bytes 786440 | tf_op jit(solution)/shard_map/ppermute | solution.py:341
  35.0 10.8 %collective-permute-start.11 = (f32[256,128]{1,0:T(8,128)S(1)}, f32[256,128]{1,0:T(8,128)S(1)}, u32[]{:S(2)}, u32[]{:S(2)}) collective-permute-start(f32[256,128]{1,0:T(8,128)S(1)} %get-tuple-element.52), channel_id=1, source_target_pairs={{0,64},{1,65},{2,66},{3,67},{4,68},{5,69},{6,70},{7,71},{8,72},{9,... | collective-permute-start | bytes 393224 | tf_op jit(solution)/shard_map/ppermute | solution.py:341
  42.9 4.3 %collective-permute-start.10 = (f32[512,128]{1,0:T(8,128)S(1)}, f32[512,128]{1,0:T(8,128)S(1)}, u32[]{:S(2)}, u32[]{:S(2)}) collective-permute-start(f32[512,128]{1,0:T(8,128)S(1)} %collective-permute-done.9.refs_1_), channel_id=1, source_target_pairs={{0,1},{1,0},{2,3},{3,2},{4,5},{5,4},{6,7},{7,6},{8,9},{9,8},{10,11... | collective-permute-start | bytes 786440 | tf_op jit(solution)/shard_map/ppermute | solution.py:341
  45.8 1.3 %collective-permute-start.12 = (f32[256,128]{1,0:T(8,128)S(1)}, f32[256,128]{1,0:T(8,128)S(1)}, u32[]{:S(2)}, u32[]{:S(2)}) collective-permute-start(f32[256,128]{1,0:T(8,128)S(1)} %collective-permute-done.11.refs_3_), channel_id=1, source_target_pairs={{0,1},{1,0},{2,3},{3,2},{4,5},{5,4},{6,7},{7,6},{8,9},{9,8},{10,11... | collective-permute-start | bytes 393224 | tf_op jit(solution)/shard_map/ppermute | solution.py:341
  48.0 6.6 %collective-permute-start.13 = (f32[96,128]{1,0:T(8,128)S(1)}, f32[96,128]{1,0:T(8,128)S(1)}, u32[]{:S(2)}, u32[]{:S(2)}) collective-permute-start(f32[96,128]{1,0:T(8,128)S(1)} %get-tuple-element.54), channel_id=1, source_target_pairs={{0,224},{1,225},{2,226},{3,227},{4,228},{5,229},{6,230},{7,231},{8... | collective-permute-start | bytes 147464 | tf_op jit(solution)/shard_map/ppermute | solution.py:368
  54.5 1.7 %collective-permute-start.14 = (f32[96,128]{1,0:T(8,128)S(1)}, f32[96,128]{1,0:T(8,128)S(1)}, u32[]{:S(2)}, u32[]{:S(2)}) collective-permute-start(f32[96,128]{1,0:T(8,128)S(1)} %collective-permute-done.13.refs_1_), channel_id=1, source_target_pairs={{0,1},{1,0},{2,3},{3,2},{4,5},{5,4},{6,7},{7,6},{8,9},{9,8},{10,11... | collective-permute-start | bytes 147464 | tf_op jit(solution)/shard_map/ppermute | solution.py:341

commit v10 on v9

--- a/solution.py
+++ b/solution.py
@@ -11,7 +11,7 @@
 PACK = 3 * B + 2 * R
 PARTS = 2
 OUT_ROWS = 3
-FACING = (7, 6, 5, 4, 3, 2, 1, 0)
+FACING = (6, 5, 4, 7, 2, 1, 0, 3)
 PLANS = ((1, (1, 2)), (3, (1, 2)), (5, (1, 3)))
 LIMIT = 12 * 2**20
 

time: 58 us -> 57.8 us (level)
    ppermute x1, starting transfers between devices: 4.6 us -> 3.41 us  [on_device(): got = lax.ppermute(half, AXES, facing)]
    ppermute x14, starting transfers between devices: 12.7 us -> 13.3 us  [on_device(): lax.ppermute(array, AXES, [(i, i ^ (odd if i & 1 else even)) for i in ran...]
where the time goes in v10:
time: 57.8 us; the launch traced here: 57.1 us
  waiting for transfers between devices  30.1 us (52%)
  starting transfers between devices  16.8 us (29%)
  Pallas kernels  10 us (17%)
    ppermute x14, waiting for transfers between devices, on_device(): lax.ppermute(array, AXES, [(i, i ^ (odd if i & 1 else even)) for i in ran...  29.1 us
    ppermute x14, starting transfers between devices, on_device(): lax.ppermute(array, AXES, [(i, i ^ (odd if i & 1 else even)) for i in ran...  13.3 us
    pallas_call x1, Pallas kernels, local(): pl.pallas_call(local_kernel, out_shape=(jax.ShapeDtypeStruct((PACK, B), j...  3.47 us
    ppermute x1, starting transfers between devices, on_device(): got = lax.ppermute(half, AXES, facing)  3.41 us
    pallas_call x4, Pallas kernels, combine(): pl.pallas_call(kernel, out_shape=(whole,) * (1 + extra) + (jax.ShapeDtype...  2.61 us
    pallas_call x1, Pallas kernels, prepare(): pl.pallas_call(lambda *refs: prepare_kernel(len(steps), *refs), out_shape...  1.72 us
    pallas_call x1, Pallas kernels, finish(): pl.pallas_call(lambda *refs: finish_kernel(level, *refs), out_shape=jax.S...  1.49 us
  transfers between devices with their start and end apart: 15, of which 12 were waited for; matrix products, arithmetic and copies ran while one was open for 0% of the time, Pallas kernels for 4%

profile of v10, /device:TPU:1, one launch (start us, length us, event | category | flops | bytes accessed | tf_op | source)
XLA Modules:
  0.0 57.1 jit_solution(3248950021354282592)
XLA Ops:
  0.0 3.5 %local.1 = (f32[512,128]{1,0:T(8,128)S(1)}, f32[2,512,128]{2,1,0:T(8,128)S(1)}, f32[2,6,320,128]{3,2,1,0:T(8,128)S(1)}) custom-call(f32[2,6,64,128]{3,2,1,0:T(8,128)} %bitcast.7, f32[2,6,128,128]{3,2,1,0:T(8,128)} %bitcast.4, f32[2,6,128,128]{3,2,1,0:T(8,128)} %bitcast.5, f32[2,6,128,128]{3,2,1,0:T(8,128)} %bitcast.6), custom_call_target="tpu_custom_call" | custom-call | tf_op jit(solution)/shard_map/local/pallas_call | solution.py:119
  3.5 3.3 %collective-permute-start = (f32[512,128]{1,0:T(8,128)S(1)}, f32[512,128]{1,0:T(8,128)S(1)}, u32[]{:S(2)}, u32[]{:S(2)}) collective-permute-start(f32[512,128]{1,0:T(8,128)S(1)} %get-tuple-element.35.own.refs_2_), channel_id=1, source_target_pairs={{0,1},{1,0},{2,3},{3,2},{4,5},{5,4},{6,7},{7,6},{8,9},{9,8},{10,11... | collective-permute-start | bytes 786440 | tf_op jit(solution)/shard_map/ppermute | solution.py:341
  6.8 1.2 %collective-permute-done.other.refs_3_ = f32[512,128]{1,0:T(8,128)S(1)} collective-permute-done((f32[512,128]{1,0:T(8,128)S(1)}, f32[512,128]{1,0:T(8,128)S(1)}, u32[]{:S(2)}, u32[]{:S(2)}) %collective-permute-start) | collective-permute-done | bytes 262176 | tf_op jit(solution)/shard_map/ppermute | solution.py:341
  8.0 0.3 pair.1
  8.3 1.1 %collective-permute-start.1 = (f32[512,128]{1,0:T(8,128)S(1)}, f32[512,128]{1,0:T(8,128)S(1)}, u32[]{:S(2)}, u32[]{:S(2)}) collective-permute-start(f32[512,128]{1,0:T(8,128)S(1)} %get-tuple-element.36.refs_0_.refs_4_), channel_id=1, source_target_pairs={{0,2},{1,5},{2,0},{3,7},{4,6},{5,1},{6,4},{7,3},{8,10},{9,13},{10,... | collective-permute-start | bytes 786440 | tf_op jit(solution)/shard_map/ppermute | solution.py:341
  9.4 0.9 %collective-permute-start.3 = (f32[256,128]{1,0:T(8,128)S(1)}, f32[256,128]{1,0:T(8,128)S(1)}, u32[]{:S(2)}, u32[]{:S(2)}) collective-permute-start(f32[256,128]{1,0:T(8,128)S(1)} %get-tuple-element.37), channel_id=1, source_target_pairs={{0,6},{1,7},{2,4},{3,5},{4,2},{5,3},{6,0},{7,1},{8,14},{9,15},{10,... | collective-permute-start | bytes 393224 | tf_op jit(solution)/shard_map/ppermute | solution.py:341
  10.3 7.6 %collective-permute-done.1.refs_1_ = f32[512,128]{1,0:T(8,128)S(1)} collective-permute-done((f32[512,128]{1,0:T(8,128)S(1)}, f32[512,128]{1,0:T(8,128)S(1)}, u32[]{:S(2)}, u32[]{:S(2)}) %collective-permute-start.1) | collective-permute-done | bytes 262176 | tf_op jit(solution)/shard_map/ppermute | solution.py:341
  17.8 0.7 %collective-permute-done.3.refs_3_ = f32[256,128]{1,0:T(8,128)S(1)} collective-permute-done((f32[256,128]{1,0:T(8,128)S(1)}, f32[256,128]{1,0:T(8,128)S(1)}, u32[]{:S(2)}, u32[]{:S(2)}) %collective-permute-start.3) | collective-permute-done | bytes 131104 | tf_op jit(solution)/shard_map/ppermute | solution.py:341
  18.5 0.4 collective-permute-start.4
  18.9 1.0 %collective-permute-done.4.refs_4_ = f32[256,128]{1,0:T(8,128)S(1)} collective-permute-done((f32[256,128]{1,0:T(8,128)S(1)}, f32[256,128]{1,0:T(8,128)S(1)}, u32[]{:S(2)}, u32[]{:S(2)}) %collective-permute-start.4) | collective-permute-done | bytes 131104 | tf_op jit(solution)/shard_map/ppermute | solution.py:341
  19.9 0.8 %quad1.1 = (f32[512,128]{1,0:T(8,128)S(1)}, f32[512,128]{1,0:T(8,128)S(1)}, f32[512,128]{1,0:T(8,128)S(1)}, f32[512,128]{1,0:T(8,128)S(1)}, f32[256,128]{1,0:T(8,128)S(1)}) custom-call(f32[512,128]{1,0:T(8,128)S(1)} %get-tuple-element.36.refs_0_.refs_4_, f32[512,128]{1,0:T(8,128)S(1)} %collective-permute-done.1.refs_1_, ...), custom_call_target="tpu_custom_call" | custom-call | tf_op jit(solution)/shard_map/quad1/pallas_call | solution.py:204
  20.7 1.0 %collective-permute-start.5 = (f32[512,128]{1,0:T(8,128)S(1)}, f32[512,128]{1,0:T(8,128)S(1)}, u32[]{:S(2)}, u32[]{:S(2)}) collective-permute-start(f32[512,128]{1,0:T(8,128)S(1)} %get-tuple-element.38.refs_0_.refs_8_), channel_id=1, source_target_pairs={{0,8},{1,17},{2,10},{3,19},{4,12},{5,21},{6,14},{7,23},{8,0},{9,25... | collective-permute-start | bytes 786440 | tf_op jit(solution)/shard_map/ppermute | solution.py:341
  21.6 0.8 %collective-permute-start.7 = (f32[256,128]{1,0:T(8,128)S(1)}, f32[256,128]{1,0:T(8,128)S(1)}, u32[]{:S(2)}, u32[]{:S(2)}) collective-permute-start(f32[256,128]{1,0:T(8,128)S(1)} %get-tuple-element.39), channel_id=1, source_target_pairs={{0,24},{1,25},{2,26},{3,27},{4,28},{5,29},{6,30},{7,31},{8,16},{9,... | collective-permute-start | bytes 393224 | tf_op jit(solution)/shard_map/ppermute | solution.py:341
  22.4 7.7 %collective-permute-done.5.refs_1_ = f32[512,128]{1,0:T(8,128)S(1)} collective-permute-done((f32[512,128]{1,0:T(8,128)S(1)}, f32[512,128]{1,0:T(8,128)S(1)}, u32[]{:S(2)}, u32[]{:S(2)}) %collective-permute-start.5) | collective-permute-done | bytes 262176 | tf_op jit(solution)/shard_map/ppermute | solution.py:341
  30.1 0.7 %collective-permute-done.7.refs_3_ = f32[256,128]{1,0:T(8,128)S(1)} collective-permute-done((f32[256,128]{1,0:T(8,128)S(1)}, f32[256,128]{1,0:T(8,128)S(1)}, u32[]{:S(2)}, u32[]{:S(2)}) %collective-permute-start.7) | collective-permute-done | bytes 131104 | tf_op jit(solution)/shard_map/ppermute | solution.py:341
  30.9 0.4 collective-permute-start.8
  31.3 1.0 %collective-permute-done.8.refs_4_ = f32[256,128]{1,0:T(8,128)S(1)} collective-permute-done((f32[256,128]{1,0:T(8,128)S(1)}, f32[256,128]{1,0:T(8,128)S(1)}, u32[]{:S(2)}, u32[]{:S(2)}) %collective-permute-start.8) | collective-permute-done | bytes 131104 | tf_op jit(solution)/shard_map/ppermute | solution.py:341
  32.3 0.8 %quad3.1 = (f32[512,128]{1,0:T(8,128)S(1)}, f32[512,128]{1,0:T(8,128)S(1)}, f32[512,128]{1,0:T(8,128)S(1)}, f32[512,128]{1,0:T(8,128)S(1)}, f32[256,128]{1,0:T(8,128)S(1)}) custom-call(f32[512,128]{1,0:T(8,128)S(1)} %get-tuple-element.38.refs_0_.refs_8_, f32[512,128]{1,0:T(8,128)S(1)} %collective-permute-done.5.refs_1_, ...), custom_call_target="tpu_custom_call" | custom-call | tf_op jit(solution)/shard_map/quad3/pallas_call | solution.py:204
  33.0 2.0 %collective-permute-start.9 = (f32[512,128]{1,0:T(8,128)S(1)}, f32[512,128]{1,0:T(8,128)S(1)}, u32[]{:S(2)}, u32[]{:S(2)}) collective-permute-start(f32[512,128]{1,0:T(8,128)S(1)} %get-tuple-element.40.refs_0_.refs_1_), channel_id=1, source_target_pairs={{0,32},{1,97},{2,34},{3,99},{4,36},{5,101},{6,38},{7,103},{8,40},{... | collective-permute-start | bytes 786440 | tf_op jit(solution)/shard_map/ppermute | solution.py:341
  35.0 1.7 %prepare.1 = (f32[2,512,128]{2,1,0:T(8,128)S(1)}, bf16[2,6,256,256]{3,2,1,0:T(8,128)(2,1)S(1)}) custom-call(f32[2,512,128]{2,1,0:T(8,128)S(1)} %get-tuple-element.41.refs_0_, f32[2,6,320,128]{3,2,1,0:T(8,128)S(1)} %get-tuple-element.42.refs_1_.refs_6_, f32[512,128]{1,0:T(8,128)S(1)} %get-tuple-element.35.own.refs_2_, ...), custom_call_target="tpu_custom_call" | custom-call | flops 2147483648 | bytes 8388608 | tf_op jit(solution)/shard_map/prepare/pallas_call | solution.py:250
  36.7 6.2 %collective-permute-done.9.refs_1_ = f32[512,128]{1,0:T(8,128)S(1)} collective-permute-done((f32[512,128]{1,0:T(8,128)S(1)}, f32[512,128]{1,0:T(8,128)S(1)}, u32[]{:S(2)}, u32[]{:S(2)}) %collective-permute-start.9) | collective-permute-done | bytes 262176 | tf_op jit(solution)/shard_map/ppermute | solution.py:341
  42.9 1.8 %collective-permute-start.10 = (f32[512,128]{1,0:T(8,128)S(1)}, f32[512,128]{1,0:T(8,128)S(1)}, u32[]{:S(2)}, u32[]{:S(2)}) collective-permute-start(f32[512,128]{1,0:T(8,128)S(1)} %collective-permute-done.9.refs_1_), channel_id=1, source_target_pairs={{0,1},{1,0},{2,3},{3,2},{4,5},{5,4},{6,7},{7,6},{8,9},{9,8},{10,11... | collective-permute-start | bytes 786440 | tf_op jit(solution)/shard_map/ppermute | solution.py:341
  44.7 1.2 %collective-permute-done.11.refs_3_ = f32[256,128]{1,0:T(8,128)S(1)} collective-permute-done((f32[256,128]{1,0:T(8,128)S(1)}, f32[256,128]{1,0:T(8,128)S(1)}, u32[]{:S(2)}, u32[]{:S(2)}) %collective-permute-start.11) | collective-permute-done | bytes 131104 | tf_op jit(solution)/shard_map/ppermute | solution.py:341
  45.8 0.3 collective-permute-start.12
  46.1 1.0 %collective-permute-done.12.refs_4_ = f32[256,128]{1,0:T(8,128)S(1)} collective-permute-done((f32[256,128]{1,0:T(8,128)S(1)}, f32[256,128]{1,0:T(8,128)S(1)}, u32[]{:S(2)}, u32[]{:S(2)}) %collective-permute-start.12) | collective-permute-done | bytes 131104 | tf_op jit(solution)/shard_map/ppermute | solution.py:341
  47.2 0.8 %quad5.1 = (f32[512,128]{1,0:T(8,128)S(1)}, f32[512,128]{1,0:T(8,128)S(1)}, f32[512,128]{1,0:T(8,128)S(1)}, f32[512,128]{1,0:T(8,128)S(1)}, f32[96,128]{1,0:T(8,128)S(1)}) custom-call(f32[512,128]{1,0:T(8,128)S(1)} %get-tuple-element.40.refs_0_.refs_1_, f32[512,128]{1,0:T(8,128)S(1)} %collective-permute-done.9.refs_1_, ...), custom_call_target="tpu_custom_call" | custom-call | tf_op jit(solution)/shard_map/quad5/pallas_call | solution.py:204
  48.0 3.4 %collective-permute-start.13 = (f32[96,128]{1,0:T(8,128)S(1)}, f32[96,128]{1,0:T(8,128)S(1)}, u32[]{:S(2)}, u32[]{:S(2)}) collective-permute-start(f32[96,128]{1,0:T(8,128)S(1)} %get-tuple-element.54), channel_id=1, source_target_pairs={{0,192},{1,193},{2,194},{3,195},{4,196},{5,197},{6,198},{7,199},{8... | collective-permute-start | bytes 147464 | tf_op jit(solution)/shard_map/ppermute | solution.py:368
  51.4 0.7 %refine.1 = (bf16[2,2,256,256]{3,2,1,0:T(8,128)(2,1)S(1)}, f32[2,2,64,128]{3,2,1,0:T(8,128)S(1)}) custom-call(f32[2,512,128]{2,1,0:T(8,128)S(1)} %get-tuple-element.55.refs_0_, f32[512,128]{1,0:T(8,128)S(1)} %get-tuple-element.40.refs_0_.refs_1_, f32[512,128]{1,0:T(8,128)S(1)} %get-tuple-element.56.refs_2_, f32[512,128]{1,0:T(8,128)S(1)} %get-tuple-element.57.refs_3_, ...), custom_call_target="tpu_custom_call" | custom-call | flops 1073741824 | bytes 4194304 | tf_op jit(solution)/shard_map/refine/pallas_call | solution.py:281
  52.1 1.0 %collective-permute-done.13.refs_1_ = f32[96,128]{1,0:T(8,128)S(1)} collective-permute-done((f32[96,128]{1,0:T(8,128)S(1)}, f32[96,128]{1,0:T(8,128)S(1)}, u32[]{:S(2)}, u32[]{:S(2)}) %collective-permute-start.13) | collective-permute-done | bytes 49184 | tf_op jit(solution)/shard_map/ppermute | solution.py:368
  53.1 1.4 %collective-permute-start.14 = (f32[96,128]{1,0:T(8,128)S(1)}, f32[96,128]{1,0:T(8,128)S(1)}, u32[]{:S(2)}, u32[]{:S(2)}) collective-permute-start(f32[96,128]{1,0:T(8,128)S(1)} %collective-permute-done.13.refs_1_), channel_id=1, source_target_pairs={{0,1},{1,0},{2,3},{3,2},{4,5},{5,4},{6,7},{7,6},{8,9},{9,8},{10,11... | collective-permute-start | bytes 147464 | tf_op jit(solution)/shard_map/ppermute | solution.py:341
  54.5 0.9 %collective-permute-done.14.refs_2_ = f32[96,128]{1,0:T(8,128)S(1)} collective-permute-done((f32[96,128]{1,0:T(8,128)S(1)}, f32[96,128]{1,0:T(8,128)S(1)}, u32[]{:S(2)}, u32[]{:S(2)}) %collective-permute-start.14) | collective-permute-done | bytes 49184 | tf_op jit(solution)/shard_map/ppermute | solution.py:341
  55.4 1.5 %finish.1 = f32[12,64,128]{2,1,0:T(8,128)} custom-call(f32[512,128]{1,0:T(8,128)S(1)} %get-tuple-element.53.refs_0_, f32[96,128]{1,0:T(8,128)S(1)} %collective-permute-done.13.refs_1_, f32[96,128]{1,0:T(8,128)S(1)} %collective-permute-done.14.refs_2_, bf16[2,2,256,256]{3,2,1,0:T(8,128)(2,1)S(1)} %get-tuple-element.62.refs_3_, ...), custom_call_target="tpu_custom_call" | custom-call | tf_op jit(solution)/shard_map/finish/pallas_call | solution.py:323
  (6 shorter events, 0.0 us)
Async XLA Ops:
  3.5 4.5 %collective-permute-start = (f32[512,128]{1,0:T(8,128)S(1)}, f32[512,128]{1,0:T(8,128)S(1)}, u32[]{:S(2)}, u32[]{:S(2)}) collective-permute-start(f32[512,128]{1,0:T(8,128)S(1)} %get-tuple-element.35.own.refs_2_), channel_id=1, source_target_pairs={{0,1},{1,0},{2,3},{3,2},{4,5},{5,4},{6,7},{7,6},{8,9},{9,8},{10,11... | collective-permute-start | bytes 786440 | tf_op jit(solution)/shard_map/ppermute | solution.py:341
  8.3 9.5 %collective-permute-start.1 = (f32[512,128]{1,0:T(8,128)S(1)}, f32[512,128]{1,0:T(8,128)S(1)}, u32[]{:S(2)}, u32[]{:S(2)}) collective-permute-start(f32[512,128]{1,0:T(8,128)S(1)} %get-tuple-element.36.refs_0_.refs_4_), channel_id=1, source_target_pairs={{0,2},{1,5},{2,0},{3,7},{4,6},{5,1},{6,4},{7,3},{8,10},{9,13},{10,... | collective-permute-start | bytes 786440 | tf_op jit(solution)/shard_map/ppermute | solution.py:341
  9.4 9.1 %collective-permute-start.3 = (f32[256,128]{1,0:T(8,128)S(1)}, f32[256,128]{1,0:T(8,128)S(1)}, u32[]{:S(2)}, u32[]{:S(2)}) collective-permute-start(f32[256,128]{1,0:T(8,128)S(1)} %get-tuple-element.37), channel_id=1, source_target_pairs={{0,6},{1,7},{2,4},{3,5},{4,2},{5,3},{6,0},{7,1},{8,14},{9,15},{10,... | collective-permute-start | bytes 393224 | tf_op jit(solution)/shard_map/ppermute | solution.py:341
  17.8 2.1 %collective-permute-start.2 = (f32[512,128]{1,0:T(8,128)S(1)}, f32[512,128]{1,0:T(8,128)S(1)}, u32[]{:S(2)}, u32[]{:S(2)}) collective-permute-start(f32[512,128]{1,0:T(8,128)S(1)} %collective-permute-done.1.refs_1_), channel_id=1, source_target_pairs={{0,1},{1,0},{2,3},{3,2},{4,5},{5,4},{6,7},{7,6},{8,9},{9,8},{10,11... | collective-permute-start | bytes 786440 | tf_op jit(solution)/shard_map/ppermute | solution.py:341
  18.5 1.4 %collective-permute-start.4 = (f32[256,128]{1,0:T(8,128)S(1)}, f32[256,128]{1,0:T(8,128)S(1)}, u32[]{:S(2)}, u32[]{:S(2)}) collective-permute-start(f32[256,128]{1,0:T(8,128)S(1)} %collective-permute-done.3.refs_3_), channel_id=1, source_target_pairs={{0,1},{1,0},{2,3},{3,2},{4,5},{5,4},{6,7},{7,6},{8,9},{9,8},{10,11... | collective-permute-start | bytes 393224 | tf_op jit(solution)/shard_map/ppermute | solution.py:341
  20.7 9.5 %collective-permute-start.5 = (f32[512,128]{1,0:T(8,128)S(1)}, f32[512,128]{1,0:T(8,128)S(1)}, u32[]{:S(2)}, u32[]{:S(2)}) collective-permute-start(f32[512,128]{1,0:T(8,128)S(1)} %get-tuple-element.38.refs_0_.refs_8_), channel_id=1, source_target_pairs={{0,8},{1,17},{2,10},{3,19},{4,12},{5,21},{6,14},{7,23},{8,0},{9,25... | collective-permute-start | bytes 786440 | tf_op jit(solution)/shard_map/ppermute | solution.py:341
  21.6 9.2 %collective-permute-start.7 = (f32[256,128]{1,0:T(8,128)S(1)}, f32[256,128]{1,0:T(8,128)S(1)}, u32[]{:S(2)}, u32[]{:S(2)}) collective-permute-start(f32[256,128]{1,0:T(8,128)S(1)} %get-tuple-element.39), channel_id=1, source_target_pairs={{0,24},{1,25},{2,26},{3,27},{4,28},{5,29},{6,30},{7,31},{8,16},{9,... | collective-permute-start | bytes 393224 | tf_op jit(solution)/shard_map/ppermute | solution.py:341
  30.1 2.1 %collective-permute-start.6 = (f32[512,128]{1,0:T(8,128)S(1)}, f32[512,128]{1,0:T(8,128)S(1)}, u32[]{:S(2)}, u32[]{:S(2)}) collective-permute-start(f32[512,128]{1,0:T(8,128)S(1)} %collective-permute-done.5.refs_1_), channel_id=1, source_target_pairs={{0,1},{1,0},{2,3},{3,2},{4,5},{5,4},{6,7},{7,6},{8,9},{9,8},{10,11... | collective-permute-start | bytes 786440 | tf_op jit(solution)/shard_map/ppermute | solution.py:341
  30.9 1.4 %collective-permute-start.8 = (f32[256,128]{1,0:T(8,128)S(1)}, f32[256,128]{1,0:T(8,128)S(1)}, u32[]{:S(2)}, u32[]{:S(2)}) collective-permute-start(f32[256,128]{1,0:T(8,128)S(1)} %collective-permute-done.7.refs_3_), channel_id=1, source_target_pairs={{0,1},{1,0},{2,3},{3,2},{4,5},{5,4},{6,7},{7,6},{8,9},{9,8},{10,11... | collective-permute-start | bytes 393224 | tf_op jit(solution)/shard_map/ppermute | solution.py:341
  33.0 9.9 %collective-permute-start.9 = (f32[512,128]{1,0:T(8,128)S(1)}, f32[512,128]{1,0:T(8,128)S(1)}, u32[]{:S(2)}, u32[]{:S(2)}) collective-permute-start(f32[512,128]{1,0:T(8,128)S(1)} %get-tuple-element.40.refs_0_.refs_1_), channel_id=1, source_target_pairs={{0,32},{1,97},{2,34},{3,99},{4,36},{5,101},{6,38},{7,103},{8,40},{... | collective-permute-start | bytes 786440 | tf_op jit(solution)/shard_map/ppermute | solution.py:341
  35.0 10.8 %collective-permute-start.11 = (f32[256,128]{1,0:T(8,128)S(1)}, f32[256,128]{1,0:T(8,128)S(1)}, u32[]{:S(2)}, u32[]{:S(2)}) collective-permute-start(f32[256,128]{1,0:T(8,128)S(1)} %get-tuple-element.52), channel_id=1, source_target_pairs={{0,64},{1,65},{2,66},{3,67},{4,68},{5,69},{6,70},{7,71},{8,72},{9,... | collective-permute-start | bytes 393224 | tf_op jit(solution)/shard_map/ppermute | solution.py:341
  42.9 4.3 %collective-permute-start.10 = (f32[512,128]{1,0:T(8,128)S(1)}, f32[512,128]{1,0:T(8,128)S(1)}, u32[]{:S(2)}, u32[]{:S(2)}) collective-permute-start(f32[512,128]{1,0:T(8,128)S(1)} %collective-permute-done.9.refs_1_), channel_id=1, source_target_pairs={{0,1},{1,0},{2,3},{3,2},{4,5},{5,4},{6,7},{7,6},{8,9},{9,8},{10,11... | collective-permute-start | bytes 786440 | tf_op jit(solution)/shard_map/ppermute | solution.py:341
  45.8 1.3 %collective-permute-start.12 = (f32[256,128]{1,0:T(8,128)S(1)}, f32[256,128]{1,0:T(8,128)S(1)}, u32[]{:S(2)}, u32[]{:S(2)}) collective-permute-start(f32[256,128]{1,0:T(8,128)S(1)} %collective-permute-done.11.refs_3_), channel_id=1, source_target_pairs={{0,1},{1,0},{2,3},{3,2},{4,5},{5,4},{6,7},{7,6},{8,9},{9,8},{10,11... | collective-permute-start | bytes 393224 | tf_op jit(solution)/shard_map/ppermute | solution.py:341
  48.0 5.1 %collective-permute-start.13 = (f32[96,128]{1,0:T(8,128)S(1)}, f32[96,128]{1,0:T(8,128)S(1)}, u32[]{:S(2)}, u32[]{:S(2)}) collective-permute-start(f32[96,128]{1,0:T(8,128)S(1)} %get-tuple-element.54), channel_id=1, source_target_pairs={{0,192},{1,193},{2,194},{3,195},{4,196},{5,197},{6,198},{7,199},{8... | collective-permute-start | bytes 147464 | tf_op jit(solution)/shard_map/ppermute | solution.py:368
  53.1 2.3 %collective-permute-start.14 = (f32[96,128]{1,0:T(8,128)S(1)}, f32[96,128]{1,0:T(8,128)S(1)}, u32[]{:S(2)}, u32[]{:S(2)}) collective-permute-start(f32[96,128]{1,0:T(8,128)S(1)} %collective-permute-done.13.refs_1_), channel_id=1, source_target_pairs={{0,1},{1,0},{2,3},{3,2},{4,5},{5,4},{6,7},{7,6},{8,9},{9,8},{10,11... | collective-permute-start | bytes 147464 | tf_op jit(solution)/shard_map/ppermute | solution.py:341

commit v11 on v7

--- a/solution.py
+++ b/solution.py
@@ -191,11 +191,17 @@
     theirs = joined(*ordered(level, partner[2], partner[3]))
     near[...] = mine
     far[...] = theirs
-    value = joined(*ordered(level + 1, mine, theirs))
-    pack[...] = value
+    first, second = ordered(level + 1, mine, theirs)
     if top:
-        store_half(send, jnp.where(is_left(level + 2), value[: B + R], value[2 * B + R :]))
+        early, back = turned(first, second)
+        down = times(early[B:], right_side(second[:B])) + second[B : B + R]
+        up = mm(back[B:], first[B + R : 2 * B + R]) + first[2 * B + R :]
+        pack[B : B + R] = down
+        left = is_left(level + 2)
+        store_half(send, jnp.concatenate([up[:B], jnp.where(left, down, up[B:])], axis=0))
     else:
+        value = joined(first, second)
+        pack[...] = value
         store_half(send, value)
 
 

time: 57.7 us -> 57.7 us (level)
  no operation moved by 1% of the time
where the time goes in v11:
time: 57.7 us; the launch traced here: 57.1 us
  waiting for transfers between devices  30.1 us (52%)
  starting transfers between devices  16.8 us (29%)
  Pallas kernels  10 us (17%)
    ppermute x14, waiting for transfers between devices, on_device(): lax.ppermute(array, AXES, [(i, i ^ (odd if i & 1 else even)) for i in ran...  29.1 us
    ppermute x14, starting transfers between devices, on_device(): lax.ppermute(array, AXES, [(i, i ^ (odd if i & 1 else even)) for i in ran...  13.4 us
    pallas_call x1, Pallas kernels, local(): pl.pallas_call(local_kernel, out_shape=(jax.ShapeDtypeStruct((PACK, B), j...  3.47 us
    ppermute x1, starting transfers between devices, on_device(): got = lax.ppermute(half, AXES, facing)  3.41 us
    pallas_call x4, Pallas kernels, combine(): pl.pallas_call(kernel, out_shape=(whole,) * (1 + extra) + (jax.ShapeDtype...  2.59 us
    pallas_call x1, Pallas kernels, prepare(): pl.pallas_call(lambda *refs: prepare_kernel(len(steps), *refs), out_shape...  1.72 us
    pallas_call x1, Pallas kernels, finish(): pl.pallas_call(lambda *refs: finish_kernel(level, *refs), out_shape=jax.S...  1.48 us
  transfers between devices with their start and end apart: 15, of which 12 were waited for; matrix products, arithmetic and copies ran while one was open for 0% of the time, Pallas kernels for 4%

profile of v11, /device:TPU:1, one launch (start us, length us, event | category | flops | bytes accessed | tf_op | source)
XLA Modules:
  0.0 57.1 jit_solution(553658671787259861)
XLA Ops:
  0.0 3.5 %local.1 = (f32[512,128]{1,0:T(8,128)S(1)}, f32[2,512,128]{2,1,0:T(8,128)S(1)}, f32[2,6,320,128]{3,2,1,0:T(8,128)S(1)}) custom-call(f32[2,6,64,128]{3,2,1,0:T(8,128)} %bitcast.7, f32[2,6,128,128]{3,2,1,0:T(8,128)} %bitcast.4, f32[2,6,128,128]{3,2,1,0:T(8,128)} %bitcast.5, f32[2,6,128,128]{3,2,1,0:T(8,128)} %bitcast.6), custom_call_target="tpu_custom_call" | custom-call | tf_op jit(solution)/shard_map/local/pallas_call | solution.py:119
  3.5 3.3 %collective-permute-start = (f32[512,128]{1,0:T(8,128)S(1)}, f32[512,128]{1,0:T(8,128)S(1)}, u32[]{:S(2)}, u32[]{:S(2)}) collective-permute-start(f32[512,128]{1,0:T(8,128)S(1)} %get-tuple-element.35.own.refs_2_), channel_id=1, source_target_pairs={{0,1},{1,0},{2,3},{3,2},{4,5},{5,4},{6,7},{7,6},{8,9},{9,8},{10,11... | collective-permute-start | bytes 786440 | tf_op jit(solution)/shard_map/ppermute | solution.py:347
  6.8 1.2 %collective-permute-done.other.refs_3_ = f32[512,128]{1,0:T(8,128)S(1)} collective-permute-done((f32[512,128]{1,0:T(8,128)S(1)}, f32[512,128]{1,0:T(8,128)S(1)}, u32[]{:S(2)}, u32[]{:S(2)}) %collective-permute-start) | collective-permute-done | bytes 262176 | tf_op jit(solution)/shard_map/ppermute | solution.py:347
  8.0 0.3 pair.1
  8.3 1.1 %collective-permute-start.1 = (f32[512,128]{1,0:T(8,128)S(1)}, f32[512,128]{1,0:T(8,128)S(1)}, u32[]{:S(2)}, u32[]{:S(2)}) collective-permute-start(f32[512,128]{1,0:T(8,128)S(1)} %get-tuple-element.36.refs_0_.refs_4_), channel_id=1, source_target_pairs={{0,2},{1,5},{2,0},{3,7},{4,6},{5,1},{6,4},{7,3},{8,10},{9,13},{10,... | collective-permute-start | bytes 786440 | tf_op jit(solution)/shard_map/ppermute | solution.py:347
  9.4 0.9 %collective-permute-start.3 = (f32[256,128]{1,0:T(8,128)S(1)}, f32[256,128]{1,0:T(8,128)S(1)}, u32[]{:S(2)}, u32[]{:S(2)}) collective-permute-start(f32[256,128]{1,0:T(8,128)S(1)} %get-tuple-element.37), channel_id=1, source_target_pairs={{0,6},{1,7},{2,4},{3,5},{4,2},{5,3},{6,0},{7,1},{8,14},{9,15},{10,... | collective-permute-start | bytes 393224 | tf_op jit(solution)/shard_map/ppermute | solution.py:347
  10.3 7.6 %collective-permute-done.1.refs_1_ = f32[512,128]{1,0:T(8,128)S(1)} collective-permute-done((f32[512,128]{1,0:T(8,128)S(1)}, f32[512,128]{1,0:T(8,128)S(1)}, u32[]{:S(2)}, u32[]{:S(2)}) %collective-permute-start.1) | collective-permute-done | bytes 262176 | tf_op jit(solution)/shard_map/ppermute | solution.py:347
  17.8 0.7 %collective-permute-done.3.refs_3_ = f32[256,128]{1,0:T(8,128)S(1)} collective-permute-done((f32[256,128]{1,0:T(8,128)S(1)}, f32[256,128]{1,0:T(8,128)S(1)}, u32[]{:S(2)}, u32[]{:S(2)}) %collective-permute-start.3) | collective-permute-done | bytes 131104 | tf_op jit(solution)/shard_map/ppermute | solution.py:347
  18.5 0.4 collective-permute-start.4
  18.9 1.0 %collective-permute-done.4.refs_4_ = f32[256,128]{1,0:T(8,128)S(1)} collective-permute-done((f32[256,128]{1,0:T(8,128)S(1)}, f32[256,128]{1,0:T(8,128)S(1)}, u32[]{:S(2)}, u32[]{:S(2)}) %collective-permute-start.4) | collective-permute-done | bytes 131104 | tf_op jit(solution)/shard_map/ppermute | solution.py:347
  19.9 0.8 %quad1.1 = (f32[512,128]{1,0:T(8,128)S(1)}, f32[512,128]{1,0:T(8,128)S(1)}, f32[512,128]{1,0:T(8,128)S(1)}, f32[512,128]{1,0:T(8,128)S(1)}, f32[256,128]{1,0:T(8,128)S(1)}) custom-call(f32[512,128]{1,0:T(8,128)S(1)} %get-tuple-element.36.refs_0_.refs_4_, f32[512,128]{1,0:T(8,128)S(1)} %collective-permute-done.1.refs_1_, ...), custom_call_target="tpu_custom_call" | custom-call | tf_op jit(solution)/shard_map/quad1/pallas_call | solution.py:210
  20.7 1.0 %collective-permute-start.5 = (f32[512,128]{1,0:T(8,128)S(1)}, f32[512,128]{1,0:T(8,128)S(1)}, u32[]{:S(2)}, u32[]{:S(2)}) collective-permute-start(f32[512,128]{1,0:T(8,128)S(1)} %get-tuple-element.38.refs_0_.refs_8_), channel_id=1, source_target_pairs={{0,8},{1,17},{2,10},{3,19},{4,12},{5,21},{6,14},{7,23},{8,0},{9,25... | collective-permute-start | bytes 786440 | tf_op jit(solution)/shard_map/ppermute | solution.py:347
  21.6 0.8 %collective-permute-start.7 = (f32[256,128]{1,0:T(8,128)S(1)}, f32[256,128]{1,0:T(8,128)S(1)}, u32[]{:S(2)}, u32[]{:S(2)}) collective-permute-start(f32[256,128]{1,0:T(8,128)S(1)} %get-tuple-element.39), channel_id=1, source_target_pairs={{0,24},{1,25},{2,26},{3,27},{4,28},{5,29},{6,30},{7,31},{8,16},{9,... | collective-permute-start | bytes 393224 | tf_op jit(solution)/shard_map/ppermute | solution.py:347
  22.4 7.7 %collective-permute-done.5.refs_1_ = f32[512,128]{1,0:T(8,128)S(1)} collective-permute-done((f32[512,128]{1,0:T(8,128)S(1)}, f32[512,128]{1,0:T(8,128)S(1)}, u32[]{:S(2)}, u32[]{:S(2)}) %collective-permute-start.5) | collective-permute-done | bytes 262176 | tf_op jit(solution)/shard_map/ppermute | solution.py:347
  30.1 0.7 %collective-permute-done.7.refs_3_ = f32[256,128]{1,0:T(8,128)S(1)} collective-permute-done((f32[256,128]{1,0:T(8,128)S(1)}, f32[256,128]{1,0:T(8,128)S(1)}, u32[]{:S(2)}, u32[]{:S(2)}) %collective-permute-start.7) | collective-permute-done | bytes 131104 | tf_op jit(solution)/shard_map/ppermute | solution.py:347
  30.9 0.4 collective-permute-start.8
  31.3 1.0 %collective-permute-done.8.refs_4_ = f32[256,128]{1,0:T(8,128)S(1)} collective-permute-done((f32[256,128]{1,0:T(8,128)S(1)}, f32[256,128]{1,0:T(8,128)S(1)}, u32[]{:S(2)}, u32[]{:S(2)}) %collective-permute-start.8) | collective-permute-done | bytes 131104 | tf_op jit(solution)/shard_map/ppermute | solution.py:347
  32.3 0.8 %quad3.1 = (f32[512,128]{1,0:T(8,128)S(1)}, f32[512,128]{1,0:T(8,128)S(1)}, f32[512,128]{1,0:T(8,128)S(1)}, f32[512,128]{1,0:T(8,128)S(1)}, f32[256,128]{1,0:T(8,128)S(1)}) custom-call(f32[512,128]{1,0:T(8,128)S(1)} %get-tuple-element.38.refs_0_.refs_8_, f32[512,128]{1,0:T(8,128)S(1)} %collective-permute-done.5.refs_1_, ...), custom_call_target="tpu_custom_call" | custom-call | tf_op jit(solution)/shard_map/quad3/pallas_call | solution.py:210
  33.0 2.0 %collective-permute-start.9 = (f32[512,128]{1,0:T(8,128)S(1)}, f32[512,128]{1,0:T(8,128)S(1)}, u32[]{:S(2)}, u32[]{:S(2)}) collective-permute-start(f32[512,128]{1,0:T(8,128)S(1)} %get-tuple-element.40.refs_0_.refs_1_), channel_id=1, source_target_pairs={{0,32},{1,97},{2,34},{3,99},{4,36},{5,101},{6,38},{7,103},{8,40},{... | collective-permute-start | bytes 786440 | tf_op jit(solution)/shard_map/ppermute | solution.py:347
  35.0 1.7 %prepare.1 = (f32[2,512,128]{2,1,0:T(8,128)S(1)}, bf16[2,6,256,256]{3,2,1,0:T(8,128)(2,1)S(1)}) custom-call(f32[2,512,128]{2,1,0:T(8,128)S(1)} %get-tuple-element.41.refs_0_, f32[2,6,320,128]{3,2,1,0:T(8,128)S(1)} %get-tuple-element.42.refs_1_.refs_6_, f32[512,128]{1,0:T(8,128)S(1)} %get-tuple-element.35.own.refs_2_, ...), custom_call_target="tpu_custom_call" | custom-call | flops 2147483648 | bytes 8388608 | tf_op jit(solution)/shard_map/prepare/pallas_call | solution.py:256
  36.7 6.2 %collective-permute-done.9.refs_1_ = f32[512,128]{1,0:T(8,128)S(1)} collective-permute-done((f32[512,128]{1,0:T(8,128)S(1)}, f32[512,128]{1,0:T(8,128)S(1)}, u32[]{:S(2)}, u32[]{:S(2)}) %collective-permute-start.9) | collective-permute-done | bytes 262176 | tf_op jit(solution)/shard_map/ppermute | solution.py:347
  42.9 1.8 %collective-permute-start.10 = (f32[512,128]{1,0:T(8,128)S(1)}, f32[512,128]{1,0:T(8,128)S(1)}, u32[]{:S(2)}, u32[]{:S(2)}) collective-permute-start(f32[512,128]{1,0:T(8,128)S(1)} %collective-permute-done.9.refs_1_), channel_id=1, source_target_pairs={{0,1},{1,0},{2,3},{3,2},{4,5},{5,4},{6,7},{7,6},{8,9},{9,8},{10,11... | collective-permute-start | bytes 786440 | tf_op jit(solution)/shard_map/ppermute | solution.py:347
  44.7 1.2 %collective-permute-done.11.refs_3_ = f32[256,128]{1,0:T(8,128)S(1)} collective-permute-done((f32[256,128]{1,0:T(8,128)S(1)}, f32[256,128]{1,0:T(8,128)S(1)}, u32[]{:S(2)}, u32[]{:S(2)}) %collective-permute-start.11) | collective-permute-done | bytes 131104 | tf_op jit(solution)/shard_map/ppermute | solution.py:347
  45.8 0.3 collective-permute-start.12
  46.1 1.0 %collective-permute-done.12.refs_4_ = f32[256,128]{1,0:T(8,128)S(1)} collective-permute-done((f32[256,128]{1,0:T(8,128)S(1)}, f32[256,128]{1,0:T(8,128)S(1)}, u32[]{:S(2)}, u32[]{:S(2)}) %collective-permute-start.12) | collective-permute-done | bytes 131104 | tf_op jit(solution)/shard_map/ppermute | solution.py:347
  47.2 0.7 %quad5.1 = (f32[512,128]{1,0:T(8,128)S(1)}, f32[512,128]{1,0:T(8,128)S(1)}, f32[512,128]{1,0:T(8,128)S(1)}, f32[512,128]{1,0:T(8,128)S(1)}, f32[96,128]{1,0:T(8,128)S(1)}) custom-call(f32[512,128]{1,0:T(8,128)S(1)} %get-tuple-element.40.refs_0_.refs_1_, f32[512,128]{1,0:T(8,128)S(1)} %collective-permute-done.9.refs_1_, ...), custom_call_target="tpu_custom_call" | custom-call | tf_op jit(solution)/shard_map/quad5/pallas_call | solution.py:210
  47.9 3.4 %collective-permute-start.13 = (f32[96,128]{1,0:T(8,128)S(1)}, f32[96,128]{1,0:T(8,128)S(1)}, u32[]{:S(2)}, u32[]{:S(2)}) collective-permute-start(f32[96,128]{1,0:T(8,128)S(1)} %get-tuple-element.54), channel_id=1, source_target_pairs={{0,192},{1,193},{2,194},{3,195},{4,196},{5,197},{6,198},{7,199},{8... | collective-permute-start | bytes 147464 | tf_op jit(solution)/shard_map/ppermute | solution.py:374
  51.4 0.7 %refine.1 = (bf16[2,2,256,256]{3,2,1,0:T(8,128)(2,1)S(1)}, f32[2,2,64,128]{3,2,1,0:T(8,128)S(1)}) custom-call(f32[2,512,128]{2,1,0:T(8,128)S(1)} %get-tuple-element.55.refs_0_, f32[512,128]{1,0:T(8,128)S(1)} %get-tuple-element.40.refs_0_.refs_1_, f32[512,128]{1,0:T(8,128)S(1)} %get-tuple-element.56.refs_2_, f32[512,128]{1,0:T(8,128)S(1)} %get-tuple-element.57.refs_3_, ...), custom_call_target="tpu_custom_call" | custom-call | flops 1073741824 | bytes 4194304 | tf_op jit(solution)/shard_map/refine/pallas_call | solution.py:287
  52.1 1.0 %collective-permute-done.13.refs_1_ = f32[96,128]{1,0:T(8,128)S(1)} collective-permute-done((f32[96,128]{1,0:T(8,128)S(1)}, f32[96,128]{1,0:T(8,128)S(1)}, u32[]{:S(2)}, u32[]{:S(2)}) %collective-permute-start.13) | collective-permute-done | bytes 49184 | tf_op jit(solution)/shard_map/ppermute | solution.py:374
  53.1 1.5 %collective-permute-start.14 = (f32[96,128]{1,0:T(8,128)S(1)}, f32[96,128]{1,0:T(8,128)S(1)}, u32[]{:S(2)}, u32[]{:S(2)}) collective-permute-start(f32[96,128]{1,0:T(8,128)S(1)} %collective-permute-done.13.refs_1_), channel_id=1, source_target_pairs={{0,1},{1,0},{2,3},{3,2},{4,5},{5,4},{6,7},{7,6},{8,9},{9,8},{10,11... | collective-permute-start | bytes 147464 | tf_op jit(solution)/shard_map/ppermute | solution.py:347
  54.6 0.9 %collective-permute-done.14.refs_2_ = f32[96,128]{1,0:T(8,128)S(1)} collective-permute-done((f32[96,128]{1,0:T(8,128)S(1)}, f32[96,128]{1,0:T(8,128)S(1)}, u32[]{:S(2)}, u32[]{:S(2)}) %collective-permute-start.14) | collective-permute-done | bytes 49184 | tf_op jit(solution)/shard_map/ppermute | solution.py:347
  55.5 1.5 %finish.1 = f32[12,64,128]{2,1,0:T(8,128)} custom-call(f32[512,128]{1,0:T(8,128)S(1)} %get-tuple-element.53.refs_0_, f32[96,128]{1,0:T(8,128)S(1)} %collective-permute-done.13.refs_1_, f32[96,128]{1,0:T(8,128)S(1)} %collective-permute-done.14.refs_2_, bf16[2,2,256,256]{3,2,1,0:T(8,128)(2,1)S(1)} %get-tuple-element.62.refs_3_, ...), custom_call_target="tpu_custom_call" | custom-call | tf_op jit(solution)/shard_map/finish/pallas_call | solution.py:329
  (6 shorter events, 0.0 us)
Async XLA Ops:
  3.5 4.5 %collective-permute-start = (f32[512,128]{1,0:T(8,128)S(1)}, f32[512,128]{1,0:T(8,128)S(1)}, u32[]{:S(2)}, u32[]{:S(2)}) collective-permute-start(f32[512,128]{1,0:T(8,128)S(1)} %get-tuple-element.35.own.refs_2_), channel_id=1, source_target_pairs={{0,1},{1,0},{2,3},{3,2},{4,5},{5,4},{6,7},{7,6},{8,9},{9,8},{10,11... | collective-permute-start | bytes 786440 | tf_op jit(solution)/shard_map/ppermute | solution.py:347
  8.3 9.5 %collective-permute-start.1 = (f32[512,128]{1,0:T(8,128)S(1)}, f32[512,128]{1,0:T(8,128)S(1)}, u32[]{:S(2)}, u32[]{:S(2)}) collective-permute-start(f32[512,128]{1,0:T(8,128)S(1)} %get-tuple-element.36.refs_0_.refs_4_), channel_id=1, source_target_pairs={{0,2},{1,5},{2,0},{3,7},{4,6},{5,1},{6,4},{7,3},{8,10},{9,13},{10,... | collective-permute-start | bytes 786440 | tf_op jit(solution)/shard_map/ppermute | solution.py:347
  9.4 9.1 %collective-permute-start.3 = (f32[256,128]{1,0:T(8,128)S(1)}, f32[256,128]{1,0:T(8,128)S(1)}, u32[]{:S(2)}, u32[]{:S(2)}) collective-permute-start(f32[256,128]{1,0:T(8,128)S(1)} %get-tuple-element.37), channel_id=1, source_target_pairs={{0,6},{1,7},{2,4},{3,5},{4,2},{5,3},{6,0},{7,1},{8,14},{9,15},{10,... | collective-permute-start | bytes 393224 | tf_op jit(solution)/shard_map/ppermute | solution.py:347
  17.8 2.1 %collective-permute-start.2 = (f32[512,128]{1,0:T(8,128)S(1)}, f32[512,128]{1,0:T(8,128)S(1)}, u32[]{:S(2)}, u32[]{:S(2)}) collective-permute-start(f32[512,128]{1,0:T(8,128)S(1)} %collective-permute-done.1.refs_1_), channel_id=1, source_target_pairs={{0,1},{1,0},{2,3},{3,2},{4,5},{5,4},{6,7},{7,6},{8,9},{9,8},{10,11... | collective-permute-start | bytes 786440 | tf_op jit(solution)/shard_map/ppermute | solution.py:347
  18.5 1.4 %collective-permute-start.4 = (f32[256,128]{1,0:T(8,128)S(1)}, f32[256,128]{1,0:T(8,128)S(1)}, u32[]{:S(2)}, u32[]{:S(2)}) collective-permute-start(f32[256,128]{1,0:T(8,128)S(1)} %collective-permute-done.3.refs_3_), channel_id=1, source_target_pairs={{0,1},{1,0},{2,3},{3,2},{4,5},{5,4},{6,7},{7,6},{8,9},{9,8},{10,11... | collective-permute-start | bytes 393224 | tf_op jit(solution)/shard_map/ppermute | solution.py:347
  20.7 9.5 %collective-permute-start.5 = (f32[512,128]{1,0:T(8,128)S(1)}, f32[512,128]{1,0:T(8,128)S(1)}, u32[]{:S(2)}, u32[]{:S(2)}) collective-permute-start(f32[512,128]{1,0:T(8,128)S(1)} %get-tuple-element.38.refs_0_.refs_8_), channel_id=1, source_target_pairs={{0,8},{1,17},{2,10},{3,19},{4,12},{5,21},{6,14},{7,23},{8,0},{9,25... | collective-permute-start | bytes 786440 | tf_op jit(solution)/shard_map/ppermute | solution.py:347
  21.6 9.2 %collective-permute-start.7 = (f32[256,128]{1,0:T(8,128)S(1)}, f32[256,128]{1,0:T(8,128)S(1)}, u32[]{:S(2)}, u32[]{:S(2)}) collective-permute-start(f32[256,128]{1,0:T(8,128)S(1)} %get-tuple-element.39), channel_id=1, source_target_pairs={{0,24},{1,25},{2,26},{3,27},{4,28},{5,29},{6,30},{7,31},{8,16},{9,... | collective-permute-start | bytes 393224 | tf_op jit(solution)/shard_map/ppermute | solution.py:347
  30.1 2.1 %collective-permute-start.6 = (f32[512,128]{1,0:T(8,128)S(1)}, f32[512,128]{1,0:T(8,128)S(1)}, u32[]{:S(2)}, u32[]{:S(2)}) collective-permute-start(f32[512,128]{1,0:T(8,128)S(1)} %collective-permute-done.5.refs_1_), channel_id=1, source_target_pairs={{0,1},{1,0},{2,3},{3,2},{4,5},{5,4},{6,7},{7,6},{8,9},{9,8},{10,11... | collective-permute-start | bytes 786440 | tf_op jit(solution)/shard_map/ppermute | solution.py:347
  30.9 1.4 %collective-permute-start.8 = (f32[256,128]{1,0:T(8,128)S(1)}, f32[256,128]{1,0:T(8,128)S(1)}, u32[]{:S(2)}, u32[]{:S(2)}) collective-permute-start(f32[256,128]{1,0:T(8,128)S(1)} %collective-permute-done.7.refs_3_), channel_id=1, source_target_pairs={{0,1},{1,0},{2,3},{3,2},{4,5},{5,4},{6,7},{7,6},{8,9},{9,8},{10,11... | collective-permute-start | bytes 393224 | tf_op jit(solution)/shard_map/ppermute | solution.py:347
  33.0 9.9 %collective-permute-start.9 = (f32[512,128]{1,0:T(8,128)S(1)}, f32[512,128]{1,0:T(8,128)S(1)}, u32[]{:S(2)}, u32[]{:S(2)}) collective-permute-start(f32[512,128]{1,0:T(8,128)S(1)} %get-tuple-element.40.refs_0_.refs_1_), channel_id=1, source_target_pairs={{0,32},{1,97},{2,34},{3,99},{4,36},{5,101},{6,38},{7,103},{8,40},{... | collective-permute-start | bytes 786440 | tf_op jit(solution)/shard_map/ppermute | solution.py:347
  35.0 10.8 %collective-permute-start.11 = (f32[256,128]{1,0:T(8,128)S(1)}, f32[256,128]{1,0:T(8,128)S(1)}, u32[]{:S(2)}, u32[]{:S(2)}) collective-permute-start(f32[256,128]{1,0:T(8,128)S(1)} %get-tuple-element.52), channel_id=1, source_target_pairs={{0,64},{1,65},{2,66},{3,67},{4,68},{5,69},{6,70},{7,71},{8,72},{9,... | collective-permute-start | bytes 393224 | tf_op jit(solution)/shard_map/ppermute | solution.py:347
  42.9 4.3 %collective-permute-start.10 = (f32[512,128]{1,0:T(8,128)S(1)}, f32[512,128]{1,0:T(8,128)S(1)}, u32[]{:S(2)}, u32[]{:S(2)}) collective-permute-start(f32[512,128]{1,0:T(8,128)S(1)} %collective-permute-done.9.refs_1_), channel_id=1, source_target_pairs={{0,1},{1,0},{2,3},{3,2},{4,5},{5,4},{6,7},{7,6},{8,9},{9,8},{10,11... | collective-permute-start | bytes 786440 | tf_op jit(solution)/shard_map/ppermute | solution.py:347
  45.8 1.3 %collective-permute-start.12 = (f32[256,128]{1,0:T(8,128)S(1)}, f32[256,128]{1,0:T(8,128)S(1)}, u32[]{:S(2)}, u32[]{:S(2)}) collective-permute-start(f32[256,128]{1,0:T(8,128)S(1)} %collective-permute-done.11.refs_3_), channel_id=1, source_target_pairs={{0,1},{1,0},{2,3},{3,2},{4,5},{5,4},{6,7},{7,6},{8,9},{9,8},{10,11... | collective-permute-start | bytes 393224 | tf_op jit(solution)/shard_map/ppermute | solution.py:347
  47.9 5.1 %collective-permute-start.13 = (f32[96,128]{1,0:T(8,128)S(1)}, f32[96,128]{1,0:T(8,128)S(1)}, u32[]{:S(2)}, u32[]{:S(2)}) collective-permute-start(f32[96,128]{1,0:T(8,128)S(1)} %get-tuple-element.54), channel_id=1, source_target_pairs={{0,192},{1,193},{2,194},{3,195},{4,196},{5,197},{6,198},{7,199},{8... | collective-permute-start | bytes 147464 | tf_op jit(solution)/shard_map/ppermute | solution.py:374
  53.1 2.4 %collective-permute-start.14 = (f32[96,128]{1,0:T(8,128)S(1)}, f32[96,128]{1,0:T(8,128)S(1)}, u32[]{:S(2)}, u32[]{:S(2)}) collective-permute-start(f32[96,128]{1,0:T(8,128)S(1)} %collective-permute-done.13.refs_1_), channel_id=1, source_target_pairs={{0,1},{1,0},{2,3},{3,2},{4,5},{5,4},{6,7},{7,6},{8,9},{9,8},{10,11... | collective-permute-start | bytes 147464 | tf_op jit(solution)/shard_map/ppermute | solution.py:347

commit v12 on v7

--- a/solution.py
+++ b/solution.py
@@ -12,7 +12,7 @@
 PARTS = 2
 OUT_ROWS = 3
 FACING = (6, 7, 4, 5, 2, 3, 0, 1)
-PLANS = ((1, (1, 2)), (3, (1, 2)), (5, (1, 3)))
+PLANS = ((1, (1, 3)), (3, (1, 3)), (5, (1, 3)))
 LIMIT = 12 * 2**20
 
 

time: 57.7 us -> 60.5 us (1.049)
  starting transfers between devices: 16.8 us -> 21.7 us
  waiting for transfers between devices: 30.1 us -> 28.4 us
    ppermute x14, starting transfers between devices: 13.4 us -> 18.3 us  [on_device(): lax.ppermute(array, AXES, [(i, i ^ (odd if i & 1 else even)) for i in ran...]
    ppermute x14, waiting for transfers between devices: 29.1 us -> 27.4 us  [on_device(): lax.ppermute(array, AXES, [(i, i ^ (odd if i & 1 else even)) for i in ran...]
  transfers between devices with their start and end apart: 15 -> 15, of which waited for: 12 -> 11; matrix products, arithmetic and copies ran while one was open for 0% -> 0% of each run, Pallas kernels for 4% -> 4%
where the time goes in v12:
time: 60.5 us; the launch traced here: 60.4 us
  waiting for transfers between devices  28.4 us (47%)
  starting transfers between devices  21.7 us (36%)
  Pallas kernels  10 us (17%)
    ppermute x14, waiting for transfers between devices, on_device(): lax.ppermute(array, AXES, [(i, i ^ (odd if i & 1 else even)) for i in ran...  27.4 us
    ppermute x14, starting transfers between devices, on_device(): lax.ppermute(array, AXES, [(i, i ^ (odd if i & 1 else even)) for i in ran...  18.3 us
    pallas_call x1, Pallas kernels, local(): pl.pallas_call(local_kernel, out_shape=(jax.ShapeDtypeStruct((PACK, B), j...  3.47 us
    ppermute x1, starting transfers between devices, on_device(): got = lax.ppermute(half, AXES, facing)  3.39 us
    pallas_call x4, Pallas kernels, combine(): pl.pallas_call(kernel, out_shape=(whole,) * (1 + extra) + (jax.ShapeDtype...  2.61 us
    pallas_call x1, Pallas kernels, prepare(): pl.pallas_call(lambda *refs: prepare_kernel(len(steps), *refs), out_shape...  1.72 us
    pallas_call x1, Pallas kernels, finish(): pl.pallas_call(lambda *refs: finish_kernel(level, *refs), out_shape=jax.S...  1.48 us
  transfers between devices with their start and end apart: 15, of which 11 were waited for; matrix products, arithmetic and copies ran while one was open for 0% of the time, Pallas kernels for 4%

profile of v12, /device:TPU:1, one launch (start us, length us, event | category | flops | bytes accessed | tf_op | source)
XLA Modules:
  0.0 60.4 jit_solution(5546467543562569221)
XLA Ops:
  0.0 3.5 %local.1 = (f32[512,128]{1,0:T(8,128)S(1)}, f32[2,512,128]{2,1,0:T(8,128)S(1)}, f32[2,6,320,128]{3,2,1,0:T(8,128)S(1)}) custom-call(f32[2,6,64,128]{3,2,1,0:T(8,128)} %bitcast.7, f32[2,6,128,128]{3,2,1,0:T(8,128)} %bitcast.4, f32[2,6,128,128]{3,2,1,0:T(8,128)} %bitcast.5, f32[2,6,128,128]{3,2,1,0:T(8,128)} %bitcast.6), custom_call_target="tpu_custom_call" | custom-call | tf_op jit(solution)/shard_map/local/pallas_call | solution.py:119
  3.5 3.3 %collective-permute-start = (f32[512,128]{1,0:T(8,128)S(1)}, f32[512,128]{1,0:T(8,128)S(1)}, u32[]{:S(2)}, u32[]{:S(2)}) collective-permute-start(f32[512,128]{1,0:T(8,128)S(1)} %get-tuple-element.35.own.refs_2_), channel_id=1, source_target_pairs={{0,1},{1,0},{2,3},{3,2},{4,5},{5,4},{6,7},{7,6},{8,9},{9,8},{10,11... | collective-permute-start | bytes 786440 | tf_op jit(solution)/shard_map/ppermute | solution.py:341
  6.8 1.2 %collective-permute-done.other.refs_3_ = f32[512,128]{1,0:T(8,128)S(1)} collective-permute-done((f32[512,128]{1,0:T(8,128)S(1)}, f32[512,128]{1,0:T(8,128)S(1)}, u32[]{:S(2)}, u32[]{:S(2)}) %collective-permute-start) | collective-permute-done | bytes 262176 | tf_op jit(solution)/shard_map/ppermute | solution.py:341
  8.0 0.3 pair.1
  8.3 0.8 %collective-permute-start.1 = (f32[512,128]{1,0:T(8,128)S(1)}, f32[512,128]{1,0:T(8,128)S(1)}, u32[]{:S(2)}, u32[]{:S(2)}) collective-permute-start(f32[512,128]{1,0:T(8,128)S(1)} %get-tuple-element.36.refs_0_.refs_4_), channel_id=1, source_target_pairs={{0,2},{1,7},{2,0},{3,5},{4,6},{5,3},{6,4},{7,1},{8,10},{9,15},{10,... | collective-permute-start | bytes 786440 | tf_op jit(solution)/shard_map/ppermute | solution.py:341
  9.1 0.5 collective-permute-start.3
  9.7 6.6 %collective-permute-done.1.refs_1_ = f32[512,128]{1,0:T(8,128)S(1)} collective-permute-done((f32[512,128]{1,0:T(8,128)S(1)}, f32[512,128]{1,0:T(8,128)S(1)}, u32[]{:S(2)}, u32[]{:S(2)}) %collective-permute-start.1) | collective-permute-done | bytes 262176 | tf_op jit(solution)/shard_map/ppermute | solution.py:341
  16.2 0.3 collective-permute-start.2
  16.5 0.0 collective-permute-done.3.refs_3_
  16.6 1.9 %collective-permute-start.4 = (f32[256,128]{1,0:T(8,128)S(1)}, f32[256,128]{1,0:T(8,128)S(1)}, u32[]{:S(2)}, u32[]{:S(2)}) collective-permute-start(f32[256,128]{1,0:T(8,128)S(1)} %collective-permute-done.3.refs_3_), channel_id=1, source_target_pairs={{0,1},{1,0},{2,3},{3,2},{4,5},{5,4},{6,7},{7,6},{8,9},{9,8},{10,11... | collective-permute-start | bytes 393224 | tf_op jit(solution)/shard_map/ppermute | solution.py:341
  18.4 1.0 %collective-permute-done.4.refs_4_ = f32[256,128]{1,0:T(8,128)S(1)} collective-permute-done((f32[256,128]{1,0:T(8,128)S(1)}, f32[256,128]{1,0:T(8,128)S(1)}, u32[]{:S(2)}, u32[]{:S(2)}) %collective-permute-start.4) | collective-permute-done | bytes 131104 | tf_op jit(solution)/shard_map/ppermute | solution.py:341
  19.4 0.8 %quad1.1 = (f32[512,128]{1,0:T(8,128)S(1)}, f32[512,128]{1,0:T(8,128)S(1)}, f32[512,128]{1,0:T(8,128)S(1)}, f32[512,128]{1,0:T(8,128)S(1)}, f32[256,128]{1,0:T(8,128)S(1)}) custom-call(f32[512,128]{1,0:T(8,128)S(1)} %get-tuple-element.36.refs_0_.refs_4_, f32[512,128]{1,0:T(8,128)S(1)} %collective-permute-done.1.refs_1_, ...), custom_call_target="tpu_custom_call" | custom-call | tf_op jit(solution)/shard_map/quad1/pallas_call | solution.py:204
  20.2 2.8 %collective-permute-start.5 = (f32[512,128]{1,0:T(8,128)S(1)}, f32[512,128]{1,0:T(8,128)S(1)}, u32[]{:S(2)}, u32[]{:S(2)}) collective-permute-start(f32[512,128]{1,0:T(8,128)S(1)} %get-tuple-element.38.refs_0_.refs_8_), channel_id=1, source_target_pairs={{0,8},{1,25},{2,10},{3,27},{4,12},{5,29},{6,14},{7,31},{8,0},{9,17... | collective-permute-start | bytes 786440 | tf_op jit(solution)/shard_map/ppermute | solution.py:341
  23.0 0.3 collective-permute-start.7
  23.3 5.8 %collective-permute-done.5.refs_1_ = f32[512,128]{1,0:T(8,128)S(1)} collective-permute-done((f32[512,128]{1,0:T(8,128)S(1)}, f32[512,128]{1,0:T(8,128)S(1)}, u32[]{:S(2)}, u32[]{:S(2)}) %collective-permute-start.5) | collective-permute-done | bytes 262176 | tf_op jit(solution)/shard_map/ppermute | solution.py:341
  29.1 0.6 collective-permute-done.7.refs_3_
  29.7 2.5 %collective-permute-start.8 = (f32[256,128]{1,0:T(8,128)S(1)}, f32[256,128]{1,0:T(8,128)S(1)}, u32[]{:S(2)}, u32[]{:S(2)}) collective-permute-start(f32[256,128]{1,0:T(8,128)S(1)} %collective-permute-done.7.refs_3_), channel_id=1, source_target_pairs={{0,1},{1,0},{2,3},{3,2},{4,5},{5,4},{6,7},{7,6},{8,9},{9,8},{10,11... | collective-permute-start | bytes 393224 | tf_op jit(solution)/shard_map/ppermute | solution.py:341
  32.2 1.0 %collective-permute-done.8.refs_4_ = f32[256,128]{1,0:T(8,128)S(1)} collective-permute-done((f32[256,128]{1,0:T(8,128)S(1)}, f32[256,128]{1,0:T(8,128)S(1)}, u32[]{:S(2)}, u32[]{:S(2)}) %collective-permute-start.8) | collective-permute-done | bytes 131104 | tf_op jit(solution)/shard_map/ppermute | solution.py:341
  33.2 0.8 %quad3.1 = (f32[512,128]{1,0:T(8,128)S(1)}, f32[512,128]{1,0:T(8,128)S(1)}, f32[512,128]{1,0:T(8,128)S(1)}, f32[512,128]{1,0:T(8,128)S(1)}, f32[256,128]{1,0:T(8,128)S(1)}) custom-call(f32[512,128]{1,0:T(8,128)S(1)} %get-tuple-element.38.refs_0_.refs_8_, f32[512,128]{1,0:T(8,128)S(1)} %collective-permute-done.5.refs_1_, ...), custom_call_target="tpu_custom_call" | custom-call | tf_op jit(solution)/shard_map/quad3/pallas_call | solution.py:204
  34.0 4.4 %collective-permute-start.9 = (f32[512,128]{1,0:T(8,128)S(1)}, f32[512,128]{1,0:T(8,128)S(1)}, u32[]{:S(2)}, u32[]{:S(2)}) collective-permute-start(f32[512,128]{1,0:T(8,128)S(1)} %get-tuple-element.40.refs_0_.refs_1_), channel_id=1, source_target_pairs={{0,32},{1,97},{2,34},{3,99},{4,36},{5,101},{6,38},{7,103},{8,40},{... | collective-permute-start | bytes 786440 | tf_op jit(solution)/shard_map/ppermute | solution.py:341
  38.4 1.7 %prepare.1 = (f32[2,512,128]{2,1,0:T(8,128)S(1)}, bf16[2,6,256,256]{3,2,1,0:T(8,128)(2,1)S(1)}) custom-call(f32[2,512,128]{2,1,0:T(8,128)S(1)} %get-tuple-element.41.refs_0_, f32[2,6,320,128]{3,2,1,0:T(8,128)S(1)} %get-tuple-element.42.refs_1_.refs_6_, f32[512,128]{1,0:T(8,128)S(1)} %get-tuple-element.35.own.refs_2_, ...), custom_call_target="tpu_custom_call" | custom-call | flops 2147483648 | bytes 8388608 | tf_op jit(solution)/shard_map/prepare/pallas_call | solution.py:250
  40.2 4.2 %collective-permute-done.9.refs_1_ = f32[512,128]{1,0:T(8,128)S(1)} collective-permute-done((f32[512,128]{1,0:T(8,128)S(1)}, f32[512,128]{1,0:T(8,128)S(1)}, u32[]{:S(2)}, u32[]{:S(2)}) %collective-permute-start.9) | collective-permute-done | bytes 262176 | tf_op jit(solution)/shard_map/ppermute | solution.py:341
  44.4 4.9 %collective-permute-done.11.refs_3_ = f32[256,128]{1,0:T(8,128)S(1)} collective-permute-done((f32[256,128]{1,0:T(8,128)S(1)}, f32[256,128]{1,0:T(8,128)S(1)}, u32[]{:S(2)}, u32[]{:S(2)}) %collective-permute-start.11) | collective-permute-done | bytes 131104 | tf_op jit(solution)/shard_map/ppermute | solution.py:341
  49.3 0.0 collective-permute-start.12
  49.3 1.3 %collective-permute-done.12.refs_4_ = f32[256,128]{1,0:T(8,128)S(1)} collective-permute-done((f32[256,128]{1,0:T(8,128)S(1)}, f32[256,128]{1,0:T(8,128)S(1)}, u32[]{:S(2)}, u32[]{:S(2)}) %collective-permute-start.12) | collective-permute-done | bytes 131104 | tf_op jit(solution)/shard_map/ppermute | solution.py:341
  50.6 0.8 %quad5.1 = (f32[512,128]{1,0:T(8,128)S(1)}, f32[512,128]{1,0:T(8,128)S(1)}, f32[512,128]{1,0:T(8,128)S(1)}, f32[512,128]{1,0:T(8,128)S(1)}, f32[96,128]{1,0:T(8,128)S(1)}) custom-call(f32[512,128]{1,0:T(8,128)S(1)} %get-tuple-element.40.refs_0_.refs_1_, f32[512,128]{1,0:T(8,128)S(1)} %collective-permute-done.9.refs_1_, ...), custom_call_target="tpu_custom_call" | custom-call | tf_op jit(solution)/shard_map/quad5/pallas_call | solution.py:204
  51.4 3.4 %collective-permute-start.13 = (f32[96,128]{1,0:T(8,128)S(1)}, f32[96,128]{1,0:T(8,128)S(1)}, u32[]{:S(2)}, u32[]{:S(2)}) collective-permute-start(f32[96,128]{1,0:T(8,128)S(1)} %get-tuple-element.54), channel_id=1, source_target_pairs={{0,192},{1,193},{2,194},{3,195},{4,196},{5,197},{6,198},{7,199},{8... | collective-permute-start | bytes 147464 | tf_op jit(solution)/shard_map/ppermute | solution.py:368
  54.8 0.7 %refine.1 = (bf16[2,2,256,256]{3,2,1,0:T(8,128)(2,1)S(1)}, f32[2,2,64,128]{3,2,1,0:T(8,128)S(1)}) custom-call(f32[2,512,128]{2,1,0:T(8,128)S(1)} %get-tuple-element.55.refs_0_, f32[512,128]{1,0:T(8,128)S(1)} %get-tuple-element.40.refs_0_.refs_1_, f32[512,128]{1,0:T(8,128)S(1)} %get-tuple-element.56.refs_2_, f32[512,128]{1,0:T(8,128)S(1)} %get-tuple-element.57.refs_3_, ...), custom_call_target="tpu_custom_call" | custom-call | flops 1073741824 | bytes 4194304 | tf_op jit(solution)/shard_map/refine/pallas_call | solution.py:281
  55.5 1.0 %collective-permute-done.13.refs_1_ = f32[96,128]{1,0:T(8,128)S(1)} collective-permute-done((f32[96,128]{1,0:T(8,128)S(1)}, f32[96,128]{1,0:T(8,128)S(1)}, u32[]{:S(2)}, u32[]{:S(2)}) %collective-permute-start.13) | collective-permute-done | bytes 49184 | tf_op jit(solution)/shard_map/ppermute | solution.py:368
  56.5 1.3 %collective-permute-start.14 = (f32[96,128]{1,0:T(8,128)S(1)}, f32[96,128]{1,0:T(8,128)S(1)}, u32[]{:S(2)}, u32[]{:S(2)}) collective-permute-start(f32[96,128]{1,0:T(8,128)S(1)} %collective-permute-done.13.refs_1_), channel_id=1, source_target_pairs={{0,1},{1,0},{2,3},{3,2},{4,5},{5,4},{6,7},{7,6},{8,9},{9,8},{10,11... | collective-permute-start | bytes 147464 | tf_op jit(solution)/shard_map/ppermute | solution.py:341
  57.9 0.9 %collective-permute-done.14.refs_2_ = f32[96,128]{1,0:T(8,128)S(1)} collective-permute-done((f32[96,128]{1,0:T(8,128)S(1)}, f32[96,128]{1,0:T(8,128)S(1)}, u32[]{:S(2)}, u32[]{:S(2)}) %collective-permute-start.14) | collective-permute-done | bytes 49184 | tf_op jit(solution)/shard_map/ppermute | solution.py:341
  58.7 1.5 %finish.1 = f32[12,64,128]{2,1,0:T(8,128)} custom-call(f32[512,128]{1,0:T(8,128)S(1)} %get-tuple-element.53.refs_0_, f32[96,128]{1,0:T(8,128)S(1)} %collective-permute-done.13.refs_1_, f32[96,128]{1,0:T(8,128)S(1)} %collective-permute-done.14.refs_2_, bf16[2,2,256,256]{3,2,1,0:T(8,128)(2,1)S(1)} %get-tuple-element.62.refs_3_, ...), custom_call_target="tpu_custom_call" | custom-call | tf_op jit(solution)/shard_map/finish/pallas_call | solution.py:323
  (6 shorter events, 0.0 us)
Async XLA Ops:
  3.5 4.5 %collective-permute-start = (f32[512,128]{1,0:T(8,128)S(1)}, f32[512,128]{1,0:T(8,128)S(1)}, u32[]{:S(2)}, u32[]{:S(2)}) collective-permute-start(f32[512,128]{1,0:T(8,128)S(1)} %get-tuple-element.35.own.refs_2_), channel_id=1, source_target_pairs={{0,1},{1,0},{2,3},{3,2},{4,5},{5,4},{6,7},{7,6},{8,9},{9,8},{10,11... | collective-permute-start | bytes 786440 | tf_op jit(solution)/shard_map/ppermute | solution.py:341
  8.3 7.9 %collective-permute-start.1 = (f32[512,128]{1,0:T(8,128)S(1)}, f32[512,128]{1,0:T(8,128)S(1)}, u32[]{:S(2)}, u32[]{:S(2)}) collective-permute-start(f32[512,128]{1,0:T(8,128)S(1)} %get-tuple-element.36.refs_0_.refs_4_), channel_id=1, source_target_pairs={{0,2},{1,7},{2,0},{3,5},{4,6},{5,3},{6,4},{7,1},{8,10},{9,15},{10,... | collective-permute-start | bytes 786440 | tf_op jit(solution)/shard_map/ppermute | solution.py:341
  9.1 7.4 %collective-permute-start.3 = (f32[256,128]{1,0:T(8,128)S(1)}, f32[256,128]{1,0:T(8,128)S(1)}, u32[]{:S(2)}, u32[]{:S(2)}) collective-permute-start(f32[256,128]{1,0:T(8,128)S(1)} %get-tuple-element.37), channel_id=1, source_target_pairs={{0,4},{1,5},{2,6},{3,7},{4,0},{5,1},{6,2},{7,3},{8,12},{9,13},{10,... | collective-permute-start | bytes 393224 | tf_op jit(solution)/shard_map/ppermute | solution.py:341
  16.2 3.2 %collective-permute-start.2 = (f32[512,128]{1,0:T(8,128)S(1)}, f32[512,128]{1,0:T(8,128)S(1)}, u32[]{:S(2)}, u32[]{:S(2)}) collective-permute-start(f32[512,128]{1,0:T(8,128)S(1)} %collective-permute-done.1.refs_1_), channel_id=1, source_target_pairs={{0,1},{1,0},{2,3},{3,2},{4,5},{5,4},{6,7},{7,6},{8,9},{9,8},{10,11... | collective-permute-start | bytes 786440 | tf_op jit(solution)/shard_map/ppermute | solution.py:341
  16.6 2.8 %collective-permute-start.4 = (f32[256,128]{1,0:T(8,128)S(1)}, f32[256,128]{1,0:T(8,128)S(1)}, u32[]{:S(2)}, u32[]{:S(2)}) collective-permute-start(f32[256,128]{1,0:T(8,128)S(1)} %collective-permute-done.3.refs_3_), channel_id=1, source_target_pairs={{0,1},{1,0},{2,3},{3,2},{4,5},{5,4},{6,7},{7,6},{8,9},{9,8},{10,11... | collective-permute-start | bytes 393224 | tf_op jit(solution)/shard_map/ppermute | solution.py:341
  20.2 8.9 %collective-permute-start.5 = (f32[512,128]{1,0:T(8,128)S(1)}, f32[512,128]{1,0:T(8,128)S(1)}, u32[]{:S(2)}, u32[]{:S(2)}) collective-permute-start(f32[512,128]{1,0:T(8,128)S(1)} %get-tuple-element.38.refs_0_.refs_8_), channel_id=1, source_target_pairs={{0,8},{1,25},{2,10},{3,27},{4,12},{5,29},{6,14},{7,31},{8,0},{9,17... | collective-permute-start | bytes 786440 | tf_op jit(solution)/shard_map/ppermute | solution.py:341
  23.0 6.7 %collective-permute-start.7 = (f32[256,128]{1,0:T(8,128)S(1)}, f32[256,128]{1,0:T(8,128)S(1)}, u32[]{:S(2)}, u32[]{:S(2)}) collective-permute-start(f32[256,128]{1,0:T(8,128)S(1)} %get-tuple-element.39), channel_id=1, source_target_pairs={{0,16},{1,17},{2,18},{3,19},{4,20},{5,21},{6,22},{7,23},{8,24},{9,... | collective-permute-start | bytes 393224 | tf_op jit(solution)/shard_map/ppermute | solution.py:341
  29.1 4.1 %collective-permute-start.6 = (f32[512,128]{1,0:T(8,128)S(1)}, f32[512,128]{1,0:T(8,128)S(1)}, u32[]{:S(2)}, u32[]{:S(2)}) collective-permute-start(f32[512,128]{1,0:T(8,128)S(1)} %collective-permute-done.5.refs_1_), channel_id=1, source_target_pairs={{0,1},{1,0},{2,3},{3,2},{4,5},{5,4},{6,7},{7,6},{8,9},{9,8},{10,11... | collective-permute-start | bytes 786440 | tf_op jit(solution)/shard_map/ppermute | solution.py:341
  29.7 3.5 %collective-permute-start.8 = (f32[256,128]{1,0:T(8,128)S(1)}, f32[256,128]{1,0:T(8,128)S(1)}, u32[]{:S(2)}, u32[]{:S(2)}) collective-permute-start(f32[256,128]{1,0:T(8,128)S(1)} %collective-permute-done.7.refs_3_), channel_id=1, source_target_pairs={{0,1},{1,0},{2,3},{3,2},{4,5},{5,4},{6,7},{7,6},{8,9},{9,8},{10,11... | collective-permute-start | bytes 393224 | tf_op jit(solution)/shard_map/ppermute | solution.py:341
  34.0 10.4 %collective-permute-start.9 = (f32[512,128]{1,0:T(8,128)S(1)}, f32[512,128]{1,0:T(8,128)S(1)}, u32[]{:S(2)}, u32[]{:S(2)}) collective-permute-start(f32[512,128]{1,0:T(8,128)S(1)} %get-tuple-element.40.refs_0_.refs_1_), channel_id=1, source_target_pairs={{0,32},{1,97},{2,34},{3,99},{4,36},{5,101},{6,38},{7,103},{8,40},{... | collective-permute-start | bytes 786440 | tf_op jit(solution)/shard_map/ppermute | solution.py:341
  38.4 10.8 %collective-permute-start.11 = (f32[256,128]{1,0:T(8,128)S(1)}, f32[256,128]{1,0:T(8,128)S(1)}, u32[]{:S(2)}, u32[]{:S(2)}) collective-permute-start(f32[256,128]{1,0:T(8,128)S(1)} %get-tuple-element.52), channel_id=1, source_target_pairs={{0,64},{1,65},{2,66},{3,67},{4,68},{5,69},{6,70},{7,71},{8,72},{9,... | collective-permute-start | bytes 393224 | tf_op jit(solution)/shard_map/ppermute | solution.py:341
  44.4 6.2 %collective-permute-start.10 = (f32[512,128]{1,0:T(8,128)S(1)}, f32[512,128]{1,0:T(8,128)S(1)}, u32[]{:S(2)}, u32[]{:S(2)}) collective-permute-start(f32[512,128]{1,0:T(8,128)S(1)} %collective-permute-done.9.refs_1_), channel_id=1, source_target_pairs={{0,1},{1,0},{2,3},{3,2},{4,5},{5,4},{6,7},{7,6},{8,9},{9,8},{10,11... | collective-permute-start | bytes 786440 | tf_op jit(solution)/shard_map/ppermute | solution.py:341
  49.3 1.3 %collective-permute-start.12 = (f32[256,128]{1,0:T(8,128)S(1)}, f32[256,128]{1,0:T(8,128)S(1)}, u32[]{:S(2)}, u32[]{:S(2)}) collective-permute-start(f32[256,128]{1,0:T(8,128)S(1)} %collective-permute-done.11.refs_3_), channel_id=1, source_target_pairs={{0,1},{1,0},{2,3},{3,2},{4,5},{5,4},{6,7},{7,6},{8,9},{9,8},{10,11... | collective-permute-start | bytes 393224 | tf_op jit(solution)/shard_map/ppermute | solution.py:341
  51.4 5.1 %collective-permute-start.13 = (f32[96,128]{1,0:T(8,128)S(1)}, f32[96,128]{1,0:T(8,128)S(1)}, u32[]{:S(2)}, u32[]{:S(2)}) collective-permute-start(f32[96,128]{1,0:T(8,128)S(1)} %get-tuple-element.54), channel_id=1, source_target_pairs={{0,192},{1,193},{2,194},{3,195},{4,196},{5,197},{6,198},{7,199},{8... | collective-permute-start | bytes 147464 | tf_op jit(solution)/shard_map/ppermute | solution.py:368
  56.5 2.2 %collective-permute-start.14 = (f32[96,128]{1,0:T(8,128)S(1)}, f32[96,128]{1,0:T(8,128)S(1)}, u32[]{:S(2)}, u32[]{:S(2)}) collective-permute-start(f32[96,128]{1,0:T(8,128)S(1)} %collective-permute-done.13.refs_1_), channel_id=1, source_target_pairs={{0,1},{1,0},{2,3},{3,2},{4,5},{5,4},{6,7},{7,6},{8,9},{9,8},{10,11... | collective-permute-start | bytes 147464 | tf_op jit(solution)/shard_map/ppermute | solution.py:341
